TPU v7x, 256 devices: a whole 4x4x8 slice. The times are simulated.
256 devices in a mesh: section: 16 (over z, core), seq: 16 (over y, x).
Axes of the slice: x: 4, y: 4, z: 8, core: 2. Of those that a mesh axis runs over, the one named last changes fastest.
Arguments:
- features: bfloat16 [1, 2048, 5120], P(None, 'seq'), may hold values from -6 to 6
- references: bfloat16 [32, 128, 5120], P('section'), may hold values from -6 to 6
- classifier: bfloat16 [32, 5120, 10], P('section', 'seq'), may hold values from -0.078125 to 0.078125
- lengths: int32 [1], replicated, may hold values from 1024 to 2048
- labels: int32 [1], replicated, may hold values from 0 to 9
Outputs:
- logits: float32 [1, 10], replicated
- grad_features: float32 [1, 2048, 5120], P(None, 'seq', 'section')
- grad_references: float32 [32, 128, 5120], P('section', None, 'seq')
All inputs are finite; a program needn't handle non-finite values.
Results may differ from a plain program's by a relative error of at most 0.03.
Values may be sent and summed in bfloat16 or wider, within the bound.
No kernel may reach another device: no remote copies, remote signals or barrier semaphores. Data moves between devices by JAX's collectives and lax.ppermute only.
A program may use at most 64 MiB of HBM per device.

v0:
```python
import math

import jax
import jax.numpy as jnp
from jax import lax
from jax.sharding import PartitionSpec as P

P_SIZE = 128
ITERS = 3


temper = 1.5
epsilon = 1e-06
loss_scale = 65536.0
highest = lax.Precision.HIGHEST


def class_grads(logits, labels, batch):
    exps = jnp.exp(logits)
    probs = exps / jnp.sum(exps, axis=1, keepdims=True)
    onehot = (labels[:, None] == jnp.arange(logits.shape[1], dtype=jnp.int32)[None, :]).astype(
        jnp.float32
    )
    return loss_scale * (probs - onehot) / batch


def local(features, references, classifier, lengths, labels):
    batch, rows, width = features.shape
    heads = references.shape[0]
    score_scale = temper / math.sqrt(width)
    scores = (
        jnp.einsum("bnd,hpd->bnhp", features, references, preferred_element_type=jnp.float32)
        * score_scale
    )
    kernel = jnp.exp(scores)
    positions = lax.axis_index("seq") * rows + jnp.arange(rows, dtype=jnp.int32)
    alive = (positions[None, :] < lengths[:, None]).astype(jnp.float32)
    masses = alive / lengths[:, None].astype(jnp.float32)
    col_scales = [jnp.ones((batch, heads, P_SIZE), jnp.float32)]
    row_scales = []
    row_totals = []
    for iteration in range(ITERS):
        row_total = jnp.einsum("bnhp,bhp->bnh", kernel, col_scales[-1], precision=highest)
        row_scale = masses[:, :, None] / row_total
        col_total = lax.psum(
            jnp.einsum("bnhp,bnh->bhp", kernel, row_scale, precision=highest), "seq"
        )
        row_totals.append(row_total)
        row_scales.append(row_scale)
        col_scales.append(1.0 / (P_SIZE * col_total))
    row_scale = row_scales[-1]
    col_scale = col_scales[-1]
    plan_low = (row_scale[..., None] * kernel * col_scale[:, None]).astype(jnp.bfloat16)
    feature_cols = lax.all_to_all(features, "seq", split_axis=2, concat_axis=1, tiled=True)
    plan_all = lax.all_gather(plan_low, "seq", axis=1, tiled=True)
    pooled_raw = float(P_SIZE) * jnp.einsum(
        "bnd,bnhp->dbhp", feature_cols, plan_all, preferred_element_type=jnp.float32
    )
    square_sum = lax.psum(jnp.sum(pooled_raw * pooled_raw, axis=0), "seq")
    inverse_rms = lax.rsqrt(square_sum / width + epsilon)
    normed = pooled_raw * inverse_rms[None]
    pooled = jnp.mean(normed, axis=3)
    weights = classifier.astype(jnp.float32)
    partial_logits = jnp.einsum("dbh,hdc->bc", pooled, weights, precision=highest)
    logits = lax.psum(partial_logits, ("section", "seq"))
    grad_logits = class_grads(logits, labels, batch)
    grad_normed = jnp.einsum("bc,hdc->dbh", grad_logits, weights, precision=highest) / P_SIZE
    dual = lax.psum(jnp.sum(grad_normed[..., None] * normed, axis=0), "seq") / width
    grad_part = (inverse_rms[None] * (grad_normed[..., None] - normed * dual[None])).astype(
        jnp.bfloat16
    )
    grad_raw = lax.all_gather(grad_part, "seq", axis=0, tiled=True)
    grad_plan = float(P_SIZE) * jnp.einsum(
        "bnd,dbhp->bnhp", features, grad_raw, preferred_element_type=jnp.float32
    )
    grad_direct = float(P_SIZE) * jnp.einsum(
        "bnhp,dbhp->bnd", plan_low, grad_raw, preferred_element_type=jnp.float32
    )
    weighted = grad_plan * kernel
    grad_row = jnp.einsum("bnhp,bhp->bnh", weighted, col_scale, precision=highest)
    col_part = jnp.einsum("bnhp,bnh->bhp", weighted, row_scale, precision=highest)
    grad_kernel = row_scale[..., None] * col_scale[:, None] * grad_plan
    for iteration in reversed(range(ITERS)):
        grad_col = lax.psum(col_part, "seq")
        grad_total = -float(P_SIZE) * col_scales[iteration + 1] ** 2 * grad_col
        grad_row = grad_row + jnp.einsum("bnhp,bhp->bnh", kernel, grad_total, precision=highest)
        grad_kernel = grad_kernel + row_scales[iteration][..., None] * grad_total[:, None]
        grad_rowsum = -grad_row * row_scales[iteration] / row_totals[iteration]
        grad_kernel = grad_kernel + grad_rowsum[..., None] * col_scales[iteration][:, None]
        if iteration > 0:
            col_part = jnp.einsum("bnhp,bnh->bhp", kernel, grad_rowsum, precision=highest)
            grad_row = jnp.zeros_like(grad_row)
    grad_scores = (score_scale * grad_kernel * kernel).astype(jnp.bfloat16)
    grad_local = grad_direct + jnp.einsum(
        "bnhp,hpd->bnd", grad_scores, references, preferred_element_type=jnp.float32
    )
    grad_features = lax.psum_scatter(
        grad_local.astype(jnp.bfloat16), "section", scatter_dimension=2, tiled=True
    ).astype(jnp.float32)
    scores_all = lax.all_gather(grad_scores, "seq", axis=1, tiled=True)
    ref_part = jnp.einsum(
        "bnhp,bnd->dhp", scores_all, feature_cols, preferred_element_type=jnp.float32
    )
    grad_references = jnp.transpose(ref_part, (1, 2, 0))
    return (logits, grad_features, grad_references)


def solution(mesh):
    in_specs = (P(None, "seq", None), P("section", None, None), P("section", "seq", None), P(), P())
    out_specs = (P(), P(None, "seq", "section"), P("section", None, "seq"))
    return jax.shard_map(local, mesh=mesh, in_specs=in_specs, out_specs=out_specs, check_vma=False)
```

profile of v0, /device:TPU:12, one launch (start us, length us, event | category | flops | bytes accessed | tf_op | source)
XLA Modules:
  0.0 629.9 jit_solution(5600737604057530855)
XLA Ops:
  8.1 0.9 copy-done
  8.9 2.3 fusion.13
  11.8 30.2 %psum.63 = f32[1,2,128]{2,1,0:T(2,128)S(1)} all-reduce(f32[1,2,128]{2,1,0:T(2,128)S(1)} %bitcast.278), channel_id=1, replica_groups=mesh['section'=16,'seq'=16] {'seq'}, use_global_device_ids=true, to_apply=%region_0.0 | all-reduce | flops 256 | bytes 2048 | tf_op jit(solution)/shard_map/psum | solution.py:45
  42.6 35.4 %psum.64 = f32[1,2,128]{2,1,0:T(2,128)S(1)} all-reduce(f32[1,2,128]{2,1,0:T(2,128)S(1)} %bitcast.279), channel_id=1, replica_groups=mesh['section'=16,'seq'=16] {'seq'}, use_global_device_ids=true, to_apply=%region_1.0 | all-reduce | flops 256 | bytes 2048 | tf_op jit(solution)/shard_map/psum | solution.py:45
  78.6 38.3 %psum.65 = f32[1,2,128]{2,1,0:T(2,128)S(1)} all-reduce(f32[1,2,128]{2,1,0:T(2,128)S(1)} %bitcast.284), channel_id=1, replica_groups=mesh['section'=16,'seq'=16] {'seq'}, use_global_device_ids=true, to_apply=%region_2.0 | all-reduce | flops 256 | bytes 2048 | tf_op jit(solution)/shard_map/psum | solution.py:45
  117.8 6.3 copy.17
  124.5 30.0 %reduce.5 = bf16[5120,128]{1,0:T(8,128)(2,1)} reduce(bf16[5120,1,128]{2,1,0:T(2,128)(2,1)} %bitcast.248, bf16[]{:T(256)} %broadcast.175), dimensions={1}, to_apply=%bitcast.205.reduce_sub_computation | reduce | bytes 2621442
  154.5 4.1 reshape.282
  158.5 14.1 %all-to-all-start = ((bf16[16,2,20480]{2,1,0:T(2,128)(2,1)}), bf16[16,2,20480]{2,1,0:T(2,128)(2,1)}, u32[]{:S(2)}, u32[]{:S(2)}) async-start(bf16[16,2,20480]{2,1,0:T(2,128)(2,1)} %reshape.282), calls=%async_computation | async-start | bytes 2621440 | tf_op jit(solution)/shard_map/all_to_all | solution.py:54
  173.3 11.0 %all-to-all-done = bf16[16,2,20480]{2,1,0:T(2,128)(2,1)} async-done(((bf16[16,2,20480]{2,1,0:T(2,128)(2,1)}), bf16[16,2,20480]{2,1,0:T(2,128)(2,1)}, u32[]{:S(2)}, u32[]{:S(2)}) %all-to-all-start) | async-done | bytes 1310752 | tf_op jit(solution)/shard_map/all_to_all | solution.py:54
  184.3 6.1 reshape.283
  190.3 1.9 copy.54
  192.3 1.9 copy.18
  194.2 3.2 reshape.258
  197.4 2.1 multiply_reduce_fusion
  199.6 30.5 %psum.66 = f32[1,2,128]{2,1,0:T(2,128)S(1)} all-reduce(f32[1,2,128]{2,1,0:T(2,128)S(1)} %bitcast.291), channel_id=1, replica_groups=mesh['section'=16,'seq'=16] {'seq'}, use_global_device_ids=true, to_apply=%region_4.0 | all-reduce | flops 256 | bytes 2048 | tf_op jit(solution)/shard_map/psum | solution.py:59
  230.4 83.7 %psum.67 = f32[1,10]{1,0:T(1,128)S(1)} all-reduce(f32[1,10]{1,0:T(1,128)S(1)} %convolution_bitcast_fusion.3), channel_id=1, replica_groups=mesh['section'=16,'seq'=16] {'section','seq'}, use_global_device_ids=true, to_apply=%region_6.0 | all-reduce | flops 10 | bytes 80 | tf_op jit(solution)/shard_map/psum | solution.py:65
  315.8 31.5 %psum.68 = f32[1,2,128]{2,1,0:T(2,128)S(1)} all-reduce(f32[1,2,128]{2,1,0:T(2,128)S(1)} %bitcast.285), channel_id=1, replica_groups=mesh['section'=16,'seq'=16] {'seq'}, use_global_device_ids=true, to_apply=%region_9.0 | all-reduce | flops 256 | bytes 2048 | tf_op jit(solution)/shard_map/psum | solution.py:68
  348.4 50.6 %all-gather.6.cloned.1.call-done = bf16[5120,1,2,128]{3,0,2,1:T(8,128)(2,1)} async-done(((bf16[320,1,2,128]{3,0,2,1:T(8,128)(2,1)}), bf16[5120,1,2,128]{3,0,2,1:T(8,128)(2,1)}) %all-gather.6.cloned.1.call-update) | async-done | bytes 2621456 | tf_op jit(solution)/shard_map/all_gather | solution.py:72
  399.0 2.7 fusion.21
  402.2 31.8 %psum.69 = f32[1,2,128]{2,1,0:T(2,128)S(1)} all-reduce(f32[1,2,128]{2,1,0:T(2,128)S(1)} %bitcast.277), channel_id=1, replica_groups=mesh['section'=16,'seq'=16] {'seq'}, use_global_device_ids=true, to_apply=%region_10.0 | all-reduce | flops 256 | bytes 2048 | tf_op jit(solution)/shard_map/psum | solution.py:84
  434.5 33.6 %psum.70 = f32[1,2,128]{2,1,0:T(2,128)S(1)} all-reduce(f32[1,2,128]{2,1,0:T(2,128)S(1)} %bitcast.286), channel_id=1, replica_groups=mesh['section'=16,'seq'=16] {'seq'}, use_global_device_ids=true, to_apply=%region_11.0 | all-reduce | flops 256 | bytes 2048 | tf_op jit(solution)/shard_map/psum | solution.py:84
  468.8 38.1 %psum.71 = f32[1,2,128]{2,1,0:T(2,128)S(1)} all-reduce(f32[1,2,128]{2,1,0:T(2,128)S(1)} %bitcast.287), channel_id=1, replica_groups=mesh['section'=16,'seq'=16] {'seq'}, use_global_device_ids=true, to_apply=%region_12.0 | all-reduce | flops 256 | bytes 2048 | tf_op jit(solution)/shard_map/psum | solution.py:84
  507.2 0.9 multiply_convert_fusion
  508.2 1.5 convolution_bitcast_fusion
  510.0 2.1 fusion.3
  512.1 6.3 copy.52
  518.4 3.0 copy.64
  521.4 38.5 %all-gather.10.cloned.1.call-done = bf16[2048,2,128]{2,0,1:T(8,128)(2,1)} async-done(((bf16[128,2,128]{2,0,1:T(8,128)(2,1)}), bf16[2048,2,128]{2,0,1:T(8,128)(2,1)}) %all-gather.10.cloned.1.call-update) | async-done | bytes 1048592 | tf_op jit(solution)/shard_map/all_gather | solution.py:100
  559.9 2.8 fusion.61
  562.8 58.7 %reduce-scatter.4.cloned.1.call-done = bf16[320,128]{1,0:T(8,128)(2,1)} async-done(((bf16[5120,128]{1,0:T(8,128)(2,1)}), bf16[320,128]{1,0:T(8,128)(2,1)}) %reduce-scatter.4.cloned.1.call-update) | async-done | bytes 81936
  621.4 1.0 reshape_bitcast_fusion
  (66 shorter events, 9.4 us)
Async XLA Ops:
  7.2 1.8 copy-start
  7.2 190.2 %all-gather.8.cloned.1.call-start = ((), (), s32[]{:S(2)}) async-start(), calls=%async_computation.3 | async-start | bytes 1114112 | tf_op jit(solution)/shard_map/all_gather | solution.py:55
  158.5 25.7 %all-to-all-start = ((bf16[16,2,20480]{2,1,0:T(2,128)(2,1)}), bf16[16,2,20480]{2,1,0:T(2,128)(2,1)}, u32[]{:S(2)}, u32[]{:S(2)}) async-start(bf16[16,2,20480]{2,1,0:T(2,128)(2,1)} %reshape.282), calls=%async_computation | async-start | bytes 2621440 | tf_op jit(solution)/shard_map/all_to_all | solution.py:54
  172.6 226.4 %all-gather.6.cloned.1.call-start = ((), (), s32[]{:S(2)}) async-start(), calls=%async_computation.2 | async-start | bytes 2785280 | tf_op jit(solution)/shard_map/all_gather | solution.py:72
  194.2 36.1 %copy-start.3 = (bf16[2,320,10]{1,0,2:T(2,128)(2,1)S(1)}, bf16[2,320,10]{1,0,2:T(2,128)(2,1)}, u32[]{:S(2)}) copy-start(bf16[2,320,10]{1,0,2:T(2,128)(2,1)} %param.7) | copy-start | bytes 38404
  314.1 87.8 %copy-start.4 = (f32[1,10]{1,0:T(1,128)}, f32[1,10]{1,0:T(1,128)S(1)}, u32[]{:S(2)}) copy-start(f32[1,10]{1,0:T(1,128)S(1)} %psum.67) | copy-start | bytes 124
  348.1 211.8 %all-gather.10.cloned.1.call-start = ((), (), s32[]{:S(2)}) async-start(), calls=%async_computation.4 | async-start | bytes 1114112 | tf_op jit(solution)/shard_map/all_gather | solution.py:100
  508.2 1.6 copy-start.2
  508.2 113.3 %reduce-scatter.4.cloned.1.call-start = ((), (), s32[]{:S(2)}) async-start(), calls=%async_computation.5 | async-start | bytes 1392640
  508.2 1.8 copy-start.1
Sparse Core Ops, SparseCore 0:
  117.9 53.0 all-gather.7
  348.2 50.7 all-gather.5
  508.3 51.5 all-gather.9
  562.3 59.0 reduce-scatter.3
where the time goes:
time: 631 us; the launch traced here: 630 us
  blocking collectives  353 us (56%)
  waiting for transfers between devices  159 us (25%)
  local copies, waits for them, and re-layouts  36.2 us (6%)
  other arithmetic  33.7 us (5%)
  matrix products  18.1 us (3%)
  between operations  15.4 us (2%)
  starting transfers between devices  14.4 us (2%)
    psum x3, blocking collectives, local(): lax.psum(jnp.einsum('bnhp,bnh->bhp', kernel, row_scale, precision=highest...  104 us
    psum x3, blocking collectives, local(): grad_col = lax.psum(col_part, 'seq')  104 us
    psum x1, blocking collectives, local(): logits = lax.psum(partial_logits, ('section', 'seq'))  83.7 us
    unnamed x5, waiting for transfers between devices  58.7 us
    all_gather x1, waiting for transfers between devices, local(): grad_raw = lax.all_gather(grad_part, 'seq', axis=0, tiled=True)  50.6 us
    all_gather x1, waiting for transfers between devices, local(): scores_all = lax.all_gather(grad_scores, 'seq', axis=1, tiled=True)  38.5 us
    psum x1, blocking collectives, local(): lax.psum(jnp.sum(grad_normed[..., None] * normed, axis=0), 'seq') / width  31.5 us
    unnamed x20, local copies, waits for them, and re-layouts  31.1 us
  transfers between devices with their start and end apart: 5, of which 4 were waited for; matrix products, arithmetic and copies ran while one was open for 11% of the time, Pallas kernels for 0%

commit v1 on v0

v1 whole, which is shorter than its diff:
```python
import functools
import math

import jax
import jax.numpy as jnp
from jax import lax
from jax.experimental import pallas as pl
from jax.experimental.pallas import tpu as pltpu
from jax.sharding import Mesh, PartitionSpec as P

P_SIZE = 128
ITERS = 3
CLASSES = 10
PAD = 16

temper = 1.5
epsilon = 1e-06
loss_scale = 65536.0
f32 = jnp.float32
bf16 = jnp.bfloat16

SIDE = 4
DEPTH = 8
BLOCKS = SIDE * SIDE
ORDER = (0, 1, 3, 2)
VMEM = pl.BlockSpec(memory_space=pltpu.VMEM)
SMEM = pl.BlockSpec(memory_space=pltpu.SMEM)
NT = (((1,), (1,)), ((), ()))
TN = (((0,), (0,)), ((), ()))


def params():
    return pltpu.CompilerParams(vmem_limit_bytes=40 * 1024 * 1024)


def block_of(s):
    y = lax.rem(lax.axis_index("y") + ORDER[s // SIDE], SIDE)
    x = lax.rem(lax.axis_index("x") + ORDER[s % SIDE], SIDE)
    return y * SIDE + x


def shift(value, axis, size, step):
    return lax.ppermute(value, axis, [(i, (i - step) % size) for i in range(size)])


def gather(value):
    row = jnp.stack([value] + [shift(value, "x", SIDE, k) for k in ORDER[1:]])
    return [row] + [shift(row, "y", SIDE, k) for k in ORDER[1:]]


def split_kernel(f_ref, slices_ref, half_ref):
    core = lax.axis_index("core")
    rows, part = slices_ref.shape[1:]
    for j in range(DEPTH):
        pair = f_ref[:, 2 * part * j : 2 * part * (j + 1)]
        slices_ref[2 * j] = pair[:, :part]
        slices_ref[2 * j + 1] = pair[:, part:]
    start = pl.multiple_of(core * (rows // 2), rows // 2)
    for j in range(BLOCKS):
        half_ref[j] = slices_ref[j, pl.ds(start, rows // 2), :]


def scores_kernel(scale, f_ref, r_ref, k_ref):
    scores = lax.dot_general(r_ref[...], f_ref[...], NT, preferred_element_type=f32)
    k_ref[...] = jnp.exp(scores * scale).astype(bf16)


def forward_kernel(
    q0, q1, q2, q3, mine_ref, other_ref, wt_ref, len_ref, r_ref, rs_ref, rt_ref, col_ref, fc_ref, p0_ref, plan_ref
):
    q = (q0, q1, q2, q3)
    core = lax.axis_index("core")
    length = len_ref[0]
    rows = q0.shape[2]
    mass = 1.0 / (jnp.zeros((1, rows), jnp.int32) + length).astype(f32)
    lane = lax.broadcasted_iota(jnp.int32, (1, rows), 1)
    masses = [jnp.where(block_of(s) * rows + lane < length, mass, 0.0) for s in range(BLOCKS)]
    half = rows // 2
    for s in range(BLOCKS):
        where = block_of(s)
        fc_ref[pl.ds(pl.multiple_of(s * rows + core * half, half), half), :] = mine_ref[where]
        fc_ref[pl.ds(pl.multiple_of(s * rows + (1 - core) * half, half), half), :] = other_ref[where]
    for t in range(ITERS):
        for h in range(2):
            here = slice(h * P_SIZE, (h + 1) * P_SIZE)
            acc = jnp.zeros((P_SIZE, rows), f32)
            for s in range(BLOCKS):
                k = q[s // SIDE][s % SIDE, here, :].astype(f32)
                weighted = k if t == 0 else k * col_ref[t - 1, here, :]
                total = jnp.sum(weighted, axis=0, keepdims=True)
                scale = masses[s] / total
                place = (t * 2 + h) * BLOCKS + s
                rt_ref[place : place + 1, :] = total
                rs_ref[place : place + 1, :] = scale
                acc = acc + k * scale
            col = 1.0 / (float(P_SIZE) * jnp.sum(acc, axis=1, keepdims=True))
            col_ref[t, here, :] = jnp.broadcast_to(col, (P_SIZE, rows))
    for h in range(2):
        here = slice(h * P_SIZE, (h + 1) * P_SIZE)
        for s in range(BLOCKS):
            k = q[s // SIDE][s % SIDE, here, :].astype(f32)
            place = ((ITERS - 1) * 2 + h) * BLOCKS + s
            plan = (rs_ref[place : place + 1, :] * k * col_ref[ITERS - 1, here, :]).astype(bf16)
            plan_ref[here, s * rows : (s + 1) * rows] = plan
            if s == 0:
                p0_ref[here, :] = plan
    raw = jnp.dot(plan_ref[...], fc_ref[...], preferred_element_type=f32)
    r_ref[: 2 * P_SIZE, :] = (float(P_SIZE) * raw).astype(bf16)
    r_ref[2 * P_SIZE :, :] = wt_ref[...]


def pooled_kernel(width, r0, r1, r2, r3, f_ref, t_ref, m_ref, inv_ref, logit_ref):
    r = (r0, r1, r2, r3)
    heads = 2 * P_SIZE
    rows = f_ref.shape[1]
    acc = jnp.zeros((r0.shape[1], rows), f32)
    for s in range(BLOCKS):
        acc = acc + lax.dot_general(
            r[s // SIDE][s % SIDE], f_ref[block_of(s)], NT, preferred_element_type=f32
        )
    t_ref[:heads, :] = acc[:heads].astype(bf16)
    high = acc[heads:].astype(bf16)
    t_ref[heads : heads + 2 * PAD, :] = high
    t_ref[heads + 2 * PAD :, :] = (acc[heads:] - high.astype(f32)).astype(bf16)
    logits = jnp.zeros((1, PAD), f32)
    for h in range(2):
        here = slice(h * P_SIZE, (h + 1) * P_SIZE)
        squares = jnp.zeros((P_SIZE, 1), f32)
        m = jnp.zeros((P_SIZE, PAD), f32)
        for s in range(BLOCKS):
            block = r[s // SIDE][s % SIDE, here, :]
            weights = r[s // SIDE][s % SIDE, heads + h * PAD : heads + (h + 1) * PAD, :]
            m = m + lax.dot_general(block, weights, NT, preferred_element_type=f32)
            wide = block.astype(f32)
            squares = squares + jnp.sum(wide * wide, axis=1, keepdims=True)
        inverse = lax.rsqrt(squares / width + epsilon)
        m_ref[here, :] = m
        inv_ref[here, :] = jnp.broadcast_to(inverse, (P_SIZE, inv_ref.shape[1]))
        logits = logits + jnp.sum(inverse * m, axis=0, keepdims=True) / P_SIZE
    logit_ref[...] = logits


def class_grads(logits, label):
    lane = lax.broadcasted_iota(jnp.int32, logits.shape, 1)
    exps = jnp.where(lane < CLASSES, jnp.exp(logits), 0.0)
    probs = exps / jnp.sum(exps, axis=1, keepdims=True)
    grads = loss_scale * (probs - (lane == label).astype(f32))
    square = (PAD, PAD)
    diagonal = lax.broadcasted_iota(jnp.int32, square, 0) == lax.broadcasted_iota(jnp.int32, square, 1)
    column = jnp.sum(jnp.where(diagonal, grads, 0.0), axis=1, keepdims=True)
    return grads, column


def raw_kernel(width, r0, r1, r2, r3, m_ref, inv_ref, logit_ref, label_ref, out_ref):
    r = (r0, r1, r2, r3)
    heads = 2 * P_SIZE
    grads, column = class_grads(logit_ref[...], label_ref[0])
    for h in range(2):
        here = slice(h * P_SIZE, (h + 1) * P_SIZE)
        inverse = inv_ref[here, :1]
        dual = inverse * jnp.sum(grads * m_ref[here, :], axis=1, keepdims=True) / (P_SIZE * width)
        for s in range(BLOCKS):
            block = r[s // SIDE][s % SIDE, here, :].astype(f32)
            weights = r[s // SIDE][s % SIDE, heads + h * PAD : heads + (h + 1) * PAD, :].astype(f32)
            normed = jnp.sum(column * weights, axis=0, keepdims=True) / P_SIZE
            out_ref[block_of(s), here, :] = (inverse * (normed - block * (inverse * dual))).astype(bf16)


def backward_kernel(
    width, score_scale,
    q0, q1, q2, q3, t0, t1, t2, t3, rs_ref, rt_ref, col_ref, m_ref, inv_ref, logit_ref, label_ref,
    gs_ref, gs0_ref, gt_ref, grs_ref, u_ref,
):
    q = (q0, q1, q2, q3)
    tt = (t0, t1, t2, t3)
    heads = 2 * P_SIZE
    rows = q0.shape[2]
    size = float(P_SIZE)
    grads, column = class_grads(logit_ref[...], label_ref[0])
    for h in range(2):
        here = slice(h * P_SIZE, (h + 1) * P_SIZE)
        inverse = inv_ref[here, :]
        dual = inverse * (jnp.sum(grads * m_ref[here, :], axis=1, keepdims=True) / (size * width))
        first = size * inverse
        second = first * inverse * dual

        def load(s):
            return q[s // SIDE][s % SIDE, here, :].astype(f32)

        def grad_plan(s, u):
            return first * u - second * tt[s // SIDE][s % SIDE, here, :].astype(f32)

        def row(ref, t, s):
            place = (t * 2 + h) * BLOCKS + s
            return ref[place : place + 1, :]

        def put(ref, t, s, value):
            place = (t * 2 + h) * BLOCKS + s
            ref[place : place + 1, :] = value

        acc = jnp.zeros((P_SIZE, rows), f32)
        for s in range(BLOCKS):
            low = heads + h * PAD
            v = tt[s // SIDE][s % SIDE, low : low + PAD, :].astype(f32)
            v = v + tt[s // SIDE][s % SIDE, low + 2 * PAD : low + 3 * PAD, :].astype(f32)
            u = jnp.sum(column * v, axis=0, keepdims=True) / size
            put(u_ref, 0, s, u)
            weighted = grad_plan(s, u) * load(s)
            put(grs_ref, ITERS - 1, s, jnp.sum(weighted * col_ref[ITERS - 1, here, :], axis=0, keepdims=True))
            acc = acc + weighted * row(rs_ref, ITERS - 1, s)
        for t in reversed(range(ITERS)):
            grad_col = jnp.sum(acc, axis=1, keepdims=True)
            grad_total = -size * col_ref[t, here, :] ** 2 * grad_col
            gt_ref[t] = grad_total
            acc = jnp.zeros((P_SIZE, rows), f32)
            for s in range(BLOCKS):
                k = load(s)
                grad_row = jnp.sum(k * gt_ref[t], axis=0, keepdims=True)
                if t == ITERS - 1:
                    grad_row = grad_row + row(grs_ref, t, s)
                grad_rowsum = -grad_row * row(rs_ref, t, s) / row(rt_ref, t, s)
                put(grs_ref, t, s, grad_rowsum)
                if t > 0:
                    acc = acc + k * grad_rowsum
        for s in range(BLOCKS):
            total = row(rs_ref, ITERS - 1, s) * col_ref[ITERS - 1, here, :] * grad_plan(s, row(u_ref, 0, s))
            for t in range(ITERS):
                total = total + row(rs_ref, t, s) * gt_ref[t]
                if t > 0:
                    total = total + row(grs_ref, t, s) * col_ref[t - 1, here, :]
                else:
                    total = total + row(grs_ref, t, s)
            value = (score_scale * total * load(s)).astype(bf16)
            gs_ref[here, s * rows : (s + 1) * rows] = value
            if s == 0:
                gs0_ref[here, :] = value


def features_kernel(p0_ref, gs_ref, refs_ref, raw_ref, out_ref):
    j = pl.program_id(0)
    core = lax.axis_index("core")
    z = lax.axis_index("z")
    part = raw_ref.shape[2]
    pair = lax.dot_general(gs_ref[...], refs_ref[...], TN, preferred_element_type=f32)
    place = 2 * lax.rem(j // 2 + 4 - z // 2, 4) + lax.rem(j + z, 2)
    for side in range(2):
        direct = lax.dot_general(p0_ref[...], raw_ref[side], TN, preferred_element_type=f32)
        value = pair[:, side * part : (side + 1) * part] + float(P_SIZE) * direct
        out_ref[lax.rem(core + side, 2), place] = value.astype(bf16)


def reduce_sections(parts):
    other = lax.ppermute(parts[1], "core", [(0, 1), (1, 0)])
    both = (parts[0].astype(f32) + other.astype(f32)).astype(bf16)
    total = both[:2].astype(f32)
    for k in (2, 3, 1):
        total = total + shift(both[2 * k : 2 * k + 2], "z", DEPTH, -2 * k).astype(f32)
    away = lax.ppermute(total[1].astype(bf16), "z", [(i, i ^ 1) for i in range(DEPTH)])
    return total[0] + away.astype(f32)


def sum_logits(part):
    total = part + lax.ppermute(part, "core", [(0, 1), (1, 0)])
    for k in (1, 2, 4):
        total = total + lax.ppermute(total, "z", [(i, i ^ k) for i in range(DEPTH)])
    return total


def local(features, references, classifier, lengths, labels):
    batch, rows, width = features.shape
    heads = references.shape[0] * P_SIZE
    part = width // BLOCKS
    score_scale = temper / math.sqrt(width)
    feats = features.reshape(rows, width)
    refs = references.reshape(heads, width)
    kind = jax.ShapeDtypeStruct

    slices, half = pl.pallas_call(
        split_kernel,
        out_shape=[kind((BLOCKS, rows, part), bf16), kind((BLOCKS, rows // 2, part), bf16)],
        in_specs=[VMEM], out_specs=[VMEM, VMEM], compiler_params=params(), name="split",
    )(feats)
    kernel = pl.pallas_call(
        functools.partial(scores_kernel, score_scale),
        out_shape=kind((heads, rows), bf16),
        in_specs=[VMEM, VMEM], out_specs=VMEM, compiler_params=params(), name="scores",
    )(feats, refs)
    mine = lax.all_to_all(half, ("y", "x"), 0, 0)
    other = lax.ppermute(mine, "core", [(0, 1), (1, 0)])
    weights = jnp.pad(jnp.transpose(classifier, (0, 2, 1)), ((0, 0), (0, PAD - CLASSES), (0, 0)))
    weights = weights.reshape(2 * PAD, part)
    q = gather(kernel)
    raw, rs, rt, col, cols, p0 = pl.pallas_call(
        forward_kernel,
        out_shape=[
            kind((heads + 2 * PAD, part), bf16),
            kind((ITERS * 2 * BLOCKS, rows), f32),
            kind((ITERS * 2 * BLOCKS, rows), f32),
            kind((ITERS, heads, rows), f32),
            kind((BLOCKS * rows, part), bf16),
            kind((heads, rows), bf16),
        ],
        in_specs=[VMEM] * 7 + [SMEM], out_specs=[VMEM] * 6,
        scratch_shapes=[pltpu.VMEM((heads, BLOCKS * rows), bf16)],
        compiler_params=params(), name="forward",
    )(*q, mine, other, weights, lengths)
    r = gather(raw)
    t, m, inverse, logit_part = pl.pallas_call(
        functools.partial(pooled_kernel, width),
        out_shape=[
            kind((heads + 4 * PAD, rows), bf16),
            kind((heads, PAD), f32),
            kind((heads, rows), f32),
            kind((1, PAD), f32),
        ],
        in_specs=[VMEM] * 5, out_specs=[VMEM] * 4, compiler_params=params(), name="pooled",
    )(*r, slices)
    logits = sum_logits(logit_part)
    ts = gather(t)
    grad_raw = pl.pallas_call(
        functools.partial(raw_kernel, width),
        out_shape=kind((BLOCKS, heads, part), bf16),
        in_specs=[VMEM] * 7 + [SMEM], out_specs=VMEM, compiler_params=params(), name="grad_raw",
    )(*r, m, inverse, logits, labels)
    grad_scores, gs0 = pl.pallas_call(
        functools.partial(backward_kernel, width, score_scale),
        out_shape=[kind((heads, BLOCKS * rows), bf16), kind((heads, rows), bf16)],
        in_specs=[VMEM] * 14 + [SMEM], out_specs=[VMEM, VMEM],
        scratch_shapes=[
            pltpu.VMEM((ITERS, P_SIZE, rows), f32),
            pltpu.VMEM((ITERS * 2 * BLOCKS, rows), f32),
            pltpu.VMEM((2 * BLOCKS, rows), f32),
        ],
        compiler_params=params(), name="backward",
    )(*q, *ts, rs, rt, col, m, inverse, logits, labels)
    parts = pl.pallas_call(
        features_kernel,
        grid=(DEPTH,),
        out_shape=kind((2, DEPTH, rows, part), bf16),
        in_specs=[
            pl.BlockSpec((heads, rows), lambda j: (0, 0)),
            pl.BlockSpec((heads, rows), lambda j: (0, 0)),
            pl.BlockSpec((heads, 2 * part), lambda j: (0, j)),
            pl.BlockSpec((2, heads, part), lambda j: (j, 0, 0)),
        ],
        out_specs=pl.BlockSpec((2, DEPTH, rows, part), lambda j: (0, 0, 0, 0)),
        compiler_params=params(), name="features",
    )(p0, gs0, refs, grad_raw)
    grad_features = reduce_sections(parts)
    grad_references = jnp.dot(grad_scores, cols, preferred_element_type=f32)
    return (
        logits[:, :CLASSES],
        grad_features.reshape(batch, rows, part),
        grad_references.reshape(references.shape[0], P_SIZE, part),
    )


def solution(mesh):
    grid = Mesh(mesh.devices.reshape(DEPTH, 2, SIDE, SIDE), ("z", "core", "y", "x"))
    section, seq = ("z", "core"), ("y", "x")
    in_specs = (P(None, seq, None), P(section, None, None), P(section, seq, None), P(), P())
    out_specs = (P(), P(None, seq, section), P(section, None, seq))
    return jax.shard_map(local, mesh=grid, in_specs=in_specs, out_specs=out_specs, check_vma=False)
```

time: 631 us -> 186 us (0.29)
  blocking collectives: 353 us -> 18.1 us
  waiting for transfers between devices: 159 us -> 79.3 us
  starting transfers between devices: 14.4 us -> 57.9 us
  other arithmetic: 33.7 us -> 1.76 us
  local copies, waits for them, and re-layouts: 36.2 us -> 8.6 us
  matrix products: 18.1 us -> 0.72 us
  Pallas kernels: 0 us -> 15.7 us
  between operations: 15.4 us -> 2.14 us
    psum x9 -> x0, blocking collectives: 353 us -> none  [the longest x3 104 us: local(): lax.psum(jnp.einsum('bnhp,bnh->bhp', kernel, row_scale, precision=highest...]
    all_gather x3 -> x0, waiting for transfers between devices: 89.1 us -> none  [the longest x1 50.6 us: local(): grad_raw = lax.all_gather(grad_part, 'seq', axis=0, tiled=True)]
    ppermute x0 -> x28, waiting for transfers between devices: none -> 79.3 us  [the longest x21 70.6 us: shift(): lax.ppermute(value, axis, [(i, (i - step) % size) for i in range(size)])]
    unnamed x5 -> x0, waiting for transfers between devices: 58.7 us -> none
    ppermute x0 -> x28, starting transfers between devices: none -> 57.9 us  [the longest x21 40.3 us: shift(): lax.ppermute(value, axis, [(i, (i - step) % size) for i in range(size)])]
    unnamed x1 -> x0, other arithmetic: 30 us -> none
    unnamed x20 -> x14, local copies, waits for them, and re-layouts: 31.1 us -> 2.27 us
    all_to_all x0 -> x1, blocking collectives: none -> 18.1 us  [local(): mine = lax.all_to_all(half, ('y', 'x'), 0, 0)]
  transfers between devices with their start and end apart: 5 -> 28, of which waited for: 4 -> 21; matrix products, arithmetic and copies ran while one was open for 11% -> 1% of each run, Pallas kernels for 0% -> 1%
where the time goes in v1:
time: 186 us; the launch traced here: 184 us
  waiting for transfers between devices  79.3 us (43%)
  starting transfers between devices  57.9 us (31%)
  blocking collectives  18.1 us (10%)
  Pallas kernels  15.7 us (8%)
  local copies, waits for them, and re-layouts  8.6 us (5%)
  between operations  2.14 us (1%)
    ppermute x21, waiting for transfers between devices, shift(): lax.ppermute(value, axis, [(i, (i - step) % size) for i in range(size)])  70.6 us
    ppermute x21, starting transfers between devices, shift(): lax.ppermute(value, axis, [(i, (i - step) % size) for i in range(size)])  40.3 us
    all_to_all x1, blocking collectives, local(): mine = lax.all_to_all(half, ('y', 'x'), 0, 0)  18.1 us
    ppermute x3, starting transfers between devices, sum_logits(): total = total + lax.ppermute(total, 'z', [(i, i ^ k) for i in range(DEPTH)])  12 us
    ppermute x1, starting transfers between devices, reduce_sections(): lax.ppermute(total[1].astype(bf16), 'z', [(i, i ^ 1) for i in range(DEPTH)])  5.58 us
    pallas_call x1, Pallas kernels, local(): pl.pallas_call(features_kernel, grid=(DEPTH,), out_shape=kind((2, DEPTH,...  4.23 us
    ppermute x3, waiting for transfers between devices, sum_logits(): total = total + lax.ppermute(total, 'z', [(i, i ^ k) for i in range(DEPTH)])  3.99 us
    pallas_call x1, Pallas kernels, local(): pl.pallas_call(functools.partial(backward_kernel, width, score_scale), ou...  3.91 us
  transfers between devices with their start and end apart: 28, of which 21 were waited for; matrix products, arithmetic and copies ran while one was open for 1% of the time, Pallas kernels for 1%

profile of v1, /device:TPU:12, one launch (start us, length us, event | category | flops | bytes accessed | tf_op | source)
XLA Modules:
  0.0 184.2 jit_solution(9675409685606678671)
XLA Ops:
  2.6 18.1 %all_to_all.5.mine_ref = bf16[16,64,320]{2,1,0:T(8,128)(2,1)S(1)} all-to-all(bf16[16,64,320]{2,1,0:T(8,128)(2,1)S(1)} %get-tuple-element.17), channel_id=1, replica_groups=mesh['z'=8,'core'=2,'y'=4,'x'=4] {'y','x'}, dimensions={0} | all-to-all | bytes 1310720 | tf_op jit(solution)/shard_map/all_to_all | solution.py:288
  25.4 2.6 %collective-permute-done.2 = bf16[256,128]{1,0:T(8,128)(2,1)S(1)} collective-permute-done((bf16[256,128]{1,0:T(8,128)(2,1)S(1)}, bf16[256,128]{1,0:T(8,128)(2,1)S(1)}, u32[]{:S(2)}, u32[]{:S(2)}) %collective-permute-start.2) | collective-permute-done | bytes 65568 | tf_op jit(solution)/shard_map/ppermute | solution.py:43
  29.1 2.2 %collective-permute-start.3 = (bf16[4,256,128]{2,1,0:T(8,128)(2,1)S(1)}, bf16[4,256,128]{2,1,0:T(8,128)(2,1)S(1)}, u32[]{:S(2)}, u32[]{:S(2)}) collective-permute-start(bf16[4,256,128]{2,1,0:T(8,128)(2,1)S(1)} %pad_maximum_fusion.2.q0), channel_id=1, source_target_pairs={{0,12},{4,0},{8,4},{12,8},{1,13},{5,1},{9,5},{13,9},{2,14},{6,2},{... | collective-permute-start | bytes 786440 | tf_op jit(solution)/shard_map/ppermute | solution.py:43
  31.2 2.9 %collective-permute-start.5 = (bf16[4,256,128]{2,1,0:T(8,128)(2,1)S(1)}, bf16[4,256,128]{2,1,0:T(8,128)(2,1)S(1)}, u32[]{:S(2)}, u32[]{:S(2)}) collective-permute-start(bf16[4,256,128]{2,1,0:T(8,128)(2,1)S(1)} %pad_maximum_fusion.2.q0), channel_id=1, source_target_pairs={{0,8},{4,12},{8,0},{12,4},{1,9},{5,13},{9,1},{13,5},{2,10},{6,14},... | collective-permute-start | bytes 786440 | tf_op jit(solution)/shard_map/ppermute | solution.py:43
  34.8 3.3 %collective-permute-done.3.q1 = bf16[4,256,128]{2,1,0:T(8,128)(2,1)S(1)} collective-permute-done((bf16[4,256,128]{2,1,0:T(8,128)(2,1)S(1)}, bf16[4,256,128]{2,1,0:T(8,128)(2,1)S(1)}, u32[]{:S(2)}, u32[]{:S(2)}) %collective-permute-start.3) | collective-permute-done | bytes 262176 | tf_op jit(solution)/shard_map/ppermute | solution.py:43
  38.2 2.3 %collective-permute-done.4.q2 = bf16[4,256,128]{2,1,0:T(8,128)(2,1)S(1)} collective-permute-done((bf16[4,256,128]{2,1,0:T(8,128)(2,1)S(1)}, bf16[4,256,128]{2,1,0:T(8,128)(2,1)S(1)}, u32[]{:S(2)}, u32[]{:S(2)}) %collective-permute-start.4) | collective-permute-done | bytes 262176 | tf_op jit(solution)/shard_map/ppermute | solution.py:43
  40.5 2.7 %collective-permute-done.5.q3 = bf16[4,256,128]{2,1,0:T(8,128)(2,1)S(1)} collective-permute-done((bf16[4,256,128]{2,1,0:T(8,128)(2,1)S(1)}, bf16[4,256,128]{2,1,0:T(8,128)(2,1)S(1)}, u32[]{:S(2)}, u32[]{:S(2)}) %collective-permute-start.5) | collective-permute-done | bytes 262176 | tf_op jit(solution)/shard_map/ppermute | solution.py:43
  43.2 2.3 %forward.1 = (bf16[288,320]{1,0:T(8,128)(2,1)S(1)}, f32[96,128]{1,0:T(8,128)S(1)}, f32[96,128]{1,0:T(8,128)S(1)}, f32[3,256,128]{2,1,0:T(8,128)S(1)}, bf16[2048,...) custom-call(bf16[4,256,128]{2,1,0:T(8,128)(2,1)S(1)} %pad_maximum_fusion.2.q0, ...), custom_call_target="tpu_custom_call" | custom-call | tf_op jit(solution)/shard_map/forward/pallas_call | solution.py:293
  49.5 6.0 %collective-permute-done.9 = bf16[288,320]{1,0:T(8,128)(2,1)S(1)} collective-permute-done((bf16[288,320]{1,0:T(8,128)(2,1)S(1)}, bf16[288,320]{1,0:T(8,128)(2,1)S(1)}, u32[]{:S(2)}, u32[]{:S(2)}) %collective-permute-start.9) | collective-permute-done | bytes 184352 | tf_op jit(solution)/shard_map/ppermute | solution.py:43
  55.5 2.7 %collective-permute-done.8 = bf16[288,320]{1,0:T(8,128)(2,1)S(1)} collective-permute-done((bf16[288,320]{1,0:T(8,128)(2,1)S(1)}, bf16[288,320]{1,0:T(8,128)(2,1)S(1)}, u32[]{:S(2)}, u32[]{:S(2)}) %collective-permute-start.8) | collective-permute-done | bytes 184352 | tf_op jit(solution)/shard_map/ppermute | solution.py:43
  58.5 2.2 %collective-permute-start.10 = (bf16[4,288,320]{2,1,0:T(8,128)(2,1)S(1)}, bf16[4,288,320]{2,1,0:T(8,128)(2,1)S(1)}, u32[]{:S(2)}, u32[]{:S(2)}) collective-permute-start(bf16[4,288,320]{2,1,0:T(8,128)(2,1)S(1)} %pad_maximum_fusion.r0), channel_id=1, source_target_pairs={{0,12},{4,0},{8,4},{12,8},{1,13},{5,1},{9,5},{13,9},{2,14},{6,2},{... | collective-permute-start | bytes 2211848 | tf_op jit(solution)/shard_map/ppermute | solution.py:43
  60.6 3.5 %collective-permute-start.12 = (bf16[4,288,320]{2,1,0:T(8,128)(2,1)S(1)}, bf16[4,288,320]{2,1,0:T(8,128)(2,1)S(1)}, u32[]{:S(2)}, u32[]{:S(2)}) collective-permute-start(bf16[4,288,320]{2,1,0:T(8,128)(2,1)S(1)} %pad_maximum_fusion.r0), channel_id=1, source_target_pairs={{0,8},{4,12},{8,0},{12,4},{1,9},{5,13},{9,1},{13,5},{2,10},{6,14},... | collective-permute-start | bytes 2211848 | tf_op jit(solution)/shard_map/ppermute | solution.py:43
  64.1 17.5 %collective-permute-done.10.r1 = bf16[4,288,320]{2,1,0:T(8,128)(2,1)S(1)} collective-permute-done((bf16[4,288,320]{2,1,0:T(8,128)(2,1)S(1)}, bf16[4,288,320]{2,1,0:T(8,128)(2,1)S(1)}, u32[]{:S(2)}, u32[]{:S(2)}) %collective-permute-start.10) | collective-permute-done | bytes 737312 | tf_op jit(solution)/shard_map/ppermute | solution.py:43
  83.2 16.2 %collective-permute-done.12.r3 = bf16[4,288,320]{2,1,0:T(8,128)(2,1)S(1)} collective-permute-done((bf16[4,288,320]{2,1,0:T(8,128)(2,1)S(1)}, bf16[4,288,320]{2,1,0:T(8,128)(2,1)S(1)}, u32[]{:S(2)}, u32[]{:S(2)}) %collective-permute-start.12) | collective-permute-done | bytes 737312 | tf_op jit(solution)/shard_map/ppermute | solution.py:43
  99.4 2.3 %pooled.1 = (bf16[320,128]{1,0:T(8,128)(2,1)S(1)}, f32[256,16]{1,0:T(8,128)S(1)}, f32[256,128]{1,0:T(8,128)S(1)}, f32[1,16]{1,0:T(1,128)S(1)}) custom-call(bf16[4,288,320]{2,1,0:T(8,128)(2,1)S(1)} %pad_maximum_fusion.r0, bf16[4,288,320]{2,1,0:T(8,128)(2,1)S(1)} %collective-permute-done.10.r1, bf16[4,288,320]{2,1,0:T(8,128)(2,1)S(1)} %collective-permute-done.11.r2, ...), custom_call_target="tpu_custom_call" | custom-call | tf_op jit(solution)/shard_map/pooled/pallas_call | solution.py:308
  101.6 3.8 %collective-permute-start.19 = (bf16[320,128]{1,0:T(8,128)(2,1)S(1)}, bf16[320,128]{1,0:T(8,128)(2,1)S(1)}, u32[]{:S(2)}, u32[]{:S(2)}) collective-permute-start(bf16[320,128]{1,0:T(8,128)(2,1)S(1)} %get-tuple-element.22), channel_id=1, source_target_pairs={{0,2},{1,3},{2,0},{3,1},{4,6},{5,7},{6,4},{7,5},{8,10},{9,11},{10,... | collective-permute-start | bytes 245768 | tf_op jit(solution)/shard_map/ppermute | solution.py:43
  109.9 3.4 %collective-permute-start.20 = (bf16[4,320,128]{2,1,0:T(8,128)(2,1)S(1)}, bf16[4,320,128]{2,1,0:T(8,128)(2,1)S(1)}, u32[]{:S(2)}, u32[]{:S(2)}) collective-permute-start(bf16[4,320,128]{2,1,0:T(8,128)(2,1)S(1)} %pad_maximum_fusion.1.t0), channel_id=1, source_target_pairs={{0,12},{4,0},{8,4},{12,8},{1,13},{5,1},{9,5},{13,9},{2,14},{6,2},{... | collective-permute-start | bytes 983048 | tf_op jit(solution)/shard_map/ppermute | solution.py:43
  113.3 2.4 %collective-permute-start.22 = (bf16[4,320,128]{2,1,0:T(8,128)(2,1)S(1)}, bf16[4,320,128]{2,1,0:T(8,128)(2,1)S(1)}, u32[]{:S(2)}, u32[]{:S(2)}) collective-permute-start(bf16[4,320,128]{2,1,0:T(8,128)(2,1)S(1)} %pad_maximum_fusion.1.t0), channel_id=1, source_target_pairs={{0,8},{4,12},{8,0},{12,4},{1,9},{5,13},{9,1},{13,5},{2,10},{6,14},... | collective-permute-start | bytes 983048 | tf_op jit(solution)/shard_map/ppermute | solution.py:43
  120.3 3.3 %collective-permute-start.15 = (f32[1,16]{1,0:T(1,128)S(1)}, f32[1,16]{1,0:T(1,128)S(1)}, u32[]{:S(2)}, u32[]{:S(2)}) collective-permute-start(f32[1,16]{1,0:T(1,128)S(1)} %add.30), channel_id=1, source_target_pairs={{0,64},{32,96},{64,0},{96,32},{128,192},{160,224},{192,128},{224,1... | collective-permute-start | bytes 200 | tf_op jit(solution)/shard_map/ppermute | solution.py:265
  125.1 6.9 %collective-permute-start.16 = (f32[1,16]{1,0:T(1,128)S(1)}, f32[1,16]{1,0:T(1,128)S(1)}, u32[]{:S(2)}, u32[]{:S(2)}) collective-permute-start(f32[1,16]{1,0:T(1,128)S(1)} %add.31), channel_id=1, source_target_pairs={{0,128},{32,160},{64,192},{96,224},{128,0},{160,32},{192,64},{224,... | collective-permute-start | bytes 200 | tf_op jit(solution)/shard_map/ppermute | solution.py:265
  135.1 3.9 %backward.1 = (bf16[256,2048]{1,0:T(8,128)(2,1)S(1)}, bf16[256,128]{1,0:T(8,128)(2,1)S(1)}) custom-call(bf16[4,256,128]{2,1,0:T(8,128)(2,1)S(1)} %pad_maximum_fusion.2.q0, bf16[4,256,128]{2,1,0:T(8,128)(2,1)S(1)} %collective-permute-done.3.q1, bf16[4,256,128]{2,1,0:T(8,128)(2,1)S(1)} %collective-permute-done.4.q2, ...), custom_call_target="tpu_custom_call" | custom-call | tf_op jit(solution)/shard_map/backward/pallas_call | solution.py:325
  139.1 4.2 %features.1 = bf16[2,8,128,320]{3,2,1,0:T(8,128)(2,1)S(1)} custom-call(bf16[256,128]{1,0:T(8,128)(2,1)S(1)} %get-tuple-element.21.p0_ref, bf16[256,128]{1,0:T(8,128)(2,1)S(1)} %get-tuple-element.28.gs_ref, bf16[256,5120]{1,0:T(8,128)(2,1)S(1)} %bitcast.42, bf16[16,256,320]{2,1,0:T(8,128)(2,1)S(1)} %grad_raw.1.raw_ref), custom_call_target="tpu_custom_call" | custom-call | tf_op jit(solution)/shard_map/features/pallas_call | solution.py:336
  144.3 2.3 %copy.12 = bf16[8,128,320]{1,2,0:T(8,128)(2,1)} copy(bf16[8,128,320]{2,1,0:T(8,128)(2,1)} %slice_bitcast_fusion) | data formatting | bytes 1310720 | tf_op jit(solution)/shard_map/squeeze | solution.py:253
  146.6 2.4 %collective-permute-done.23 = bf16[8,128,320]{1,2,0:T(8,128)(2,1)} collective-permute-done((bf16[8,128,320]{1,2,0:T(8,128)(2,1)}, bf16[8,128,320]{1,2,0:T(8,128)(2,1)}, u32[]{:S(2)}, u32[]{:S(2)}) %collective-permute-start.23) | collective-permute-done | bytes 655392 | tf_op jit(solution)/shard_map/ppermute | solution.py:253
  149.0 2.3 %copy.13 = bf16[8,128,320]{2,1,0:T(8,128)(2,1)} copy(bf16[8,128,320]{1,2,0:T(8,128)(2,1)} %collective-permute-done.23) | data formatting | bytes 1310720 | tf_op jit(solution)/shard_map/ppermute | solution.py:253
  152.7 2.1 %collective-permute-start.26 = (bf16[2,128,320]{2,1,0:T(8,128)(2,1)S(1)}, bf16[2,128,320]{2,1,0:T(8,128)(2,1)S(1)}, u32[]{:S(2)}, u32[]{:S(2)}) collective-permute-start(bf16[2,128,320]{2,1,0:T(8,128)(2,1)S(1)} %get-tuple-element.38), channel_id=1, source_target_pairs={{0,64},{32,96},{64,128},{96,160},{128,192},{160,224},{192,0},{224,... | collective-permute-start | bytes 491528 | tf_op jit(solution)/shard_map/ppermute | solution.py:43
  154.7 3.1 %collective-permute-start.25 = (bf16[2,128,320]{2,1,0:T(8,128)(2,1)S(1)}, bf16[2,128,320]{2,1,0:T(8,128)(2,1)S(1)}, u32[]{:S(2)}, u32[]{:S(2)}) collective-permute-start(bf16[2,128,320]{2,1,0:T(8,128)(2,1)S(1)} %get-tuple-element.39), channel_id=1, source_target_pairs={{0,192},{32,224},{64,0},{96,32},{128,64},{160,96},{192,128},{224,1... | collective-permute-start | bytes 491528 | tf_op jit(solution)/shard_map/ppermute | solution.py:43
  157.9 4.9 %collective-permute-start.24 = (bf16[2,128,320]{2,1,0:T(8,128)(2,1)S(1)}, bf16[2,128,320]{2,1,0:T(8,128)(2,1)S(1)}, u32[]{:S(2)}, u32[]{:S(2)}) collective-permute-start(bf16[2,128,320]{2,1,0:T(8,128)(2,1)S(1)} %get-tuple-element.37), channel_id=1, source_target_pairs={{0,128},{32,160},{64,192},{96,224},{128,0},{160,32},{192,64},{224,... | collective-permute-start | bytes 491528 | tf_op jit(solution)/shard_map/ppermute | solution.py:43
  162.8 2.2 %collective-permute-done.26 = bf16[2,128,320]{2,1,0:T(8,128)(2,1)S(1)} collective-permute-done((bf16[2,128,320]{2,1,0:T(8,128)(2,1)S(1)}, bf16[2,128,320]{2,1,0:T(8,128)(2,1)S(1)}, u32[]{:S(2)}, u32[]{:S(2)}) %collective-permute-start.26) | collective-permute-done | bytes 163872 | tf_op jit(solution)/shard_map/ppermute | solution.py:43
  165.0 7.9 %collective-permute-done.25 = bf16[2,128,320]{2,1,0:T(8,128)(2,1)S(1)} collective-permute-done((bf16[2,128,320]{2,1,0:T(8,128)(2,1)S(1)}, bf16[2,128,320]{2,1,0:T(8,128)(2,1)S(1)}, u32[]{:S(2)}, u32[]{:S(2)}) %collective-permute-start.25) | collective-permute-done | bytes 163872 | tf_op jit(solution)/shard_map/ppermute | solution.py:43
  173.0 2.1 %collective-permute-done.24 = bf16[2,128,320]{2,1,0:T(8,128)(2,1)S(1)} collective-permute-done((bf16[2,128,320]{2,1,0:T(8,128)(2,1)S(1)}, bf16[2,128,320]{2,1,0:T(8,128)(2,1)S(1)}, u32[]{:S(2)}, u32[]{:S(2)}) %collective-permute-start.24) | collective-permute-done | bytes 163872 | tf_op jit(solution)/shard_map/ppermute | solution.py:43
  175.2 5.6 %collective-permute-start.27 = (bf16[128,320]{1,0:T(8,128)(2,1)S(1)}, bf16[128,320]{1,0:T(8,128)(2,1)S(1)}, u32[]{:S(2)}, u32[]{:S(2)}) collective-permute-start(bf16[128,320]{1,0:T(8,128)(2,1)S(1)} %fusion.3), channel_id=1, source_target_pairs={{0,32},{32,0},{64,96},{96,64},{128,160},{160,128},{192,224},{224,1... | collective-permute-start | bytes 245768 | tf_op jit(solution)/shard_map/ppermute | solution.py:258
  (64 shorter events, 32.6 us)
Async XLA Ops:
  0.6 20.0 %copy-start = (bf16[2,128,5120]{2,1,0:T(8,128)(2,1)S(1)}, bf16[2,128,5120]{2,1,0:T(8,128)(2,1)}, u32[]{:S(2)}) copy-start(bf16[2,128,5120]{2,1,0:T(8,128)(2,1)} %param.6) | copy-start | bytes 7864324
  20.7 22.5 %collective-permute-start.6 = (bf16[16,64,320]{2,1,0:T(8,128)(2,1)S(1)}, bf16[16,64,320]{2,1,0:T(8,128)(2,1)S(1)}, u32[]{:S(2)}, u32[]{:S(2)}) collective-permute-start(bf16[16,64,320]{2,1,0:T(8,128)(2,1)S(1)} %all_to_all.5.mine_ref), channel_id=1, source_target_pairs={{0,16},{16,0},{1,17},{17,1},{2,18},{18,2},{3,19},{19,3},{4,20},{20... | collective-permute-start | bytes 1966088 | tf_op jit(solution)/shard_map/ppermute | solution.py:289
  20.7 13.5 %copy-start.5 = (bf16[2,320,10]{1,0,2:T(2,128)(2,1)S(1)}, bf16[2,320,10]{1,0,2:T(2,128)(2,1)}, u32[]{:S(2)}) copy-start(bf16[2,320,10]{1,0,2:T(2,128)(2,1)} %param.7) | copy-start | bytes 38404
  21.5 6.5 %collective-permute-start.2 = (bf16[256,128]{1,0:T(8,128)(2,1)S(1)}, bf16[256,128]{1,0:T(8,128)(2,1)S(1)}, u32[]{:S(2)}, u32[]{:S(2)}) collective-permute-start(bf16[256,128]{1,0:T(8,128)(2,1)S(1)} %scores.1), channel_id=1, source_target_pairs={{0,2},{1,3},{2,0},{3,1},{4,6},{5,7},{6,4},{7,5},{8,10},{9,11},{10,... | collective-permute-start | bytes 196616 | tf_op jit(solution)/shard_map/ppermute | solution.py:43
  23.4 5.6 %collective-permute-start.1 = (bf16[256,128]{1,0:T(8,128)(2,1)S(1)}, bf16[256,128]{1,0:T(8,128)(2,1)S(1)}, u32[]{:S(2)}, u32[]{:S(2)}) collective-permute-start(bf16[256,128]{1,0:T(8,128)(2,1)S(1)} %scores.1), channel_id=1, source_target_pairs={{0,1},{1,2},{2,3},{3,0},{4,5},{5,6},{6,7},{7,4},{8,9},{9,10},{10,1... | collective-permute-start | bytes 196616 | tf_op jit(solution)/shard_map/ppermute | solution.py:43
  24.5 4.5 %collective-permute-start = (bf16[256,128]{1,0:T(8,128)(2,1)S(1)}, bf16[256,128]{1,0:T(8,128)(2,1)S(1)}, u32[]{:S(2)}, u32[]{:S(2)}) collective-permute-start(bf16[256,128]{1,0:T(8,128)(2,1)S(1)} %scores.1), channel_id=1, source_target_pairs={{0,3},{1,0},{2,1},{3,2},{4,7},{5,4},{6,5},{7,6},{8,11},{9,8},{10,9... | collective-permute-start | bytes 196616 | tf_op jit(solution)/shard_map/ppermute | solution.py:43
  29.1 9.1 %collective-permute-start.3 = (bf16[4,256,128]{2,1,0:T(8,128)(2,1)S(1)}, bf16[4,256,128]{2,1,0:T(8,128)(2,1)S(1)}, u32[]{:S(2)}, u32[]{:S(2)}) collective-permute-start(bf16[4,256,128]{2,1,0:T(8,128)(2,1)S(1)} %pad_maximum_fusion.2.q0), channel_id=1, source_target_pairs={{0,12},{4,0},{8,4},{12,8},{1,13},{5,1},{9,5},{13,9},{2,14},{6,2},{... | collective-permute-start | bytes 786440 | tf_op jit(solution)/shard_map/ppermute | solution.py:43
  31.2 9.2 %collective-permute-start.4 = (bf16[4,256,128]{2,1,0:T(8,128)(2,1)S(1)}, bf16[4,256,128]{2,1,0:T(8,128)(2,1)S(1)}, u32[]{:S(2)}, u32[]{:S(2)}) collective-permute-start(bf16[4,256,128]{2,1,0:T(8,128)(2,1)S(1)} %pad_maximum_fusion.2.q0), channel_id=1, source_target_pairs={{0,4},{4,8},{8,12},{12,0},{1,5},{5,9},{9,13},{13,1},{2,6},{6,10},{... | collective-permute-start | bytes 786440 | tf_op jit(solution)/shard_map/ppermute | solution.py:43
  31.2 12.0 %collective-permute-start.5 = (bf16[4,256,128]{2,1,0:T(8,128)(2,1)S(1)}, bf16[4,256,128]{2,1,0:T(8,128)(2,1)S(1)}, u32[]{:S(2)}, u32[]{:S(2)}) collective-permute-start(bf16[4,256,128]{2,1,0:T(8,128)(2,1)S(1)} %pad_maximum_fusion.2.q0), channel_id=1, source_target_pairs={{0,8},{4,12},{8,0},{12,4},{1,9},{5,13},{9,1},{13,5},{2,10},{6,14},... | collective-permute-start | bytes 786440 | tf_op jit(solution)/shard_map/ppermute | solution.py:43
  45.6 10.0 %collective-permute-start.9 = (bf16[288,320]{1,0:T(8,128)(2,1)S(1)}, bf16[288,320]{1,0:T(8,128)(2,1)S(1)}, u32[]{:S(2)}, u32[]{:S(2)}) collective-permute-start(bf16[288,320]{1,0:T(8,128)(2,1)S(1)} %get-tuple-element.18), channel_id=1, source_target_pairs={{0,2},{1,3},{2,0},{3,1},{4,6},{5,7},{6,4},{7,5},{8,10},{9,11},{10,... | collective-permute-start | bytes 552968 | tf_op jit(solution)/shard_map/ppermute | solution.py:43
  47.5 10.7 %collective-permute-start.8 = (bf16[288,320]{1,0:T(8,128)(2,1)S(1)}, bf16[288,320]{1,0:T(8,128)(2,1)S(1)}, u32[]{:S(2)}, u32[]{:S(2)}) collective-permute-start(bf16[288,320]{1,0:T(8,128)(2,1)S(1)} %get-tuple-element.18), channel_id=1, source_target_pairs={{0,1},{1,2},{2,3},{3,0},{4,5},{5,6},{6,7},{7,4},{8,9},{9,10},{10,1... | collective-permute-start | bytes 552968 | tf_op jit(solution)/shard_map/ppermute | solution.py:43
  48.5 9.7 %collective-permute-start.7 = (bf16[288,320]{1,0:T(8,128)(2,1)S(1)}, bf16[288,320]{1,0:T(8,128)(2,1)S(1)}, u32[]{:S(2)}, u32[]{:S(2)}) collective-permute-start(bf16[288,320]{1,0:T(8,128)(2,1)S(1)} %get-tuple-element.18), channel_id=1, source_target_pairs={{0,3},{1,0},{2,1},{3,2},{4,7},{5,4},{6,5},{7,6},{8,11},{9,8},{10,9... | collective-permute-start | bytes 552968 | tf_op jit(solution)/shard_map/ppermute | solution.py:43
  58.5 23.1 %collective-permute-start.10 = (bf16[4,288,320]{2,1,0:T(8,128)(2,1)S(1)}, bf16[4,288,320]{2,1,0:T(8,128)(2,1)S(1)}, u32[]{:S(2)}, u32[]{:S(2)}) collective-permute-start(bf16[4,288,320]{2,1,0:T(8,128)(2,1)S(1)} %pad_maximum_fusion.r0), channel_id=1, source_target_pairs={{0,12},{4,0},{8,4},{12,8},{1,13},{5,1},{9,5},{13,9},{2,14},{6,2},{... | collective-permute-start | bytes 2211848 | tf_op jit(solution)/shard_map/ppermute | solution.py:43
  60.6 22.6 %collective-permute-start.11 = (bf16[4,288,320]{2,1,0:T(8,128)(2,1)S(1)}, bf16[4,288,320]{2,1,0:T(8,128)(2,1)S(1)}, u32[]{:S(2)}, u32[]{:S(2)}) collective-permute-start(bf16[4,288,320]{2,1,0:T(8,128)(2,1)S(1)} %pad_maximum_fusion.r0), channel_id=1, source_target_pairs={{0,4},{4,8},{8,12},{12,0},{1,5},{5,9},{9,13},{13,1},{2,6},{6,10},{... | collective-permute-start | bytes 2211848 | tf_op jit(solution)/shard_map/ppermute | solution.py:43
  60.6 38.7 %collective-permute-start.12 = (bf16[4,288,320]{2,1,0:T(8,128)(2,1)S(1)}, bf16[4,288,320]{2,1,0:T(8,128)(2,1)S(1)}, u32[]{:S(2)}, u32[]{:S(2)}) collective-permute-start(bf16[4,288,320]{2,1,0:T(8,128)(2,1)S(1)} %pad_maximum_fusion.r0), channel_id=1, source_target_pairs={{0,8},{4,12},{8,0},{12,4},{1,9},{5,13},{9,1},{13,5},{2,10},{6,14},... | collective-permute-start | bytes 2211848 | tf_op jit(solution)/shard_map/ppermute | solution.py:43
  101.6 6.3 %collective-permute-start.19 = (bf16[320,128]{1,0:T(8,128)(2,1)S(1)}, bf16[320,128]{1,0:T(8,128)(2,1)S(1)}, u32[]{:S(2)}, u32[]{:S(2)}) collective-permute-start(bf16[320,128]{1,0:T(8,128)(2,1)S(1)} %get-tuple-element.22), channel_id=1, source_target_pairs={{0,2},{1,3},{2,0},{3,1},{4,6},{5,7},{6,4},{7,5},{8,10},{9,11},{10,... | collective-permute-start | bytes 245768 | tf_op jit(solution)/shard_map/ppermute | solution.py:43
  105.4 4.4 %collective-permute-start.18 = (bf16[320,128]{1,0:T(8,128)(2,1)S(1)}, bf16[320,128]{1,0:T(8,128)(2,1)S(1)}, u32[]{:S(2)}, u32[]{:S(2)}) collective-permute-start(bf16[320,128]{1,0:T(8,128)(2,1)S(1)} %get-tuple-element.22), channel_id=1, source_target_pairs={{0,1},{1,2},{2,3},{3,0},{4,5},{5,6},{6,7},{7,4},{8,9},{9,10},{10,1... | collective-permute-start | bytes 245768 | tf_op jit(solution)/shard_map/ppermute | solution.py:43
  105.4 4.4 %collective-permute-start.17 = (bf16[320,128]{1,0:T(8,128)(2,1)S(1)}, bf16[320,128]{1,0:T(8,128)(2,1)S(1)}, u32[]{:S(2)}, u32[]{:S(2)}) collective-permute-start(bf16[320,128]{1,0:T(8,128)(2,1)S(1)} %get-tuple-element.22), channel_id=1, source_target_pairs={{0,3},{1,0},{2,1},{3,2},{4,7},{5,4},{6,5},{7,6},{8,11},{9,8},{10,9... | collective-permute-start | bytes 245768 | tf_op jit(solution)/shard_map/ppermute | solution.py:43
  109.9 25.2 %collective-permute-start.20 = (bf16[4,320,128]{2,1,0:T(8,128)(2,1)S(1)}, bf16[4,320,128]{2,1,0:T(8,128)(2,1)S(1)}, u32[]{:S(2)}, u32[]{:S(2)}) collective-permute-start(bf16[4,320,128]{2,1,0:T(8,128)(2,1)S(1)} %pad_maximum_fusion.1.t0), channel_id=1, source_target_pairs={{0,12},{4,0},{8,4},{12,8},{1,13},{5,1},{9,5},{13,9},{2,14},{6,2},{... | collective-permute-start | bytes 983048 | tf_op jit(solution)/shard_map/ppermute | solution.py:43
  113.3 21.8 %collective-permute-start.21 = (bf16[4,320,128]{2,1,0:T(8,128)(2,1)S(1)}, bf16[4,320,128]{2,1,0:T(8,128)(2,1)S(1)}, u32[]{:S(2)}, u32[]{:S(2)}) collective-permute-start(bf16[4,320,128]{2,1,0:T(8,128)(2,1)S(1)} %pad_maximum_fusion.1.t0), channel_id=1, source_target_pairs={{0,4},{4,8},{8,12},{12,0},{1,5},{5,9},{9,13},{13,1},{2,6},{6,10},{... | collective-permute-start | bytes 983048 | tf_op jit(solution)/shard_map/ppermute | solution.py:43
  113.3 21.9 %collective-permute-start.22 = (bf16[4,320,128]{2,1,0:T(8,128)(2,1)S(1)}, bf16[4,320,128]{2,1,0:T(8,128)(2,1)S(1)}, u32[]{:S(2)}, u32[]{:S(2)}) collective-permute-start(bf16[4,320,128]{2,1,0:T(8,128)(2,1)S(1)} %pad_maximum_fusion.1.t0), channel_id=1, source_target_pairs={{0,8},{4,12},{8,0},{12,4},{1,9},{5,13},{9,1},{13,5},{2,10},{6,14},... | collective-permute-start | bytes 983048 | tf_op jit(solution)/shard_map/ppermute | solution.py:43
  115.6 1.1 collective-permute-start.13
  116.7 3.5 %collective-permute-start.14 = (f32[1,16]{1,0:T(1,128)S(1)}, f32[1,16]{1,0:T(1,128)S(1)}, u32[]{:S(2)}, u32[]{:S(2)}) collective-permute-start(f32[1,16]{1,0:T(1,128)S(1)} %add.29), channel_id=1, source_target_pairs={{0,32},{32,0},{64,96},{96,64},{128,160},{160,128},{192,224},{224,1... | collective-permute-start | bytes 200 | tf_op jit(solution)/shard_map/ppermute | solution.py:265
  120.3 4.8 %collective-permute-start.15 = (f32[1,16]{1,0:T(1,128)S(1)}, f32[1,16]{1,0:T(1,128)S(1)}, u32[]{:S(2)}, u32[]{:S(2)}) collective-permute-start(f32[1,16]{1,0:T(1,128)S(1)} %add.30), channel_id=1, source_target_pairs={{0,64},{32,96},{64,0},{96,32},{128,192},{160,224},{192,128},{224,1... | collective-permute-start | bytes 200 | tf_op jit(solution)/shard_map/ppermute | solution.py:265
  125.1 8.4 %collective-permute-start.16 = (f32[1,16]{1,0:T(1,128)S(1)}, f32[1,16]{1,0:T(1,128)S(1)}, u32[]{:S(2)}, u32[]{:S(2)}) collective-permute-start(f32[1,16]{1,0:T(1,128)S(1)} %add.31), channel_id=1, source_target_pairs={{0,128},{32,160},{64,192},{96,224},{128,0},{160,32},{192,64},{224,... | collective-permute-start | bytes 200 | tf_op jit(solution)/shard_map/ppermute | solution.py:265
  139.1 4.2 %copy-start.2 = (bf16[256,2048]{1,0:T(8,128)(2,1)}, bf16[256,2048]{1,0:T(8,128)(2,1)S(1)}, u32[]{:S(2)}) copy-start(bf16[256,2048]{1,0:T(8,128)(2,1)S(1)} %get-tuple-element.29) | copy-start | bytes 3145732
  146.6 2.4 %collective-permute-start.23 = (bf16[8,128,320]{1,2,0:T(8,128)(2,1)}, bf16[8,128,320]{1,2,0:T(8,128)(2,1)}, u32[]{:S(2)}, u32[]{:S(2)}) collective-permute-start(bf16[8,128,320]{1,2,0:T(8,128)(2,1)} %copy.12), channel_id=1, source_target_pairs={{0,16},{16,0},{1,17},{17,1},{2,18},{18,2},{3,19},{19,3},{4,20},{20... | collective-permute-start | bytes 1966088 | tf_op jit(solution)/shard_map/ppermute | solution.py:253
  152.6 28.2 %copy-start.3 = (bf16[256,2048]{1,0:T(8,128)(2,1)S(1)}, bf16[256,2048]{1,0:T(8,128)(2,1)}, u32[]{:S(2)}) copy-start(bf16[256,2048]{1,0:T(8,128)(2,1)} %copy-done.2) | copy-start | bytes 3145732
  152.7 12.4 %collective-permute-start.26 = (bf16[2,128,320]{2,1,0:T(8,128)(2,1)S(1)}, bf16[2,128,320]{2,1,0:T(8,128)(2,1)S(1)}, u32[]{:S(2)}, u32[]{:S(2)}) collective-permute-start(bf16[2,128,320]{2,1,0:T(8,128)(2,1)S(1)} %get-tuple-element.38), channel_id=1, source_target_pairs={{0,64},{32,96},{64,128},{96,160},{128,192},{160,224},{192,0},{224,... | collective-permute-start | bytes 491528 | tf_op jit(solution)/shard_map/ppermute | solution.py:43
  154.7 18.2 %collective-permute-start.25 = (bf16[2,128,320]{2,1,0:T(8,128)(2,1)S(1)}, bf16[2,128,320]{2,1,0:T(8,128)(2,1)S(1)}, u32[]{:S(2)}, u32[]{:S(2)}) collective-permute-start(bf16[2,128,320]{2,1,0:T(8,128)(2,1)S(1)} %get-tuple-element.39), channel_id=1, source_target_pairs={{0,192},{32,224},{64,0},{96,32},{128,64},{160,96},{192,128},{224,1... | collective-permute-start | bytes 491528 | tf_op jit(solution)/shard_map/ppermute | solution.py:43
  157.9 17.2 %collective-permute-start.24 = (bf16[2,128,320]{2,1,0:T(8,128)(2,1)S(1)}, bf16[2,128,320]{2,1,0:T(8,128)(2,1)S(1)}, u32[]{:S(2)}, u32[]{:S(2)}) collective-permute-start(bf16[2,128,320]{2,1,0:T(8,128)(2,1)S(1)} %get-tuple-element.37), channel_id=1, source_target_pairs={{0,128},{32,160},{64,192},{96,224},{128,0},{160,32},{192,64},{224,... | collective-permute-start | bytes 491528 | tf_op jit(solution)/shard_map/ppermute | solution.py:43
  175.2 8.2 %collective-permute-start.27 = (bf16[128,320]{1,0:T(8,128)(2,1)S(1)}, bf16[128,320]{1,0:T(8,128)(2,1)S(1)}, u32[]{:S(2)}, u32[]{:S(2)}) collective-permute-start(bf16[128,320]{1,0:T(8,128)(2,1)S(1)} %fusion.3), channel_id=1, source_target_pairs={{0,32},{32,0},{64,96},{96,64},{128,160},{160,128},{192,224},{224,1... | collective-permute-start | bytes 245768 | tf_op jit(solution)/shard_map/ppermute | solution.py:258
  (2 other events, 3.2 us)

commit v2 on v0

v2 whole, which is shorter than its diff:
```python
import functools
import math

import jax
import jax.numpy as jnp
from jax import lax
from jax.experimental import pallas as pl
from jax.experimental.pallas import tpu as pltpu
from jax.sharding import Mesh, PartitionSpec as P

P_SIZE = 128
ITERS = 3
CLASSES = 10
PAD = 16
HEADS = 2
REFS = HEADS * P_SIZE

temper = 1.5
epsilon = 1e-06
loss_scale = 65536.0
f32 = jnp.float32
bf16 = jnp.bfloat16

SIDE = 4
DEPTH = 8
BLOCKS = SIDE * SIDE
FAR = ((0, 0), (2, 0), (0, 2), (2, 2))
NEAR = ((0, 0), (1, 0), (0, 1), (3, 3))
CHIPS = ((0, 1, 7, 2), (0, 1, 7, 6))
T_ROWS = REFS + HEADS * PAD
M_ROWS = 4 * PAD
VMEM = pl.BlockSpec(memory_space=pltpu.VMEM)
SMEM = pl.BlockSpec(memory_space=pltpu.SMEM)
NT = (((1,), (1,)), ((), ()))
TN = (((0,), (0,)), ((), ()))


def call(kernel, name, shapes, n_vmem, n_smem=0, scratch=(), flops=0):
    many = isinstance(shapes, list)
    return pl.pallas_call(
        kernel,
        out_shape=shapes,
        in_specs=[VMEM] * n_vmem + [SMEM] * n_smem,
        out_specs=[VMEM] * len(shapes) if many else VMEM,
        scratch_shapes=list(scratch),
        compiler_params=pltpu.CompilerParams(vmem_limit_bytes=40 * 1024 * 1024),
        cost_estimate=pl.CostEstimate(flops=flops, bytes_accessed=1 << 20, transcendentals=0) if flops else None,
        name=name,
    )


def moved(first, second):
    y = lax.rem(lax.axis_index("y") + first[0] + second[0], SIDE)
    x = lax.rem(lax.axis_index("x") + first[1] + second[1], SIDE)
    return y * SIDE + x


def block_of(s):
    return moved(NEAR[s // 4], FAR[s % 4])


def lanes(block, rows):
    return pl.ds(pl.multiple_of(block * rows, rows), rows)


def send(value, step, sign=1):
    pairs = []
    for y in range(SIDE):
        for x in range(SIDE):
            to = (y + sign * step[0]) % SIDE * SIDE + (x + sign * step[1]) % SIDE
            pairs.append((y * SIDE + x, to))
    return lax.ppermute(value, ("y", "x"), pairs)


def gather(value):
    row = jnp.stack([value] + [send(value, step, -1) for step in FAR[1:]])
    return [row] + [send(row, step, -1) for step in NEAR[1:]]


def scores_kernel(scale, f_ref, r_ref, k_ref):
    scores = lax.dot_general(r_ref[...], f_ref[...], NT, preferred_element_type=f32)
    k_ref[...] = jnp.exp(scores * scale).astype(bf16)


def split_kernel(f_ref, refs_ref, half_ref, mine_ref, turned_ref):
    part = mine_ref.shape[1]
    half = part // 2
    for j in range(BLOCKS // 2):
        where = slice(2 * part * j, 2 * part * (j + 1))
        turned_ref[where, :] = jnp.transpose(f_ref[:, where])
    core = lax.axis_index("core")
    for j in range(BLOCKS):
        half_ref[j] = turned_ref[pl.ds(pl.multiple_of(part * j + half * core, half), half), :]
    place = moved((0, 0), (0, 0))
    pair = refs_ref[:, pl.ds(pl.multiple_of((place // 2) * (2 * part), 2 * part), 2 * part)]
    mine_ref[...] = jnp.where(lax.rem(place, 2) == 0, pair[:, :part], pair[:, part:])


def diagonal():
    square = (P_SIZE, P_SIZE)
    return lax.broadcasted_iota(jnp.int32, square, 0) == lax.broadcasted_iota(jnp.int32, square, 1)


def to_row(column):
    return jnp.sum(jnp.where(diagonal(), column, 0.0), axis=0, keepdims=True)


def to_column(row):
    return jnp.sum(jnp.where(diagonal(), row, 0.0), axis=1, keepdims=True)


def put_moments(ref, row, moments):
    for h in range(HEADS):
        high = moments[h].astype(bf16)
        ref[row + h * PAD : row + (h + 1) * PAD, :] = high
        low = row + (HEADS + h) * PAD
        ref[low : low + PAD, :] = (moments[h] - high.astype(f32)).astype(bf16)


def add_moments(refs, row):
    moments = []
    for h in range(HEADS):
        total = jnp.zeros((PAD, P_SIZE), f32)
        for ref in refs:
            total = total + ref[row + h * PAD : row + (h + 1) * PAD, :].astype(f32)
            low = row + (HEADS + h) * PAD
            total = total + ref[low : low + PAD, :].astype(f32)
        moments.append(total)
    return moments


def forward_kernel(
    q0, q1, q2, q3, near_ref, other_ref, wt_ref, len_ref,
    a0, a1, a2, a3, raw_ref, rs_ref, rt_ref, col_ref, fc_ref, plan_ref, wide_ref, ext_ref,
):
    q = (q0, q1, q2, q3)
    core = lax.axis_index("core")
    length = len_ref[0]
    rows = q0.shape[2]
    half = near_ref.shape[1]
    mass = 1.0 / (jnp.zeros((1, rows), jnp.int32) + length).astype(f32)
    lane = lax.broadcasted_iota(jnp.int32, (1, rows), 1)
    masses = [jnp.where(block_of(s) * rows + lane < length, mass, 0.0) for s in range(BLOCKS)]
    for s in range(BLOCKS):
        here = slice(s * rows, (s + 1) * rows)
        fc_ref[pl.ds(pl.multiple_of(core * half, half), half), here] = near_ref[s]
        fc_ref[pl.ds(pl.multiple_of((1 - core) * half, half), half), here] = other_ref[s]
    for t in range(ITERS):
        for h in range(HEADS):
            here = slice(h * P_SIZE, (h + 1) * P_SIZE)
            acc = jnp.zeros((P_SIZE, rows), f32)
            for s in range(BLOCKS):
                k = q[s // 4][s % 4, here, :].astype(f32)
                weighted = k if t == 0 else k * col_ref[t - 1, here, :]
                total = jnp.sum(weighted, axis=0, keepdims=True)
                scale = masses[s] / total
                place = (t * HEADS + h) * BLOCKS + s
                rt_ref[place : place + 1, :] = total
                rs_ref[place : place + 1, :] = scale
                acc = acc + k * scale
            col = 1.0 / (float(P_SIZE) * jnp.sum(acc, axis=1, keepdims=True))
            col_ref[t, here, :] = jnp.broadcast_to(col, (P_SIZE, rows))
    for h in range(HEADS):
        here = slice(h * P_SIZE, (h + 1) * P_SIZE)
        for s in range(BLOCKS):
            k = q[s // 4][s % 4, here, :].astype(f32)
            place = ((ITERS - 1) * HEADS + h) * BLOCKS + s
            plan = rs_ref[place : place + 1, :] * k * col_ref[ITERS - 1, here, :]
            plan_ref[here, lanes(block_of(s), rows)] = plan.astype(bf16)
    raw = float(P_SIZE) * lax.dot_general(plan_ref[...], fc_ref[...], NT, preferred_element_type=f32)
    raw_ref[...] = raw
    ext_ref[:REFS, :] = raw.astype(bf16)
    ext_ref[REFS:, :] = wt_ref[...]
    wide_ref[...] = jnp.dot(ext_ref[...], fc_ref[...], preferred_element_type=f32).astype(bf16)
    moments = []
    for h in range(HEADS):
        here = slice(h * P_SIZE, (h + 1) * P_SIZE)
        squares = jnp.sum(raw_ref[here, :] * raw_ref[here, :], axis=1, keepdims=True)
        products = lax.dot_general(
            wt_ref[h * PAD : (h + 1) * PAD, :], ext_ref[here, :], NT, preferred_element_type=f32
        )
        kind = lax.broadcasted_iota(jnp.int32, products.shape, 0)
        moments.append(jnp.where(kind == CLASSES, to_row(squares), products))
    for i, out in enumerate((a0, a1, a2, a3)):
        for k in range(4):
            out[k * T_ROWS : (k + 1) * T_ROWS, :] = wide_ref[:, lanes(moved(NEAR[i], FAR[k]), rows)]
        put_moments(out, 4 * T_ROWS, moments)


def add_blocks(refs, rows):
    total = refs[0][rows, :].astype(f32)
    for ref in refs[1:]:
        total = total + ref[rows, :].astype(f32)
    return total.astype(bf16)


def first_sum_kernel(a0, a1, a2, a3, c0, c1, c2, c3):
    parts = (a0, a1, a2, a3)
    moments = add_moments(parts, 4 * T_ROWS)
    for k, out in enumerate((c0, c1, c2, c3)):
        for low in range(0, T_ROWS, 96):
            out[low : low + 96, :] = add_blocks(parts, slice(k * T_ROWS + low, k * T_ROWS + low + 96))
        put_moments(out, T_ROWS, moments)


def inverse_rms(moments, width):
    return lax.rsqrt(moments[CLASSES : CLASSES + 1, :] / width + epsilon)


def second_sum_kernel(width, c0, c1, c2, c3, t_ref, m_ref, logit_ref):
    parts = (c0, c1, c2, c3)
    moments = add_moments(parts, T_ROWS)
    logits = jnp.zeros((PAD, 1), f32)
    for h in range(HEADS):
        m_ref[h * PAD : (h + 1) * PAD, :] = moments[h]
        part = jnp.sum(inverse_rms(moments[h], width) * moments[h], axis=1, keepdims=True)
        logits = logits + part / P_SIZE
    logit_ref[...] = jnp.broadcast_to(logits, logit_ref.shape)
    for low in range(0, T_ROWS, 96):
        t_ref[low : low + 96, :] = add_blocks(parts, slice(low, low + 96))


def backward_kernel(
    width, score_scale,
    q0, q1, q2, q3, t0, t1, t2, t3, rs_ref, rt_ref, col_ref, m_ref, logit_ref, raw_ref, wt_ref, plan_ref, refs_ref, label_ref,
    gs_ref, p0, p1, p2, p3, other_ref, gt_ref, grs_ref, u_ref, left_ref, right_ref, wide_ref,
):
    q = (q0, q1, q2, q3)
    tt = (t0, t1, t2, t3)
    rows = q0.shape[2]
    size = float(P_SIZE)
    logits = logit_ref[...]
    kind = lax.broadcasted_iota(jnp.int32, logits.shape, 0)
    exps = jnp.where(kind < CLASSES, jnp.exp(logits), 0.0)
    probs = exps / jnp.sum(exps, axis=0, keepdims=True)
    grads = loss_scale * (probs - (kind == label_ref[0]).astype(f32))
    grads = jnp.where(kind < CLASSES, grads, 0.0)
    left_ref[:REFS, :] = refs_ref[...]
    right_ref[REFS:, :] = plan_ref[...]
    for h in range(HEADS):
        here = slice(h * P_SIZE, (h + 1) * P_SIZE)
        moments = m_ref[h * PAD : (h + 1) * PAD, :]
        inverse_row = inverse_rms(moments, width)
        dual_row = inverse_row * jnp.sum(grads * moments, axis=0, keepdims=True) / (size * width)
        inverse = to_column(inverse_row)
        pull = to_column(inverse_row * dual_row)
        normed = jnp.sum(grads[:, :1] * wt_ref[h * PAD : (h + 1) * PAD, :].astype(f32), axis=0, keepdims=True) / size
        grad_raw = (inverse * (normed - raw_ref[here, :] * pull)).astype(bf16)
        left_ref[REFS + h * P_SIZE : REFS + (h + 1) * P_SIZE, :] = (size * grad_raw.astype(f32)).astype(bf16)
        first = jnp.broadcast_to(size * inverse, (P_SIZE, rows))
        second = first * pull

        def load(s):
            return q[s // 4][s % 4, here, :].astype(f32)

        def grad_plan(s, u):
            return first * u - second * tt[s // 4][s % 4, here, :].astype(f32)

        def row(ref, t, s):
            place = (t * HEADS + h) * BLOCKS + s
            return ref[place : place + 1, :]

        def put(ref, t, s, value):
            place = (t * HEADS + h) * BLOCKS + s
            ref[place : place + 1, :] = value

        acc = jnp.zeros((P_SIZE, rows), f32)
        for s in range(BLOCKS):
            low = REFS + h * PAD
            v = tt[s // 4][s % 4, low : low + PAD, :].astype(f32)
            u = jnp.sum(grads * v, axis=0, keepdims=True) / size
            put(u_ref, 0, s, u)
            weighted = grad_plan(s, u) * load(s)
            put(grs_ref, ITERS - 1, s, jnp.sum(weighted * col_ref[ITERS - 1, here, :], axis=0, keepdims=True))
            acc = acc + weighted * row(rs_ref, ITERS - 1, s)
        for t in reversed(range(ITERS)):
            grad_col = jnp.sum(acc, axis=1, keepdims=True)
            gt_ref[t] = -size * col_ref[t, here, :] ** 2 * grad_col
            acc = jnp.zeros((P_SIZE, rows), f32)
            for s in range(BLOCKS):
                k = load(s)
                grad_row = jnp.sum(k * gt_ref[t], axis=0, keepdims=True)
                if t == ITERS - 1:
                    grad_row = grad_row + row(grs_ref, t, s)
                grad_rowsum = -grad_row * row(rs_ref, t, s) / row(rt_ref, t, s)
                put(grs_ref, t, s, grad_rowsum)
                if t > 0:
                    acc = acc + k * grad_rowsum
        for s in range(BLOCKS):
            total = row(rs_ref, ITERS - 1, s) * col_ref[ITERS - 1, here, :] * grad_plan(s, row(u_ref, 0, s))
            for t in range(ITERS):
                total = total + row(rs_ref, t, s) * gt_ref[t]
                if t > 0:
                    total = total + row(grs_ref, t, s) * col_ref[t - 1, here, :]
                else:
                    total = total + row(grs_ref, t, s)
            right_ref[here, lanes(block_of(s), rows)] = (score_scale * total * load(s)).astype(bf16)
    gs_ref[...] = right_ref[:REFS, :]
    wide_ref[...] = lax.dot_general(left_ref[...], right_ref[...], TN, preferred_element_type=f32)
    core, z = lax.axis_index("core"), lax.axis_index("z")
    outs = (p0, p1, p2, p3)

    def take(step, which):
        return wide_ref[:, lanes(2 * lax.rem(z + step, DEPTH) + which, rows)].astype(bf16)

    for k in range(4):
        for b in range(2):
            step = jnp.where(core == 0, CHIPS[0][k], CHIPS[1][k]) + 4 * b
            outs[k][b] = take(step, core)
            step = jnp.where(core == 0, CHIPS[1][k], CHIPS[0][k]) + 4 * b
            other_ref[2 * k + b] = take(step, 1 - core)


def cores_kernel(p0, p1, p2, p3, other_ref, o0, o1, o2, o3):
    for k, (part, out) in enumerate(zip((p0, p1, p2, p3), (o0, o1, o2, o3))):
        for b in range(2):
            out[b] = (part[b].astype(f32) + other_ref[2 * k + b].astype(f32)).astype(bf16)


def chips_kernel(o0, o1, o2, o3, u0, u1):
    for b, out in enumerate((u0, u1)):
        total = o0[b].astype(f32) + o1[b].astype(f32) + o2[b].astype(f32) + o3[b].astype(f32)
        out[...] = total.astype(bf16)


def last_kernel(u0, u1, out_ref):
    eye = diagonal().astype(bf16)
    out_ref[...] = lax.dot_general(eye, u0[...], NT, preferred_element_type=f32) + lax.dot_general(
        eye, u1[...], NT, preferred_element_type=f32
    )


def references_kernel(gs_ref, fc_ref, out_ref):
    out_ref[...] = lax.dot_general(gs_ref[...], fc_ref[...], NT, preferred_element_type=f32)


def along_z(value, k):
    pairs = []
    for z in range(DEPTH):
        for core in range(2):
            pairs.append((2 * z + core, 2 * ((z + CHIPS[core][k]) % DEPTH) + core))
    return lax.ppermute(value, ("z", "core"), pairs)


def to_place(value, b):
    pairs = []
    for z in range(DEPTH):
        for core in range(2):
            for j in range(BLOCKS):
                block = 2 * ((z + 4 * b) % DEPTH) + core
                pairs.append(((2 * z + core) * BLOCKS + j, j * BLOCKS + block))
    return lax.ppermute(value, ("z", "core", "y", "x"), pairs)


def sum_logits(part):
    total = part + lax.ppermute(part, "core", [(0, 1), (1, 0)])
    for k in (1, 2, 4):
        total = total + lax.ppermute(total, "z", [(i, i ^ k) for i in range(DEPTH)])
    return total


def local(features, references, classifier, lengths, labels):
    batch, rows, width = features.shape
    part = width // BLOCKS
    everything = BLOCKS * rows
    score_scale = temper / math.sqrt(width)
    feats = features.reshape(rows, width)
    refs = references.reshape(REFS, width)
    kind = jax.ShapeDtypeStruct

    kernel = call(functools.partial(scores_kernel, score_scale), "scores", kind((REFS, rows), bf16), 2)(feats, refs)
    q = gather(kernel)
    half, refs_part = call(
        split_kernel, "split", [kind((BLOCKS, part // 2, rows), bf16), kind((REFS, part), bf16)], 2,
        scratch=[pltpu.VMEM((width, rows), bf16)],
    )(feats, refs)
    half = lax.optimization_barrier((half, q[0]))[0]
    near = lax.all_to_all(half, ("y", "x"), 0, 0)
    other = lax.ppermute(near, "core", [(0, 1), (1, 0)])
    weights = jnp.pad(jnp.transpose(classifier, (0, 2, 1)), ((0, 0), (0, PAD - CLASSES), (0, 0)))
    weights = weights.reshape(HEADS * PAD, part)

    scales = kind((ITERS * HEADS * BLOCKS, rows), f32)
    *a, raw, rs, rt, col, cols, plan = call(
        forward_kernel, "forward",
        [kind((4 * T_ROWS + M_ROWS, rows), bf16)] * 4
        + [
            kind((REFS, part), f32), scales, scales, kind((ITERS, REFS, rows), f32),
            kind((part, everything), bf16), kind((REFS, everything), bf16),
        ],
        7, 1,
        scratch=[pltpu.VMEM((T_ROWS, everything), bf16), pltpu.VMEM((T_ROWS, part), bf16)],
    )(*q, near, other, weights, lengths)
    a = [a[0]] + [send(value, step) for value, step in zip(a[1:], NEAR[1:])]
    c = call(first_sum_kernel, "first_sum", [kind((T_ROWS + M_ROWS, rows), bf16)] * 4, 4)(*a)
    c = [c[0]] + [send(value, step) for value, step in zip(c[1:], FAR[1:])]
    t, moments, logit_part = call(
        functools.partial(second_sum_kernel, width), "second_sum",
        [kind((T_ROWS, rows), bf16), kind((HEADS * PAD, P_SIZE), f32), kind((PAD, P_SIZE), f32)], 4,
    )(*c)
    logits = sum_logits(logit_part)
    ts = gather(t)
    pair = kind((2, part, rows), bf16)
    grad_scores, *mine, away = call(
        functools.partial(backward_kernel, width, score_scale), "backward",
        [kind((REFS, everything), bf16)] + [pair] * 4 + [kind((DEPTH, part, rows), bf16)],
        17, 1,
        scratch=[
            pltpu.VMEM((ITERS, P_SIZE, rows), f32),
            pltpu.VMEM((ITERS * HEADS * BLOCKS, rows), f32),
            pltpu.VMEM((HEADS * BLOCKS, rows), f32),
            pltpu.VMEM((2 * REFS, part), bf16),
            pltpu.VMEM((2 * REFS, everything), bf16),
            pltpu.VMEM((part, everything), f32),
        ],
    )(*q, *ts, rs, rt, col, moments, logits, raw, weights, plan, refs_part, labels)
    away = lax.ppermute(away, "core", [(0, 1), (1, 0)])
    o = call(cores_kernel, "cores", [pair] * 4, 5)(*mine, away)
    o = [o[0]] + [along_z(o[k], k) for k in (1, 2, 3)]
    u = call(chips_kernel, "chips", [kind((part, rows), bf16)] * 2, 4)(*o)
    u = [to_place(u[b], b) for b in range(2)]
    grad_features = call(last_kernel, "last", kind((rows, part), f32), 2)(*u)
    grad_references = call(references_kernel, "references", kind((REFS, part), f32), 2, flops=2 * REFS * part * everything)(
        grad_scores, cols
    )
    return (
        logits[:CLASSES, 0].reshape(batch, CLASSES),
        grad_features.reshape(batch, rows, part),
        grad_references.reshape(HEADS, P_SIZE, part),
    )


def solution(mesh):
    grid = Mesh(mesh.devices.reshape(DEPTH, 2, SIDE, SIDE), ("z", "core", "y", "x"))
    section, seq = ("z", "core"), ("y", "x")
    in_specs = (P(None, seq, None), P(section, None, None), P(section, seq, None), P(), P())
    out_specs = (P(), P(None, seq, section), P(section, None, seq))
    return jax.shard_map(local, mesh=grid, in_specs=in_specs, out_specs=out_specs, check_vma=False)
```

time: 631 us -> 156 us (0.25)
  blocking collectives: 353 us -> 14.9 us
  waiting for transfers between devices: 159 us -> 58.8 us
  starting transfers between devices: 14.4 us -> 60.7 us
  other arithmetic: 33.7 us -> 0.09 us
  local copies, waits for them, and re-layouts: 36.2 us -> 5.38 us
  matrix products: 18.1 us -> 0 us
  Pallas kernels: 0 us -> 13.4 us
  between operations: 15.4 us -> 2.08 us
    psum x9 -> x0, blocking collectives: 353 us -> none  [the longest x3 104 us: local(): lax.psum(jnp.einsum('bnhp,bnh->bhp', kernel, row_scale, precision=highest...]
    all_gather x3 -> x0, waiting for transfers between devices: 89.1 us -> none  [the longest x1 50.6 us: local(): grad_raw = lax.all_gather(grad_part, 'seq', axis=0, tiled=True)]
    ppermute x0 -> x29, starting transfers between devices: none -> 60.7 us  [the longest x18 33.3 us: send(): return lax.ppermute(value, ('y', 'x'), pairs)]
    ppermute x0 -> x29, waiting for transfers between devices: none -> 58.8 us  [the longest x18 30.9 us: send(): return lax.ppermute(value, ('y', 'x'), pairs)]
    unnamed x5 -> x0, waiting for transfers between devices: 58.7 us -> none
    unnamed x1 -> x0, other arithmetic: 30 us -> none
    unnamed x20 -> x9, local copies, waits for them, and re-layouts: 31.1 us -> 4.74 us
    dot_general x21 -> x0, matrix products: 18.1 us -> none  [the longest x1 2.85 us: local(): jnp.einsum('bnhp,bnd->dhp', scores_all, feature_cols, preferred_element_t...]
  transfers between devices with their start and end apart: 5 -> 29, of which waited for: 4 -> 21; matrix products, arithmetic and copies ran while one was open for 11% -> 1% of each run, Pallas kernels for 0% -> 1%
where the time goes in v2:
time: 156 us; the launch traced here: 155 us
  starting transfers between devices  60.7 us (39%)
  waiting for transfers between devices  58.8 us (38%)
  blocking collectives  14.9 us (10%)
  Pallas kernels  13.4 us (9%)
  local copies, waits for them, and re-layouts  5.38 us (3%)
  between operations  2.08 us (1%)
    ppermute x18, starting transfers between devices, send(): return lax.ppermute(value, ('y', 'x'), pairs)  33.3 us
    ppermute x18, waiting for transfers between devices, send(): return lax.ppermute(value, ('y', 'x'), pairs)  30.9 us
    all_to_all x1, blocking collectives, local(): near = lax.all_to_all(half, ('y', 'x'), 0, 0)  14.9 us
    ppermute x2, waiting for transfers between devices, to_place(): return lax.ppermute(value, ('z', 'core', 'y', 'x'), pairs)  12.2 us
    ppermute x3, starting transfers between devices, sum_logits(): total = total + lax.ppermute(total, 'z', [(i, i ^ k) for i in range(DEPTH)])  12 us
    ppermute x2, starting transfers between devices, to_place(): return lax.ppermute(value, ('z', 'core', 'y', 'x'), pairs)  10.6 us
    ppermute x3, waiting for transfers between devices, along_z(): return lax.ppermute(value, ('z', 'core'), pairs)  7.97 us
    pallas_call x1, Pallas kernels, local(): call(functools.partial(backward_kernel, width, score_scale), 'backward',...  6.73 us
  transfers between devices with their start and end apart: 29, of which 21 were waited for; matrix products, arithmetic and copies ran while one was open for 1% of the time, Pallas kernels for 1%

profile of v2, /device:TPU:12, one launch (start us, length us, event | category | flops | bytes accessed | tf_op | source)
XLA Modules:
  0.0 155.4 jit_solution(5373790645275875040)
XLA Ops:
  0.6 1.7 %copy-done = bf16[2,128,5120]{2,1,0:T(8,128)(2,1)S(1)} copy-done((bf16[2,128,5120]{2,1,0:T(8,128)(2,1)S(1)}, bf16[2,128,5120]{2,1,0:T(8,128)(2,1)}, u32[]{:S(2)}) %copy-start) | copy-done | bytes 2621464
  4.5 2.4 %collective-permute-start = (bf16[256,128]{1,0:T(8,128)(2,1)S(1)}, bf16[256,128]{1,0:T(8,128)(2,1)S(1)}, u32[]{:S(2)}, u32[]{:S(2)}) collective-permute-start(bf16[256,128]{1,0:T(8,128)(2,1)S(1)} %scores.1), channel_id=1, source_target_pairs={{0,8},{1,9},{2,10},{3,11},{4,12},{5,13},{6,14},{7,15},{8,0},{9,1},... | collective-permute-start | bytes 196616 | tf_op jit(solution)/shard_map/ppermute | solution.py:72
  7.4 3.7 %collective-permute-start.2 = (bf16[256,128]{1,0:T(8,128)(2,1)S(1)}, bf16[256,128]{1,0:T(8,128)(2,1)S(1)}, u32[]{:S(2)}, u32[]{:S(2)}) collective-permute-start(bf16[256,128]{1,0:T(8,128)(2,1)S(1)} %scores.1), channel_id=1, source_target_pairs={{0,10},{1,11},{2,8},{3,9},{4,14},{5,15},{6,12},{7,13},{8,2},{9,3},... | collective-permute-start | bytes 196616 | tf_op jit(solution)/shard_map/ppermute | solution.py:72
  12.9 2.7 %collective-permute-done.2 = bf16[256,128]{1,0:T(8,128)(2,1)S(1)} collective-permute-done((bf16[256,128]{1,0:T(8,128)(2,1)S(1)}, bf16[256,128]{1,0:T(8,128)(2,1)S(1)}, u32[]{:S(2)}, u32[]{:S(2)}) %collective-permute-start.2) | collective-permute-done | bytes 65568 | tf_op jit(solution)/shard_map/ppermute | solution.py:72
  15.6 14.9 %all_to_all.5.near_ref = bf16[16,160,128]{2,1,0:T(8,128)(2,1)S(1)} all-to-all(bf16[16,160,128]{2,1,0:T(8,128)(2,1)S(1)} %get-tuple-element.36), channel_id=1, replica_groups=mesh['z'=8,'core'=2,'y'=4,'x'=4] {'y','x'}, dimensions={0} | all-to-all | bytes 1310720 | tf_op jit(solution)/shard_map/all_to_all | solution.py:378
  34.8 4.5 %collective-permute-done.3.q1 = bf16[4,256,128]{2,1,0:T(8,128)(2,1)S(1)} collective-permute-done((bf16[4,256,128]{2,1,0:T(8,128)(2,1)S(1)}, bf16[4,256,128]{2,1,0:T(8,128)(2,1)S(1)}, u32[]{:S(2)}, u32[]{:S(2)}) %collective-permute-start.3) | collective-permute-done | bytes 262176 | tf_op jit(solution)/shard_map/ppermute | solution.py:72
  40.5 2.1 %collective-permute-done.5.q3 = bf16[4,256,128]{2,1,0:T(8,128)(2,1)S(1)} collective-permute-done((bf16[4,256,128]{2,1,0:T(8,128)(2,1)S(1)}, bf16[4,256,128]{2,1,0:T(8,128)(2,1)S(1)}, u32[]{:S(2)}, u32[]{:S(2)}) %collective-permute-start.5) | collective-permute-done | bytes 262176 | tf_op jit(solution)/shard_map/ppermute | solution.py:72
  42.5 3.7 %forward.1 = (bf16[1216,128]{1,0:T(8,128)(2,1)S(1)}, bf16[1216,128]{1,0:T(8,128)(2,1)S(1)}, bf16[1216,128]{1,0:T(8,128)(2,1)S(1)}, bf16[1216,128]{1,0:T(8,128)(2...) custom-call(bf16[4,256,128]{2,1,0:T(8,128)(2,1)S(1)} %pad_maximum_fu, ...), custom_call_target="tpu_custom_call" | custom-call | tf_op jit(solution)/shard_map/forward/pallas_call | solution.py:384
  47.5 2.5 %collective-permute-start.9 = (bf16[1216,128]{1,0:T(8,128)(2,1)S(1)}, bf16[1216,128]{1,0:T(8,128)(2,1)S(1)}, u32[]{:S(2)}, u32[]{:S(2)}) collective-permute-start(bf16[1216,128]{1,0:T(8,128)(2,1)S(1)} %get-tuple-element.40), channel_id=1, source_target_pairs={{0,15},{1,12},{2,13},{3,14},{4,3},{5,0},{6,1},{7,2},{8,7},{9,4},{1... | collective-permute-start | bytes 933896 | tf_op jit(solution)/shard_map/ppermute | solution.py:72
  49.9 5.1 %collective-permute-done.7.a1 = bf16[1216,128]{1,0:T(8,128)(2,1)S(1)} collective-permute-done((bf16[1216,128]{1,0:T(8,128)(2,1)S(1)}, bf16[1216,128]{1,0:T(8,128)(2,1)S(1)}, u32[]{:S(2)}, u32[]{:S(2)}) %collective-permute-start.7) | collective-permute-done | bytes 311328 | tf_op jit(solution)/shard_map/ppermute | solution.py:72
  55.0 2.2 %collective-permute-done.9.a3 = bf16[1216,128]{1,0:T(8,128)(2,1)S(1)} collective-permute-done((bf16[1216,128]{1,0:T(8,128)(2,1)S(1)}, bf16[1216,128]{1,0:T(8,128)(2,1)S(1)}, u32[]{:S(2)}, u32[]{:S(2)}) %collective-permute-start.9) | collective-permute-done | bytes 311328 | tf_op jit(solution)/shard_map/ppermute | solution.py:72
  57.4 4.3 %collective-permute-start.10 = (bf16[352,128]{1,0:T(8,128)(2,1)S(1)}, bf16[352,128]{1,0:T(8,128)(2,1)S(1)}, u32[]{:S(2)}, u32[]{:S(2)}) collective-permute-start(bf16[352,128]{1,0:T(8,128)(2,1)S(1)} %get-tuple-element.42), channel_id=1, source_target_pairs={{0,8},{1,9},{2,10},{3,11},{4,12},{5,13},{6,14},{7,15},{8,0},{9,1},... | collective-permute-start | bytes 270344 | tf_op jit(solution)/shard_map/ppermute | solution.py:72
  61.7 2.7 %collective-permute-start.11 = (bf16[352,128]{1,0:T(8,128)(2,1)S(1)}, bf16[352,128]{1,0:T(8,128)(2,1)S(1)}, u32[]{:S(2)}, u32[]{:S(2)}) collective-permute-start(bf16[352,128]{1,0:T(8,128)(2,1)S(1)} %get-tuple-element.43), channel_id=1, source_target_pairs={{0,2},{1,3},{2,0},{3,1},{4,6},{5,7},{6,4},{7,5},{8,10},{9,11},{10,... | collective-permute-start | bytes 270344 | tf_op jit(solution)/shard_map/ppermute | solution.py:72
  64.8 3.0 %collective-permute-done.11.c2 = bf16[352,128]{1,0:T(8,128)(2,1)S(1)} collective-permute-done((bf16[352,128]{1,0:T(8,128)(2,1)S(1)}, bf16[352,128]{1,0:T(8,128)(2,1)S(1)}, u32[]{:S(2)}, u32[]{:S(2)}) %collective-permute-start.11) | collective-permute-done | bytes 90144 | tf_op jit(solution)/shard_map/ppermute | solution.py:72
  67.7 5.1 %collective-permute-done.12.c3 = bf16[352,128]{1,0:T(8,128)(2,1)S(1)} collective-permute-done((bf16[352,128]{1,0:T(8,128)(2,1)S(1)}, bf16[352,128]{1,0:T(8,128)(2,1)S(1)}, u32[]{:S(2)}, u32[]{:S(2)}) %collective-permute-start.12) | collective-permute-done | bytes 90144 | tf_op jit(solution)/shard_map/ppermute | solution.py:72
  73.8 2.3 %collective-permute-start.19 = (bf16[288,128]{1,0:T(8,128)(2,1)S(1)}, bf16[288,128]{1,0:T(8,128)(2,1)S(1)}, u32[]{:S(2)}, u32[]{:S(2)}) collective-permute-start(bf16[288,128]{1,0:T(8,128)(2,1)S(1)} %get-tuple-element.46), channel_id=1, source_target_pairs={{0,10},{1,11},{2,8},{3,9},{4,14},{5,15},{6,12},{7,13},{8,2},{9,3},... | collective-permute-start | bytes 221192 | tf_op jit(solution)/shard_map/ppermute | solution.py:72
  76.1 3.4 %collective-permute-start.17 = (bf16[288,128]{1,0:T(8,128)(2,1)S(1)}, bf16[288,128]{1,0:T(8,128)(2,1)S(1)}, u32[]{:S(2)}, u32[]{:S(2)}) collective-permute-start(bf16[288,128]{1,0:T(8,128)(2,1)S(1)} %get-tuple-element.46), channel_id=1, source_target_pairs={{0,8},{1,9},{2,10},{3,11},{4,12},{5,13},{6,14},{7,15},{8,0},{9,1},... | collective-permute-start | bytes 221192 | tf_op jit(solution)/shard_map/ppermute | solution.py:72
  79.5 2.7 %collective-permute-done.19 = bf16[288,128]{1,0:T(8,128)(2,1)S(1)} collective-permute-done((bf16[288,128]{1,0:T(8,128)(2,1)S(1)}, bf16[288,128]{1,0:T(8,128)(2,1)S(1)}, u32[]{:S(2)}, u32[]{:S(2)}) %collective-permute-start.19) | collective-permute-done | bytes 73760 | tf_op jit(solution)/shard_map/ppermute | solution.py:72
  84.9 2.0 %collective-permute-start.21 = (bf16[4,288,128]{2,1,0:T(8,128)(2,1)S(1)}, bf16[4,288,128]{2,1,0:T(8,128)(2,1)S(1)}, u32[]{:S(2)}, u32[]{:S(2)}) collective-permute-start(bf16[4,288,128]{2,1,0:T(8,128)(2,1)S(1)} %pad_maximum_fusion.t0), channel_id=1, source_target_pairs={{0,3},{1,0},{2,1},{3,2},{4,7},{5,4},{6,5},{7,6},{8,11},{9,8},{10,9... | collective-permute-start | bytes 884744 | tf_op jit(solution)/shard_map/ppermute | solution.py:72
  86.8 2.4 %collective-permute-start.22 = (bf16[4,288,128]{2,1,0:T(8,128)(2,1)S(1)}, bf16[4,288,128]{2,1,0:T(8,128)(2,1)S(1)}, u32[]{:S(2)}, u32[]{:S(2)}) collective-permute-start(bf16[4,288,128]{2,1,0:T(8,128)(2,1)S(1)} %pad_maximum_fusion.t0), channel_id=1, source_target_pairs={{0,5},{1,6},{2,7},{3,4},{4,9},{5,10},{6,11},{7,8},{8,13},{9,14},{1... | collective-permute-start | bytes 884744 | tf_op jit(solution)/shard_map/ppermute | solution.py:72
  90.4 1.9 %collective-permute-start.14 = (f32[16,128]{1,0:T(8,128)S(1)}, f32[16,128]{1,0:T(8,128)S(1)}, u32[]{:S(2)}, u32[]{:S(2)}) collective-permute-start(f32[16,128]{1,0:T(8,128)S(1)} %add.14), channel_id=1, source_target_pairs={{0,32},{32,0},{64,96},{96,64},{128,160},{160,128},{192,224},{224,1... | collective-permute-start | bytes 24584 | tf_op jit(solution)/shard_map/ppermute | solution.py:358
  92.3 1.7 %collective-permute-done.14 = f32[16,128]{1,0:T(8,128)S(1)} collective-permute-done((f32[16,128]{1,0:T(8,128)S(1)}, f32[16,128]{1,0:T(8,128)S(1)}, u32[]{:S(2)}, u32[]{:S(2)}) %collective-permute-start.14) | collective-permute-done | bytes 8224 | tf_op jit(solution)/shard_map/ppermute | solution.py:358
  94.0 3.3 %collective-permute-start.15 = (f32[16,128]{1,0:T(8,128)S(1)}, f32[16,128]{1,0:T(8,128)S(1)}, u32[]{:S(2)}, u32[]{:S(2)}) collective-permute-start(f32[16,128]{1,0:T(8,128)S(1)} %add.15), channel_id=1, source_target_pairs={{0,64},{32,96},{64,0},{96,32},{128,192},{160,224},{192,128},{224,1... | collective-permute-start | bytes 24584 | tf_op jit(solution)/shard_map/ppermute | solution.py:358
  99.0 6.8 %collective-permute-start.16 = (f32[16,128]{1,0:T(8,128)S(1)}, f32[16,128]{1,0:T(8,128)S(1)}, u32[]{:S(2)}, u32[]{:S(2)}) collective-permute-start(f32[16,128]{1,0:T(8,128)S(1)} %add.16), channel_id=1, source_target_pairs={{0,128},{32,160},{64,192},{96,224},{128,0},{160,32},{192,64},{224,... | collective-permute-start | bytes 24584 | tf_op jit(solution)/shard_map/ppermute | solution.py:358
  107.4 6.7 %backward.1 = (bf16[256,2048]{1,0:T(8,128)(2,1)S(1)}, bf16[2,320,128]{2,1,0:T(8,128)(2,1)S(1)}, bf16[2,320,128]{2,1,0:T(8,128)(2,1)S(1)}, bf16[2,320,128]{2,1,0:...) custom-call(bf16[4,256,128]{2,1,0:T(8,128)(2,1)S(1)} %pad_maximum_fusion.1.q0, ...), custom_call_target="tpu_custom_call" | custom-call | tf_op jit(solution)/shard_map/backward/pallas_call | solution.py:404
  114.3 2.1 %collective-permute-done.23.other_ref = bf16[8,320,128]{2,1,0:T(8,128)(2,1)S(1)} collective-permute-done((bf16[8,320,128]{2,1,0:T(8,128)(2,1)S(1)}, bf16[8,320,128]{2,1,0:T(8,128)(2,1)S(1)}, u32[]{:S(2)}, u32[]{:S(2)}) %collective-permute-start.23) | collective-permute-done | bytes 655392 | tf_op jit(solution)/shard_map/ppermute | solution.py:417
  117.6 3.7 %collective-permute-start.25 = (bf16[2,320,128]{2,1,0:T(8,128)(2,1)S(1)}, bf16[2,320,128]{2,1,0:T(8,128)(2,1)S(1)}, u32[]{:S(2)}, u32[]{:S(2)}) collective-permute-start(bf16[2,320,128]{2,1,0:T(8,128)(2,1)S(1)} %get-tuple-element.61), channel_id=1, source_target_pairs={{0,224},{16,240},{32,0},{48,16},{64,32},{80,48},{96,64},{112,80},{... | collective-permute-start | bytes 491528 | tf_op jit(solution)/shard_map/ppermute | solution.py:342
  121.3 4.4 %collective-permute-done.24.o1 = bf16[2,320,128]{2,1,0:T(8,128)(2,1)S(1)} collective-permute-done((bf16[2,320,128]{2,1,0:T(8,128)(2,1)S(1)}, bf16[2,320,128]{2,1,0:T(8,128)(2,1)S(1)}, u32[]{:S(2)}, u32[]{:S(2)}) %collective-permute-start.24) | collective-permute-done | bytes 163872 | tf_op jit(solution)/shard_map/ppermute | solution.py:342
  125.8 3.4 %collective-permute-done.26.o3 = bf16[2,320,128]{2,1,0:T(8,128)(2,1)S(1)} collective-permute-done((bf16[2,320,128]{2,1,0:T(8,128)(2,1)S(1)}, bf16[2,320,128]{2,1,0:T(8,128)(2,1)S(1)}, u32[]{:S(2)}, u32[]{:S(2)}) %collective-permute-start.26) | collective-permute-done | bytes 163872 | tf_op jit(solution)/shard_map/ppermute | solution.py:342
  129.3 7.5 %collective-permute-start.27 = (bf16[320,128]{1,0:T(8,128)(2,1)S(1)}, bf16[320,128]{1,0:T(8,128)(2,1)S(1)}, u32[]{:S(2)}, u32[]{:S(2)}) collective-permute-start(bf16[320,128]{1,0:T(8,128)(2,1)S(1)} %get-tuple-element.63), channel_id=1, source_target_pairs={{0,0},{1,16},{2,32},{3,48},{4,64},{5,80},{6,96},{7,112},{8,128},{9... | collective-permute-start | bytes 245768 | tf_op jit(solution)/shard_map/ppermute | solution.py:352
  136.8 3.1 %collective-permute-start.28 = (bf16[320,128]{1,0:T(8,128)(2,1)S(1)}, bf16[320,128]{1,0:T(8,128)(2,1)S(1)}, u32[]{:S(2)}, u32[]{:S(2)}) collective-permute-start(bf16[320,128]{1,0:T(8,128)(2,1)S(1)} %get-tuple-element.64), channel_id=1, source_target_pairs={{0,8},{1,24},{2,40},{3,56},{4,72},{5,88},{6,104},{7,120},{8,136},{... | collective-permute-start | bytes 245768 | tf_op jit(solution)/shard_map/ppermute | solution.py:352
  142.5 11.9 %collective-permute-done.28.u1 = bf16[320,128]{1,0:T(8,128)(2,1)S(1)} collective-permute-done((bf16[320,128]{1,0:T(8,128)(2,1)S(1)}, bf16[320,128]{1,0:T(8,128)(2,1)S(1)}, u32[]{:S(2)}, u32[]{:S(2)}) %collective-permute-start.28) | collective-permute-done | bytes 81952 | tf_op jit(solution)/shard_map/ppermute | solution.py:352
  (54 shorter events, 23.4 us)
Async XLA Ops:
  0.6 1.7 %copy-start = (bf16[2,128,5120]{2,1,0:T(8,128)(2,1)S(1)}, bf16[2,128,5120]{2,1,0:T(8,128)(2,1)}, u32[]{:S(2)}) copy-start(bf16[2,128,5120]{2,1,0:T(8,128)(2,1)} %param.6) | copy-start | bytes 7864324
  2.4 1.3 copy-start.1
  4.5 7.3 %collective-permute-start = (bf16[256,128]{1,0:T(8,128)(2,1)S(1)}, bf16[256,128]{1,0:T(8,128)(2,1)S(1)}, u32[]{:S(2)}, u32[]{:S(2)}) collective-permute-start(bf16[256,128]{1,0:T(8,128)(2,1)S(1)} %scores.1), channel_id=1, source_target_pairs={{0,8},{1,9},{2,10},{3,11},{4,12},{5,13},{6,14},{7,15},{8,0},{9,1},... | collective-permute-start | bytes 196616 | tf_op jit(solution)/shard_map/ppermute | solution.py:72
  6.9 6.0 %collective-permute-start.1 = (bf16[256,128]{1,0:T(8,128)(2,1)S(1)}, bf16[256,128]{1,0:T(8,128)(2,1)S(1)}, u32[]{:S(2)}, u32[]{:S(2)}) collective-permute-start(bf16[256,128]{1,0:T(8,128)(2,1)S(1)} %scores.1), channel_id=1, source_target_pairs={{0,2},{1,3},{2,0},{3,1},{4,6},{5,7},{6,4},{7,5},{8,10},{9,11},{10,... | collective-permute-start | bytes 196616 | tf_op jit(solution)/shard_map/ppermute | solution.py:72
  7.4 8.2 %collective-permute-start.2 = (bf16[256,128]{1,0:T(8,128)(2,1)S(1)}, bf16[256,128]{1,0:T(8,128)(2,1)S(1)}, u32[]{:S(2)}, u32[]{:S(2)}) collective-permute-start(bf16[256,128]{1,0:T(8,128)(2,1)S(1)} %scores.1), channel_id=1, source_target_pairs={{0,10},{1,11},{2,8},{3,9},{4,14},{5,15},{6,12},{7,13},{8,2},{9,3},... | collective-permute-start | bytes 196616 | tf_op jit(solution)/shard_map/ppermute | solution.py:72
  11.9 22.2 %copy-start.2 = (bf16[2,320,10]{1,0,2:T(2,128)(2,1)S(1)}, bf16[2,320,10]{1,0,2:T(2,128)(2,1)}, u32[]{:S(2)}) copy-start(bf16[2,320,10]{1,0,2:T(2,128)(2,1)} %param.7) | copy-start | bytes 38404
  30.6 12.0 %collective-permute-start.6 = (bf16[16,160,128]{2,1,0:T(8,128)(2,1)S(1)}, bf16[16,160,128]{2,1,0:T(8,128)(2,1)S(1)}, u32[]{:S(2)}, u32[]{:S(2)}) collective-permute-start(bf16[16,160,128]{2,1,0:T(8,128)(2,1)S(1)} %all_to_all.5.near_ref), channel_id=1, source_target_pairs={{0,16},{16,0},{1,17},{17,1},{2,18},{18,2},{3,19},{19,3},{4,20},{20... | collective-permute-start | bytes 1966088 | tf_op jit(solution)/shard_map/ppermute | solution.py:379
  30.6 8.7 %collective-permute-start.3 = (bf16[4,256,128]{2,1,0:T(8,128)(2,1)S(1)}, bf16[4,256,128]{2,1,0:T(8,128)(2,1)S(1)}, u32[]{:S(2)}, u32[]{:S(2)}) collective-permute-start(bf16[4,256,128]{2,1,0:T(8,128)(2,1)S(1)} %pad_maximum_fusion.1.q0), channel_id=1, source_target_pairs={{0,12},{1,13},{2,14},{3,15},{4,0},{5,1},{6,2},{7,3},{8,4},{9,5},{1... | collective-permute-start | bytes 786440 | tf_op jit(solution)/shard_map/ppermute | solution.py:72
  32.0 8.4 %collective-permute-start.4 = (bf16[4,256,128]{2,1,0:T(8,128)(2,1)S(1)}, bf16[4,256,128]{2,1,0:T(8,128)(2,1)S(1)}, u32[]{:S(2)}, u32[]{:S(2)}) collective-permute-start(bf16[4,256,128]{2,1,0:T(8,128)(2,1)S(1)} %pad_maximum_fusion.1.q0), channel_id=1, source_target_pairs={{0,3},{1,0},{2,1},{3,2},{4,7},{5,4},{6,5},{7,6},{8,11},{9,8},{10,9... | collective-permute-start | bytes 786440 | tf_op jit(solution)/shard_map/ppermute | solution.py:72
  33.5 9.1 %collective-permute-start.5 = (bf16[4,256,128]{2,1,0:T(8,128)(2,1)S(1)}, bf16[4,256,128]{2,1,0:T(8,128)(2,1)S(1)}, u32[]{:S(2)}, u32[]{:S(2)}) collective-permute-start(bf16[4,256,128]{2,1,0:T(8,128)(2,1)S(1)} %pad_maximum_fusion.1.q0), channel_id=1, source_target_pairs={{0,5},{1,6},{2,7},{3,4},{4,9},{5,10},{6,11},{7,8},{8,13},{9,14},{1... | collective-permute-start | bytes 786440 | tf_op jit(solution)/shard_map/ppermute | solution.py:72
  46.2 8.8 %collective-permute-start.7 = (bf16[1216,128]{1,0:T(8,128)(2,1)S(1)}, bf16[1216,128]{1,0:T(8,128)(2,1)S(1)}, u32[]{:S(2)}, u32[]{:S(2)}) collective-permute-start(bf16[1216,128]{1,0:T(8,128)(2,1)S(1)} %get-tuple-element.38), channel_id=1, source_target_pairs={{0,4},{1,5},{2,6},{3,7},{4,8},{5,9},{6,10},{7,11},{8,12},{9,13},{1... | collective-permute-start | bytes 933896 | tf_op jit(solution)/shard_map/ppermute | solution.py:72
  46.6 8.4 %collective-permute-start.8 = (bf16[1216,128]{1,0:T(8,128)(2,1)S(1)}, bf16[1216,128]{1,0:T(8,128)(2,1)S(1)}, u32[]{:S(2)}, u32[]{:S(2)}) collective-permute-start(bf16[1216,128]{1,0:T(8,128)(2,1)S(1)} %get-tuple-element.39), channel_id=1, source_target_pairs={{0,1},{1,2},{2,3},{3,0},{4,5},{5,6},{6,7},{7,4},{8,9},{9,10},{10,1... | collective-permute-start | bytes 933896 | tf_op jit(solution)/shard_map/ppermute | solution.py:72
  47.5 9.8 %collective-permute-start.9 = (bf16[1216,128]{1,0:T(8,128)(2,1)S(1)}, bf16[1216,128]{1,0:T(8,128)(2,1)S(1)}, u32[]{:S(2)}, u32[]{:S(2)}) collective-permute-start(bf16[1216,128]{1,0:T(8,128)(2,1)S(1)} %get-tuple-element.40), channel_id=1, source_target_pairs={{0,15},{1,12},{2,13},{3,14},{4,3},{5,0},{6,1},{7,2},{8,7},{9,4},{1... | collective-permute-start | bytes 933896 | tf_op jit(solution)/shard_map/ppermute | solution.py:72
  57.4 7.4 %collective-permute-start.10 = (bf16[352,128]{1,0:T(8,128)(2,1)S(1)}, bf16[352,128]{1,0:T(8,128)(2,1)S(1)}, u32[]{:S(2)}, u32[]{:S(2)}) collective-permute-start(bf16[352,128]{1,0:T(8,128)(2,1)S(1)} %get-tuple-element.42), channel_id=1, source_target_pairs={{0,8},{1,9},{2,10},{3,11},{4,12},{5,13},{6,14},{7,15},{8,0},{9,1},... | collective-permute-start | bytes 270344 | tf_op jit(solution)/shard_map/ppermute | solution.py:72
  61.7 6.0 %collective-permute-start.11 = (bf16[352,128]{1,0:T(8,128)(2,1)S(1)}, bf16[352,128]{1,0:T(8,128)(2,1)S(1)}, u32[]{:S(2)}, u32[]{:S(2)}) collective-permute-start(bf16[352,128]{1,0:T(8,128)(2,1)S(1)} %get-tuple-element.43), channel_id=1, source_target_pairs={{0,2},{1,3},{2,0},{3,1},{4,6},{5,7},{6,4},{7,5},{8,10},{9,11},{10,... | collective-permute-start | bytes 270344 | tf_op jit(solution)/shard_map/ppermute | solution.py:72
  64.4 8.4 %collective-permute-start.12 = (bf16[352,128]{1,0:T(8,128)(2,1)S(1)}, bf16[352,128]{1,0:T(8,128)(2,1)S(1)}, u32[]{:S(2)}, u32[]{:S(2)}) collective-permute-start(bf16[352,128]{1,0:T(8,128)(2,1)S(1)} %get-tuple-element.44), channel_id=1, source_target_pairs={{0,10},{1,11},{2,8},{3,9},{4,14},{5,15},{6,12},{7,13},{8,2},{9,3},... | collective-permute-start | bytes 270344 | tf_op jit(solution)/shard_map/ppermute | solution.py:72
  73.0 6.5 %collective-permute-start.18 = (bf16[288,128]{1,0:T(8,128)(2,1)S(1)}, bf16[288,128]{1,0:T(8,128)(2,1)S(1)}, u32[]{:S(2)}, u32[]{:S(2)}) collective-permute-start(bf16[288,128]{1,0:T(8,128)(2,1)S(1)} %get-tuple-element.46), channel_id=1, source_target_pairs={{0,2},{1,3},{2,0},{3,1},{4,6},{5,7},{6,4},{7,5},{8,10},{9,11},{10,... | collective-permute-start | bytes 221192 | tf_op jit(solution)/shard_map/ppermute | solution.py:72
  73.8 8.4 %collective-permute-start.19 = (bf16[288,128]{1,0:T(8,128)(2,1)S(1)}, bf16[288,128]{1,0:T(8,128)(2,1)S(1)}, u32[]{:S(2)}, u32[]{:S(2)}) collective-permute-start(bf16[288,128]{1,0:T(8,128)(2,1)S(1)} %get-tuple-element.46), channel_id=1, source_target_pairs={{0,10},{1,11},{2,8},{3,9},{4,14},{5,15},{6,12},{7,13},{8,2},{9,3},... | collective-permute-start | bytes 221192 | tf_op jit(solution)/shard_map/ppermute | solution.py:72
  76.1 7.4 %collective-permute-start.17 = (bf16[288,128]{1,0:T(8,128)(2,1)S(1)}, bf16[288,128]{1,0:T(8,128)(2,1)S(1)}, u32[]{:S(2)}, u32[]{:S(2)}) collective-permute-start(bf16[288,128]{1,0:T(8,128)(2,1)S(1)} %get-tuple-element.46), channel_id=1, source_target_pairs={{0,8},{1,9},{2,10},{3,11},{4,12},{5,13},{6,14},{7,15},{8,0},{9,1},... | collective-permute-start | bytes 221192 | tf_op jit(solution)/shard_map/ppermute | solution.py:72
  83.6 23.8 %collective-permute-start.20 = (bf16[4,288,128]{2,1,0:T(8,128)(2,1)S(1)}, bf16[4,288,128]{2,1,0:T(8,128)(2,1)S(1)}, u32[]{:S(2)}, u32[]{:S(2)}) collective-permute-start(bf16[4,288,128]{2,1,0:T(8,128)(2,1)S(1)} %pad_maximum_fusion.t0), channel_id=1, source_target_pairs={{0,12},{1,13},{2,14},{3,15},{4,0},{5,1},{6,2},{7,3},{8,4},{9,5},{1... | collective-permute-start | bytes 884744 | tf_op jit(solution)/shard_map/ppermute | solution.py:72
  84.9 22.6 %collective-permute-start.21 = (bf16[4,288,128]{2,1,0:T(8,128)(2,1)S(1)}, bf16[4,288,128]{2,1,0:T(8,128)(2,1)S(1)}, u32[]{:S(2)}, u32[]{:S(2)}) collective-permute-start(bf16[4,288,128]{2,1,0:T(8,128)(2,1)S(1)} %pad_maximum_fusion.t0), channel_id=1, source_target_pairs={{0,3},{1,0},{2,1},{3,2},{4,7},{5,4},{6,5},{7,6},{8,11},{9,8},{10,9... | collective-permute-start | bytes 884744 | tf_op jit(solution)/shard_map/ppermute | solution.py:72
  86.8 20.6 %collective-permute-start.22 = (bf16[4,288,128]{2,1,0:T(8,128)(2,1)S(1)}, bf16[4,288,128]{2,1,0:T(8,128)(2,1)S(1)}, u32[]{:S(2)}, u32[]{:S(2)}) collective-permute-start(bf16[4,288,128]{2,1,0:T(8,128)(2,1)S(1)} %pad_maximum_fusion.t0), channel_id=1, source_target_pairs={{0,5},{1,6},{2,7},{3,4},{4,9},{5,10},{6,11},{7,8},{8,13},{9,14},{1... | collective-permute-start | bytes 884744 | tf_op jit(solution)/shard_map/ppermute | solution.py:72
  89.2 1.2 collective-permute-start.13
  90.4 3.7 %collective-permute-start.14 = (f32[16,128]{1,0:T(8,128)S(1)}, f32[16,128]{1,0:T(8,128)S(1)}, u32[]{:S(2)}, u32[]{:S(2)}) collective-permute-start(f32[16,128]{1,0:T(8,128)S(1)} %add.14), channel_id=1, source_target_pairs={{0,32},{32,0},{64,96},{96,64},{128,160},{160,128},{192,224},{224,1... | collective-permute-start | bytes 24584 | tf_op jit(solution)/shard_map/ppermute | solution.py:358
  94.0 4.9 %collective-permute-start.15 = (f32[16,128]{1,0:T(8,128)S(1)}, f32[16,128]{1,0:T(8,128)S(1)}, u32[]{:S(2)}, u32[]{:S(2)}) collective-permute-start(f32[16,128]{1,0:T(8,128)S(1)} %add.15), channel_id=1, source_target_pairs={{0,64},{32,96},{64,0},{96,32},{128,192},{160,224},{192,128},{224,1... | collective-permute-start | bytes 24584 | tf_op jit(solution)/shard_map/ppermute | solution.py:358
  99.0 8.4 %collective-permute-start.16 = (f32[16,128]{1,0:T(8,128)S(1)}, f32[16,128]{1,0:T(8,128)S(1)}, u32[]{:S(2)}, u32[]{:S(2)}) collective-permute-start(f32[16,128]{1,0:T(8,128)S(1)} %add.16), channel_id=1, source_target_pairs={{0,128},{32,160},{64,192},{96,224},{128,0},{160,32},{192,64},{224,... | collective-permute-start | bytes 24584 | tf_op jit(solution)/shard_map/ppermute | solution.py:358
  114.2 2.2 %collective-permute-start.23 = (bf16[8,320,128]{2,1,0:T(8,128)(2,1)S(1)}, bf16[8,320,128]{2,1,0:T(8,128)(2,1)S(1)}, u32[]{:S(2)}, u32[]{:S(2)}) collective-permute-start(bf16[8,320,128]{2,1,0:T(8,128)(2,1)S(1)} %get-tuple-element.58), channel_id=1, source_target_pairs={{0,16},{16,0},{1,17},{17,1},{2,18},{18,2},{3,19},{19,3},{4,20},{20... | collective-permute-start | bytes 1966088 | tf_op jit(solution)/shard_map/ppermute | solution.py:417
  116.5 9.2 %collective-permute-start.24 = (bf16[2,320,128]{2,1,0:T(8,128)(2,1)S(1)}, bf16[2,320,128]{2,1,0:T(8,128)(2,1)S(1)}, u32[]{:S(2)}, u32[]{:S(2)}) collective-permute-start(bf16[2,320,128]{2,1,0:T(8,128)(2,1)S(1)} %get-tuple-element.60), channel_id=1, source_target_pairs={{0,32},{16,48},{32,64},{48,80},{64,96},{80,112},{96,128},{112,144}... | collective-permute-start | bytes 491528 | tf_op jit(solution)/shard_map/ppermute | solution.py:342
  117.6 8.2 %collective-permute-start.25 = (bf16[2,320,128]{2,1,0:T(8,128)(2,1)S(1)}, bf16[2,320,128]{2,1,0:T(8,128)(2,1)S(1)}, u32[]{:S(2)}, u32[]{:S(2)}) collective-permute-start(bf16[2,320,128]{2,1,0:T(8,128)(2,1)S(1)} %get-tuple-element.61), channel_id=1, source_target_pairs={{0,224},{16,240},{32,0},{48,16},{64,32},{80,48},{96,64},{112,80},{... | collective-permute-start | bytes 491528 | tf_op jit(solution)/shard_map/ppermute | solution.py:342
  121.3 8.0 %collective-permute-start.26 = (bf16[2,320,128]{2,1,0:T(8,128)(2,1)S(1)}, bf16[2,320,128]{2,1,0:T(8,128)(2,1)S(1)}, u32[]{:S(2)}, u32[]{:S(2)}) collective-permute-start(bf16[2,320,128]{2,1,0:T(8,128)(2,1)S(1)} %get-tuple-element.62), channel_id=1, source_target_pairs={{0,64},{16,208},{32,96},{48,240},{64,128},{80,16},{96,160},{112,48... | collective-permute-start | bytes 491528 | tf_op jit(solution)/shard_map/ppermute | solution.py:342
  129.3 13.2 %collective-permute-start.27 = (bf16[320,128]{1,0:T(8,128)(2,1)S(1)}, bf16[320,128]{1,0:T(8,128)(2,1)S(1)}, u32[]{:S(2)}, u32[]{:S(2)}) collective-permute-start(bf16[320,128]{1,0:T(8,128)(2,1)S(1)} %get-tuple-element.63), channel_id=1, source_target_pairs={{0,0},{1,16},{2,32},{3,48},{4,64},{5,80},{6,96},{7,112},{8,128},{9... | collective-permute-start | bytes 245768 | tf_op jit(solution)/shard_map/ppermute | solution.py:352
  136.8 17.6 %collective-permute-start.28 = (bf16[320,128]{1,0:T(8,128)(2,1)S(1)}, bf16[320,128]{1,0:T(8,128)(2,1)S(1)}, u32[]{:S(2)}, u32[]{:S(2)}) collective-permute-start(bf16[320,128]{1,0:T(8,128)(2,1)S(1)} %get-tuple-element.64), channel_id=1, source_target_pairs={{0,8},{1,24},{2,40},{3,56},{4,72},{5,88},{6,104},{7,120},{8,136},{... | collective-permute-start | bytes 245768 | tf_op jit(solution)/shard_map/ppermute | solution.py:352

commit v3 on v2

--- a/solution.py
+++ b/solution.py
@@ -29,6 +29,7 @@
 CHIPS = ((0, 1, 7, 2), (0, 1, 7, 6))
 T_ROWS = REFS + HEADS * PAD
 M_ROWS = 4 * PAD
+L_ROWS = 2 * PAD
 VMEM = pl.BlockSpec(memory_space=pltpu.VMEM)
 SMEM = pl.BlockSpec(memory_space=pltpu.SMEM)
 NT = (((1,), (1,)), ((), ()))
@@ -50,9 +51,13 @@
 
 
 def moved(first, second):
-    y = lax.rem(lax.axis_index("y") + first[0] + second[0], SIDE)
-    x = lax.rem(lax.axis_index("x") + first[1] + second[1], SIDE)
+    y = lax.rem(lax.axis_index("y") + (first[0] + second[0]) % SIDE, SIDE)
+    x = lax.rem(lax.axis_index("x") + (first[1] + second[1]) % SIDE, SIDE)
     return y * SIDE + x
+
+
+def back(step):
+    return (-step[0], -step[1])
 
 
 def block_of(s):
@@ -72,9 +77,14 @@
     return lax.ppermute(value, ("y", "x"), pairs)
 
 
-def gather(value):
-    row = jnp.stack([value] + [send(value, step, -1) for step in FAR[1:]])
-    return [row] + [send(row, step, -1) for step in NEAR[1:]]
+def stack_kernel(a, b, c, d, out_ref):
+    for k, ref in enumerate((a, b, c, d)):
+        out_ref[k] = ref[...]
+
+
+def stack(values):
+    shape = values[0].shape
+    return call(stack_kernel, "stack", jax.ShapeDtypeStruct((4,) + shape, bf16), 4)(*values)
 
 
 def scores_kernel(scale, f_ref, r_ref, k_ref):
@@ -82,15 +92,24 @@
     k_ref[...] = jnp.exp(scores * scale).astype(bf16)
 
 
-def split_kernel(f_ref, refs_ref, half_ref, mine_ref, turned_ref):
-    part = mine_ref.shape[1]
-    half = part // 2
+def split_kernel(f_ref, g0, g1, g2, g3, turned_ref):
+    half = g0.shape[1]
+    part = 2 * half
     for j in range(BLOCKS // 2):
         where = slice(2 * part * j, 2 * part * (j + 1))
         turned_ref[where, :] = jnp.transpose(f_ref[:, where])
     core = lax.axis_index("core")
-    for j in range(BLOCKS):
-        half_ref[j] = turned_ref[pl.ds(pl.multiple_of(part * j + half * core, half), half), :]
+    for k, out in enumerate((g0, g1, g2, g3)):
+        for i in range(4):
+            start = part * moved(FAR[k], NEAR[i]) + half * core
+            out[i] = turned_ref[pl.ds(pl.multiple_of(start, half), half), :]
+
+
+def regroup_kernel(h0, h1, h2, h3, refs_ref, e0, e1, e2, e3, mine_ref):
+    part = mine_ref.shape[1]
+    for i, out in enumerate((e0, e1, e2, e3)):
+        for k, ref in enumerate((h0, h1, h2, h3)):
+            out[k] = ref[i]
     place = moved((0, 0), (0, 0))
     pair = refs_ref[:, pl.ds(pl.multiple_of((place // 2) * (2 * part), 2 * part), 2 * part)]
     mine_ref[...] = jnp.where(lax.rem(place, 2) == 0, pair[:, :part], pair[:, part:])
@@ -129,22 +148,13 @@
     return moments
 
 
-def forward_kernel(
-    q0, q1, q2, q3, near_ref, other_ref, wt_ref, len_ref,
-    a0, a1, a2, a3, raw_ref, rs_ref, rt_ref, col_ref, fc_ref, plan_ref, wide_ref, ext_ref,
-):
+def sinkhorn_kernel(q0, q1, q2, q3, len_ref, rs_ref, rt_ref, col_ref, plan_ref):
     q = (q0, q1, q2, q3)
-    core = lax.axis_index("core")
     length = len_ref[0]
     rows = q0.shape[2]
-    half = near_ref.shape[1]
     mass = 1.0 / (jnp.zeros((1, rows), jnp.int32) + length).astype(f32)
     lane = lax.broadcasted_iota(jnp.int32, (1, rows), 1)
     masses = [jnp.where(block_of(s) * rows + lane < length, mass, 0.0) for s in range(BLOCKS)]
-    for s in range(BLOCKS):
-        here = slice(s * rows, (s + 1) * rows)
-        fc_ref[pl.ds(pl.multiple_of(core * half, half), half), here] = near_ref[s]
-        fc_ref[pl.ds(pl.multiple_of((1 - core) * half, half), half), here] = other_ref[s]
     for t in range(ITERS):
         for h in range(HEADS):
             here = slice(h * P_SIZE, (h + 1) * P_SIZE)
@@ -167,6 +177,18 @@
             place = ((ITERS - 1) * HEADS + h) * BLOCKS + s
             plan = rs_ref[place : place + 1, :] * k * col_ref[ITERS - 1, here, :]
             plan_ref[here, lanes(block_of(s), rows)] = plan.astype(bf16)
+
+
+def forward_kernel(
+    e_ref, other_ref, wt_ref, plan_ref, a0, a1, a2, a3, raw_ref, fc_ref, wide_ref, ext_ref
+):
+    core = lax.axis_index("core")
+    half, rows = e_ref.shape[2:]
+    for i in range(4):
+        for k in range(4):
+            here = lanes(moved(back(NEAR[i]), FAR[k]), rows)
+            fc_ref[pl.ds(pl.multiple_of(core * half, half), half), here] = e_ref[i, k]
+            fc_ref[pl.ds(pl.multiple_of((1 - core) * half, half), half), here] = other_ref[i, k]
     raw = float(P_SIZE) * lax.dot_general(plan_ref[...], fc_ref[...], NT, preferred_element_type=f32)
     raw_ref[...] = raw
     ext_ref[:REFS, :] = raw.astype(bf16)
@@ -220,16 +242,43 @@
         t_ref[low : low + 96, :] = add_blocks(parts, slice(low, low + 96))
 
 
+def row_kernel(t0, t1, t2, t3, l0, l1, out_ref):
+    for k, ref in enumerate((t0, t1, t2, t3)):
+        out_ref[k * T_ROWS : (k + 1) * T_ROWS, :] = ref[...]
+    logits = l0[...] + l1[...]
+    high = logits.astype(bf16)
+    low = 4 * T_ROWS
+    out_ref[low : low + PAD, :] = high
+    out_ref[low + PAD : low + 2 * PAD, :] = (logits - high.astype(f32)).astype(bf16)
+
+
+def sum_logits(rows):
+    y, x, z = lax.axis_index("y"), lax.axis_index("x"), lax.axis_index("z")
+    total = jnp.zeros((PAD, P_SIZE), f32)
+    parts, starts = [], []
+    for ref, step in zip(rows, NEAR):
+        low = 4 * T_ROWS
+        parts.append(ref[low : low + PAD, :].astype(f32) + ref[low + PAD : low + 2 * PAD, :].astype(f32))
+        away = 2 * lax.rem(y + step[0], 2) + lax.rem(x + step[1], 2)
+        starts.append(lax.rem(z + away, 4))
+    for a in range(4):
+        for part, start in zip(parts, starts):
+            total = total + jnp.where(start == a, part, 0.0)
+    return total
+
+
 def backward_kernel(
     width, score_scale,
-    q0, q1, q2, q3, t0, t1, t2, t3, rs_ref, rt_ref, col_ref, m_ref, logit_ref, raw_ref, wt_ref, plan_ref, refs_ref, label_ref,
-    gs_ref, p0, p1, p2, p3, other_ref, gt_ref, grs_ref, u_ref, left_ref, right_ref, wide_ref,
+    q0, q1, q2, q3, t0, t1, t2, t3, rs_ref, rt_ref, col_ref, m_ref, raw_ref, wt_ref, plan_ref, refs_ref, label_ref,
+    logit_ref, gs_ref, p0, p1, p2, p3, other_ref, gt_ref, grs_ref, u_ref, left_ref, right_ref, wide_ref,
 ):
     q = (q0, q1, q2, q3)
     tt = (t0, t1, t2, t3)
     rows = q0.shape[2]
     size = float(P_SIZE)
-    logits = logit_ref[...]
+    logits = sum_logits(tt)
+    square = lax.broadcasted_iota(jnp.int32, (PAD, PAD), 0) == lax.broadcasted_iota(jnp.int32, (PAD, PAD), 1)
+    logit_ref[...] = jnp.sum(jnp.where(square, logits[:, :PAD], 0.0), axis=0, keepdims=True)
     kind = lax.broadcasted_iota(jnp.int32, logits.shape, 0)
     exps = jnp.where(kind < CLASSES, jnp.exp(logits), 0.0)
     probs = exps / jnp.sum(exps, axis=0, keepdims=True)
@@ -254,7 +303,7 @@
             return q[s // 4][s % 4, here, :].astype(f32)
 
         def grad_plan(s, u):
-            return first * u - second * tt[s // 4][s % 4, here, :].astype(f32)
+            return first * u - second * tt[s // 4][s % 4 * T_ROWS + h * P_SIZE : s % 4 * T_ROWS + (h + 1) * P_SIZE, :].astype(f32)
 
         def row(ref, t, s):
             place = (t * HEADS + h) * BLOCKS + s
@@ -266,8 +315,8 @@
 
         acc = jnp.zeros((P_SIZE, rows), f32)
         for s in range(BLOCKS):
-            low = REFS + h * PAD
-            v = tt[s // 4][s % 4, low : low + PAD, :].astype(f32)
+            low = s % 4 * T_ROWS + REFS + h * PAD
+            v = tt[s // 4][low : low + PAD, :].astype(f32)
             u = jnp.sum(grads * v, axis=0, keepdims=True) / size
             put(u_ref, 0, s, u)
             weighted = grad_plan(s, u) * load(s)
@@ -324,14 +373,13 @@
 
 
 def last_kernel(u0, u1, out_ref):
-    eye = diagonal().astype(bf16)
-    out_ref[...] = lax.dot_general(eye, u0[...], NT, preferred_element_type=f32) + lax.dot_general(
-        eye, u1[...], NT, preferred_element_type=f32
-    )
+    out_ref[...] = u0[...].astype(f32) + u1[...].astype(f32)
 
 
 def references_kernel(gs_ref, fc_ref, out_ref):
-    out_ref[...] = lax.dot_general(gs_ref[...], fc_ref[...], NT, preferred_element_type=f32)
+    for h in range(HEADS):
+        heads = gs_ref[h * P_SIZE : (h + 1) * P_SIZE, :]
+        out_ref[h] = lax.dot_general(fc_ref[...], heads, NT, preferred_element_type=f32)
 
 
 def along_z(value, k):
@@ -352,11 +400,15 @@
     return lax.ppermute(value, ("z", "core", "y", "x"), pairs)
 
 
-def sum_logits(part):
-    total = part + lax.ppermute(part, "core", [(0, 1), (1, 0)])
-    for k in (1, 2, 4):
-        total = total + lax.ppermute(total, "z", [(i, i ^ k) for i in range(DEPTH)])
-    return total
+def far_logits(value, b):
+    pairs = []
+    for z in range(DEPTH):
+        for y in range(SIDE):
+            for x in range(SIDE):
+                source = (z + 4 * b + 2 * (y % 2) + x % 2) % DEPTH
+                place = y * SIDE + x
+                pairs.append((source * BLOCKS + place, z * BLOCKS + place))
+    return lax.ppermute(value, ("z", "y", "x"), pairs)
 
 
 def local(features, references, classifier, lengths, labels):
@@ -368,29 +420,28 @@
     refs = references.reshape(REFS, width)
     kind = jax.ShapeDtypeStruct
 
+    blocks = [kind((4, part // 2, rows), bf16)] * 4
+    g = call(split_kernel, "split", blocks, 1, scratch=[pltpu.VMEM((width, rows), bf16)])(feats)
     kernel = call(functools.partial(scores_kernel, score_scale), "scores", kind((REFS, rows), bf16), 2)(feats, refs)
-    q = gather(kernel)
-    half, refs_part = call(
-        split_kernel, "split", [kind((BLOCKS, part // 2, rows), bf16), kind((REFS, part), bf16)], 2,
-        scratch=[pltpu.VMEM((width, rows), bf16)],
-    )(feats, refs)
-    half = lax.optimization_barrier((half, q[0]))[0]
-    near = lax.all_to_all(half, ("y", "x"), 0, 0)
-    other = lax.ppermute(near, "core", [(0, 1), (1, 0)])
+    g = [g[0]] + [send(value, step) for value, step in zip(g[1:], FAR[1:])]
+    row = stack([kernel] + [send(kernel, step, -1) for step in FAR[1:]])
+    *e, refs_part = call(regroup_kernel, "regroup", blocks + [kind((REFS, part), bf16)], 5)(*g, refs)
+    e = stack([e[0]] + [send(value, step) for value, step in zip(e[1:], NEAR[1:])])
+    q = [row] + [send(row, step, -1) for step in NEAR[1:]]
+    other = lax.ppermute(e, "core", [(0, 1), (1, 0)])
     weights = jnp.pad(jnp.transpose(classifier, (0, 2, 1)), ((0, 0), (0, PAD - CLASSES), (0, 0)))
     weights = weights.reshape(HEADS * PAD, part)
 
     scales = kind((ITERS * HEADS * BLOCKS, rows), f32)
-    *a, raw, rs, rt, col, cols, plan = call(
+    rs, rt, col, plan = call(
+        sinkhorn_kernel, "sinkhorn",
+        [scales, scales, kind((ITERS, REFS, rows), f32), kind((REFS, everything), bf16)], 4, 1,
+    )(*q, lengths)
+    *a, raw, cols = call(
         forward_kernel, "forward",
-        [kind((4 * T_ROWS + M_ROWS, rows), bf16)] * 4
-        + [
-            kind((REFS, part), f32), scales, scales, kind((ITERS, REFS, rows), f32),
-            kind((part, everything), bf16), kind((REFS, everything), bf16),
-        ],
-        7, 1,
+        [kind((4 * T_ROWS + M_ROWS, rows), bf16)] * 4 + [kind((REFS, part), f32), kind((part, everything), bf16)], 4,
         scratch=[pltpu.VMEM((T_ROWS, everything), bf16), pltpu.VMEM((T_ROWS, part), bf16)],
-    )(*q, near, other, weights, lengths)
+    )(e, other, weights, plan)
     a = [a[0]] + [send(value, step) for value, step in zip(a[1:], NEAR[1:])]
     c = call(first_sum_kernel, "first_sum", [kind((T_ROWS + M_ROWS, rows), bf16)] * 4, 4)(*a)
     c = [c[0]] + [send(value, step) for value, step in zip(c[1:], FAR[1:])]
@@ -398,13 +449,17 @@
         functools.partial(second_sum_kernel, width), "second_sum",
         [kind((T_ROWS, rows), bf16), kind((HEADS * PAD, P_SIZE), f32), kind((PAD, P_SIZE), f32)], 4,
     )(*c)
-    logits = sum_logits(logit_part)
-    ts = gather(t)
+    t = [t] + [send(t, step, -1) for step in FAR[1:]]
+    logit_part = logit_part + lax.ppermute(logit_part, "core", [(0, 1), (1, 0)])
+    row = call(row_kernel, "row", kind((4 * T_ROWS + L_ROWS, rows), bf16), 6)(
+        *t, far_logits(logit_part, 0), far_logits(logit_part, 1)
+    )
+    ts = [row] + [send(row, step, -1) for step in NEAR[1:]]
     pair = kind((2, part, rows), bf16)
-    grad_scores, *mine, away = call(
+    logits, grad_scores, *mine, away = call(
         functools.partial(backward_kernel, width, score_scale), "backward",
-        [kind((REFS, everything), bf16)] + [pair] * 4 + [kind((DEPTH, part, rows), bf16)],
-        17, 1,
+        [kind((1, PAD), f32), kind((REFS, everything), bf16)] + [pair] * 4 + [kind((DEPTH, part, rows), bf16)],
+        16, 1,
         scratch=[
             pltpu.VMEM((ITERS, P_SIZE, rows), f32),
             pltpu.VMEM((ITERS * HEADS * BLOCKS, rows), f32),
@@ -413,20 +468,20 @@
             pltpu.VMEM((2 * REFS, everything), bf16),
             pltpu.VMEM((part, everything), f32),
         ],
-    )(*q, *ts, rs, rt, col, moments, logits, raw, weights, plan, refs_part, labels)
+    )(*q, *ts, rs, rt, col, moments, raw, weights, plan, refs_part, labels)
     away = lax.ppermute(away, "core", [(0, 1), (1, 0)])
     o = call(cores_kernel, "cores", [pair] * 4, 5)(*mine, away)
     o = [o[0]] + [along_z(o[k], k) for k in (1, 2, 3)]
     u = call(chips_kernel, "chips", [kind((part, rows), bf16)] * 2, 4)(*o)
     u = [to_place(u[b], b) for b in range(2)]
-    grad_features = call(last_kernel, "last", kind((rows, part), f32), 2)(*u)
-    grad_references = call(references_kernel, "references", kind((REFS, part), f32), 2, flops=2 * REFS * part * everything)(
+    grad_features = call(last_kernel, "last", kind((part, rows), f32), 2)(*u)
+    grad_references = call(references_kernel, "references", kind((HEADS, part, rows), f32), 2, flops=2 * REFS * part * everything)(
         grad_scores, cols
     )
     return (
-        logits[:CLASSES, 0].reshape(batch, CLASSES),
-        grad_features.reshape(batch, rows, part),
-        grad_references.reshape(HEADS, P_SIZE, part),
+        logits[:, :CLASSES],
+        jnp.transpose(grad_features).reshape(batch, rows, part),
+        jnp.transpose(grad_references, (0, 2, 1)),
     )
 
 

time: 156 us -> 157 us (level)
  blocking collectives: 14.9 us -> 0 us
  waiting for transfers between devices: 58.8 us -> 67.6 us
  starting transfers between devices: 60.7 us -> 67.9 us
  local copies, waits for them, and re-layouts: 5.38 us -> 3.08 us
  Pallas kernels: 13.4 us -> 15.3 us
    all_to_all x1 -> x0, blocking collectives: 14.9 us -> none  [local(): near = lax.all_to_all(half, ('y', 'x'), 0, 0)]
    ppermute x18 -> x24, waiting for transfers between devices: 30.9 us -> 42.7 us  [send(): return lax.ppermute(value, ('y', 'x'), pairs)]
    ppermute x18 -> x24, starting transfers between devices: 33.3 us -> 42.9 us  [send(): return lax.ppermute(value, ('y', 'x'), pairs)]
    ppermute x5 -> x4, starting transfers between devices: 12 us -> 8.29 us  [the longest x2 8.19 us: far_logits(): return lax.ppermute(value, ('z', 'y', 'x'), pairs)]
    pallas_call x3 -> x8, Pallas kernels: 1.65 us -> 4.63 us  [the longest x1 1.73 us: local(): call(sinkhorn_kernel, 'sinkhorn', [scales, scales, kind((ITERS, REFS, row...]
    ppermute x3, waiting for transfers between devices: 7.97 us -> 5.94 us  [along_z(): return lax.ppermute(value, ('z', 'core'), pairs)]
    unnamed x9 -> x11, local copies, waits for them, and re-layouts: 4.74 us -> 3.07 us
    ppermute x5 -> x4, waiting for transfers between devices: 5.58 us -> 4.23 us  [the longest x2 3.06 us: far_logits(): return lax.ppermute(value, ('z', 'y', 'x'), pairs)]
  transfers between devices with their start and end apart: 29 -> 34, of which waited for: 21 -> 27; matrix products, arithmetic and copies ran while one was open for 1% -> 0% of each run, Pallas kernels for 1% -> 3%
where the time goes in v3:
time: 157 us; the launch traced here: 156 us
  starting transfers between devices  67.9 us (43%)
  waiting for transfers between devices  67.6 us (43%)
  Pallas kernels  15.3 us (10%)
  local copies, waits for them, and re-layouts  3.08 us (2%)
  between operations  2.14 us (1%)
    ppermute x24, starting transfers between devices, send(): return lax.ppermute(value, ('y', 'x'), pairs)  42.9 us
    ppermute x24, waiting for transfers between devices, send(): return lax.ppermute(value, ('y', 'x'), pairs)  42.7 us
    ppermute x2, waiting for transfers between devices, to_place(): return lax.ppermute(value, ('z', 'core', 'y', 'x'), pairs)  12.7 us
    ppermute x2, starting transfers between devices, to_place(): return lax.ppermute(value, ('z', 'core', 'y', 'x'), pairs)  11.3 us
    ppermute x2, starting transfers between devices, far_logits(): return lax.ppermute(value, ('z', 'y', 'x'), pairs)  8.19 us
    pallas_call x1, Pallas kernels, local(): call(functools.partial(backward_kernel, width, score_scale), 'backward',...  7.17 us
    ppermute x3, waiting for transfers between devices, along_z(): return lax.ppermute(value, ('z', 'core'), pairs)  5.94 us
    ppermute x3, starting transfers between devices, along_z(): return lax.ppermute(value, ('z', 'core'), pairs)  5.36 us
  transfers between devices with their start and end apart: 34, of which 27 were waited for; matrix products, arithmetic and copies ran while one was open for 0% of the time, Pallas kernels for 3%

profile of v3, /device:TPU:12, one launch (start us, length us, event | category | flops | bytes accessed | tf_op | source)
XLA Modules:
  0.0 156.0 jit_solution(4803369992408825375)
XLA Ops:
  2.4 2.4 %collective-permute-start.6 = (bf16[4,160,128]{2,1,0:T(8,128)(2,1)S(1)}, bf16[4,160,128]{2,1,0:T(8,128)(2,1)S(1)}, u32[]{:S(2)}, u32[]{:S(2)}) collective-permute-start(bf16[4,160,128]{2,1,0:T(8,128)(2,1)S(1)} %get-tuple-element.43), channel_id=1, source_target_pairs={{0,8},{1,9},{2,10},{3,11},{4,12},{5,13},{6,14},{7,15},{8,0},{9,1},... | collective-permute-start | bytes 491528 | tf_op jit(solution)/shard_map/ppermute | solution.py:77
  5.3 3.7 %collective-permute-start.8 = (bf16[4,160,128]{2,1,0:T(8,128)(2,1)S(1)}, bf16[4,160,128]{2,1,0:T(8,128)(2,1)S(1)}, u32[]{:S(2)}, u32[]{:S(2)}) collective-permute-start(bf16[4,160,128]{2,1,0:T(8,128)(2,1)S(1)} %get-tuple-element.45), channel_id=1, source_target_pairs={{0,10},{1,11},{2,8},{3,9},{4,14},{5,15},{6,12},{7,13},{8,2},{9,3},... | collective-permute-start | bytes 491528 | tf_op jit(solution)/shard_map/ppermute | solution.py:77
  9.9 3.5 %collective-permute-done.7.h2 = bf16[4,160,128]{2,1,0:T(8,128)(2,1)S(1)} collective-permute-done((bf16[4,160,128]{2,1,0:T(8,128)(2,1)S(1)}, bf16[4,160,128]{2,1,0:T(8,128)(2,1)S(1)}, u32[]{:S(2)}, u32[]{:S(2)}) %collective-permute-start.7) | collective-permute-done | bytes 163872 | tf_op jit(solution)/shard_map/ppermute | solution.py:77
  13.4 2.7 %collective-permute-done.8.h3 = bf16[4,160,128]{2,1,0:T(8,128)(2,1)S(1)} collective-permute-done((bf16[4,160,128]{2,1,0:T(8,128)(2,1)S(1)}, bf16[4,160,128]{2,1,0:T(8,128)(2,1)S(1)}, u32[]{:S(2)}, u32[]{:S(2)}) %collective-permute-start.8) | collective-permute-done | bytes 163872 | tf_op jit(solution)/shard_map/ppermute | solution.py:77
  25.0 2.1 %collective-permute-done.11.d = bf16[4,160,128]{2,1,0:T(8,128)(2,1)S(1)} collective-permute-done((bf16[4,160,128]{2,1,0:T(8,128)(2,1)S(1)}, bf16[4,160,128]{2,1,0:T(8,128)(2,1)S(1)}, u32[]{:S(2)}, u32[]{:S(2)}) %collective-permute-start.11) | collective-permute-done | bytes 163872 | tf_op jit(solution)/shard_map/ppermute | solution.py:77
  28.1 3.4 %collective-permute-start.2 = (bf16[256,128]{1,0:T(8,128)(2,1)S(1)}, bf16[256,128]{1,0:T(8,128)(2,1)S(1)}, u32[]{:S(2)}, u32[]{:S(2)}) collective-permute-start(bf16[256,128]{1,0:T(8,128)(2,1)S(1)} %scores.1.a), channel_id=1, source_target_pairs={{0,10},{1,11},{2,8},{3,9},{4,14},{5,15},{6,12},{7,13},{8,2},{9,3},... | collective-permute-start | bytes 196616 | tf_op jit(solution)/shard_map/ppermute | solution.py:77
  31.6 2.0 %collective-permute-start.1 = (bf16[256,128]{1,0:T(8,128)(2,1)S(1)}, bf16[256,128]{1,0:T(8,128)(2,1)S(1)}, u32[]{:S(2)}, u32[]{:S(2)}) collective-permute-start(bf16[256,128]{1,0:T(8,128)(2,1)S(1)} %scores.1.a), channel_id=1, source_target_pairs={{0,2},{1,3},{2,0},{3,1},{4,6},{5,7},{6,4},{7,5},{8,10},{9,11},{10,... | collective-permute-start | bytes 196616 | tf_op jit(solution)/shard_map/ppermute | solution.py:77
  34.7 2.3 %collective-permute-done.2.d = bf16[256,128]{1,0:T(8,128)(2,1)S(1)} collective-permute-done((bf16[256,128]{1,0:T(8,128)(2,1)S(1)}, bf16[256,128]{1,0:T(8,128)(2,1)S(1)}, u32[]{:S(2)}, u32[]{:S(2)}) %collective-permute-start.2) | collective-permute-done | bytes 65568 | tf_op jit(solution)/shard_map/ppermute | solution.py:77
  41.0 3.2 %collective-permute-start.3 = (bf16[4,256,128]{2,1,0:T(8,128)(2,1)S(1)}, bf16[4,256,128]{2,1,0:T(8,128)(2,1)S(1)}, u32[]{:S(2)}, u32[]{:S(2)}) collective-permute-start(bf16[4,256,128]{2,1,0:T(8,128)(2,1)S(1)} %stack.2.q0), channel_id=1, source_target_pairs={{0,12},{1,13},{2,14},{3,15},{4,0},{5,1},{6,2},{7,3},{8,4},{9,5},{1... | collective-permute-start | bytes 786440 | tf_op jit(solution)/shard_map/ppermute | solution.py:77
  44.9 2.4 %collective-permute-done.5.q3 = bf16[4,256,128]{2,1,0:T(8,128)(2,1)S(1)} collective-permute-done((bf16[4,256,128]{2,1,0:T(8,128)(2,1)S(1)}, bf16[4,256,128]{2,1,0:T(8,128)(2,1)S(1)}, u32[]{:S(2)}, u32[]{:S(2)}) %collective-permute-start.5) | collective-permute-done | bytes 262176 | tf_op jit(solution)/shard_map/ppermute | solution.py:77
  48.1 2.0 %collective-permute-done.3.q1 = bf16[4,256,128]{2,1,0:T(8,128)(2,1)S(1)} collective-permute-done((bf16[4,256,128]{2,1,0:T(8,128)(2,1)S(1)}, bf16[4,256,128]{2,1,0:T(8,128)(2,1)S(1)}, u32[]{:S(2)}, u32[]{:S(2)}) %collective-permute-start.3) | collective-permute-done | bytes 262176 | tf_op jit(solution)/shard_map/ppermute | solution.py:77
  51.8 2.1 %forward.1 = (bf16[1216,128]{1,0:T(8,128)(2,1)S(1)}, bf16[1216,128]{1,0:T(8,128)(2,1)S(1)}, bf16[1216,128]{1,0:T(8,128)(2,1)S(1)}, bf16[1216,128]{1,0:T(8,128)(2...) custom-call(bf16[4,4,160,128]{3,2,1,0:T(8,128)(2,1)S(1)} %stack.3.e_ref, ...), custom_call_target="tpu_custom_call" | custom-call | tf_op jit(solution)/shard_map/forward/pallas_call | solution.py:440
  57.5 5.0 %collective-permute-done.13.a1 = bf16[1216,128]{1,0:T(8,128)(2,1)S(1)} collective-permute-done((bf16[1216,128]{1,0:T(8,128)(2,1)S(1)}, bf16[1216,128]{1,0:T(8,128)(2,1)S(1)}, u32[]{:S(2)}, u32[]{:S(2)}) %collective-permute-start.13) | collective-permute-done | bytes 311328 | tf_op jit(solution)/shard_map/ppermute | solution.py:77
  63.6 2.5 %collective-permute-done.15.a3 = bf16[1216,128]{1,0:T(8,128)(2,1)S(1)} collective-permute-done((bf16[1216,128]{1,0:T(8,128)(2,1)S(1)}, bf16[1216,128]{1,0:T(8,128)(2,1)S(1)}, u32[]{:S(2)}, u32[]{:S(2)}) %collective-permute-start.15) | collective-permute-done | bytes 311328 | tf_op jit(solution)/shard_map/ppermute | solution.py:77
  69.8 3.0 %collective-permute-start.18 = (bf16[352,128]{1,0:T(8,128)(2,1)S(1)}, bf16[352,128]{1,0:T(8,128)(2,1)S(1)}, u32[]{:S(2)}, u32[]{:S(2)}) collective-permute-start(bf16[352,128]{1,0:T(8,128)(2,1)S(1)} %get-tuple-element.58), channel_id=1, source_target_pairs={{0,10},{1,11},{2,8},{3,9},{4,14},{5,15},{6,12},{7,13},{8,2},{9,3},... | collective-permute-start | bytes 270344 | tf_op jit(solution)/shard_map/ppermute | solution.py:77
  74.0 4.3 %collective-permute-done.18.c3 = bf16[352,128]{1,0:T(8,128)(2,1)S(1)} collective-permute-done((bf16[352,128]{1,0:T(8,128)(2,1)S(1)}, bf16[352,128]{1,0:T(8,128)(2,1)S(1)}, u32[]{:S(2)}, u32[]{:S(2)}) %collective-permute-start.18) | collective-permute-done | bytes 90144 | tf_op jit(solution)/shard_map/ppermute | solution.py:77
  78.4 3.1 %collective-permute-start.21 = (bf16[288,128]{1,0:T(8,128)(2,1)S(1)}, bf16[288,128]{1,0:T(8,128)(2,1)S(1)}, u32[]{:S(2)}, u32[]{:S(2)}) collective-permute-start(bf16[288,128]{1,0:T(8,128)(2,1)S(1)} %get-tuple-element.59.t0), channel_id=1, source_target_pairs={{0,10},{1,11},{2,8},{3,9},{4,14},{5,15},{6,12},{7,13},{8,2},{9,3},... | collective-permute-start | bytes 221192 | tf_op jit(solution)/shard_map/ppermute | solution.py:77
  81.6 3.3 %collective-permute-start.19 = (bf16[288,128]{1,0:T(8,128)(2,1)S(1)}, bf16[288,128]{1,0:T(8,128)(2,1)S(1)}, u32[]{:S(2)}, u32[]{:S(2)}) collective-permute-start(bf16[288,128]{1,0:T(8,128)(2,1)S(1)} %get-tuple-element.59.t0), channel_id=1, source_target_pairs={{0,8},{1,9},{2,10},{3,11},{4,12},{5,13},{6,14},{7,15},{8,0},{9,1},... | collective-permute-start | bytes 221192 | tf_op jit(solution)/shard_map/ppermute | solution.py:77
  86.1 3.3 %collective-permute-start.24 = (f32[16,128]{1,0:T(8,128)S(1)}, f32[16,128]{1,0:T(8,128)S(1)}, u32[]{:S(2)}, u32[]{:S(2)}) collective-permute-start(f32[16,128]{1,0:T(8,128)S(1)} %add.5), channel_id=1, source_target_pairs={{128,0},{161,1},{130,2},{163,3},{196,4},{229,5},{198,6},{231,7},{1... | collective-permute-start | bytes 24584 | tf_op jit(solution)/shard_map/ppermute | solution.py:411
  89.3 4.9 %collective-permute-start.23 = (f32[16,128]{1,0:T(8,128)S(1)}, f32[16,128]{1,0:T(8,128)S(1)}, u32[]{:S(2)}, u32[]{:S(2)}) collective-permute-start(f32[16,128]{1,0:T(8,128)S(1)} %add.5), channel_id=1, source_target_pairs={{0,0},{33,1},{2,2},{35,3},{68,4},{101,5},{70,6},{103,7},{8,8},{41,... | collective-permute-start | bytes 24584 | tf_op jit(solution)/shard_map/ppermute | solution.py:411
  94.3 3.1 %collective-permute-done.23.l0 = f32[16,128]{1,0:T(8,128)S(1)} collective-permute-done((f32[16,128]{1,0:T(8,128)S(1)}, f32[16,128]{1,0:T(8,128)S(1)}, u32[]{:S(2)}, u32[]{:S(2)}) %collective-permute-start.23) | collective-permute-done | bytes 8224 | tf_op jit(solution)/shard_map/ppermute | solution.py:411
  97.4 2.0 %collective-permute-start.27 = (bf16[1184,128]{1,0:T(8,128)(2,1)S(1)}, bf16[1184,128]{1,0:T(8,128)(2,1)S(1)}, u32[]{:S(2)}, u32[]{:S(2)}) collective-permute-start(bf16[1184,128]{1,0:T(8,128)(2,1)S(1)} %row.1.t0), channel_id=1, source_target_pairs={{0,5},{1,6},{2,7},{3,4},{4,9},{5,10},{6,11},{7,8},{8,13},{9,14},{1... | collective-permute-start | bytes 909320 | tf_op jit(solution)/shard_map/ppermute | solution.py:77
  102.7 5.1 %collective-permute-done.27.t3 = bf16[1184,128]{1,0:T(8,128)(2,1)S(1)} collective-permute-done((bf16[1184,128]{1,0:T(8,128)(2,1)S(1)}, bf16[1184,128]{1,0:T(8,128)(2,1)S(1)}, u32[]{:S(2)}, u32[]{:S(2)}) %collective-permute-start.27) | collective-permute-done | bytes 303136 | tf_op jit(solution)/shard_map/ppermute | solution.py:77
  108.9 7.2 %backward.1 = (f32[1,16]{1,0:T(1,128)}, bf16[256,2048]{1,0:T(8,128)(2,1)S(1)}, bf16[2,320,128]{2,1,0:T(8,128)(2,1)S(1)}, bf16[2,320,128]{2,1,0:T(8,128)(2,1)S(1)...) custom-call(bf16[4,256,128]{2,1,0:T(8,128)(2,1)S(1)} %stack.2.q0, ...), custom_call_target="tpu_custom_call" | custom-call | tf_op jit(solution)/shard_map/backward/pallas_call | solution.py:459
  116.1 2.1 %collective-permute-done.28.other_ref = bf16[8,320,128]{2,1,0:T(8,128)(2,1)S(1)} collective-permute-done((bf16[8,320,128]{2,1,0:T(8,128)(2,1)S(1)}, bf16[8,320,128]{2,1,0:T(8,128)(2,1)S(1)}, u32[]{:S(2)}, u32[]{:S(2)}) %collective-permute-start.28) | collective-permute-done | bytes 655392 | tf_op jit(solution)/shard_map/ppermute | solution.py:472
  119.5 2.2 %collective-permute-start.30 = (bf16[2,320,128]{2,1,0:T(8,128)(2,1)S(1)}, bf16[2,320,128]{2,1,0:T(8,128)(2,1)S(1)}, u32[]{:S(2)}, u32[]{:S(2)}) collective-permute-start(bf16[2,320,128]{2,1,0:T(8,128)(2,1)S(1)} %get-tuple-element.75), channel_id=1, source_target_pairs={{0,224},{16,240},{32,0},{48,16},{64,32},{80,48},{96,64},{112,80},{... | collective-permute-start | bytes 491528 | tf_op jit(solution)/shard_map/ppermute | solution.py:390
  121.7 2.0 %collective-permute-start.31 = (bf16[2,320,128]{2,1,0:T(8,128)(2,1)S(1)}, bf16[2,320,128]{2,1,0:T(8,128)(2,1)S(1)}, u32[]{:S(2)}, u32[]{:S(2)}) collective-permute-start(bf16[2,320,128]{2,1,0:T(8,128)(2,1)S(1)} %get-tuple-element.76), channel_id=1, source_target_pairs={{0,64},{16,208},{32,96},{48,240},{64,128},{80,16},{96,160},{112,48... | collective-permute-start | bytes 491528 | tf_op jit(solution)/shard_map/ppermute | solution.py:390
  123.7 2.3 %collective-permute-done.29.o1 = bf16[2,320,128]{2,1,0:T(8,128)(2,1)S(1)} collective-permute-done((bf16[2,320,128]{2,1,0:T(8,128)(2,1)S(1)}, bf16[2,320,128]{2,1,0:T(8,128)(2,1)S(1)}, u32[]{:S(2)}, u32[]{:S(2)}) %collective-permute-start.29) | collective-permute-done | bytes 163872 | tf_op jit(solution)/shard_map/ppermute | solution.py:390
  126.1 2.0 %collective-permute-done.30.o2 = bf16[2,320,128]{2,1,0:T(8,128)(2,1)S(1)} collective-permute-done((bf16[2,320,128]{2,1,0:T(8,128)(2,1)S(1)}, bf16[2,320,128]{2,1,0:T(8,128)(2,1)S(1)}, u32[]{:S(2)}, u32[]{:S(2)}) %collective-permute-start.30) | collective-permute-done | bytes 163872 | tf_op jit(solution)/shard_map/ppermute | solution.py:390
  129.8 7.2 %collective-permute-start.32 = (bf16[320,128]{1,0:T(8,128)(2,1)S(1)}, bf16[320,128]{1,0:T(8,128)(2,1)S(1)}, u32[]{:S(2)}, u32[]{:S(2)}) collective-permute-start(bf16[320,128]{1,0:T(8,128)(2,1)S(1)} %get-tuple-element.77), channel_id=1, source_target_pairs={{0,0},{1,16},{2,32},{3,48},{4,64},{5,80},{6,96},{7,112},{8,128},{9... | collective-permute-start | bytes 245768 | tf_op jit(solution)/shard_map/ppermute | solution.py:400
  137.0 4.1 %collective-permute-start.33 = (bf16[320,128]{1,0:T(8,128)(2,1)S(1)}, bf16[320,128]{1,0:T(8,128)(2,1)S(1)}, u32[]{:S(2)}, u32[]{:S(2)}) collective-permute-start(bf16[320,128]{1,0:T(8,128)(2,1)S(1)} %get-tuple-element.78), channel_id=1, source_target_pairs={{0,8},{1,24},{2,40},{3,56},{4,72},{5,88},{6,104},{7,120},{8,136},{... | collective-permute-start | bytes 245768 | tf_op jit(solution)/shard_map/ppermute | solution.py:400
  143.1 12.2 %collective-permute-done.33.u1 = bf16[320,128]{1,0:T(8,128)(2,1)S(1)} collective-permute-done((bf16[320,128]{1,0:T(8,128)(2,1)S(1)}, bf16[320,128]{1,0:T(8,128)(2,1)S(1)}, u32[]{:S(2)}, u32[]{:S(2)}) %collective-permute-start.33) | collective-permute-done | bytes 81952 | tf_op jit(solution)/shard_map/ppermute | solution.py:400
  (64 shorter events, 41.4 us)
Async XLA Ops:
  2.4 7.5 %collective-permute-start.6 = (bf16[4,160,128]{2,1,0:T(8,128)(2,1)S(1)}, bf16[4,160,128]{2,1,0:T(8,128)(2,1)S(1)}, u32[]{:S(2)}, u32[]{:S(2)}) collective-permute-start(bf16[4,160,128]{2,1,0:T(8,128)(2,1)S(1)} %get-tuple-element.43), channel_id=1, source_target_pairs={{0,8},{1,9},{2,10},{3,11},{4,12},{5,13},{6,14},{7,15},{8,0},{9,1},... | collective-permute-start | bytes 491528 | tf_op jit(solution)/shard_map/ppermute | solution.py:77
  4.8 8.6 %collective-permute-start.7 = (bf16[4,160,128]{2,1,0:T(8,128)(2,1)S(1)}, bf16[4,160,128]{2,1,0:T(8,128)(2,1)S(1)}, u32[]{:S(2)}, u32[]{:S(2)}) collective-permute-start(bf16[4,160,128]{2,1,0:T(8,128)(2,1)S(1)} %get-tuple-element.44), channel_id=1, source_target_pairs={{0,2},{1,3},{2,0},{3,1},{4,6},{5,7},{6,4},{7,5},{8,10},{9,11},{10,... | collective-permute-start | bytes 491528 | tf_op jit(solution)/shard_map/ppermute | solution.py:77
  5.3 10.8 %collective-permute-start.8 = (bf16[4,160,128]{2,1,0:T(8,128)(2,1)S(1)}, bf16[4,160,128]{2,1,0:T(8,128)(2,1)S(1)}, u32[]{:S(2)}, u32[]{:S(2)}) collective-permute-start(bf16[4,160,128]{2,1,0:T(8,128)(2,1)S(1)} %get-tuple-element.45), channel_id=1, source_target_pairs={{0,10},{1,11},{2,8},{3,9},{4,14},{5,15},{6,12},{7,13},{8,2},{9,3},... | collective-permute-start | bytes 491528 | tf_op jit(solution)/shard_map/ppermute | solution.py:77
  18.0 5.4 %collective-permute-start.9 = (bf16[4,160,128]{2,1,0:T(8,128)(2,1)S(1)}, bf16[4,160,128]{2,1,0:T(8,128)(2,1)S(1)}, u32[]{:S(2)}, u32[]{:S(2)}) collective-permute-start(bf16[4,160,128]{2,1,0:T(8,128)(2,1)S(1)} %get-tuple-element.47), channel_id=1, source_target_pairs={{0,4},{1,5},{2,6},{3,7},{4,8},{5,9},{6,10},{7,11},{8,12},{9,13},{1... | collective-permute-start | bytes 491528 | tf_op jit(solution)/shard_map/ppermute | solution.py:77
  19.7 5.3 %collective-permute-start.10 = (bf16[4,160,128]{2,1,0:T(8,128)(2,1)S(1)}, bf16[4,160,128]{2,1,0:T(8,128)(2,1)S(1)}, u32[]{:S(2)}, u32[]{:S(2)}) collective-permute-start(bf16[4,160,128]{2,1,0:T(8,128)(2,1)S(1)} %get-tuple-element.48), channel_id=1, source_target_pairs={{0,1},{1,2},{2,3},{3,0},{4,5},{5,6},{6,7},{7,4},{8,9},{9,10},{10,1... | collective-permute-start | bytes 491528 | tf_op jit(solution)/shard_map/ppermute | solution.py:77
  20.9 6.2 %collective-permute-start.11 = (bf16[4,160,128]{2,1,0:T(8,128)(2,1)S(1)}, bf16[4,160,128]{2,1,0:T(8,128)(2,1)S(1)}, u32[]{:S(2)}, u32[]{:S(2)}) collective-permute-start(bf16[4,160,128]{2,1,0:T(8,128)(2,1)S(1)} %get-tuple-element.49), channel_id=1, source_target_pairs={{0,15},{1,12},{2,13},{3,14},{4,3},{5,0},{6,1},{7,2},{8,7},{9,4},{1... | collective-permute-start | bytes 491528 | tf_op jit(solution)/shard_map/ppermute | solution.py:77
  27.1 24.6 %collective-permute-start.12 = (bf16[4,4,160,128]{3,2,1,0:T(8,128)(2,1)S(1)}, bf16[4,4,160,128]{3,2,1,0:T(8,128)(2,1)S(1)}, u32[]{:S(2)}, u32[]{:S(2)}) collective-permute-start(bf16[4,4,160,128]{3,2,1,0:T(8,128)(2,1)S(1)} %stack.3.e_ref), channel_id=1, source_target_pairs={{0,16},{16,0},{1,17},{17,1},{2,18},{18,2},{3,19},{19,3},{4,20},{20... | collective-permute-start | bytes 1966088 | tf_op jit(solution)/shard_map/ppermute | solution.py:431
  28.1 8.9 %collective-permute-start.2 = (bf16[256,128]{1,0:T(8,128)(2,1)S(1)}, bf16[256,128]{1,0:T(8,128)(2,1)S(1)}, u32[]{:S(2)}, u32[]{:S(2)}) collective-permute-start(bf16[256,128]{1,0:T(8,128)(2,1)S(1)} %scores.1.a), channel_id=1, source_target_pairs={{0,10},{1,11},{2,8},{3,9},{4,14},{5,15},{6,12},{7,13},{8,2},{9,3},... | collective-permute-start | bytes 196616 | tf_op jit(solution)/shard_map/ppermute | solution.py:77
  31.6 5.9 %collective-permute-start.1 = (bf16[256,128]{1,0:T(8,128)(2,1)S(1)}, bf16[256,128]{1,0:T(8,128)(2,1)S(1)}, u32[]{:S(2)}, u32[]{:S(2)}) collective-permute-start(bf16[256,128]{1,0:T(8,128)(2,1)S(1)} %scores.1.a), channel_id=1, source_target_pairs={{0,2},{1,3},{2,0},{3,1},{4,6},{5,7},{6,4},{7,5},{8,10},{9,11},{10,... | collective-permute-start | bytes 196616 | tf_op jit(solution)/shard_map/ppermute | solution.py:77
  33.6 5.8 %collective-permute-start = (bf16[256,128]{1,0:T(8,128)(2,1)S(1)}, bf16[256,128]{1,0:T(8,128)(2,1)S(1)}, u32[]{:S(2)}, u32[]{:S(2)}) collective-permute-start(bf16[256,128]{1,0:T(8,128)(2,1)S(1)} %scores.1.a), channel_id=1, source_target_pairs={{0,8},{1,9},{2,10},{3,11},{4,12},{5,13},{6,14},{7,15},{8,0},{9,1},... | collective-permute-start | bytes 196616 | tf_op jit(solution)/shard_map/ppermute | solution.py:77
  39.4 8.0 %collective-permute-start.5 = (bf16[4,256,128]{2,1,0:T(8,128)(2,1)S(1)}, bf16[4,256,128]{2,1,0:T(8,128)(2,1)S(1)}, u32[]{:S(2)}, u32[]{:S(2)}) collective-permute-start(bf16[4,256,128]{2,1,0:T(8,128)(2,1)S(1)} %stack.2.q0), channel_id=1, source_target_pairs={{0,5},{1,6},{2,7},{3,4},{4,9},{5,10},{6,11},{7,8},{8,13},{9,14},{1... | collective-permute-start | bytes 786440 | tf_op jit(solution)/shard_map/ppermute | solution.py:77
  41.0 7.0 %collective-permute-start.4 = (bf16[4,256,128]{2,1,0:T(8,128)(2,1)S(1)}, bf16[4,256,128]{2,1,0:T(8,128)(2,1)S(1)}, u32[]{:S(2)}, u32[]{:S(2)}) collective-permute-start(bf16[4,256,128]{2,1,0:T(8,128)(2,1)S(1)} %stack.2.q0), channel_id=1, source_target_pairs={{0,3},{1,0},{2,1},{3,2},{4,7},{5,4},{6,5},{7,6},{8,11},{9,8},{10,9... | collective-permute-start | bytes 786440 | tf_op jit(solution)/shard_map/ppermute | solution.py:77
  41.0 9.0 %collective-permute-start.3 = (bf16[4,256,128]{2,1,0:T(8,128)(2,1)S(1)}, bf16[4,256,128]{2,1,0:T(8,128)(2,1)S(1)}, u32[]{:S(2)}, u32[]{:S(2)}) collective-permute-start(bf16[4,256,128]{2,1,0:T(8,128)(2,1)S(1)} %stack.2.q0), channel_id=1, source_target_pairs={{0,12},{1,13},{2,14},{3,15},{4,0},{5,1},{6,2},{7,3},{8,4},{9,5},{1... | collective-permute-start | bytes 786440 | tf_op jit(solution)/shard_map/ppermute | solution.py:77
  53.9 8.5 %collective-permute-start.13 = (bf16[1216,128]{1,0:T(8,128)(2,1)S(1)}, bf16[1216,128]{1,0:T(8,128)(2,1)S(1)}, u32[]{:S(2)}, u32[]{:S(2)}) collective-permute-start(bf16[1216,128]{1,0:T(8,128)(2,1)S(1)} %get-tuple-element.52), channel_id=1, source_target_pairs={{0,4},{1,5},{2,6},{3,7},{4,8},{5,9},{6,10},{7,11},{8,12},{9,13},{1... | collective-permute-start | bytes 933896 | tf_op jit(solution)/shard_map/ppermute | solution.py:77
  55.7 7.9 %collective-permute-start.14 = (bf16[1216,128]{1,0:T(8,128)(2,1)S(1)}, bf16[1216,128]{1,0:T(8,128)(2,1)S(1)}, u32[]{:S(2)}, u32[]{:S(2)}) collective-permute-start(bf16[1216,128]{1,0:T(8,128)(2,1)S(1)} %get-tuple-element.53), channel_id=1, source_target_pairs={{0,1},{1,2},{2,3},{3,0},{4,5},{5,6},{6,7},{7,4},{8,9},{9,10},{10,1... | collective-permute-start | bytes 933896 | tf_op jit(solution)/shard_map/ppermute | solution.py:77
  57.5 8.6 %collective-permute-start.15 = (bf16[1216,128]{1,0:T(8,128)(2,1)S(1)}, bf16[1216,128]{1,0:T(8,128)(2,1)S(1)}, u32[]{:S(2)}, u32[]{:S(2)}) collective-permute-start(bf16[1216,128]{1,0:T(8,128)(2,1)S(1)} %get-tuple-element.54), channel_id=1, source_target_pairs={{0,15},{1,12},{2,13},{3,14},{4,3},{5,0},{6,1},{7,2},{8,7},{9,4},{1... | collective-permute-start | bytes 933896 | tf_op jit(solution)/shard_map/ppermute | solution.py:77
  66.3 6.6 %collective-permute-start.16 = (bf16[352,128]{1,0:T(8,128)(2,1)S(1)}, bf16[352,128]{1,0:T(8,128)(2,1)S(1)}, u32[]{:S(2)}, u32[]{:S(2)}) collective-permute-start(bf16[352,128]{1,0:T(8,128)(2,1)S(1)} %get-tuple-element.56), channel_id=1, source_target_pairs={{0,8},{1,9},{2,10},{3,11},{4,12},{5,13},{6,14},{7,15},{8,0},{9,1},... | collective-permute-start | bytes 270344 | tf_op jit(solution)/shard_map/ppermute | solution.py:77
  67.9 6.0 %collective-permute-start.17 = (bf16[352,128]{1,0:T(8,128)(2,1)S(1)}, bf16[352,128]{1,0:T(8,128)(2,1)S(1)}, u32[]{:S(2)}, u32[]{:S(2)}) collective-permute-start(bf16[352,128]{1,0:T(8,128)(2,1)S(1)} %get-tuple-element.57), channel_id=1, source_target_pairs={{0,2},{1,3},{2,0},{3,1},{4,6},{5,7},{6,4},{7,5},{8,10},{9,11},{10,... | collective-permute-start | bytes 270344 | tf_op jit(solution)/shard_map/ppermute | solution.py:77
  69.8 8.4 %collective-permute-start.18 = (bf16[352,128]{1,0:T(8,128)(2,1)S(1)}, bf16[352,128]{1,0:T(8,128)(2,1)S(1)}, u32[]{:S(2)}, u32[]{:S(2)}) collective-permute-start(bf16[352,128]{1,0:T(8,128)(2,1)S(1)} %get-tuple-element.58), channel_id=1, source_target_pairs={{0,10},{1,11},{2,8},{3,9},{4,14},{5,15},{6,12},{7,13},{8,2},{9,3},... | collective-permute-start | bytes 270344 | tf_op jit(solution)/shard_map/ppermute | solution.py:77
  78.4 19.0 %collective-permute-start.21 = (bf16[288,128]{1,0:T(8,128)(2,1)S(1)}, bf16[288,128]{1,0:T(8,128)(2,1)S(1)}, u32[]{:S(2)}, u32[]{:S(2)}) collective-permute-start(bf16[288,128]{1,0:T(8,128)(2,1)S(1)} %get-tuple-element.59.t0), channel_id=1, source_target_pairs={{0,10},{1,11},{2,8},{3,9},{4,14},{5,15},{6,12},{7,13},{8,2},{9,3},... | collective-permute-start | bytes 221192 | tf_op jit(solution)/shard_map/ppermute | solution.py:77
  81.4 15.9 %collective-permute-start.20 = (bf16[288,128]{1,0:T(8,128)(2,1)S(1)}, bf16[288,128]{1,0:T(8,128)(2,1)S(1)}, u32[]{:S(2)}, u32[]{:S(2)}) collective-permute-start(bf16[288,128]{1,0:T(8,128)(2,1)S(1)} %get-tuple-element.59.t0), channel_id=1, source_target_pairs={{0,2},{1,3},{2,0},{3,1},{4,6},{5,7},{6,4},{7,5},{8,10},{9,11},{10,... | collective-permute-start | bytes 221192 | tf_op jit(solution)/shard_map/ppermute | solution.py:77
  81.6 15.7 %collective-permute-start.19 = (bf16[288,128]{1,0:T(8,128)(2,1)S(1)}, bf16[288,128]{1,0:T(8,128)(2,1)S(1)}, u32[]{:S(2)}, u32[]{:S(2)}) collective-permute-start(bf16[288,128]{1,0:T(8,128)(2,1)S(1)} %get-tuple-element.59.t0), channel_id=1, source_target_pairs={{0,8},{1,9},{2,10},{3,11},{4,12},{5,13},{6,14},{7,15},{8,0},{9,1},... | collective-permute-start | bytes 221192 | tf_op jit(solution)/shard_map/ppermute | solution.py:77
  86.1 8.2 %collective-permute-start.24 = (f32[16,128]{1,0:T(8,128)S(1)}, f32[16,128]{1,0:T(8,128)S(1)}, u32[]{:S(2)}, u32[]{:S(2)}) collective-permute-start(f32[16,128]{1,0:T(8,128)S(1)} %add.5), channel_id=1, source_target_pairs={{128,0},{161,1},{130,2},{163,3},{196,4},{229,5},{198,6},{231,7},{1... | collective-permute-start | bytes 24584 | tf_op jit(solution)/shard_map/ppermute | solution.py:411
  89.3 8.0 %collective-permute-start.23 = (f32[16,128]{1,0:T(8,128)S(1)}, f32[16,128]{1,0:T(8,128)S(1)}, u32[]{:S(2)}, u32[]{:S(2)}) collective-permute-start(f32[16,128]{1,0:T(8,128)S(1)} %add.5), channel_id=1, source_target_pairs={{0,0},{33,1},{2,2},{35,3},{68,4},{101,5},{70,6},{103,7},{8,8},{41,... | collective-permute-start | bytes 24584 | tf_op jit(solution)/shard_map/ppermute | solution.py:411
  97.4 10.4 %collective-permute-start.27 = (bf16[1184,128]{1,0:T(8,128)(2,1)S(1)}, bf16[1184,128]{1,0:T(8,128)(2,1)S(1)}, u32[]{:S(2)}, u32[]{:S(2)}) collective-permute-start(bf16[1184,128]{1,0:T(8,128)(2,1)S(1)} %row.1.t0), channel_id=1, source_target_pairs={{0,5},{1,6},{2,7},{3,4},{4,9},{5,10},{6,11},{7,8},{8,13},{9,14},{1... | collective-permute-start | bytes 909320 | tf_op jit(solution)/shard_map/ppermute | solution.py:77
  99.4 8.4 %collective-permute-start.26 = (bf16[1184,128]{1,0:T(8,128)(2,1)S(1)}, bf16[1184,128]{1,0:T(8,128)(2,1)S(1)}, u32[]{:S(2)}, u32[]{:S(2)}) collective-permute-start(bf16[1184,128]{1,0:T(8,128)(2,1)S(1)} %row.1.t0), channel_id=1, source_target_pairs={{0,3},{1,0},{2,1},{3,2},{4,7},{5,4},{6,5},{7,6},{8,11},{9,8},{10,9... | collective-permute-start | bytes 909320 | tf_op jit(solution)/shard_map/ppermute | solution.py:77
  101.1 7.8 %collective-permute-start.25 = (bf16[1184,128]{1,0:T(8,128)(2,1)S(1)}, bf16[1184,128]{1,0:T(8,128)(2,1)S(1)}, u32[]{:S(2)}, u32[]{:S(2)}) collective-permute-start(bf16[1184,128]{1,0:T(8,128)(2,1)S(1)} %row.1.t0), channel_id=1, source_target_pairs={{0,12},{1,13},{2,14},{3,15},{4,0},{5,1},{6,2},{7,3},{8,4},{9,5},{1... | collective-permute-start | bytes 909320 | tf_op jit(solution)/shard_map/ppermute | solution.py:77
  118.4 7.7 %collective-permute-start.29 = (bf16[2,320,128]{2,1,0:T(8,128)(2,1)S(1)}, bf16[2,320,128]{2,1,0:T(8,128)(2,1)S(1)}, u32[]{:S(2)}, u32[]{:S(2)}) collective-permute-start(bf16[2,320,128]{2,1,0:T(8,128)(2,1)S(1)} %get-tuple-element.74), channel_id=1, source_target_pairs={{0,32},{16,48},{32,64},{48,80},{64,96},{80,112},{96,128},{112,144}... | collective-permute-start | bytes 491528 | tf_op jit(solution)/shard_map/ppermute | solution.py:390
  119.5 8.5 %collective-permute-start.30 = (bf16[2,320,128]{2,1,0:T(8,128)(2,1)S(1)}, bf16[2,320,128]{2,1,0:T(8,128)(2,1)S(1)}, u32[]{:S(2)}, u32[]{:S(2)}) collective-permute-start(bf16[2,320,128]{2,1,0:T(8,128)(2,1)S(1)} %get-tuple-element.75), channel_id=1, source_target_pairs={{0,224},{16,240},{32,0},{48,16},{64,32},{80,48},{96,64},{112,80},{... | collective-permute-start | bytes 491528 | tf_op jit(solution)/shard_map/ppermute | solution.py:390
  121.7 8.0 %collective-permute-start.31 = (bf16[2,320,128]{2,1,0:T(8,128)(2,1)S(1)}, bf16[2,320,128]{2,1,0:T(8,128)(2,1)S(1)}, u32[]{:S(2)}, u32[]{:S(2)}) collective-permute-start(bf16[2,320,128]{2,1,0:T(8,128)(2,1)S(1)} %get-tuple-element.76), channel_id=1, source_target_pairs={{0,64},{16,208},{32,96},{48,240},{64,128},{80,16},{96,160},{112,48... | collective-permute-start | bytes 491528 | tf_op jit(solution)/shard_map/ppermute | solution.py:390
  129.8 13.4 %collective-permute-start.32 = (bf16[320,128]{1,0:T(8,128)(2,1)S(1)}, bf16[320,128]{1,0:T(8,128)(2,1)S(1)}, u32[]{:S(2)}, u32[]{:S(2)}) collective-permute-start(bf16[320,128]{1,0:T(8,128)(2,1)S(1)} %get-tuple-element.77), channel_id=1, source_target_pairs={{0,0},{1,16},{2,32},{3,48},{4,64},{5,80},{6,96},{7,112},{8,128},{9... | collective-permute-start | bytes 245768 | tf_op jit(solution)/shard_map/ppermute | solution.py:400
  137.0 18.4 %collective-permute-start.33 = (bf16[320,128]{1,0:T(8,128)(2,1)S(1)}, bf16[320,128]{1,0:T(8,128)(2,1)S(1)}, u32[]{:S(2)}, u32[]{:S(2)}) collective-permute-start(bf16[320,128]{1,0:T(8,128)(2,1)S(1)} %get-tuple-element.78), channel_id=1, source_target_pairs={{0,8},{1,24},{2,40},{3,56},{4,72},{5,88},{6,104},{7,120},{8,136},{... | collective-permute-start | bytes 245768 | tf_op jit(solution)/shard_map/ppermute | solution.py:400
  (7 other events, 42.7 us)

commit v4 on v3

--- a/solution.py
+++ b/solution.py
@@ -424,10 +424,14 @@
     g = call(split_kernel, "split", blocks, 1, scratch=[pltpu.VMEM((width, rows), bf16)])(feats)
     kernel = call(functools.partial(scores_kernel, score_scale), "scores", kind((REFS, rows), bf16), 2)(feats, refs)
     g = [g[0]] + [send(value, step) for value, step in zip(g[1:], FAR[1:])]
-    row = stack([kernel] + [send(kernel, step, -1) for step in FAR[1:]])
+    row = [kernel] + [send(kernel, step, -1) for step in FAR[1:]]
+    g, row = lax.optimization_barrier((g, row))
+    row = stack(row)
     *e, refs_part = call(regroup_kernel, "regroup", blocks + [kind((REFS, part), bf16)], 5)(*g, refs)
-    e = stack([e[0]] + [send(value, step) for value, step in zip(e[1:], NEAR[1:])])
+    e = [e[0]] + [send(value, step) for value, step in zip(e[1:], NEAR[1:])]
     q = [row] + [send(row, step, -1) for step in NEAR[1:]]
+    e, q = lax.optimization_barrier((e, q))
+    e = stack(e)
     other = lax.ppermute(e, "core", [(0, 1), (1, 0)])
     weights = jnp.pad(jnp.transpose(classifier, (0, 2, 1)), ((0, 0), (0, PAD - CLASSES), (0, 0)))
     weights = weights.reshape(HEADS * PAD, part)

time: 157 us -> 150 us (0.955)
  waiting for transfers between devices: 67.6 us -> 58.6 us
  starting transfers between devices: 67.9 us -> 69.7 us
    ppermute x24, waiting for transfers between devices: 42.7 us -> 33.8 us  [send(): return lax.ppermute(value, ('y', 'x'), pairs)]
    ppermute x24, starting transfers between devices: 42.9 us -> 44.6 us  [send(): return lax.ppermute(value, ('y', 'x'), pairs)]
  transfers between devices with their start and end apart: 34 -> 34, of which waited for: 27 -> 18; matrix products, arithmetic and copies ran while one was open for 0% -> 0% of each run, Pallas kernels for 3% -> 3%
where the time goes in v4:
time: 150 us; the launch traced here: 149 us
  starting transfers between devices  69.7 us (46%)
  waiting for transfers between devices  58.6 us (39%)
  Pallas kernels  15.4 us (10%)
  local copies, waits for them, and re-layouts  3.07 us (2%)
  between operations  2.13 us (1%)
    ppermute x24, starting transfers between devices, send(): return lax.ppermute(value, ('y', 'x'), pairs)  44.6 us
    ppermute x24, waiting for transfers between devices, send(): return lax.ppermute(value, ('y', 'x'), pairs)  33.8 us
    ppermute x2, waiting for transfers between devices, to_place(): return lax.ppermute(value, ('z', 'core', 'y', 'x'), pairs)  12.5 us
    ppermute x2, starting transfers between devices, to_place(): return lax.ppermute(value, ('z', 'core', 'y', 'x'), pairs)  11.3 us
    ppermute x2, starting transfers between devices, far_logits(): return lax.ppermute(value, ('z', 'y', 'x'), pairs)  8.2 us
    pallas_call x1, Pallas kernels, local(): call(functools.partial(backward_kernel, width, score_scale), 'backward',...  7.24 us
    ppermute x3, waiting for transfers between devices, along_z(): return lax.ppermute(value, ('z', 'core'), pairs)  5.94 us
    ppermute x3, starting transfers between devices, along_z(): return lax.ppermute(value, ('z', 'core'), pairs)  5.36 us
  transfers between devices with their start and end apart: 34, of which 18 were waited for; matrix products, arithmetic and copies ran while one was open for 0% of the time, Pallas kernels for 3%

profile of v4, /device:TPU:12, one launch (start us, length us, event | category | flops | bytes accessed | tf_op | source)
XLA Modules:
  0.0 148.9 jit_solution(16633312481323662254)
XLA Ops:
  2.4 2.4 %collective-permute-start = (bf16[4,160,128]{2,1,0:T(8,128)(2,1)S(1)}, bf16[4,160,128]{2,1,0:T(8,128)(2,1)S(1)}, u32[]{:S(2)}, u32[]{:S(2)}) collective-permute-start(bf16[4,160,128]{2,1,0:T(8,128)(2,1)S(1)} %get-tuple-element.59), channel_id=1, source_target_pairs={{0,8},{1,9},{2,10},{3,11},{4,12},{5,13},{6,14},{7,15},{8,0},{9,1},... | collective-permute-start | bytes 491528 | tf_op jit(solution)/shard_map/ppermute | solution.py:77
  5.3 3.7 %collective-permute-start.2 = (bf16[4,160,128]{2,1,0:T(8,128)(2,1)S(1)}, bf16[4,160,128]{2,1,0:T(8,128)(2,1)S(1)}, u32[]{:S(2)}, u32[]{:S(2)}) collective-permute-start(bf16[4,160,128]{2,1,0:T(8,128)(2,1)S(1)} %get-tuple-element.61), channel_id=1, source_target_pairs={{0,10},{1,11},{2,8},{3,9},{4,14},{5,15},{6,12},{7,13},{8,2},{9,3},... | collective-permute-start | bytes 491528 | tf_op jit(solution)/shard_map/ppermute | solution.py:77
  11.6 2.3 %collective-permute-start.5 = (bf16[256,128]{1,0:T(8,128)(2,1)S(1)}, bf16[256,128]{1,0:T(8,128)(2,1)S(1)}, u32[]{:S(2)}, u32[]{:S(2)}) collective-permute-start(bf16[256,128]{1,0:T(8,128)(2,1)S(1)} %scores.1.a), channel_id=1, source_target_pairs={{0,10},{1,11},{2,8},{3,9},{4,14},{5,15},{6,12},{7,13},{8,2},{9,3},... | collective-permute-start | bytes 196616 | tf_op jit(solution)/shard_map/ppermute | solution.py:77
  13.9 3.0 %collective-permute-start.4 = (bf16[256,128]{1,0:T(8,128)(2,1)S(1)}, bf16[256,128]{1,0:T(8,128)(2,1)S(1)}, u32[]{:S(2)}, u32[]{:S(2)}) collective-permute-start(bf16[256,128]{1,0:T(8,128)(2,1)S(1)} %scores.1.a), channel_id=1, source_target_pairs={{0,2},{1,3},{2,0},{3,1},{4,6},{5,7},{6,4},{7,5},{8,10},{9,11},{10,... | collective-permute-start | bytes 196616 | tf_op jit(solution)/shard_map/ppermute | solution.py:77
  16.9 2.9 %collective-permute-done.5.d = bf16[256,128]{1,0:T(8,128)(2,1)S(1)} collective-permute-done((bf16[256,128]{1,0:T(8,128)(2,1)S(1)}, bf16[256,128]{1,0:T(8,128)(2,1)S(1)}, u32[]{:S(2)}, u32[]{:S(2)}) %collective-permute-start.5) | collective-permute-done | bytes 65568 | tf_op jit(solution)/shard_map/ppermute | solution.py:77
  19.8 2.3 %collective-permute-start.3 = (bf16[256,128]{1,0:T(8,128)(2,1)S(1)}, bf16[256,128]{1,0:T(8,128)(2,1)S(1)}, u32[]{:S(2)}, u32[]{:S(2)}) collective-permute-start(bf16[256,128]{1,0:T(8,128)(2,1)S(1)} %scores.1.a), channel_id=1, source_target_pairs={{0,8},{1,9},{2,10},{3,11},{4,12},{5,13},{6,14},{7,15},{8,0},{9,1},... | collective-permute-start | bytes 196616 | tf_op jit(solution)/shard_map/ppermute | solution.py:77
  22.1 3.5 %collective-permute-done.3.b = bf16[256,128]{1,0:T(8,128)(2,1)S(1)} collective-permute-done((bf16[256,128]{1,0:T(8,128)(2,1)S(1)}, bf16[256,128]{1,0:T(8,128)(2,1)S(1)}, u32[]{:S(2)}, u32[]{:S(2)}) %collective-permute-start.3) | collective-permute-done | bytes 65568 | tf_op jit(solution)/shard_map/ppermute | solution.py:77
  25.8 2.2 %collective-permute-start.6 = (bf16[4,160,128]{2,1,0:T(8,128)(2,1)S(1)}, bf16[4,160,128]{2,1,0:T(8,128)(2,1)S(1)}, u32[]{:S(2)}, u32[]{:S(2)}) collective-permute-start(bf16[4,160,128]{2,1,0:T(8,128)(2,1)S(1)} %get-tuple-element.67), channel_id=1, source_target_pairs={{0,4},{1,5},{2,6},{3,7},{4,8},{5,9},{6,10},{7,11},{8,12},{9,13},{1... | collective-permute-start | bytes 491528 | tf_op jit(solution)/shard_map/ppermute | solution.py:77
  34.2 2.7 %collective-permute-done.7.c = bf16[4,160,128]{2,1,0:T(8,128)(2,1)S(1)} collective-permute-done((bf16[4,160,128]{2,1,0:T(8,128)(2,1)S(1)}, bf16[4,160,128]{2,1,0:T(8,128)(2,1)S(1)}, u32[]{:S(2)}, u32[]{:S(2)}) %collective-permute-start.7) | collective-permute-done | bytes 163872 | tf_op jit(solution)/shard_map/ppermute | solution.py:77
  36.9 3.4 %collective-permute-done.8.d = bf16[4,160,128]{2,1,0:T(8,128)(2,1)S(1)} collective-permute-done((bf16[4,160,128]{2,1,0:T(8,128)(2,1)S(1)}, bf16[4,160,128]{2,1,0:T(8,128)(2,1)S(1)}, u32[]{:S(2)}, u32[]{:S(2)}) %collective-permute-start.8) | collective-permute-done | bytes 163872 | tf_op jit(solution)/shard_map/ppermute | solution.py:77
  43.1 2.1 %forward.1 = (bf16[1216,128]{1,0:T(8,128)(2,1)S(1)}, bf16[1216,128]{1,0:T(8,128)(2,1)S(1)}, bf16[1216,128]{1,0:T(8,128)(2,1)S(1)}, bf16[1216,128]{1,0:T(8,128)(2...) custom-call(bf16[4,4,160,128]{3,2,1,0:T(8,128)(2,1)S(1)} %stack.3.e_ref, ...), custom_call_target="tpu_custom_call" | custom-call | tf_op jit(solution)/shard_map/forward/pallas_call | solution.py:444
  45.2 2.4 %collective-permute-start.13 = (bf16[1216,128]{1,0:T(8,128)(2,1)S(1)}, bf16[1216,128]{1,0:T(8,128)(2,1)S(1)}, u32[]{:S(2)}, u32[]{:S(2)}) collective-permute-start(bf16[1216,128]{1,0:T(8,128)(2,1)S(1)} %get-tuple-element.84), channel_id=1, source_target_pairs={{0,4},{1,5},{2,6},{3,7},{4,8},{5,9},{6,10},{7,11},{8,12},{9,13},{1... | collective-permute-start | bytes 933896 | tf_op jit(solution)/shard_map/ppermute | solution.py:77
  47.6 2.4 %collective-permute-start.14 = (bf16[1216,128]{1,0:T(8,128)(2,1)S(1)}, bf16[1216,128]{1,0:T(8,128)(2,1)S(1)}, u32[]{:S(2)}, u32[]{:S(2)}) collective-permute-start(bf16[1216,128]{1,0:T(8,128)(2,1)S(1)} %get-tuple-element.85), channel_id=1, source_target_pairs={{0,1},{1,2},{2,3},{3,0},{4,5},{5,6},{6,7},{7,4},{8,9},{9,10},{10,1... | collective-permute-start | bytes 933896 | tf_op jit(solution)/shard_map/ppermute | solution.py:77
  50.0 5.1 %collective-permute-done.13.a1 = bf16[1216,128]{1,0:T(8,128)(2,1)S(1)} collective-permute-done((bf16[1216,128]{1,0:T(8,128)(2,1)S(1)}, bf16[1216,128]{1,0:T(8,128)(2,1)S(1)}, u32[]{:S(2)}, u32[]{:S(2)}) %collective-permute-start.13) | collective-permute-done | bytes 311328 | tf_op jit(solution)/shard_map/ppermute | solution.py:77
  57.0 3.0 %collective-permute-done.15.a3 = bf16[1216,128]{1,0:T(8,128)(2,1)S(1)} collective-permute-done((bf16[1216,128]{1,0:T(8,128)(2,1)S(1)}, bf16[1216,128]{1,0:T(8,128)(2,1)S(1)}, u32[]{:S(2)}, u32[]{:S(2)}) %collective-permute-start.15) | collective-permute-done | bytes 311328 | tf_op jit(solution)/shard_map/ppermute | solution.py:77
  60.2 3.1 %collective-permute-start.16 = (bf16[352,128]{1,0:T(8,128)(2,1)S(1)}, bf16[352,128]{1,0:T(8,128)(2,1)S(1)}, u32[]{:S(2)}, u32[]{:S(2)}) collective-permute-start(bf16[352,128]{1,0:T(8,128)(2,1)S(1)} %get-tuple-element.88), channel_id=1, source_target_pairs={{0,8},{1,9},{2,10},{3,11},{4,12},{5,13},{6,14},{7,15},{8,0},{9,1},... | collective-permute-start | bytes 270344 | tf_op jit(solution)/shard_map/ppermute | solution.py:77
  63.3 3.5 %collective-permute-start.18 = (bf16[352,128]{1,0:T(8,128)(2,1)S(1)}, bf16[352,128]{1,0:T(8,128)(2,1)S(1)}, u32[]{:S(2)}, u32[]{:S(2)}) collective-permute-start(bf16[352,128]{1,0:T(8,128)(2,1)S(1)} %get-tuple-element.90), channel_id=1, source_target_pairs={{0,10},{1,11},{2,8},{3,9},{4,14},{5,15},{6,12},{7,13},{8,2},{9,3},... | collective-permute-start | bytes 270344 | tf_op jit(solution)/shard_map/ppermute | solution.py:77
  66.8 2.6 %collective-permute-done.17.c2 = bf16[352,128]{1,0:T(8,128)(2,1)S(1)} collective-permute-done((bf16[352,128]{1,0:T(8,128)(2,1)S(1)}, bf16[352,128]{1,0:T(8,128)(2,1)S(1)}, u32[]{:S(2)}, u32[]{:S(2)}) %collective-permute-start.17) | collective-permute-done | bytes 90144 | tf_op jit(solution)/shard_map/ppermute | solution.py:77
  69.5 2.3 %collective-permute-done.18.c3 = bf16[352,128]{1,0:T(8,128)(2,1)S(1)} collective-permute-done((bf16[352,128]{1,0:T(8,128)(2,1)S(1)}, bf16[352,128]{1,0:T(8,128)(2,1)S(1)}, u32[]{:S(2)}, u32[]{:S(2)}) %collective-permute-start.18) | collective-permute-done | bytes 90144 | tf_op jit(solution)/shard_map/ppermute | solution.py:77
  71.9 3.5 %collective-permute-start.21 = (bf16[288,128]{1,0:T(8,128)(2,1)S(1)}, bf16[288,128]{1,0:T(8,128)(2,1)S(1)}, u32[]{:S(2)}, u32[]{:S(2)}) collective-permute-start(bf16[288,128]{1,0:T(8,128)(2,1)S(1)} %get-tuple-element.91.t0), channel_id=1, source_target_pairs={{0,10},{1,11},{2,8},{3,9},{4,14},{5,15},{6,12},{7,13},{8,2},{9,3},... | collective-permute-start | bytes 221192 | tf_op jit(solution)/shard_map/ppermute | solution.py:77
  79.6 3.3 %collective-permute-start.24 = (f32[16,128]{1,0:T(8,128)S(1)}, f32[16,128]{1,0:T(8,128)S(1)}, u32[]{:S(2)}, u32[]{:S(2)}) collective-permute-start(f32[16,128]{1,0:T(8,128)S(1)} %add.5), channel_id=1, source_target_pairs={{128,0},{161,1},{130,2},{163,3},{196,4},{229,5},{198,6},{231,7},{1... | collective-permute-start | bytes 24584 | tf_op jit(solution)/shard_map/ppermute | solution.py:411
  82.9 4.9 %collective-permute-start.23 = (f32[16,128]{1,0:T(8,128)S(1)}, f32[16,128]{1,0:T(8,128)S(1)}, u32[]{:S(2)}, u32[]{:S(2)}) collective-permute-start(f32[16,128]{1,0:T(8,128)S(1)} %add.5), channel_id=1, source_target_pairs={{0,0},{33,1},{2,2},{35,3},{68,4},{101,5},{70,6},{103,7},{8,8},{41,... | collective-permute-start | bytes 24584 | tf_op jit(solution)/shard_map/ppermute | solution.py:411
  87.8 3.1 %collective-permute-done.23.l0 = f32[16,128]{1,0:T(8,128)S(1)} collective-permute-done((f32[16,128]{1,0:T(8,128)S(1)}, f32[16,128]{1,0:T(8,128)S(1)}, u32[]{:S(2)}, u32[]{:S(2)}) %collective-permute-start.23) | collective-permute-done | bytes 8224 | tf_op jit(solution)/shard_map/ppermute | solution.py:411
  95.8 5.1 %collective-permute-done.27.t3 = bf16[1184,128]{1,0:T(8,128)(2,1)S(1)} collective-permute-done((bf16[1184,128]{1,0:T(8,128)(2,1)S(1)}, bf16[1184,128]{1,0:T(8,128)(2,1)S(1)}, u32[]{:S(2)}, u32[]{:S(2)}) %collective-permute-start.27) | collective-permute-done | bytes 303136 | tf_op jit(solution)/shard_map/ppermute | solution.py:77
  102.0 7.2 %backward.1 = (f32[1,16]{1,0:T(1,128)}, bf16[256,2048]{1,0:T(8,128)(2,1)S(1)}, bf16[2,320,128]{2,1,0:T(8,128)(2,1)S(1)}, bf16[2,320,128]{2,1,0:T(8,128)(2,1)S(1)...) custom-call(bf16[4,256,128]{2,1,0:T(8,128)(2,1)S(1)} %stack.2.q0, ...), custom_call_target="tpu_custom_call" | custom-call | tf_op jit(solution)/shard_map/backward/pallas_call | solution.py:463
  109.2 2.1 %collective-permute-done.28.other_ref = bf16[8,320,128]{2,1,0:T(8,128)(2,1)S(1)} collective-permute-done((bf16[8,320,128]{2,1,0:T(8,128)(2,1)S(1)}, bf16[8,320,128]{2,1,0:T(8,128)(2,1)S(1)}, u32[]{:S(2)}, u32[]{:S(2)}) %collective-permute-start.28) | collective-permute-done | bytes 655392 | tf_op jit(solution)/shard_map/ppermute | solution.py:476
  112.6 2.2 %collective-permute-start.30 = (bf16[2,320,128]{2,1,0:T(8,128)(2,1)S(1)}, bf16[2,320,128]{2,1,0:T(8,128)(2,1)S(1)}, u32[]{:S(2)}, u32[]{:S(2)}) collective-permute-start(bf16[2,320,128]{2,1,0:T(8,128)(2,1)S(1)} %get-tuple-element.107), channel_id=1, source_target_pairs={{0,224},{16,240},{32,0},{48,16},{64,32},{80,48},{96,64},{112,80},{... | collective-permute-start | bytes 491528 | tf_op jit(solution)/shard_map/ppermute | solution.py:390
  114.8 2.0 %collective-permute-start.31 = (bf16[2,320,128]{2,1,0:T(8,128)(2,1)S(1)}, bf16[2,320,128]{2,1,0:T(8,128)(2,1)S(1)}, u32[]{:S(2)}, u32[]{:S(2)}) collective-permute-start(bf16[2,320,128]{2,1,0:T(8,128)(2,1)S(1)} %get-tuple-element.108), channel_id=1, source_target_pairs={{0,64},{16,208},{32,96},{48,240},{64,128},{80,16},{96,160},{112,48... | collective-permute-start | bytes 491528 | tf_op jit(solution)/shard_map/ppermute | solution.py:390
  116.8 2.3 %collective-permute-done.29.o1 = bf16[2,320,128]{2,1,0:T(8,128)(2,1)S(1)} collective-permute-done((bf16[2,320,128]{2,1,0:T(8,128)(2,1)S(1)}, bf16[2,320,128]{2,1,0:T(8,128)(2,1)S(1)}, u32[]{:S(2)}, u32[]{:S(2)}) %collective-permute-start.29) | collective-permute-done | bytes 163872 | tf_op jit(solution)/shard_map/ppermute | solution.py:390
  122.9 8.9 %collective-permute-start.32 = (bf16[320,128]{1,0:T(8,128)(2,1)S(1)}, bf16[320,128]{1,0:T(8,128)(2,1)S(1)}, u32[]{:S(2)}, u32[]{:S(2)}) collective-permute-start(bf16[320,128]{1,0:T(8,128)(2,1)S(1)} %get-tuple-element.109), channel_id=1, source_target_pairs={{0,0},{1,16},{2,32},{3,48},{4,64},{5,80},{6,96},{7,112},{8,128},{9... | collective-permute-start | bytes 245768 | tf_op jit(solution)/shard_map/ppermute | solution.py:400
  131.7 2.4 %collective-permute-start.33 = (bf16[320,128]{1,0:T(8,128)(2,1)S(1)}, bf16[320,128]{1,0:T(8,128)(2,1)S(1)}, u32[]{:S(2)}, u32[]{:S(2)}) collective-permute-start(bf16[320,128]{1,0:T(8,128)(2,1)S(1)} %get-tuple-element.110), channel_id=1, source_target_pairs={{0,8},{1,24},{2,40},{3,56},{4,72},{5,88},{6,104},{7,120},{8,136},{... | collective-permute-start | bytes 245768 | tf_op jit(solution)/shard_map/ppermute | solution.py:400
  135.7 12.5 %collective-permute-done.33.u1 = bf16[320,128]{1,0:T(8,128)(2,1)S(1)} collective-permute-done((bf16[320,128]{1,0:T(8,128)(2,1)S(1)}, bf16[320,128]{1,0:T(8,128)(2,1)S(1)}, u32[]{:S(2)}, u32[]{:S(2)}) %collective-permute-start.33) | collective-permute-done | bytes 81952 | tf_op jit(solution)/shard_map/ppermute | solution.py:400
  (62 shorter events, 32.4 us)
Async XLA Ops:
  2.4 23.2 %collective-permute-start = (bf16[4,160,128]{2,1,0:T(8,128)(2,1)S(1)}, bf16[4,160,128]{2,1,0:T(8,128)(2,1)S(1)}, u32[]{:S(2)}, u32[]{:S(2)}) collective-permute-start(bf16[4,160,128]{2,1,0:T(8,128)(2,1)S(1)} %get-tuple-element.59), channel_id=1, source_target_pairs={{0,8},{1,9},{2,10},{3,11},{4,12},{5,13},{6,14},{7,15},{8,0},{9,1},... | collective-permute-start | bytes 491528 | tf_op jit(solution)/shard_map/ppermute | solution.py:77
  4.8 20.8 %collective-permute-start.1 = (bf16[4,160,128]{2,1,0:T(8,128)(2,1)S(1)}, bf16[4,160,128]{2,1,0:T(8,128)(2,1)S(1)}, u32[]{:S(2)}, u32[]{:S(2)}) collective-permute-start(bf16[4,160,128]{2,1,0:T(8,128)(2,1)S(1)} %get-tuple-element.60), channel_id=1, source_target_pairs={{0,2},{1,3},{2,0},{3,1},{4,6},{5,7},{6,4},{7,5},{8,10},{9,11},{10,... | collective-permute-start | bytes 491528 | tf_op jit(solution)/shard_map/ppermute | solution.py:77
  5.3 20.3 %collective-permute-start.2 = (bf16[4,160,128]{2,1,0:T(8,128)(2,1)S(1)}, bf16[4,160,128]{2,1,0:T(8,128)(2,1)S(1)}, u32[]{:S(2)}, u32[]{:S(2)}) collective-permute-start(bf16[4,160,128]{2,1,0:T(8,128)(2,1)S(1)} %get-tuple-element.61), channel_id=1, source_target_pairs={{0,10},{1,11},{2,8},{3,9},{4,14},{5,15},{6,12},{7,13},{8,2},{9,3},... | collective-permute-start | bytes 491528 | tf_op jit(solution)/shard_map/ppermute | solution.py:77
  11.6 8.3 %collective-permute-start.5 = (bf16[256,128]{1,0:T(8,128)(2,1)S(1)}, bf16[256,128]{1,0:T(8,128)(2,1)S(1)}, u32[]{:S(2)}, u32[]{:S(2)}) collective-permute-start(bf16[256,128]{1,0:T(8,128)(2,1)S(1)} %scores.1.a), channel_id=1, source_target_pairs={{0,10},{1,11},{2,8},{3,9},{4,14},{5,15},{6,12},{7,13},{8,2},{9,3},... | collective-permute-start | bytes 196616 | tf_op jit(solution)/shard_map/ppermute | solution.py:77
  13.9 8.2 %collective-permute-start.4 = (bf16[256,128]{1,0:T(8,128)(2,1)S(1)}, bf16[256,128]{1,0:T(8,128)(2,1)S(1)}, u32[]{:S(2)}, u32[]{:S(2)}) collective-permute-start(bf16[256,128]{1,0:T(8,128)(2,1)S(1)} %scores.1.a), channel_id=1, source_target_pairs={{0,2},{1,3},{2,0},{3,1},{4,6},{5,7},{6,4},{7,5},{8,10},{9,11},{10,... | collective-permute-start | bytes 196616 | tf_op jit(solution)/shard_map/ppermute | solution.py:77
  19.8 5.8 %collective-permute-start.3 = (bf16[256,128]{1,0:T(8,128)(2,1)S(1)}, bf16[256,128]{1,0:T(8,128)(2,1)S(1)}, u32[]{:S(2)}, u32[]{:S(2)}) collective-permute-start(bf16[256,128]{1,0:T(8,128)(2,1)S(1)} %scores.1.a), channel_id=1, source_target_pairs={{0,8},{1,9},{2,10},{3,11},{4,12},{5,13},{6,14},{7,15},{8,0},{9,1},... | collective-permute-start | bytes 196616 | tf_op jit(solution)/shard_map/ppermute | solution.py:77
  25.8 7.0 %collective-permute-start.6 = (bf16[4,160,128]{2,1,0:T(8,128)(2,1)S(1)}, bf16[4,160,128]{2,1,0:T(8,128)(2,1)S(1)}, u32[]{:S(2)}, u32[]{:S(2)}) collective-permute-start(bf16[4,160,128]{2,1,0:T(8,128)(2,1)S(1)} %get-tuple-element.67), channel_id=1, source_target_pairs={{0,4},{1,5},{2,6},{3,7},{4,8},{5,9},{6,10},{7,11},{8,12},{9,13},{1... | collective-permute-start | bytes 491528 | tf_op jit(solution)/shard_map/ppermute | solution.py:77
  28.0 12.3 %collective-permute-start.11 = (bf16[4,256,128]{2,1,0:T(8,128)(2,1)S(1)}, bf16[4,256,128]{2,1,0:T(8,128)(2,1)S(1)}, u32[]{:S(2)}, u32[]{:S(2)}) collective-permute-start(bf16[4,256,128]{2,1,0:T(8,128)(2,1)S(1)} %stack.2.q0), channel_id=1, source_target_pairs={{0,5},{1,6},{2,7},{3,4},{4,9},{5,10},{6,11},{7,8},{8,13},{9,14},{1... | collective-permute-start | bytes 786440 | tf_op jit(solution)/shard_map/ppermute | solution.py:77
  29.5 10.8 %collective-permute-start.10 = (bf16[4,256,128]{2,1,0:T(8,128)(2,1)S(1)}, bf16[4,256,128]{2,1,0:T(8,128)(2,1)S(1)}, u32[]{:S(2)}, u32[]{:S(2)}) collective-permute-start(bf16[4,256,128]{2,1,0:T(8,128)(2,1)S(1)} %stack.2.q0), channel_id=1, source_target_pairs={{0,3},{1,0},{2,1},{3,2},{4,7},{5,4},{6,5},{7,6},{8,11},{9,8},{10,9... | collective-permute-start | bytes 786440 | tf_op jit(solution)/shard_map/ppermute | solution.py:77
  30.3 10.0 %collective-permute-start.9 = (bf16[4,256,128]{2,1,0:T(8,128)(2,1)S(1)}, bf16[4,256,128]{2,1,0:T(8,128)(2,1)S(1)}, u32[]{:S(2)}, u32[]{:S(2)}) collective-permute-start(bf16[4,256,128]{2,1,0:T(8,128)(2,1)S(1)} %stack.2.q0), channel_id=1, source_target_pairs={{0,12},{1,13},{2,14},{3,15},{4,0},{5,1},{6,2},{7,3},{8,4},{9,5},{1... | collective-permute-start | bytes 786440 | tf_op jit(solution)/shard_map/ppermute | solution.py:77
  31.6 5.3 %collective-permute-start.7 = (bf16[4,160,128]{2,1,0:T(8,128)(2,1)S(1)}, bf16[4,160,128]{2,1,0:T(8,128)(2,1)S(1)}, u32[]{:S(2)}, u32[]{:S(2)}) collective-permute-start(bf16[4,160,128]{2,1,0:T(8,128)(2,1)S(1)} %get-tuple-element.68), channel_id=1, source_target_pairs={{0,1},{1,2},{2,3},{3,0},{4,5},{5,6},{6,7},{7,4},{8,9},{9,10},{10,1... | collective-permute-start | bytes 491528 | tf_op jit(solution)/shard_map/ppermute | solution.py:77
  32.8 7.5 %collective-permute-start.8 = (bf16[4,160,128]{2,1,0:T(8,128)(2,1)S(1)}, bf16[4,160,128]{2,1,0:T(8,128)(2,1)S(1)}, u32[]{:S(2)}, u32[]{:S(2)}) collective-permute-start(bf16[4,160,128]{2,1,0:T(8,128)(2,1)S(1)} %get-tuple-element.69), channel_id=1, source_target_pairs={{0,15},{1,12},{2,13},{3,14},{4,3},{5,0},{6,1},{7,2},{8,7},{9,4},{1... | collective-permute-start | bytes 491528 | tf_op jit(solution)/shard_map/ppermute | solution.py:77
  40.3 2.7 %collective-permute-start.12 = (bf16[4,4,160,128]{3,2,1,0:T(8,128)(2,1)S(1)}, bf16[4,4,160,128]{3,2,1,0:T(8,128)(2,1)S(1)}, u32[]{:S(2)}, u32[]{:S(2)}) collective-permute-start(bf16[4,4,160,128]{3,2,1,0:T(8,128)(2,1)S(1)} %stack.3.e_ref), channel_id=1, source_target_pairs={{0,16},{16,0},{1,17},{17,1},{2,18},{18,2},{3,19},{19,3},{4,20},{20... | collective-permute-start | bytes 1966088 | tf_op jit(solution)/shard_map/ppermute | solution.py:435
  45.2 9.8 %collective-permute-start.13 = (bf16[1216,128]{1,0:T(8,128)(2,1)S(1)}, bf16[1216,128]{1,0:T(8,128)(2,1)S(1)}, u32[]{:S(2)}, u32[]{:S(2)}) collective-permute-start(bf16[1216,128]{1,0:T(8,128)(2,1)S(1)} %get-tuple-element.84), channel_id=1, source_target_pairs={{0,4},{1,5},{2,6},{3,7},{4,8},{5,9},{6,10},{7,11},{8,12},{9,13},{1... | collective-permute-start | bytes 933896 | tf_op jit(solution)/shard_map/ppermute | solution.py:77
  47.6 9.5 %collective-permute-start.14 = (bf16[1216,128]{1,0:T(8,128)(2,1)S(1)}, bf16[1216,128]{1,0:T(8,128)(2,1)S(1)}, u32[]{:S(2)}, u32[]{:S(2)}) collective-permute-start(bf16[1216,128]{1,0:T(8,128)(2,1)S(1)} %get-tuple-element.85), channel_id=1, source_target_pairs={{0,1},{1,2},{2,3},{3,0},{4,5},{5,6},{6,7},{7,4},{8,9},{9,10},{10,1... | collective-permute-start | bytes 933896 | tf_op jit(solution)/shard_map/ppermute | solution.py:77
  50.0 10.1 %collective-permute-start.15 = (bf16[1216,128]{1,0:T(8,128)(2,1)S(1)}, bf16[1216,128]{1,0:T(8,128)(2,1)S(1)}, u32[]{:S(2)}, u32[]{:S(2)}) collective-permute-start(bf16[1216,128]{1,0:T(8,128)(2,1)S(1)} %get-tuple-element.86), channel_id=1, source_target_pairs={{0,15},{1,12},{2,13},{3,14},{4,3},{5,0},{6,1},{7,2},{8,7},{9,4},{1... | collective-permute-start | bytes 933896 | tf_op jit(solution)/shard_map/ppermute | solution.py:77
  60.2 6.6 %collective-permute-start.16 = (bf16[352,128]{1,0:T(8,128)(2,1)S(1)}, bf16[352,128]{1,0:T(8,128)(2,1)S(1)}, u32[]{:S(2)}, u32[]{:S(2)}) collective-permute-start(bf16[352,128]{1,0:T(8,128)(2,1)S(1)} %get-tuple-element.88), channel_id=1, source_target_pairs={{0,8},{1,9},{2,10},{3,11},{4,12},{5,13},{6,14},{7,15},{8,0},{9,1},... | collective-permute-start | bytes 270344 | tf_op jit(solution)/shard_map/ppermute | solution.py:77
  63.3 6.1 %collective-permute-start.17 = (bf16[352,128]{1,0:T(8,128)(2,1)S(1)}, bf16[352,128]{1,0:T(8,128)(2,1)S(1)}, u32[]{:S(2)}, u32[]{:S(2)}) collective-permute-start(bf16[352,128]{1,0:T(8,128)(2,1)S(1)} %get-tuple-element.89), channel_id=1, source_target_pairs={{0,2},{1,3},{2,0},{3,1},{4,6},{5,7},{6,4},{7,5},{8,10},{9,11},{10,... | collective-permute-start | bytes 270344 | tf_op jit(solution)/shard_map/ppermute | solution.py:77
  63.3 8.4 %collective-permute-start.18 = (bf16[352,128]{1,0:T(8,128)(2,1)S(1)}, bf16[352,128]{1,0:T(8,128)(2,1)S(1)}, u32[]{:S(2)}, u32[]{:S(2)}) collective-permute-start(bf16[352,128]{1,0:T(8,128)(2,1)S(1)} %get-tuple-element.90), channel_id=1, source_target_pairs={{0,10},{1,11},{2,8},{3,9},{4,14},{5,15},{6,12},{7,13},{8,2},{9,3},... | collective-permute-start | bytes 270344 | tf_op jit(solution)/shard_map/ppermute | solution.py:77
  71.9 19.0 %collective-permute-start.21 = (bf16[288,128]{1,0:T(8,128)(2,1)S(1)}, bf16[288,128]{1,0:T(8,128)(2,1)S(1)}, u32[]{:S(2)}, u32[]{:S(2)}) collective-permute-start(bf16[288,128]{1,0:T(8,128)(2,1)S(1)} %get-tuple-element.91.t0), channel_id=1, source_target_pairs={{0,10},{1,11},{2,8},{3,9},{4,14},{5,15},{6,12},{7,13},{8,2},{9,3},... | collective-permute-start | bytes 221192 | tf_op jit(solution)/shard_map/ppermute | solution.py:77
  75.4 15.5 %collective-permute-start.20 = (bf16[288,128]{1,0:T(8,128)(2,1)S(1)}, bf16[288,128]{1,0:T(8,128)(2,1)S(1)}, u32[]{:S(2)}, u32[]{:S(2)}) collective-permute-start(bf16[288,128]{1,0:T(8,128)(2,1)S(1)} %get-tuple-element.91.t0), channel_id=1, source_target_pairs={{0,2},{1,3},{2,0},{3,1},{4,6},{5,7},{6,4},{7,5},{8,10},{9,11},{10,... | collective-permute-start | bytes 221192 | tf_op jit(solution)/shard_map/ppermute | solution.py:77
  76.5 14.4 %collective-permute-start.19 = (bf16[288,128]{1,0:T(8,128)(2,1)S(1)}, bf16[288,128]{1,0:T(8,128)(2,1)S(1)}, u32[]{:S(2)}, u32[]{:S(2)}) collective-permute-start(bf16[288,128]{1,0:T(8,128)(2,1)S(1)} %get-tuple-element.91.t0), channel_id=1, source_target_pairs={{0,8},{1,9},{2,10},{3,11},{4,12},{5,13},{6,14},{7,15},{8,0},{9,1},... | collective-permute-start | bytes 221192 | tf_op jit(solution)/shard_map/ppermute | solution.py:77
  79.6 8.2 %collective-permute-start.24 = (f32[16,128]{1,0:T(8,128)S(1)}, f32[16,128]{1,0:T(8,128)S(1)}, u32[]{:S(2)}, u32[]{:S(2)}) collective-permute-start(f32[16,128]{1,0:T(8,128)S(1)} %add.5), channel_id=1, source_target_pairs={{128,0},{161,1},{130,2},{163,3},{196,4},{229,5},{198,6},{231,7},{1... | collective-permute-start | bytes 24584 | tf_op jit(solution)/shard_map/ppermute | solution.py:411
  82.9 8.0 %collective-permute-start.23 = (f32[16,128]{1,0:T(8,128)S(1)}, f32[16,128]{1,0:T(8,128)S(1)}, u32[]{:S(2)}, u32[]{:S(2)}) collective-permute-start(f32[16,128]{1,0:T(8,128)S(1)} %add.5), channel_id=1, source_target_pairs={{0,0},{33,1},{2,2},{35,3},{68,4},{101,5},{70,6},{103,7},{8,8},{41,... | collective-permute-start | bytes 24584 | tf_op jit(solution)/shard_map/ppermute | solution.py:411
  90.9 9.9 %collective-permute-start.27 = (bf16[1184,128]{1,0:T(8,128)(2,1)S(1)}, bf16[1184,128]{1,0:T(8,128)(2,1)S(1)}, u32[]{:S(2)}, u32[]{:S(2)}) collective-permute-start(bf16[1184,128]{1,0:T(8,128)(2,1)S(1)} %row.1.t0), channel_id=1, source_target_pairs={{0,5},{1,6},{2,7},{3,4},{4,9},{5,10},{6,11},{7,8},{8,13},{9,14},{1... | collective-permute-start | bytes 909320 | tf_op jit(solution)/shard_map/ppermute | solution.py:77
  92.5 8.3 %collective-permute-start.26 = (bf16[1184,128]{1,0:T(8,128)(2,1)S(1)}, bf16[1184,128]{1,0:T(8,128)(2,1)S(1)}, u32[]{:S(2)}, u32[]{:S(2)}) collective-permute-start(bf16[1184,128]{1,0:T(8,128)(2,1)S(1)} %row.1.t0), channel_id=1, source_target_pairs={{0,3},{1,0},{2,1},{3,2},{4,7},{5,4},{6,5},{7,6},{8,11},{9,8},{10,9... | collective-permute-start | bytes 909320 | tf_op jit(solution)/shard_map/ppermute | solution.py:77
  94.2 7.8 %collective-permute-start.25 = (bf16[1184,128]{1,0:T(8,128)(2,1)S(1)}, bf16[1184,128]{1,0:T(8,128)(2,1)S(1)}, u32[]{:S(2)}, u32[]{:S(2)}) collective-permute-start(bf16[1184,128]{1,0:T(8,128)(2,1)S(1)} %row.1.t0), channel_id=1, source_target_pairs={{0,12},{1,13},{2,14},{3,15},{4,0},{5,1},{6,2},{7,3},{8,4},{9,5},{1... | collective-permute-start | bytes 909320 | tf_op jit(solution)/shard_map/ppermute | solution.py:77
  111.5 7.7 %collective-permute-start.29 = (bf16[2,320,128]{2,1,0:T(8,128)(2,1)S(1)}, bf16[2,320,128]{2,1,0:T(8,128)(2,1)S(1)}, u32[]{:S(2)}, u32[]{:S(2)}) collective-permute-start(bf16[2,320,128]{2,1,0:T(8,128)(2,1)S(1)} %get-tuple-element.106), channel_id=1, source_target_pairs={{0,32},{16,48},{32,64},{48,80},{64,96},{80,112},{96,128},{112,144}... | collective-permute-start | bytes 491528 | tf_op jit(solution)/shard_map/ppermute | solution.py:390
  112.6 8.5 %collective-permute-start.30 = (bf16[2,320,128]{2,1,0:T(8,128)(2,1)S(1)}, bf16[2,320,128]{2,1,0:T(8,128)(2,1)S(1)}, u32[]{:S(2)}, u32[]{:S(2)}) collective-permute-start(bf16[2,320,128]{2,1,0:T(8,128)(2,1)S(1)} %get-tuple-element.107), channel_id=1, source_target_pairs={{0,224},{16,240},{32,0},{48,16},{64,32},{80,48},{96,64},{112,80},{... | collective-permute-start | bytes 491528 | tf_op jit(solution)/shard_map/ppermute | solution.py:390
  114.8 8.0 %collective-permute-start.31 = (bf16[2,320,128]{2,1,0:T(8,128)(2,1)S(1)}, bf16[2,320,128]{2,1,0:T(8,128)(2,1)S(1)}, u32[]{:S(2)}, u32[]{:S(2)}) collective-permute-start(bf16[2,320,128]{2,1,0:T(8,128)(2,1)S(1)} %get-tuple-element.108), channel_id=1, source_target_pairs={{0,64},{16,208},{32,96},{48,240},{64,128},{80,16},{96,160},{112,48... | collective-permute-start | bytes 491528 | tf_op jit(solution)/shard_map/ppermute | solution.py:390
  122.9 12.9 %collective-permute-start.32 = (bf16[320,128]{1,0:T(8,128)(2,1)S(1)}, bf16[320,128]{1,0:T(8,128)(2,1)S(1)}, u32[]{:S(2)}, u32[]{:S(2)}) collective-permute-start(bf16[320,128]{1,0:T(8,128)(2,1)S(1)} %get-tuple-element.109), channel_id=1, source_target_pairs={{0,0},{1,16},{2,32},{3,48},{4,64},{5,80},{6,96},{7,112},{8,128},{9... | collective-permute-start | bytes 245768 | tf_op jit(solution)/shard_map/ppermute | solution.py:400
  131.7 16.5 %collective-permute-start.33 = (bf16[320,128]{1,0:T(8,128)(2,1)S(1)}, bf16[320,128]{1,0:T(8,128)(2,1)S(1)}, u32[]{:S(2)}, u32[]{:S(2)}) collective-permute-start(bf16[320,128]{1,0:T(8,128)(2,1)S(1)} %get-tuple-element.110), channel_id=1, source_target_pairs={{0,8},{1,24},{2,40},{3,56},{4,72},{5,88},{6,104},{7,120},{8,136},{... | collective-permute-start | bytes 245768 | tf_op jit(solution)/shard_map/ppermute | solution.py:400
  (6 other events, 36.7 us)

commit v5 on v2

v5 whole, which is shorter than its diff:
```python
import functools
import math

import jax
import jax.numpy as jnp
from jax import lax
from jax.experimental import pallas as pl
from jax.experimental.pallas import tpu as pltpu
from jax.sharding import Mesh, PartitionSpec as P

P_SIZE = 128
ITERS = 3
CLASSES = 10
PAD = 16
HEADS = 2
REFS = HEADS * P_SIZE

temper = 1.5
epsilon = 1e-06
loss_scale = 65536.0
f32 = jnp.float32
bf16 = jnp.bfloat16

SIDE = 4
DEPTH = 8
BLOCKS = SIDE * SIDE
CHIPS = ((0, 1, 7, 2), (0, 1, 7, 6))
T_ROWS = REFS + HEADS * PAD
M_ROWS = 2 * PAD
VMEM = pl.BlockSpec(memory_space=pltpu.VMEM)
SMEM = pl.BlockSpec(memory_space=pltpu.SMEM)
NT = (((1,), (1,)), ((), ()))
TN = (((0,), (0,)), ((), ()))


HBM = pl.BlockSpec(memory_space=pltpu.HBM)


def call(kernel, name, shapes, specs, scratch=(), flops=0):
    many = isinstance(shapes, list)
    return pl.pallas_call(
        kernel,
        out_shape=shapes,
        in_specs=[VMEM] * specs if isinstance(specs, int) else specs,
        out_specs=[VMEM] * len(shapes) if many else VMEM,
        scratch_shapes=list(scratch),
        compiler_params=pltpu.CompilerParams(vmem_limit_bytes=40 * 1024 * 1024),
        cost_estimate=pl.CostEstimate(flops=flops, bytes_accessed=1 << 20, transcendentals=0) if flops else None,
        name=name,
    )


def lanes(block, rows):
    return pl.ds(pl.multiple_of(block * rows, rows), rows)


def exchange(value):
    return lax.all_to_all(value, ("y", "x"), 0, 0)


def scores_kernel(scale, f_hbm, r_hbm, out_ref, part_ref, f_ref, r_ref, turned_ref, sems):
    half = out_ref.shape[1] - REFS
    part = 2 * half
    steps = r_ref.shape[0]
    rows = r_ref.shape[1]
    load = pltpu.make_async_copy(f_hbm, f_ref, sems.at[steps])
    load.start()
    loads = []
    for k in range(steps):
        loads.append(pltpu.make_async_copy(r_hbm.at[pl.ds(k * rows, rows)], r_ref.at[k], sems.at[k]))
        loads[k].start()
    load.wait()
    for j in range(BLOCKS // 2):
        where = slice(2 * part * j, 2 * part * (j + 1))
        turned_ref[where, :] = jnp.transpose(f_ref[:, where])
    core = lax.axis_index("core")
    for j in range(BLOCKS):
        out_ref[j, :half, :] = turned_ref[pl.ds(pl.multiple_of(part * j + half * core, half), half), :]
    place = lax.axis_index("y") * SIDE + lax.axis_index("x")
    for k in range(steps):
        loads[k].wait()
        scores = lax.dot_general(r_ref[k], f_ref[...], NT, preferred_element_type=f32)
        kernel = jnp.exp(scores * scale).astype(bf16)
        for j in range(BLOCKS):
            out_ref[j, half + k * rows : half + (k + 1) * rows, :] = kernel
        pair = r_ref[k, :, pl.ds(pl.multiple_of((place // 2) * (2 * part), 2 * part), 2 * part)]
        part_ref[k * rows : (k + 1) * rows, :] = jnp.where(lax.rem(place, 2) == 0, pair[:, :part], pair[:, part:])


def peel_kernel(in_ref, out_ref):
    half = out_ref.shape[1]
    for j in range(BLOCKS):
        out_ref[j] = in_ref[j, :half, :]


def diagonal():
    square = (P_SIZE, P_SIZE)
    return lax.broadcasted_iota(jnp.int32, square, 0) == lax.broadcasted_iota(jnp.int32, square, 1)


def to_row(column):
    return jnp.sum(jnp.where(diagonal(), column, 0.0), axis=0, keepdims=True)


def to_column(row):
    return jnp.sum(jnp.where(diagonal(), row, 0.0), axis=1, keepdims=True)


def sinkhorn_kernel(q_ref, len_ref, rs_ref, rt_ref, col_ref, plan_ref):
    length = len_ref[0]
    rows = q_ref.shape[2]
    low = q_ref.shape[1] - REFS
    mass = 1.0 / (jnp.zeros((1, rows), jnp.int32) + length).astype(f32)
    lane = lax.broadcasted_iota(jnp.int32, (1, rows), 1)
    masses = [jnp.where(s * rows + lane < length, mass, 0.0) for s in range(BLOCKS)]
    for t in range(ITERS):
        for h in range(HEADS):
            here = slice(h * P_SIZE, (h + 1) * P_SIZE)
            acc = jnp.zeros((P_SIZE, rows), f32)
            for s in range(BLOCKS):
                k = q_ref[s, low + h * P_SIZE : low + (h + 1) * P_SIZE, :].astype(f32)
                weighted = k if t == 0 else k * col_ref[t - 1, here, :]
                total = jnp.sum(weighted, axis=0, keepdims=True)
                scale = masses[s] / total
                place = (t * HEADS + h) * BLOCKS + s
                rt_ref[place : place + 1, :] = total
                rs_ref[place : place + 1, :] = scale
                acc = acc + k * scale
            col = 1.0 / (float(P_SIZE) * jnp.sum(acc, axis=1, keepdims=True))
            col_ref[t, here, :] = jnp.broadcast_to(col, (P_SIZE, rows))
    for h in range(HEADS):
        here = slice(h * P_SIZE, (h + 1) * P_SIZE)
        for s in range(BLOCKS):
            k = q_ref[s, low + h * P_SIZE : low + (h + 1) * P_SIZE, :].astype(f32)
            place = ((ITERS - 1) * HEADS + h) * BLOCKS + s
            plan = rs_ref[place : place + 1, :] * k * col_ref[ITERS - 1, here, :]
            plan_ref[here, s * rows : (s + 1) * rows] = plan.astype(bf16)


def forward_kernel(e_ref, other_ref, wt_ref, plan_ref, out_ref, raw_ref, fc_ref, ext_ref):
    core = lax.axis_index("core")
    half, rows = e_ref.shape[1:]
    for j in range(BLOCKS):
        here = slice(j * rows, (j + 1) * rows)
        fc_ref[pl.ds(pl.multiple_of(core * half, half), half), here] = e_ref[j]
        fc_ref[pl.ds(pl.multiple_of((1 - core) * half, half), half), here] = other_ref[j]
    raw = float(P_SIZE) * lax.dot_general(plan_ref[...], fc_ref[...], NT, preferred_element_type=f32)
    raw_ref[...] = raw
    ext_ref[:REFS, :] = raw.astype(bf16)
    ext_ref[REFS:, :] = wt_ref[...]
    for i in range(4):
        wide = jnp.dot(
            ext_ref[...], fc_ref[:, 4 * i * rows : 4 * (i + 1) * rows], preferred_element_type=f32
        ).astype(bf16)
        for k in range(4):
            out_ref[4 * i + k, :T_ROWS, :] = wide[:, k * rows : (k + 1) * rows]
    for h in range(HEADS):
        here = slice(h * P_SIZE, (h + 1) * P_SIZE)
        squares = jnp.sum(raw_ref[here, :] * raw_ref[here, :], axis=1, keepdims=True)
        products = lax.dot_general(
            wt_ref[h * PAD : (h + 1) * PAD, :], ext_ref[here, :], NT, preferred_element_type=f32
        )
        kind = lax.broadcasted_iota(jnp.int32, products.shape, 0)
        moments = jnp.where(kind == CLASSES, to_row(squares), products).astype(bf16)
        for j in range(BLOCKS):
            out_ref[j, T_ROWS + h * PAD : T_ROWS + (h + 1) * PAD, :] = moments


def add_blocks(ref, low, high):
    total = ref[0, low:high, :].astype(f32)
    for j in range(1, BLOCKS):
        total = total + ref[j, low:high, :].astype(f32)
    return total


def inverse_rms(moments, width):
    return lax.rsqrt(moments[CLASSES : CLASSES + 1, :] / width + epsilon)


def sum_kernel(width, in_ref, t_ref, m_ref, logit_ref):
    logits = jnp.zeros((PAD, 1), f32)
    for h in range(HEADS):
        moments = add_blocks(in_ref, T_ROWS + h * PAD, T_ROWS + (h + 1) * PAD)
        m_ref[h * PAD : (h + 1) * PAD, :] = moments
        part = jnp.sum(inverse_rms(moments, width) * moments, axis=1, keepdims=True)
        logits = logits + part / P_SIZE
    logit_ref[...] = jnp.broadcast_to(logits, logit_ref.shape)
    for low in range(0, T_ROWS, 96):
        t_ref[low : low + 96, :] = add_blocks(in_ref, low, low + 96).astype(bf16)


def row_kernel(t_ref, logit_ref, out_ref):
    logits = logit_ref[...]
    high = logits.astype(bf16)
    lane = lax.broadcasted_iota(jnp.int32, logits.shape, 1)
    both = jnp.where(lane < P_SIZE // 2, high.astype(f32), logits - high.astype(f32)).astype(bf16)
    for j in range(BLOCKS):
        out_ref[j, :T_ROWS, :] = t_ref[...]
        out_ref[j, T_ROWS:, :] = both


def sum_logits(ref):
    section = 2 * lax.axis_index("z") + lax.axis_index("core")
    total = jnp.zeros((PAD, P_SIZE), f32)
    for other in range(BLOCKS):
        total = total + ref[lax.rem(other + BLOCKS - section, BLOCKS), T_ROWS:, :].astype(f32)
    return jnp.broadcast_to(total[:, :1] + total[:, P_SIZE // 2 : P_SIZE // 2 + 1], total.shape)


def backward_kernel(
    width, score_scale,
    q_ref, t_ref, rs_ref, rt_ref, col_ref, m_ref, raw_ref, wt_ref, plan_ref, refs_ref, label_ref,
    logit_ref, gs_ref, p0, p1, p2, p3, other_ref, gt_ref, grs_ref, u_ref, left_ref, right_ref, wide_ref,
):
    rows = q_ref.shape[2]
    base = q_ref.shape[1] - REFS
    size = float(P_SIZE)
    logits = sum_logits(t_ref)
    square = lax.broadcasted_iota(jnp.int32, (PAD, PAD), 0) == lax.broadcasted_iota(jnp.int32, (PAD, PAD), 1)
    logit_ref[...] = jnp.sum(jnp.where(square, logits[:, :PAD], 0.0), axis=0, keepdims=True)
    kind = lax.broadcasted_iota(jnp.int32, logits.shape, 0)
    exps = jnp.where(kind < CLASSES, jnp.exp(logits), 0.0)
    probs = exps / jnp.sum(exps, axis=0, keepdims=True)
    grads = loss_scale * (probs - (kind == label_ref[0]).astype(f32))
    grads = jnp.where(kind < CLASSES, grads, 0.0)
    left_ref[:REFS, :] = refs_ref[...]
    right_ref[REFS:, :] = plan_ref[...]
    for h in range(HEADS):
        here = slice(h * P_SIZE, (h + 1) * P_SIZE)
        moments = m_ref[h * PAD : (h + 1) * PAD, :]
        inverse_row = inverse_rms(moments, width)
        dual_row = inverse_row * jnp.sum(grads * moments, axis=0, keepdims=True) / (size * width)
        inverse = to_column(inverse_row)
        pull = to_column(inverse_row * dual_row)
        normed = jnp.sum(grads[:, :1] * wt_ref[h * PAD : (h + 1) * PAD, :].astype(f32), axis=0, keepdims=True) / size
        grad_raw = (inverse * (normed - raw_ref[here, :] * pull)).astype(bf16)
        left_ref[REFS + h * P_SIZE : REFS + (h + 1) * P_SIZE, :] = (size * grad_raw.astype(f32)).astype(bf16)
        first = jnp.broadcast_to(size * inverse, (P_SIZE, rows))
        second = first * pull

        def load(s):
            return q_ref[s, base + h * P_SIZE : base + (h + 1) * P_SIZE, :].astype(f32)

        def grad_plan(s, u):
            return first * u - second * t_ref[s, here, :].astype(f32)

        def row(ref, t, s):
            place = (t * HEADS + h) * BLOCKS + s
            return ref[place : place + 1, :]

        def put(ref, t, s, value):
            place = (t * HEADS + h) * BLOCKS + s
            ref[place : place + 1, :] = value

        acc = jnp.zeros((P_SIZE, rows), f32)
        for s in range(BLOCKS):
            v = t_ref[s, REFS + h * PAD : REFS + (h + 1) * PAD, :].astype(f32)
            u = jnp.sum(grads * v, axis=0, keepdims=True) / size
            put(u_ref, 0, s, u)
            weighted = grad_plan(s, u) * load(s)
            put(grs_ref, ITERS - 1, s, jnp.sum(weighted * col_ref[ITERS - 1, here, :], axis=0, keepdims=True))
            acc = acc + weighted * row(rs_ref, ITERS - 1, s)
        for t in reversed(range(ITERS)):
            grad_col = jnp.sum(acc, axis=1, keepdims=True)
            gt_ref[t] = -size * col_ref[t, here, :] ** 2 * grad_col
            acc = jnp.zeros((P_SIZE, rows), f32)
            for s in range(BLOCKS):
                k = load(s)
                grad_row = jnp.sum(k * gt_ref[t], axis=0, keepdims=True)
                if t == ITERS - 1:
                    grad_row = grad_row + row(grs_ref, t, s)
                grad_rowsum = -grad_row * row(rs_ref, t, s) / row(rt_ref, t, s)
                put(grs_ref, t, s, grad_rowsum)
                if t > 0:
                    acc = acc + k * grad_rowsum
        for s in range(BLOCKS):
            total = row(rs_ref, ITERS - 1, s) * col_ref[ITERS - 1, here, :] * grad_plan(s, row(u_ref, 0, s))
            for t in range(ITERS):
                total = total + row(rs_ref, t, s) * gt_ref[t]
                if t > 0:
                    total = total + row(grs_ref, t, s) * col_ref[t - 1, here, :]
                else:
                    total = total + row(grs_ref, t, s)
            right_ref[here, s * rows : (s + 1) * rows] = (score_scale * total * load(s)).astype(bf16)
    gs_ref[...] = right_ref[:REFS, :]
    wide_ref[...] = lax.dot_general(left_ref[...], right_ref[...], TN, preferred_element_type=f32)
    core, z = lax.axis_index("core"), lax.axis_index("z")
    outs = (p0, p1, p2, p3)

    def take(step, which):
        return wide_ref[:, lanes(2 * lax.rem(z + step, DEPTH) + which, rows)].astype(bf16)

    for k in range(4):
        for b in range(2):
            step = jnp.where(core == 0, CHIPS[0][k], CHIPS[1][k]) + 4 * b
            outs[k][b] = take(step, core)
            step = jnp.where(core == 0, CHIPS[1][k], CHIPS[0][k]) + 4 * b
            other_ref[2 * k + b] = take(step, 1 - core)


def cores_kernel(p0, p1, p2, p3, other_ref, o0, o1, o2, o3):
    for k, (part, out) in enumerate(zip((p0, p1, p2, p3), (o0, o1, o2, o3))):
        for b in range(2):
            out[b] = (part[b].astype(f32) + other_ref[2 * k + b].astype(f32)).astype(bf16)


def chips_kernel(o0, o1, o2, o3, u0, u1):
    for b, out in enumerate((u0, u1)):
        total = o0[b].astype(f32) + o1[b].astype(f32) + o2[b].astype(f32) + o3[b].astype(f32)
        out[...] = total.astype(bf16)


def last_kernel(u0, u1, out_ref):
    out_ref[...] = u0[...].astype(f32) + u1[...].astype(f32)


def references_kernel(gs_ref, fc_ref, out_ref):
    for h in range(HEADS):
        heads = gs_ref[h * P_SIZE : (h + 1) * P_SIZE, :]
        out_ref[h] = lax.dot_general(fc_ref[...], heads, NT, preferred_element_type=f32)


def along_z(value, k):
    pairs = []
    for z in range(DEPTH):
        for core in range(2):
            pairs.append((2 * z + core, 2 * ((z + CHIPS[core][k]) % DEPTH) + core))
    return lax.ppermute(value, ("z", "core"), pairs)


def to_place(value, b):
    pairs = []
    for z in range(DEPTH):
        for core in range(2):
            for j in range(BLOCKS):
                block = 2 * ((z + 4 * b) % DEPTH) + core
                pairs.append(((2 * z + core) * BLOCKS + j, j * BLOCKS + block))
    return lax.ppermute(value, ("z", "core", "y", "x"), pairs)


def spread_logits(value):
    pairs = [((s + j) % BLOCKS * BLOCKS + j, s * BLOCKS + j) for s in range(BLOCKS) for j in range(BLOCKS)]
    return lax.ppermute(value, ("z", "core", "y", "x"), pairs)


def local(features, references, classifier, lengths, labels):
    batch, rows, width = features.shape
    part = width // BLOCKS
    everything = BLOCKS * rows
    score_scale = temper / math.sqrt(width)
    feats = features.reshape(rows, width)
    refs = references.reshape(REFS, width)
    kind = jax.ShapeDtypeStruct

    steps = 4
    half = part // 2
    mixed, refs_part = call(
        functools.partial(scores_kernel, score_scale), "scores",
        [kind((BLOCKS, half + REFS, rows), bf16), kind((REFS, part), bf16)], [HBM, HBM],
        scratch=[
            pltpu.VMEM((rows, width), bf16), pltpu.VMEM((steps, REFS // steps, width), bf16),
            pltpu.VMEM((width, rows), bf16), pltpu.SemaphoreType.DMA((steps + 1,)),
        ],
    )(feats, refs)
    mixed = exchange(mixed)
    e = call(peel_kernel, "peel", kind((BLOCKS, half, rows), bf16), 1)(mixed)
    other = lax.ppermute(e, "core", [(0, 1), (1, 0)])
    weights = jnp.pad(jnp.transpose(classifier, (0, 2, 1)), ((0, 0), (0, PAD - CLASSES), (0, 0)))
    weights = weights.reshape(HEADS * PAD, part)

    scales = kind((ITERS * HEADS * BLOCKS, rows), f32)
    rs, rt, col, plan = call(
        sinkhorn_kernel, "sinkhorn",
        [scales, scales, kind((ITERS, REFS, rows), f32), kind((REFS, everything), bf16)], [VMEM, SMEM],
    )(mixed, lengths)
    products, raw, cols = call(
        forward_kernel, "forward",
        [kind((BLOCKS, T_ROWS + M_ROWS, rows), bf16), kind((REFS, part), f32), kind((part, everything), bf16)], 4,
        scratch=[pltpu.VMEM((T_ROWS, part), bf16)],
    )(e, other, weights, plan)
    t, moments, logit_part = call(
        functools.partial(sum_kernel, width), "sum",
        [kind((T_ROWS, rows), bf16), kind((HEADS * PAD, P_SIZE), f32), kind((PAD, P_SIZE), f32)], 1,
    )(exchange(products))
    ts = exchange(
        call(row_kernel, "row", kind((BLOCKS, T_ROWS + PAD, rows), bf16), 2)(t, spread_logits(logit_part))
    )
    pair = kind((2, part, rows), bf16)
    logits, grad_scores, *mine, away = call(
        functools.partial(backward_kernel, width, score_scale), "backward",
        [kind((1, PAD), f32), kind((REFS, everything), bf16)] + [pair] * 4 + [kind((DEPTH, part, rows), bf16)],
        [VMEM] * 10 + [SMEM],
        scratch=[
            pltpu.VMEM((ITERS, P_SIZE, rows), f32),
            pltpu.VMEM((ITERS * HEADS * BLOCKS, rows), f32),
            pltpu.VMEM((HEADS * BLOCKS, rows), f32),
            pltpu.VMEM((2 * REFS, part), bf16),
            pltpu.VMEM((2 * REFS, everything), bf16),
            pltpu.VMEM((part, everything), f32),
        ],
    )(mixed, ts, rs, rt, col, moments, raw, weights, plan, refs_part, labels)
    away = lax.ppermute(away, "core", [(0, 1), (1, 0)])
    o = call(cores_kernel, "cores", [pair] * 4, 5)(*mine, away)
    o = [o[0]] + [along_z(o[k], k) for k in (1, 2, 3)]
    u = call(chips_kernel, "chips", [kind((part, rows), bf16)] * 2, 4)(*o)
    u = [to_place(u[b], b) for b in range(2)]
    grad_features = call(last_kernel, "last", kind((part, rows), f32), 2)(*u)
    grad_references = call(references_kernel, "references", kind((HEADS, part, rows), f32), 2, flops=2 * REFS * part * everything)(
        grad_scores, cols
    )
    return (
        logits[:, :CLASSES],
        jnp.transpose(grad_features).reshape(batch, rows, part),
        jnp.transpose(grad_references, (0, 2, 1)),
    )


def solution(mesh):
    grid = Mesh(mesh.devices.reshape(DEPTH, 2, SIDE, SIDE), ("z", "core", "y", "x"))
    section, seq = ("z", "core"), ("y", "x")
    in_specs = (P(None, seq, None), P(section, None, None), P(section, seq, None), P(), P())
    out_specs = (P(), P(None, seq, section), P(section, None, seq))
    return jax.shard_map(local, mesh=grid, in_specs=in_specs, out_specs=out_specs, check_vma=False)
```

time: 156 us -> 149 us (0.955); the launches traced: 155 us -> 146 us
  blocking collectives: 14.9 us -> 51.7 us
  starting transfers between devices: 60.7 us -> 30.1 us
  waiting for transfers between devices: 58.8 us -> 37.6 us
  Pallas kernels: 13.4 us -> 16.5 us
  local copies, waits for them, and re-layouts: 5.38 us -> 8.35 us
    all_to_all x1 -> x2, blocking collectives: 14.9 us -> 51.7 us  [exchange(): return lax.all_to_all(value, ('y', 'x'), 0, 0)]
    ppermute x23 -> x2, starting transfers between devices: 45.2 us -> 8.75 us  [the longest x1 8.65 us: spread_logits(): return lax.ppermute(value, ('z', 'core', 'y', 'x'), pairs)]
    ppermute x23 -> x2, waiting for transfers between devices: 36.5 us -> 1.35 us  [the longest x1 1.34 us: spread_logits(): return lax.ppermute(value, ('z', 'core', 'y', 'x'), pairs)]
    all_to_all x0 -> x1, waiting for transfers between devices: none -> 14.4 us  [exchange(): return lax.all_to_all(value, ('y', 'x'), 0, 0)]
    all_to_all x0 -> x1, starting transfers between devices: none -> 6.77 us  [exchange(): return lax.all_to_all(value, ('y', 'x'), 0, 0)]
    pallas_call x7 -> x8, Pallas kernels: 6.47 us -> 10.9 us  [the longest x1 4.91 us: local(): call(functools.partial(scores_kernel, score_scale), 'scores', [kind((BLOC...]
    unnamed x9 -> x25, local copies, waits for them, and re-layouts: 4.74 us -> 8.34 us
  transfers between devices with their start and end apart: 29 -> 9, of which waited for: 21 -> 7; matrix products, arithmetic and copies ran while one was open for 1% -> 0% of each run, Pallas kernels for 1% -> 2%
where the time goes in v5:
time: 149 us; the launch traced here: 146 us
  blocking collectives  51.7 us (35%)
  waiting for transfers between devices  37.6 us (25%)
  starting transfers between devices  30.1 us (20%)
  Pallas kernels  16.5 us (11%)
  local copies, waits for them, and re-layouts  8.35 us (6%)
  between operations  2.08 us (1%)
    all_to_all x2, blocking collectives, exchange(): return lax.all_to_all(value, ('y', 'x'), 0, 0)  51.7 us
    all_to_all x1, waiting for transfers between devices, exchange(): return lax.all_to_all(value, ('y', 'x'), 0, 0)  14.4 us
    ppermute x2, waiting for transfers between devices, to_place(): return lax.ppermute(value, ('z', 'core', 'y', 'x'), pairs)  11.8 us
    ppermute x2, starting transfers between devices, to_place(): return lax.ppermute(value, ('z', 'core', 'y', 'x'), pairs)  10.6 us
    ppermute x1, starting transfers between devices, spread_logits(): return lax.ppermute(value, ('z', 'core', 'y', 'x'), pairs)  8.65 us
    unnamed x25, local copies, waits for them, and re-layouts  8.34 us
    ppermute x3, waiting for transfers between devices, along_z(): return lax.ppermute(value, ('z', 'core'), pairs)  7.97 us
    all_to_all x1, starting transfers between devices, exchange(): return lax.all_to_all(value, ('y', 'x'), 0, 0)  6.77 us
  transfers between devices with their start and end apart: 9, of which 7 were waited for; matrix products, arithmetic and copies ran while one was open for 0% of the time, Pallas kernels for 2%

profile of v5, /device:TPU:12, one launch (start us, length us, event | category | flops | bytes accessed | tf_op | source)
XLA Modules:
  0.0 146.3 jit_solution(16471223765786460512)
XLA Ops:
  0.6 1.7 %copy-done.3 = bf16[2,128,5120]{2,1,0:T(8,128)(2,1)S(1)} copy-done((bf16[2,128,5120]{2,1,0:T(8,128)(2,1)S(1)}, bf16[2,128,5120]{2,1,0:T(8,128)(2,1)}, u32[]{:S(2)}) %copy-start.3) | copy-done | bytes 2621464
  2.4 1.3 copy-done.6
  3.7 4.9 %scores.1 = (bf16[16,416,128]{2,1,0:T(8,128)(2,1)S(1)}, bf16[256,320]{1,0:T(8,128)(2,1)S(1)}) custom-call(bf16[128,5120]{1,0:T(8,128)(2,1)S(1)} %bitcast.10, bf16[256,5120]{1,0:T(8,128)(2,1)S(1)} %bitcast.9), custom_call_target="tpu_custom_call" | custom-call | tf_op jit(solution)/shard_map/scores/pallas_call | solution.py:357
  8.6 28.2 %all_to_all.15.in_ref.q_ref = bf16[16,416,128]{2,1,0:T(8,128)(2,1)S(1)} all-to-all(bf16[16,416,128]{2,1,0:T(8,128)(2,1)S(1)} %get-tuple-element.28), channel_id=1, replica_groups=mesh['z'=8,'core'=2,'y'=4,'x'=4] {'y','x'}, dimensions={0} | all-to-all | bytes 3407872 | tf_op jit(solution)/shard_map/all_to_all | solution.py:58
  36.9 0.1 collective-permute-start
  37.7 1.7 %sinkhorn.1 = (f32[96,128]{1,0:T(8,128)S(1)}, f32[96,128]{1,0:T(8,128)S(1)}, f32[3,256,128]{2,1,0:T(8,128)S(1)}, bf16[256,2048]{1,0:T(8,128)(2,1)S(1)}) custom-call(bf16[16,416,128]{2,1,0:T(8,128)(2,1)S(1)} %all_to_all.15.in_ref.q_ref, s32[1]{0:T(128)S(6)} %copy.10.len_ref), custom_call_target="tpu_custom_call" | custom-call | tf_op jit(solution)/shard_map/sinkhorn/pallas_call | solution.py:372
  39.4 1.7 %forward.1 = (bf16[16,320,128]{2,1,0:T(8,128)(2,1)S(1)}, f32[256,320]{1,0:T(8,128)S(1)}, bf16[320,2048]{1,0:T(8,128)(2,1)S(1)}) custom-call(bf16[16,160,128]{2,1,0:T(8,128)(2,1)S(1)} %peel.1.e_ref, bf16[16,160,128]{2,1,0:T(8,128)(2,1)S(1)} %collective-permute-done.other_ref, bf16[32,320]{1,0:T(8,128)(2,1)S(1)} %bitcast.11, ...), custom_call_target="tpu_custom_call" | custom-call | tf_op jit(solution)/shard_map/forward/pallas_call | solution.py:376
  41.1 1.1 copy-done.4
  42.2 23.5 %all_to_all.16.in_ref = bf16[16,320,128]{2,1,0:T(8,128)(2,1)S(1)} all-to-all(bf16[16,320,128]{2,1,0:T(8,128)(2,1)S(1)} %get-tuple-element.30), channel_id=1, replica_groups=mesh['z'=8,'core'=2,'y'=4,'x'=4] {'y','x'}, dimensions={0} | all-to-all | bytes 2621440 | tf_op jit(solution)/shard_map/all_to_all | solution.py:58
  65.7 0.2 sum.1
  65.8 8.7 %collective-permute-start.1 = (f32[16,128]{1,0:T(8,128)S(1)}, f32[16,128]{1,0:T(8,128)S(1)}, u32[]{:S(2)}, u32[]{:S(2)}) collective-permute-start(f32[16,128]{1,0:T(8,128)S(1)} %get-tuple-element.32), channel_id=1, source_target_pairs={{0,0},{17,1},{34,2},{51,3},{68,4},{85,5},{102,6},{119,7},{136,8},{... | collective-permute-start | bytes 24584 | tf_op jit(solution)/shard_map/ppermute | solution.py:343
  74.5 1.3 collective-permute-done.1.logit_ref
  75.9 0.2 row.1
  76.0 1.0 copy-done
  77.0 6.8 %all-to-all-start.2 = ((bf16[16,304,128]{2,1,0:T(8,128)(2,1)}), bf16[16,304,128]{2,1,0:T(8,128)(2,1)S(1)}, u32[]{:S(2)}, u32[]{:S(2)}) async-start(bf16[16,304,128]{2,1,0:T(8,128)(2,1)} %copy-done), calls=%async_computation.2 | async-start | bytes 2490368 | tf_op jit(solution)/shard_map/all_to_all | solution.py:58
  84.5 14.4 %all-to-all-done.2.t_ref = bf16[16,304,128]{2,1,0:T(8,128)(2,1)S(1)} async-done(((bf16[16,304,128]{2,1,0:T(8,128)(2,1)}), bf16[16,304,128]{2,1,0:T(8,128)(2,1)S(1)}, u32[]{:S(2)}, u32[]{:S(2)}) %all-to-all-start.2) | async-done | bytes 1245216 | tf_op jit(solution)/shard_map/all_to_all | solution.py:58
  98.9 1.2 copy-done.2
  100.1 1.0 copy-done.8
  101.1 0.9 copy-done.10
  102.0 5.3 %backward.1 = (f32[1,16]{1,0:T(1,128)}, bf16[256,2048]{1,0:T(8,128)(2,1)S(1)}, bf16[2,320,128]{2,1,0:T(8,128)(2,1)S(1)}, bf16[2,320,128]{2,1,0:T(8,128)(2,1)S(1)...) custom-call(bf16[16,416,128]{2,1,0:T(8,128)(2,1)S(1)} %all_to_all.15.in_ref.q, ...), custom_call_target="tpu_custom_call" | custom-call | tf_op jit(solution)/shard_map/backward/pallas_call | solution.py:389
  107.4 2.1 %collective-permute-done.2.other_ref = bf16[8,320,128]{2,1,0:T(8,128)(2,1)S(1)} collective-permute-done((bf16[8,320,128]{2,1,0:T(8,128)(2,1)S(1)}, bf16[8,320,128]{2,1,0:T(8,128)(2,1)S(1)}, u32[]{:S(2)}, u32[]{:S(2)}) %collective-permute-start.2) | collective-permute-done | bytes 655392 | tf_op jit(solution)/shard_map/ppermute | solution.py:402
  109.4 0.2 cores.1
  109.6 1.2 collective-permute-start.3
  110.8 2.8 %collective-permute-start.4 = (bf16[2,320,128]{2,1,0:T(8,128)(2,1)S(1)}, bf16[2,320,128]{2,1,0:T(8,128)(2,1)S(1)}, u32[]{:S(2)}, u32[]{:S(2)}) collective-permute-start(bf16[2,320,128]{2,1,0:T(8,128)(2,1)S(1)} %get-tuple-element.47), channel_id=1, source_target_pairs={{0,224},{16,240},{32,0},{48,16},{64,32},{80,48},{96,64},{112,80},{... | collective-permute-start | bytes 491528 | tf_op jit(solution)/shard_map/ppermute | solution.py:328
  113.5 4.4 %collective-permute-done.3.o1 = bf16[2,320,128]{2,1,0:T(8,128)(2,1)S(1)} collective-permute-done((bf16[2,320,128]{2,1,0:T(8,128)(2,1)S(1)}, bf16[2,320,128]{2,1,0:T(8,128)(2,1)S(1)}, u32[]{:S(2)}, u32[]{:S(2)}) %collective-permute-start.3) | collective-permute-done | bytes 163872 | tf_op jit(solution)/shard_map/ppermute | solution.py:328
  117.9 0.7 collective-permute-done.4.o2
  118.6 2.9 %collective-permute-done.5.o3 = bf16[2,320,128]{2,1,0:T(8,128)(2,1)S(1)} collective-permute-done((bf16[2,320,128]{2,1,0:T(8,128)(2,1)S(1)}, bf16[2,320,128]{2,1,0:T(8,128)(2,1)S(1)}, u32[]{:S(2)}, u32[]{:S(2)}) %collective-permute-start.5) | collective-permute-done | bytes 163872 | tf_op jit(solution)/shard_map/ppermute | solution.py:328
  121.6 9.0 %collective-permute-start.6 = (bf16[320,128]{1,0:T(8,128)(2,1)S(1)}, bf16[320,128]{1,0:T(8,128)(2,1)S(1)}, u32[]{:S(2)}, u32[]{:S(2)}) collective-permute-start(bf16[320,128]{1,0:T(8,128)(2,1)S(1)} %get-tuple-element.49), channel_id=1, source_target_pairs={{0,0},{1,16},{2,32},{3,48},{4,64},{5,80},{6,96},{7,112},{8,128},{9... | collective-permute-start | bytes 245768 | tf_op jit(solution)/shard_map/ppermute | solution.py:338
  130.6 1.6 %collective-permute-start.7 = (bf16[320,128]{1,0:T(8,128)(2,1)S(1)}, bf16[320,128]{1,0:T(8,128)(2,1)S(1)}, u32[]{:S(2)}, u32[]{:S(2)}) collective-permute-start(bf16[320,128]{1,0:T(8,128)(2,1)S(1)} %get-tuple-element.50), channel_id=1, source_target_pairs={{0,8},{1,24},{2,40},{3,56},{4,72},{5,88},{6,104},{7,120},{8,136},{... | collective-permute-start | bytes 245768 | tf_op jit(solution)/shard_map/ppermute | solution.py:338
  132.2 1.6 %references.1 = f32[2,320,128]{2,1,0:T(8,128)} custom-call(bf16[256,2048]{1,0:T(8,128)(2,1)S(1)} %get-tuple-element.51.gs_ref, bf16[320,2048]{1,0:T(8,128)(2,1)S(1)} %copy-done.5), custom_call_target="tpu_custom_call" | custom-call | flops 335544320 | bytes 1048576 | tf_op jit(solution)/shard_map/references/pallas_call | solution.py:408
  133.8 11.8 %collective-permute-done.7.u1 = bf16[320,128]{1,0:T(8,128)(2,1)S(1)} collective-permute-done((bf16[320,128]{1,0:T(8,128)(2,1)S(1)}, bf16[320,128]{1,0:T(8,128)(2,1)S(1)}, u32[]{:S(2)}, u32[]{:S(2)}) %collective-permute-start.7) | collective-permute-done | bytes 81952 | tf_op jit(solution)/shard_map/ppermute | solution.py:338
  145.6 0.7 last.1
  (25 shorter events, 0.2 us)
Async XLA Ops:
  0.6 1.7 %copy-start.3 = (bf16[2,128,5120]{2,1,0:T(8,128)(2,1)S(1)}, bf16[2,128,5120]{2,1,0:T(8,128)(2,1)}, u32[]{:S(2)}) copy-start(bf16[2,128,5120]{2,1,0:T(8,128)(2,1)} %param.6) | copy-start | bytes 7864324
  2.4 1.3 copy-start.6
  8.6 28.2 %copy-start.9 = (bf16[256,320]{1,0:T(8,128)(2,1)}, bf16[256,320]{1,0:T(8,128)(2,1)S(1)}, u32[]{:S(2)}) copy-start(bf16[256,320]{1,0:T(8,128)(2,1)S(1)} %get-tuple-element.38.refs_ref) | copy-start | bytes 491524
  36.8 0.8 copy-start.11
  36.9 2.5 %collective-permute-start = (bf16[16,160,128]{2,1,0:T(8,128)(2,1)S(1)}, bf16[16,160,128]{2,1,0:T(8,128)(2,1)S(1)}, u32[]{:S(2)}, u32[]{:S(2)}) collective-permute-start(bf16[16,160,128]{2,1,0:T(8,128)(2,1)S(1)} %peel.1.e_ref), channel_id=1, source_target_pairs={{0,16},{16,0},{1,17},{17,1},{2,18},{18,2},{3,19},{19,3},{4,20},{20... | collective-permute-start | bytes 1966088 | tf_op jit(solution)/shard_map/ppermute | solution.py:367
  39.4 26.3 %copy-start.1 = (bf16[256,2048]{1,0:T(8,128)(2,1)}, bf16[256,2048]{1,0:T(8,128)(2,1)S(1)}, u32[]{:S(2)}) copy-start(bf16[256,2048]{1,0:T(8,128)(2,1)S(1)} %get-tuple-element.29.plan_ref) | copy-start | bytes 3145732
  41.1 1.1 copy-start.4
  42.2 23.5 %copy-start.7 = (f32[256,320]{1,0:T(8,128)}, f32[256,320]{1,0:T(8,128)S(1)}, u32[]{:S(2)}) copy-start(f32[256,320]{1,0:T(8,128)S(1)} %get-tuple-element.37.raw_ref) | copy-start | bytes 983044
  65.8 10.0 %collective-permute-start.1 = (f32[16,128]{1,0:T(8,128)S(1)}, f32[16,128]{1,0:T(8,128)S(1)}, u32[]{:S(2)}, u32[]{:S(2)}) collective-permute-start(f32[16,128]{1,0:T(8,128)S(1)} %get-tuple-element.32), channel_id=1, source_target_pairs={{0,0},{17,1},{34,2},{51,3},{68,4},{85,5},{102,6},{119,7},{136,8},{... | collective-permute-start | bytes 24584 | tf_op jit(solution)/shard_map/ppermute | solution.py:343
  76.0 1.0 copy-start
  77.0 21.8 %all-to-all-start.2 = ((bf16[16,304,128]{2,1,0:T(8,128)(2,1)}), bf16[16,304,128]{2,1,0:T(8,128)(2,1)S(1)}, u32[]{:S(2)}, u32[]{:S(2)}) async-start(bf16[16,304,128]{2,1,0:T(8,128)(2,1)} %copy-done), calls=%async_computation.2 | async-start | bytes 2490368 | tf_op jit(solution)/shard_map/all_to_all | solution.py:58
  98.9 1.2 copy-start.2
  100.1 1.0 copy-start.8
  101.1 0.9 copy-start.10
  107.3 24.9 %copy-start.5 = (bf16[320,2048]{1,0:T(8,128)(2,1)S(1)}, bf16[320,2048]{1,0:T(8,128)(2,1)}, u32[]{:S(2)}) copy-start(bf16[320,2048]{1,0:T(8,128)(2,1)} %copy-done.4) | copy-start | bytes 3932164
  107.3 2.1 %collective-permute-start.2 = (bf16[8,320,128]{2,1,0:T(8,128)(2,1)S(1)}, bf16[8,320,128]{2,1,0:T(8,128)(2,1)S(1)}, u32[]{:S(2)}, u32[]{:S(2)}) collective-permute-start(bf16[8,320,128]{2,1,0:T(8,128)(2,1)S(1)} %get-tuple-element.44), channel_id=1, source_target_pairs={{0,16},{16,0},{1,17},{17,1},{2,18},{18,2},{3,19},{19,3},{4,20},{20... | collective-permute-start | bytes 1966088 | tf_op jit(solution)/shard_map/ppermute | solution.py:402
  109.6 8.3 %collective-permute-start.3 = (bf16[2,320,128]{2,1,0:T(8,128)(2,1)S(1)}, bf16[2,320,128]{2,1,0:T(8,128)(2,1)S(1)}, u32[]{:S(2)}, u32[]{:S(2)}) collective-permute-start(bf16[2,320,128]{2,1,0:T(8,128)(2,1)S(1)} %get-tuple-element.46), channel_id=1, source_target_pairs={{0,32},{16,48},{32,64},{48,80},{64,96},{80,112},{96,128},{112,144}... | collective-permute-start | bytes 491528 | tf_op jit(solution)/shard_map/ppermute | solution.py:328
  110.8 7.9 %collective-permute-start.4 = (bf16[2,320,128]{2,1,0:T(8,128)(2,1)S(1)}, bf16[2,320,128]{2,1,0:T(8,128)(2,1)S(1)}, u32[]{:S(2)}, u32[]{:S(2)}) collective-permute-start(bf16[2,320,128]{2,1,0:T(8,128)(2,1)S(1)} %get-tuple-element.47), channel_id=1, source_target_pairs={{0,224},{16,240},{32,0},{48,16},{64,32},{80,48},{96,64},{112,80},{... | collective-permute-start | bytes 491528 | tf_op jit(solution)/shard_map/ppermute | solution.py:328
  113.5 8.0 %collective-permute-start.5 = (bf16[2,320,128]{2,1,0:T(8,128)(2,1)S(1)}, bf16[2,320,128]{2,1,0:T(8,128)(2,1)S(1)}, u32[]{:S(2)}, u32[]{:S(2)}) collective-permute-start(bf16[2,320,128]{2,1,0:T(8,128)(2,1)S(1)} %get-tuple-element.48), channel_id=1, source_target_pairs={{0,64},{16,208},{32,96},{48,240},{64,128},{80,16},{96,160},{112,48... | collective-permute-start | bytes 491528 | tf_op jit(solution)/shard_map/ppermute | solution.py:328
  121.6 12.2 %collective-permute-start.6 = (bf16[320,128]{1,0:T(8,128)(2,1)S(1)}, bf16[320,128]{1,0:T(8,128)(2,1)S(1)}, u32[]{:S(2)}, u32[]{:S(2)}) collective-permute-start(bf16[320,128]{1,0:T(8,128)(2,1)S(1)} %get-tuple-element.49), channel_id=1, source_target_pairs={{0,0},{1,16},{2,32},{3,48},{4,64},{5,80},{6,96},{7,112},{8,128},{9... | collective-permute-start | bytes 245768 | tf_op jit(solution)/shard_map/ppermute | solution.py:338
  130.6 15.0 %collective-permute-start.7 = (bf16[320,128]{1,0:T(8,128)(2,1)S(1)}, bf16[320,128]{1,0:T(8,128)(2,1)S(1)}, u32[]{:S(2)}, u32[]{:S(2)}) collective-permute-start(bf16[320,128]{1,0:T(8,128)(2,1)S(1)} %get-tuple-element.50), channel_id=1, source_target_pairs={{0,8},{1,24},{2,40},{3,56},{4,72},{5,88},{6,104},{7,120},{8,136},{... | collective-permute-start | bytes 245768 | tf_op jit(solution)/shard_map/ppermute | solution.py:338

commit v6 on v5

--- a/solution.py
+++ b/solution.py
@@ -33,10 +33,7 @@
 TN = (((0,), (0,)), ((), ()))
 
 
-HBM = pl.BlockSpec(memory_space=pltpu.HBM)
-
-
-def call(kernel, name, shapes, specs, scratch=(), flops=0):
+def call(kernel, name, shapes, specs, scratch=(), flops=0, mib=8):
     many = isinstance(shapes, list)
     return pl.pallas_call(
         kernel,
@@ -44,7 +41,7 @@
         in_specs=[VMEM] * specs if isinstance(specs, int) else specs,
         out_specs=[VMEM] * len(shapes) if many else VMEM,
         scratch_shapes=list(scratch),
-        compiler_params=pltpu.CompilerParams(vmem_limit_bytes=40 * 1024 * 1024),
+        compiler_params=pltpu.CompilerParams(vmem_limit_bytes=mib * 1024 * 1024),
         cost_estimate=pl.CostEstimate(flops=flops, bytes_accessed=1 << 20, transcendentals=0) if flops else None,
         name=name,
     )
@@ -58,33 +55,24 @@
     return lax.all_to_all(value, ("y", "x"), 0, 0)
 
 
-def scores_kernel(scale, f_hbm, r_hbm, out_ref, part_ref, f_ref, r_ref, turned_ref, sems):
-    half = out_ref.shape[1] - REFS
+def split_kernel(f_ref, out_ref, turned_ref):
+    half = out_ref.shape[1]
     part = 2 * half
-    steps = r_ref.shape[0]
-    rows = r_ref.shape[1]
-    load = pltpu.make_async_copy(f_hbm, f_ref, sems.at[steps])
-    load.start()
-    loads = []
-    for k in range(steps):
-        loads.append(pltpu.make_async_copy(r_hbm.at[pl.ds(k * rows, rows)], r_ref.at[k], sems.at[k]))
-        loads[k].start()
-    load.wait()
     for j in range(BLOCKS // 2):
         where = slice(2 * part * j, 2 * part * (j + 1))
         turned_ref[where, :] = jnp.transpose(f_ref[:, where])
     core = lax.axis_index("core")
     for j in range(BLOCKS):
-        out_ref[j, :half, :] = turned_ref[pl.ds(pl.multiple_of(part * j + half * core, half), half), :]
-    place = lax.axis_index("y") * SIDE + lax.axis_index("x")
-    for k in range(steps):
-        loads[k].wait()
-        scores = lax.dot_general(r_ref[k], f_ref[...], NT, preferred_element_type=f32)
-        kernel = jnp.exp(scores * scale).astype(bf16)
-        for j in range(BLOCKS):
-            out_ref[j, half + k * rows : half + (k + 1) * rows, :] = kernel
-        pair = r_ref[k, :, pl.ds(pl.multiple_of((place // 2) * (2 * part), 2 * part), 2 * part)]
-        part_ref[k * rows : (k + 1) * rows, :] = jnp.where(lax.rem(place, 2) == 0, pair[:, :part], pair[:, part:])
+        out_ref[j] = turned_ref[pl.ds(pl.multiple_of(part * j + half * core, half), half), :]
+
+
+def scores_kernel(scale, f_ref, r_ref, half_ref, out_ref):
+    half = half_ref.shape[1]
+    scores = lax.dot_general(r_ref[...], f_ref[...], NT, preferred_element_type=f32)
+    kernel = jnp.exp(scores * scale).astype(bf16)
+    for j in range(BLOCKS):
+        out_ref[j, :half, :] = half_ref[j]
+        out_ref[j, half:, :] = kernel
 
 
 def peel_kernel(in_ref, out_ref):
@@ -93,6 +81,15 @@
         out_ref[j] = in_ref[j, :half, :]
 
 
+def put_columns(mixed_ref, other_ref, out_ref):
+    core = lax.axis_index("core")
+    half, rows = other_ref.shape[1:]
+    for j in range(BLOCKS):
+        here = slice(j * rows, (j + 1) * rows)
+        out_ref[pl.ds(pl.multiple_of(core * half, half), half), here] = mixed_ref[j, :half, :]
+        out_ref[pl.ds(pl.multiple_of((1 - core) * half, half), half), here] = other_ref[j]
+
+
 def diagonal():
     square = (P_SIZE, P_SIZE)
     return lax.broadcasted_iota(jnp.int32, square, 0) == lax.broadcasted_iota(jnp.int32, square, 1)
@@ -106,7 +103,7 @@
     return jnp.sum(jnp.where(diagonal(), row, 0.0), axis=1, keepdims=True)
 
 
-def sinkhorn_kernel(q_ref, len_ref, rs_ref, rt_ref, col_ref, plan_ref):
+def sinkhorn_kernel(q_ref, len_ref, label_ref, rs_ref, rt_ref, col_ref, plan_ref):
     length = len_ref[0]
     rows = q_ref.shape[2]
     low = q_ref.shape[1] - REFS
@@ -137,13 +134,9 @@
             plan_ref[here, s * rows : (s + 1) * rows] = plan.astype(bf16)
 
 
-def forward_kernel(e_ref, other_ref, wt_ref, plan_ref, out_ref, raw_ref, fc_ref, ext_ref):
-    core = lax.axis_index("core")
-    half, rows = e_ref.shape[1:]
-    for j in range(BLOCKS):
-        here = slice(j * rows, (j + 1) * rows)
-        fc_ref[pl.ds(pl.multiple_of(core * half, half), half), here] = e_ref[j]
-        fc_ref[pl.ds(pl.multiple_of((1 - core) * half, half), half), here] = other_ref[j]
+def forward_kernel(mixed_ref, other_ref, wt_ref, plan_ref, out_ref, raw_ref, fc_ref, ext_ref):
+    rows = other_ref.shape[2]
+    put_columns(mixed_ref, other_ref, fc_ref)
     raw = float(P_SIZE) * lax.dot_general(plan_ref[...], fc_ref[...], NT, preferred_element_type=f32)
     raw_ref[...] = raw
     ext_ref[:REFS, :] = raw.astype(bf16)
@@ -207,10 +200,16 @@
     return jnp.broadcast_to(total[:, :1] + total[:, P_SIZE // 2 : P_SIZE // 2 + 1], total.shape)
 
 
+def scales_of(grads, moments, width):
+    inverse = inverse_rms(moments, width)
+    dual = inverse * jnp.sum(grads * moments, axis=0, keepdims=True) / (float(P_SIZE) * width)
+    return to_column(inverse), to_column(inverse * dual)
+
+
 def backward_kernel(
     width, score_scale,
-    q_ref, t_ref, rs_ref, rt_ref, col_ref, m_ref, raw_ref, wt_ref, plan_ref, refs_ref, label_ref,
-    logit_ref, gs_ref, p0, p1, p2, p3, other_ref, gt_ref, grs_ref, u_ref, left_ref, right_ref, wide_ref,
+    q_ref, t_ref, rs_ref, rt_ref, col_ref, m_ref, label_ref,
+    logit_ref, grads_ref, gs_ref, gt_ref, grs_ref, u_ref,
 ):
     rows = q_ref.shape[2]
     base = q_ref.shape[1] - REFS
@@ -223,18 +222,10 @@
     probs = exps / jnp.sum(exps, axis=0, keepdims=True)
     grads = loss_scale * (probs - (kind == label_ref[0]).astype(f32))
     grads = jnp.where(kind < CLASSES, grads, 0.0)
-    left_ref[:REFS, :] = refs_ref[...]
-    right_ref[REFS:, :] = plan_ref[...]
+    grads_ref[...] = grads
     for h in range(HEADS):
         here = slice(h * P_SIZE, (h + 1) * P_SIZE)
-        moments = m_ref[h * PAD : (h + 1) * PAD, :]
-        inverse_row = inverse_rms(moments, width)
-        dual_row = inverse_row * jnp.sum(grads * moments, axis=0, keepdims=True) / (size * width)
-        inverse = to_column(inverse_row)
-        pull = to_column(inverse_row * dual_row)
-        normed = jnp.sum(grads[:, :1] * wt_ref[h * PAD : (h + 1) * PAD, :].astype(f32), axis=0, keepdims=True) / size
-        grad_raw = (inverse * (normed - raw_ref[here, :] * pull)).astype(bf16)
-        left_ref[REFS + h * P_SIZE : REFS + (h + 1) * P_SIZE, :] = (size * grad_raw.astype(f32)).astype(bf16)
+        inverse, pull = scales_of(grads, m_ref[h * PAD : (h + 1) * PAD, :], width)
         first = jnp.broadcast_to(size * inverse, (P_SIZE, rows))
         second = first * pull
 
@@ -281,14 +272,35 @@
                     total = total + row(grs_ref, t, s) * col_ref[t - 1, here, :]
                 else:
                     total = total + row(grs_ref, t, s)
-            right_ref[here, s * rows : (s + 1) * rows] = (score_scale * total * load(s)).astype(bf16)
-    gs_ref[...] = right_ref[:REFS, :]
+            gs_ref[here, s * rows : (s + 1) * rows] = (score_scale * total * load(s)).astype(bf16)
+
+
+def parts_kernel(
+    width, gs_ref, grads_ref, m_ref, wt_ref, raw_ref, plan_ref, refs_ref,
+    p0, p1, p2, p3, other_ref, left_ref, right_ref, wide_ref,
+):
+    rows = other_ref.shape[2]
+    part = raw_ref.shape[1]
+    size = float(P_SIZE)
+    grads = grads_ref[...]
+    place = lax.axis_index("y") * SIDE + lax.axis_index("x")
+    pair = refs_ref[:, pl.ds(pl.multiple_of((place // 2) * (2 * part), 2 * part), 2 * part)]
+    left_ref[:REFS, :] = jnp.where(lax.rem(place, 2) == 0, pair[:, :part], pair[:, part:])
+    for h in range(HEADS):
+        here = slice(h * P_SIZE, (h + 1) * P_SIZE)
+        inverse, pull = scales_of(grads, m_ref[h * PAD : (h + 1) * PAD, :], width)
+        normed = jnp.sum(grads[:, :1] * wt_ref[h * PAD : (h + 1) * PAD, :].astype(f32), axis=0, keepdims=True) / size
+        grad_raw = (inverse * (normed - raw_ref[here, :] * pull)).astype(bf16)
+        left_ref[REFS + h * P_SIZE : REFS + (h + 1) * P_SIZE, :] = (size * grad_raw.astype(f32)).astype(bf16)
+    right_ref[:REFS, :] = gs_ref[...]
+    right_ref[REFS:, :] = plan_ref[...]
     wide_ref[...] = lax.dot_general(left_ref[...], right_ref[...], TN, preferred_element_type=f32)
     core, z = lax.axis_index("core"), lax.axis_index("z")
     outs = (p0, p1, p2, p3)
 
     def take(step, which):
-        return wide_ref[:, lanes(2 * lax.rem(z + step, DEPTH) + which, rows)].astype(bf16)
+        block = lax.bitwise_xor(2 * lax.rem(z + step, DEPTH) + which, place)
+        return wide_ref[:, lanes(block, rows)].astype(bf16)
 
     for k in range(4):
         for b in range(2):
@@ -314,7 +326,8 @@
     out_ref[...] = u0[...].astype(f32) + u1[...].astype(f32)
 
 
-def references_kernel(gs_ref, fc_ref, out_ref):
+def references_kernel(gs_ref, mixed_ref, other_ref, out_ref, fc_ref):
+    put_columns(mixed_ref, other_ref, fc_ref)
     for h in range(HEADS):
         heads = gs_ref[h * P_SIZE : (h + 1) * P_SIZE, :]
         out_ref[h] = lax.dot_general(fc_ref[...], heads, NT, preferred_element_type=f32)
@@ -333,7 +346,7 @@
     for z in range(DEPTH):
         for core in range(2):
             for j in range(BLOCKS):
-                block = 2 * ((z + 4 * b) % DEPTH) + core
+                block = (2 * ((z + 4 * b) % DEPTH) + core) ^ j
                 pairs.append(((2 * z + core) * BLOCKS + j, j * BLOCKS + block))
     return lax.ppermute(value, ("z", "core", "y", "x"), pairs)
 
@@ -352,32 +365,27 @@
     refs = references.reshape(REFS, width)
     kind = jax.ShapeDtypeStruct
 
-    steps = 4
     half = part // 2
-    mixed, refs_part = call(
-        functools.partial(scores_kernel, score_scale), "scores",
-        [kind((BLOCKS, half + REFS, rows), bf16), kind((REFS, part), bf16)], [HBM, HBM],
-        scratch=[
-            pltpu.VMEM((rows, width), bf16), pltpu.VMEM((steps, REFS // steps, width), bf16),
-            pltpu.VMEM((width, rows), bf16), pltpu.SemaphoreType.DMA((steps + 1,)),
-        ],
-    )(feats, refs)
+    halves = kind((BLOCKS, half, rows), bf16)
+    split = call(split_kernel, "split", halves, 1, scratch=[pltpu.VMEM((width, rows), bf16)])(feats)
+    mixed = call(
+        functools.partial(scores_kernel, score_scale), "scores", kind((BLOCKS, half + REFS, rows), bf16), 3
+    )(feats, refs, split)
     mixed = exchange(mixed)
-    e = call(peel_kernel, "peel", kind((BLOCKS, half, rows), bf16), 1)(mixed)
-    other = lax.ppermute(e, "core", [(0, 1), (1, 0)])
+    other = lax.ppermute(call(peel_kernel, "peel", halves, 1)(mixed), "core", [(0, 1), (1, 0)])
     weights = jnp.pad(jnp.transpose(classifier, (0, 2, 1)), ((0, 0), (0, PAD - CLASSES), (0, 0)))
     weights = weights.reshape(HEADS * PAD, part)
 
     scales = kind((ITERS * HEADS * BLOCKS, rows), f32)
     rs, rt, col, plan = call(
         sinkhorn_kernel, "sinkhorn",
-        [scales, scales, kind((ITERS, REFS, rows), f32), kind((REFS, everything), bf16)], [VMEM, SMEM],
-    )(mixed, lengths)
-    products, raw, cols = call(
+        [scales, scales, kind((ITERS, REFS, rows), f32), kind((REFS, everything), bf16)], [VMEM, SMEM, SMEM],
+    )(mixed, lengths, labels)
+    products, raw = call(
         forward_kernel, "forward",
-        [kind((BLOCKS, T_ROWS + M_ROWS, rows), bf16), kind((REFS, part), f32), kind((part, everything), bf16)], 4,
-        scratch=[pltpu.VMEM((T_ROWS, part), bf16)],
-    )(e, other, weights, plan)
+        [kind((BLOCKS, T_ROWS + M_ROWS, rows), bf16), kind((REFS, part), f32)], 4,
+        scratch=[pltpu.VMEM((part, everything), bf16), pltpu.VMEM((T_ROWS, part), bf16)],
+    )(mixed, other, weights, plan)
     t, moments, logit_part = call(
         functools.partial(sum_kernel, width), "sum",
         [kind((T_ROWS, rows), bf16), kind((HEADS * PAD, P_SIZE), f32), kind((PAD, P_SIZE), f32)], 1,
@@ -386,28 +394,35 @@
         call(row_kernel, "row", kind((BLOCKS, T_ROWS + PAD, rows), bf16), 2)(t, spread_logits(logit_part))
     )
     pair = kind((2, part, rows), bf16)
-    logits, grad_scores, *mine, away = call(
+    logits, grads, grad_scores = call(
         functools.partial(backward_kernel, width, score_scale), "backward",
-        [kind((1, PAD), f32), kind((REFS, everything), bf16)] + [pair] * 4 + [kind((DEPTH, part, rows), bf16)],
-        [VMEM] * 10 + [SMEM],
+        [kind((1, PAD), f32), kind((PAD, P_SIZE), f32), kind((REFS, everything), bf16)],
+        [VMEM] * 6 + [SMEM],
         scratch=[
             pltpu.VMEM((ITERS, P_SIZE, rows), f32),
             pltpu.VMEM((ITERS * HEADS * BLOCKS, rows), f32),
             pltpu.VMEM((HEADS * BLOCKS, rows), f32),
+        ],
+    )(mixed, ts, rs, rt, col, moments, labels)
+    *mine, away = call(
+        functools.partial(parts_kernel, width), "parts", [pair] * 4 + [kind((DEPTH, part, rows), bf16)], 7,
+        scratch=[
             pltpu.VMEM((2 * REFS, part), bf16),
             pltpu.VMEM((2 * REFS, everything), bf16),
             pltpu.VMEM((part, everything), f32),
         ],
-    )(mixed, ts, rs, rt, col, moments, raw, weights, plan, refs_part, labels)
+        mib=12,
+    )(grad_scores, grads, moments, weights, raw, plan, refs)
     away = lax.ppermute(away, "core", [(0, 1), (1, 0)])
     o = call(cores_kernel, "cores", [pair] * 4, 5)(*mine, away)
     o = [o[0]] + [along_z(o[k], k) for k in (1, 2, 3)]
     u = call(chips_kernel, "chips", [kind((part, rows), bf16)] * 2, 4)(*o)
     u = [to_place(u[b], b) for b in range(2)]
     grad_features = call(last_kernel, "last", kind((part, rows), f32), 2)(*u)
-    grad_references = call(references_kernel, "references", kind((HEADS, part, rows), f32), 2, flops=2 * REFS * part * everything)(
-        grad_scores, cols
-    )
+    grad_references = call(
+        references_kernel, "references", kind((HEADS, part, rows), f32), 3,
+        scratch=[pltpu.VMEM((part, everything), bf16)], flops=2 * REFS * part * everything,
+    )(grad_scores, mixed, other)
     return (
         logits[:, :CLASSES],
         jnp.transpose(grad_features).reshape(batch, rows, part),

time: 149 us -> 139 us (0.933); the launches traced: 146 us -> 138 us
  blocking collectives: 51.7 us -> 73.6 us
  waiting for transfers between devices: 37.6 us -> 21.4 us
  starting transfers between devices: 30.1 us -> 24.6 us
  local copies, waits for them, and re-layouts: 8.35 us -> 3.07 us
  Pallas kernels: 16.5 us -> 13.3 us
    all_to_all x2 -> x3, blocking collectives: 51.7 us -> 73.6 us  [exchange(): return lax.all_to_all(value, ('y', 'x'), 0, 0)]
    all_to_all x1 -> x0, waiting for transfers between devices: 14.4 us -> none  [exchange(): return lax.all_to_all(value, ('y', 'x'), 0, 0)]
    all_to_all x1 -> x0, starting transfers between devices: 6.77 us -> none  [exchange(): return lax.all_to_all(value, ('y', 'x'), 0, 0)]
    unnamed x25 -> x9, local copies, waits for them, and re-layouts: 8.34 us -> 3.06 us
    pallas_call x3 -> x5, Pallas kernels: 6.52 us -> 4.65 us  [the longest x1 1.59 us: local(): call(references_kernel, 'references', kind((HEADS, part, rows), f32), 3,...]
    ppermute x2, waiting for transfers between devices: 11.8 us -> 10.3 us  [to_place(): return lax.ppermute(value, ('z', 'core', 'y', 'x'), pairs)]
  transfers between devices with their start and end apart: 9 -> 8, of which waited for: 7 -> 6; matrix products, arithmetic and copies ran while one was open for 0% -> 0% of each run, Pallas kernels for 2% -> 2%
where the time goes in v6:
time: 139 us; the launch traced here: 138 us
  blocking collectives  73.6 us (53%)
  starting transfers between devices  24.6 us (18%)
  waiting for transfers between devices  21.4 us (15%)
  Pallas kernels  13.3 us (10%)
  local copies, waits for them, and re-layouts  3.07 us (2%)
  between operations  2.08 us (1%)
    all_to_all x3, blocking collectives, exchange(): return lax.all_to_all(value, ('y', 'x'), 0, 0)  73.6 us
    ppermute x2, starting transfers between devices, to_place(): return lax.ppermute(value, ('z', 'core', 'y', 'x'), pairs)  11.9 us
    ppermute x2, waiting for transfers between devices, to_place(): return lax.ppermute(value, ('z', 'core', 'y', 'x'), pairs)  10.3 us
    ppermute x1, starting transfers between devices, spread_logits(): return lax.ppermute(value, ('z', 'core', 'y', 'x'), pairs)  8.65 us
    ppermute x3, waiting for transfers between devices, along_z(): return lax.ppermute(value, ('z', 'core'), pairs)  7.7 us
    pallas_call x1, Pallas kernels, local(): call(functools.partial(backward_kernel, width, score_scale), 'backward',...  3.97 us
    ppermute x3, starting transfers between devices, along_z(): return lax.ppermute(value, ('z', 'core'), pairs)  3.95 us
    unnamed x9, local copies, waits for them, and re-layouts  3.06 us
  transfers between devices with their start and end apart: 8, of which 6 were waited for; matrix products, arithmetic and copies ran while one was open for 0% of the time, Pallas kernels for 2%

profile of v6, /device:TPU:12, one launch (start us, length us, event | category | flops | bytes accessed | tf_op | source)
XLA Modules:
  0.0 138.1 jit_solution(7916892336003455862)
XLA Ops:
  0.6 1.3 copy-done.2
  1.9 0.6 split.1.half_ref
  2.6 0.0 copy-start
  2.6 1.7 %copy-done = bf16[2,128,5120]{2,1,0:T(8,128)(2,1)S(1)} copy-done((bf16[2,128,5120]{2,1,0:T(8,128)(2,1)S(1)}, bf16[2,128,5120]{2,1,0:T(8,128)(2,1)}, u32[]{:S(2)}) %copy-start) | copy-done | bytes 2621464
  4.3 0.9 scores.1
  5.2 28.2 %all_to_all.15.in_ref.q_ref.mixed_ref = bf16[16,416,128]{2,1,0:T(8,128)(2,1)S(1)} all-to-all(bf16[16,416,128]{2,1,0:T(8,128)(2,1)S(1)} %scores.1), channel_id=1, replica_groups=mesh['z'=8,'core'=2,'y'=4,'x'=4] {'y','x'}, dimensions={0} | all-to-all | bytes 3407872 | tf_op jit(solution)/shard_map/all_to_all | solution.py:55
  33.5 0.1 collective-permute-start
  34.9 1.7 %sinkhorn.1 = (f32[96,128]{1,0:T(8,128)S(1)}, f32[96,128]{1,0:T(8,128)S(1)}, f32[3,256,128]{2,1,0:T(8,128)S(1)}, bf16[256,2048]{1,0:T(8,128)(2,1)S(1)}) custom-call(bf16[16,416,128]{2,1,0:T(8,128)(2,1)S(1)} %all_to_all.15.in_ref.q_ref.mixed_ref, s32[1]{0:T(128)S(6)} %copy.10.len_ref, s32[1]{0:T(128)S(6)} %copy.11.label_ref), custom_call_target="tpu_custom_call" | custom-call | tf_op jit(solution)/shard_map/sinkhorn/pallas_call | solution.py:380
  36.7 1.7 %forward.1 = (bf16[16,320,128]{2,1,0:T(8,128)(2,1)S(1)}, f32[256,320]{1,0:T(8,128)S(1)}) custom-call(bf16[16,416,128]{2,1,0:T(8,128)(2,1)S(1)} %all_to_all.15.in_ref.q_ref.mixed_ref, bf16[16,160,128]{2,1,0:T(8,128)(2,1)S(1)} %collective-permute-done.other_ref, bf16[32,320]{1,0:T(8,128)(2,1)S(1)} %bitcast.13, bf16[256,2048]{1,0:T(8,128)(2,1)S(1)} %get-tuple-element.26.plan_ref), custom_call_target="tpu_custom_call" | custom-call | tf_op jit(solution)/shard_map/forward/pallas_call | solution.py:384
  38.4 23.5 %all_to_all.16.in_ref = bf16[16,320,128]{2,1,0:T(8,128)(2,1)S(1)} all-to-all(bf16[16,320,128]{2,1,0:T(8,128)(2,1)S(1)} %get-tuple-element.27), channel_id=1, replica_groups=mesh['z'=8,'core'=2,'y'=4,'x'=4] {'y','x'}, dimensions={0} | all-to-all | bytes 2621440 | tf_op jit(solution)/shard_map/all_to_all | solution.py:55
  61.8 0.2 sum.1
  62.0 8.7 %collective-permute-start.1 = (f32[16,128]{1,0:T(8,128)S(1)}, f32[16,128]{1,0:T(8,128)S(1)}, u32[]{:S(2)}, u32[]{:S(2)}) collective-permute-start(f32[16,128]{1,0:T(8,128)S(1)} %get-tuple-element.29), channel_id=1, source_target_pairs={{0,0},{17,1},{34,2},{51,3},{68,4},{85,5},{102,6},{119,7},{136,8},{... | collective-permute-start | bytes 24584 | tf_op jit(solution)/shard_map/ppermute | solution.py:356
  70.7 1.3 collective-permute-done.1.logit_ref
  72.0 0.2 row.1
  72.2 21.9 %all_to_all.17.t_ref = bf16[16,304,128]{2,1,0:T(8,128)(2,1)S(1)} all-to-all(bf16[16,304,128]{2,1,0:T(8,128)(2,1)S(1)} %row.1), channel_id=1, replica_groups=mesh['z'=8,'core'=2,'y'=4,'x'=4] {'y','x'}, dimensions={0} | all-to-all | bytes 2490368 | tf_op jit(solution)/shard_map/all_to_all | solution.py:55
  94.1 4.0 %backward.1 = (f32[1,16]{1,0:T(1,128)}, f32[16,128]{1,0:T(8,128)S(1)}, bf16[256,2048]{1,0:T(8,128)(2,1)S(1)}) custom-call(bf16[16,416,128]{2,1,0:T(8,128)(2,1)S(1)} %all_to_all.15.in_ref.q_ref.mixed_ref, bf16[16,304,128]{2,1,0:T(8,128)(2,1)S(1)} %all_to_all.17.t_ref, f32[96,128]{1,0:T(8,128)S(1)} %get-tuple-element.30.rs_ref, ...), custom_call_target="tpu_custom_call" | custom-call | tf_op jit(solution)/shard_map/backward/pallas_call | solution.py:397
  98.1 1.5 %parts.1 = (bf16[2,320,128]{2,1,0:T(8,128)(2,1)S(1)}, bf16[2,320,128]{2,1,0:T(8,128)(2,1)S(1)}, bf16[2,320,128]{2,1,0:T(8,128)(2,1)S(1)}, bf16[2,320,128]{2,1,0:T(8,128)(2,1)S(1)}, bf16[8,320,128]{2,1,0:T(8,128)(2,1)S(1)}) custom-call(bf16[256,2048]{1,0:T(8,128)(2,1)S(1)} %get-tuple-element.35.gs_ref, f32[16,128]{1,0:T(8,128)S(1)} %get-tuple-element.36.grads_ref, ...), custom_call_target="tpu_custom_call" | custom-call | tf_op jit(solution)/shard_map/parts/pallas_call | solution.py:407
  99.6 0.1 collective-permute-start.2
  99.7 2.1 %collective-permute-done.2.other_ref = bf16[8,320,128]{2,1,0:T(8,128)(2,1)S(1)} collective-permute-done((bf16[8,320,128]{2,1,0:T(8,128)(2,1)S(1)}, bf16[8,320,128]{2,1,0:T(8,128)(2,1)S(1)}, u32[]{:S(2)}, u32[]{:S(2)}) %collective-permute-start.2) | collective-permute-done | bytes 655392 | tf_op jit(solution)/shard_map/ppermute | solution.py:416
  101.8 0.2 cores.1
  101.9 1.3 collective-permute-start.3
  103.3 2.3 %collective-permute-start.4 = (bf16[2,320,128]{2,1,0:T(8,128)(2,1)S(1)}, bf16[2,320,128]{2,1,0:T(8,128)(2,1)S(1)}, u32[]{:S(2)}, u32[]{:S(2)}) collective-permute-start(bf16[2,320,128]{2,1,0:T(8,128)(2,1)S(1)} %get-tuple-element.45), channel_id=1, source_target_pairs={{0,224},{16,240},{32,0},{48,16},{64,32},{80,48},{96,64},{112,80},{... | collective-permute-start | bytes 491528 | tf_op jit(solution)/shard_map/ppermute | solution.py:341
  105.6 0.3 collective-permute-start.5
  105.9 4.1 %collective-permute-done.3.o1 = bf16[2,320,128]{2,1,0:T(8,128)(2,1)S(1)} collective-permute-done((bf16[2,320,128]{2,1,0:T(8,128)(2,1)S(1)}, bf16[2,320,128]{2,1,0:T(8,128)(2,1)S(1)}, u32[]{:S(2)}, u32[]{:S(2)}) %collective-permute-start.3) | collective-permute-done | bytes 163872 | tf_op jit(solution)/shard_map/ppermute | solution.py:341
  110.0 0.9 collective-permute-done.4.o2
  110.9 2.7 %collective-permute-done.5.o3 = bf16[2,320,128]{2,1,0:T(8,128)(2,1)S(1)} collective-permute-done((bf16[2,320,128]{2,1,0:T(8,128)(2,1)S(1)}, bf16[2,320,128]{2,1,0:T(8,128)(2,1)S(1)}, u32[]{:S(2)}, u32[]{:S(2)}) %collective-permute-start.5) | collective-permute-done | bytes 163872 | tf_op jit(solution)/shard_map/ppermute | solution.py:341
  113.6 0.1 chips.1
  113.7 6.1 %collective-permute-start.6 = (bf16[320,128]{1,0:T(8,128)(2,1)S(1)}, bf16[320,128]{1,0:T(8,128)(2,1)S(1)}, u32[]{:S(2)}, u32[]{:S(2)}) collective-permute-start(bf16[320,128]{1,0:T(8,128)(2,1)S(1)} %get-tuple-element.47), channel_id=1, source_target_pairs={{0,0},{1,17},{2,34},{3,51},{4,68},{5,85},{6,102},{7,119},{8,136},{... | collective-permute-start | bytes 245768 | tf_op jit(solution)/shard_map/ppermute | solution.py:351
  119.8 5.8 %collective-permute-start.7 = (bf16[320,128]{1,0:T(8,128)(2,1)S(1)}, bf16[320,128]{1,0:T(8,128)(2,1)S(1)}, u32[]{:S(2)}, u32[]{:S(2)}) collective-permute-start(bf16[320,128]{1,0:T(8,128)(2,1)S(1)} %get-tuple-element.48), channel_id=1, source_target_pairs={{0,8},{1,25},{2,42},{3,59},{4,76},{5,93},{6,110},{7,127},{8,128},{... | collective-permute-start | bytes 245768 | tf_op jit(solution)/shard_map/ppermute | solution.py:351
  125.5 1.6 %references.1 = f32[2,320,128]{2,1,0:T(8,128)} custom-call(bf16[256,2048]{1,0:T(8,128)(2,1)S(1)} %get-tuple-element.35.gs_ref, bf16[16,416,128]{2,1,0:T(8,128)(2,1)S(1)} %all_to_all.15.in_ref.q_ref.mixed_ref, bf16[16,160,128]{2,1,0:T(8,128)(2,1)S(1)} %collective-permute-done.other_ref), custom_call_target="tpu_custom_call" | custom-call | flops 335544320 | bytes 1048576 | tf_op jit(solution)/shard_map/references/pallas_call | solution.py:422
  127.1 10.3 %collective-permute-done.7.u1 = bf16[320,128]{1,0:T(8,128)(2,1)S(1)} collective-permute-done((bf16[320,128]{1,0:T(8,128)(2,1)S(1)}, bf16[320,128]{1,0:T(8,128)(2,1)S(1)}, u32[]{:S(2)}, u32[]{:S(2)}) %collective-permute-start.7) | collective-permute-done | bytes 81952 | tf_op jit(solution)/shard_map/ppermute | solution.py:351
  137.4 0.7 last.1
  (10 shorter events, 0.1 us)
Async XLA Ops:
  0.6 1.3 copy-start.2
  2.6 1.7 %copy-start = (bf16[2,128,5120]{2,1,0:T(8,128)(2,1)S(1)}, bf16[2,128,5120]{2,1,0:T(8,128)(2,1)}, u32[]{:S(2)}) copy-start(bf16[2,128,5120]{2,1,0:T(8,128)(2,1)} %param.6) | copy-start | bytes 7864324
  33.4 1.4 %copy-start.3 = (bf16[2,320,10]{1,0,2:T(2,128)(2,1)S(1)}, bf16[2,320,10]{1,0,2:T(2,128)(2,1)}, u32[]{:S(2)}) copy-start(bf16[2,320,10]{1,0,2:T(2,128)(2,1)} %param.7) | copy-start | bytes 38404
  33.5 3.2 %collective-permute-start = (bf16[16,160,128]{2,1,0:T(8,128)(2,1)S(1)}, bf16[16,160,128]{2,1,0:T(8,128)(2,1)S(1)}, u32[]{:S(2)}, u32[]{:S(2)}) collective-permute-start(bf16[16,160,128]{2,1,0:T(8,128)(2,1)S(1)} %peel.1), channel_id=1, source_target_pairs={{0,16},{16,0},{1,17},{17,1},{2,18},{18,2},{3,19},{19,3},{4,20},{20... | collective-permute-start | bytes 1966088 | tf_op jit(solution)/shard_map/ppermute | solution.py:375
  62.0 10.0 %collective-permute-start.1 = (f32[16,128]{1,0:T(8,128)S(1)}, f32[16,128]{1,0:T(8,128)S(1)}, u32[]{:S(2)}, u32[]{:S(2)}) collective-permute-start(f32[16,128]{1,0:T(8,128)S(1)} %get-tuple-element.29), channel_id=1, source_target_pairs={{0,0},{17,1},{34,2},{51,3},{68,4},{85,5},{102,6},{119,7},{136,8},{... | collective-permute-start | bytes 24584 | tf_op jit(solution)/shard_map/ppermute | solution.py:356
  94.1 4.0 %copy-start.1 = (bf16[2,128,5120]{2,1,0:T(8,128)(2,1)S(1)}, bf16[2,128,5120]{2,1,0:T(8,128)(2,1)}, u32[]{:S(2)}) copy-start(bf16[2,128,5120]{2,1,0:T(8,128)(2,1)} %param.6) | copy-start | bytes 7864324
  99.6 2.2 %collective-permute-start.2 = (bf16[8,320,128]{2,1,0:T(8,128)(2,1)S(1)}, bf16[8,320,128]{2,1,0:T(8,128)(2,1)S(1)}, u32[]{:S(2)}, u32[]{:S(2)}) collective-permute-start(bf16[8,320,128]{2,1,0:T(8,128)(2,1)S(1)} %get-tuple-element.42), channel_id=1, source_target_pairs={{0,16},{16,0},{1,17},{17,1},{2,18},{18,2},{3,19},{19,3},{4,20},{20... | collective-permute-start | bytes 1966088 | tf_op jit(solution)/shard_map/ppermute | solution.py:416
  101.9 8.1 %collective-permute-start.3 = (bf16[2,320,128]{2,1,0:T(8,128)(2,1)S(1)}, bf16[2,320,128]{2,1,0:T(8,128)(2,1)S(1)}, u32[]{:S(2)}, u32[]{:S(2)}) collective-permute-start(bf16[2,320,128]{2,1,0:T(8,128)(2,1)S(1)} %get-tuple-element.44), channel_id=1, source_target_pairs={{0,32},{16,48},{32,64},{48,80},{64,96},{80,112},{96,128},{112,144}... | collective-permute-start | bytes 491528 | tf_op jit(solution)/shard_map/ppermute | solution.py:341
  103.3 7.6 %collective-permute-start.4 = (bf16[2,320,128]{2,1,0:T(8,128)(2,1)S(1)}, bf16[2,320,128]{2,1,0:T(8,128)(2,1)S(1)}, u32[]{:S(2)}, u32[]{:S(2)}) collective-permute-start(bf16[2,320,128]{2,1,0:T(8,128)(2,1)S(1)} %get-tuple-element.45), channel_id=1, source_target_pairs={{0,224},{16,240},{32,0},{48,16},{64,32},{80,48},{96,64},{112,80},{... | collective-permute-start | bytes 491528 | tf_op jit(solution)/shard_map/ppermute | solution.py:341
  105.6 8.0 %collective-permute-start.5 = (bf16[2,320,128]{2,1,0:T(8,128)(2,1)S(1)}, bf16[2,320,128]{2,1,0:T(8,128)(2,1)S(1)}, u32[]{:S(2)}, u32[]{:S(2)}) collective-permute-start(bf16[2,320,128]{2,1,0:T(8,128)(2,1)S(1)} %get-tuple-element.46), channel_id=1, source_target_pairs={{0,64},{16,208},{32,96},{48,240},{64,128},{80,16},{96,160},{112,48... | collective-permute-start | bytes 491528 | tf_op jit(solution)/shard_map/ppermute | solution.py:341
  113.7 13.5 %collective-permute-start.6 = (bf16[320,128]{1,0:T(8,128)(2,1)S(1)}, bf16[320,128]{1,0:T(8,128)(2,1)S(1)}, u32[]{:S(2)}, u32[]{:S(2)}) collective-permute-start(bf16[320,128]{1,0:T(8,128)(2,1)S(1)} %get-tuple-element.47), channel_id=1, source_target_pairs={{0,0},{1,17},{2,34},{3,51},{4,68},{5,85},{6,102},{7,119},{8,136},{... | collective-permute-start | bytes 245768 | tf_op jit(solution)/shard_map/ppermute | solution.py:351
  119.8 17.6 %collective-permute-start.7 = (bf16[320,128]{1,0:T(8,128)(2,1)S(1)}, bf16[320,128]{1,0:T(8,128)(2,1)S(1)}, u32[]{:S(2)}, u32[]{:S(2)}) collective-permute-start(bf16[320,128]{1,0:T(8,128)(2,1)S(1)} %get-tuple-element.48), channel_id=1, source_target_pairs={{0,8},{1,25},{2,42},{3,59},{4,76},{5,93},{6,110},{7,127},{8,128},{... | collective-permute-start | bytes 245768 | tf_op jit(solution)/shard_map/ppermute | solution.py:351

commit v7 on v6

--- a/solution.py
+++ b/solution.py
@@ -26,8 +26,10 @@
 BLOCKS = SIDE * SIDE
 CHIPS = ((0, 1, 7, 2), (0, 1, 7, 6))
 T_ROWS = REFS + HEADS * PAD
-M_ROWS = 2 * PAD
+MOVE = 4
+M_ROWS = PAD
 VMEM = pl.BlockSpec(memory_space=pltpu.VMEM)
+HBM = pl.BlockSpec(memory_space=pltpu.HBM)
 SMEM = pl.BlockSpec(memory_space=pltpu.SMEM)
 NT = (((1,), (1,)), ((), ()))
 TN = (((0,), (0,)), ((), ()))
@@ -55,24 +57,26 @@
     return lax.all_to_all(value, ("y", "x"), 0, 0)
 
 
-def split_kernel(f_ref, out_ref, turned_ref):
-    half = out_ref.shape[1]
+def scores_kernel(scale, f_ref, r_hbm, out_ref, r_ref, turned_ref, sems):
+    half = out_ref.shape[1] - REFS
     part = 2 * half
+    steps, rows = r_ref.shape[:2]
+    loads = []
+    for k in range(steps):
+        loads.append(pltpu.make_async_copy(r_hbm.at[pl.ds(k * rows, rows)], r_ref.at[k], sems.at[k]))
+        loads[k].start()
     for j in range(BLOCKS // 2):
         where = slice(2 * part * j, 2 * part * (j + 1))
         turned_ref[where, :] = jnp.transpose(f_ref[:, where])
     core = lax.axis_index("core")
     for j in range(BLOCKS):
-        out_ref[j] = turned_ref[pl.ds(pl.multiple_of(part * j + half * core, half), half), :]
-
-
-def scores_kernel(scale, f_ref, r_ref, half_ref, out_ref):
-    half = half_ref.shape[1]
-    scores = lax.dot_general(r_ref[...], f_ref[...], NT, preferred_element_type=f32)
-    kernel = jnp.exp(scores * scale).astype(bf16)
-    for j in range(BLOCKS):
-        out_ref[j, :half, :] = half_ref[j]
-        out_ref[j, half:, :] = kernel
+        out_ref[j, :half, :] = turned_ref[pl.ds(pl.multiple_of(part * j + half * core, half), half), :]
+    for k in range(steps):
+        loads[k].wait()
+        scores = lax.dot_general(r_ref[k], f_ref[...], NT, preferred_element_type=f32)
+        kernel = jnp.exp(scores * scale).astype(bf16)
+        for j in range(BLOCKS):
+            out_ref[j, half + k * rows : half + (k + 1) * rows, :] = kernel
 
 
 def peel_kernel(in_ref, out_ref):
@@ -141,12 +145,7 @@
     raw_ref[...] = raw
     ext_ref[:REFS, :] = raw.astype(bf16)
     ext_ref[REFS:, :] = wt_ref[...]
-    for i in range(4):
-        wide = jnp.dot(
-            ext_ref[...], fc_ref[:, 4 * i * rows : 4 * (i + 1) * rows], preferred_element_type=f32
-        ).astype(bf16)
-        for k in range(4):
-            out_ref[4 * i + k, :T_ROWS, :] = wide[:, k * rows : (k + 1) * rows]
+    tails, heads = [], []
     for h in range(HEADS):
         here = slice(h * P_SIZE, (h + 1) * P_SIZE)
         squares = jnp.sum(raw_ref[here, :] * raw_ref[here, :], axis=1, keepdims=True)
@@ -154,9 +153,22 @@
             wt_ref[h * PAD : (h + 1) * PAD, :], ext_ref[here, :], NT, preferred_element_type=f32
         )
         kind = lax.broadcasted_iota(jnp.int32, products.shape, 0)
-        moments = jnp.where(kind == CLASSES, to_row(squares), products).astype(bf16)
-        for j in range(BLOCKS):
-            out_ref[j, T_ROWS + h * PAD : T_ROWS + (h + 1) * PAD, :] = moments
+        moments = jnp.where(kind == CLASSES, to_row(squares), products)
+        heads.append(moments[:8])
+        tails.append(pltpu.roll(moments, MOVE, 0))
+    first = jnp.concatenate(heads, axis=0).astype(bf16)
+    for i in range(4):
+        wide = jnp.dot(
+            ext_ref[...], fc_ref[:, 4 * i * rows : 4 * (i + 1) * rows], preferred_element_type=f32
+        )
+        for k in range(4):
+            here = slice(k * rows, (k + 1) * rows)
+            out_ref[4 * i + k, :REFS, :] = wide[:REFS, here].astype(bf16)
+            for h in range(HEADS):
+                low = REFS + h * PAD
+                value = jnp.where(kind < CLASSES, wide[low : low + PAD, here], tails[h])
+                out_ref[4 * i + k, low : low + PAD, :] = value.astype(bf16)
+            out_ref[4 * i + k, T_ROWS:, :] = first
 
 
 def add_blocks(ref, low, high):
@@ -170,34 +182,48 @@
     return lax.rsqrt(moments[CLASSES : CLASSES + 1, :] / width + epsilon)
 
 
+def sixteen():
+    square = (PAD, PAD)
+    return lax.broadcasted_iota(jnp.int32, square, 0) == lax.broadcasted_iota(jnp.int32, square, 1)
+
+
 def sum_kernel(width, in_ref, t_ref, m_ref, logit_ref):
     logits = jnp.zeros((PAD, 1), f32)
-    for h in range(HEADS):
-        moments = add_blocks(in_ref, T_ROWS + h * PAD, T_ROWS + (h + 1) * PAD)
+    first = add_blocks(in_ref, T_ROWS, T_ROWS + M_ROWS)
+    for h in range(HEADS):
+        low = REFS + h * PAD
+        block = add_blocks(in_ref, low, low + PAD)
+        t_ref[low : low + PAD, :] = block.astype(bf16)
+        kind = lax.broadcasted_iota(jnp.int32, block.shape, 0)
+        head = first if h == 0 else pltpu.roll(first, 8, 0)
+        moments = jnp.where(kind < 8, head, jnp.where(kind <= CLASSES, pltpu.roll(block, PAD - MOVE, 0), 0.0))
         m_ref[h * PAD : (h + 1) * PAD, :] = moments
         part = jnp.sum(inverse_rms(moments, width) * moments, axis=1, keepdims=True)
         logits = logits + part / P_SIZE
-    logit_ref[...] = jnp.broadcast_to(logits, logit_ref.shape)
-    for low in range(0, T_ROWS, 96):
-        t_ref[low : low + 96, :] = add_blocks(in_ref, low, low + 96).astype(bf16)
+    row = jnp.sum(jnp.where(sixteen(), logits, 0.0), axis=0, keepdims=True)
+    logit_ref[...] = jnp.broadcast_to(row, logit_ref.shape)
+    for low in range(0, REFS, 64):
+        t_ref[low : low + 64, :] = add_blocks(in_ref, low, low + 64).astype(bf16)
 
 
 def row_kernel(t_ref, logit_ref, out_ref):
     logits = logit_ref[...]
-    high = logits.astype(bf16)
-    lane = lax.broadcasted_iota(jnp.int32, logits.shape, 1)
-    both = jnp.where(lane < P_SIZE // 2, high.astype(f32), logits - high.astype(f32)).astype(bf16)
+    high = logits.astype(bf16).astype(f32)
+    low = REFS + PAD
+    kind = lax.broadcasted_iota(jnp.int32, logits.shape, 0)
+    block = t_ref[REFS:low, :PAD].astype(f32)
+    block = jnp.where(kind == CLASSES, high, jnp.where(kind == CLASSES + 1, logits - high, block)).astype(bf16)
     for j in range(BLOCKS):
-        out_ref[j, :T_ROWS, :] = t_ref[...]
-        out_ref[j, T_ROWS:, :] = both
+        out_ref[j] = t_ref[...]
+        out_ref[j, REFS:low, :PAD] = block
 
 
 def sum_logits(ref):
     section = 2 * lax.axis_index("z") + lax.axis_index("core")
-    total = jnp.zeros((PAD, P_SIZE), f32)
+    total = jnp.zeros((PAD, PAD), f32)
     for other in range(BLOCKS):
-        total = total + ref[lax.rem(other + BLOCKS - section, BLOCKS), T_ROWS:, :].astype(f32)
-    return jnp.broadcast_to(total[:, :1] + total[:, P_SIZE // 2 : P_SIZE // 2 + 1], total.shape)
+        total = total + ref[lax.rem(other + BLOCKS - section, BLOCKS), REFS : REFS + PAD, :PAD].astype(f32)
+    return total[CLASSES : CLASSES + 1] + total[CLASSES + 1 : CLASSES + 2]
 
 
 def scales_of(grads, moments, width):
@@ -215,8 +241,9 @@
     base = q_ref.shape[1] - REFS
     size = float(P_SIZE)
     logits = sum_logits(t_ref)
-    square = lax.broadcasted_iota(jnp.int32, (PAD, PAD), 0) == lax.broadcasted_iota(jnp.int32, (PAD, PAD), 1)
-    logit_ref[...] = jnp.sum(jnp.where(square, logits[:, :PAD], 0.0), axis=0, keepdims=True)
+    logit_ref[...] = logits
+    logits = jnp.sum(jnp.where(sixteen(), logits, 0.0), axis=1, keepdims=True)
+    logits = jnp.broadcast_to(logits, (PAD, P_SIZE))
     kind = lax.broadcasted_iota(jnp.int32, logits.shape, 0)
     exps = jnp.where(kind < CLASSES, jnp.exp(logits), 0.0)
     probs = exps / jnp.sum(exps, axis=0, keepdims=True)
@@ -367,10 +394,15 @@
 
     half = part // 2
     halves = kind((BLOCKS, half, rows), bf16)
-    split = call(split_kernel, "split", halves, 1, scratch=[pltpu.VMEM((width, rows), bf16)])(feats)
+    steps = 4
     mixed = call(
-        functools.partial(scores_kernel, score_scale), "scores", kind((BLOCKS, half + REFS, rows), bf16), 3
-    )(feats, refs, split)
+        functools.partial(scores_kernel, score_scale), "scores", kind((BLOCKS, half + REFS, rows), bf16), [VMEM, HBM],
+        scratch=[
+            pltpu.VMEM((steps, REFS // steps, width), bf16), pltpu.VMEM((width, rows), bf16),
+            pltpu.SemaphoreType.DMA((steps,)),
+        ],
+        mib=60,
+    )(feats, refs)
     mixed = exchange(mixed)
     other = lax.ppermute(call(peel_kernel, "peel", halves, 1)(mixed), "core", [(0, 1), (1, 0)])
     weights = jnp.pad(jnp.transpose(classifier, (0, 2, 1)), ((0, 0), (0, PAD - CLASSES), (0, 0)))
@@ -388,10 +420,10 @@
     )(mixed, other, weights, plan)
     t, moments, logit_part = call(
         functools.partial(sum_kernel, width), "sum",
-        [kind((T_ROWS, rows), bf16), kind((HEADS * PAD, P_SIZE), f32), kind((PAD, P_SIZE), f32)], 1,
+        [kind((T_ROWS, rows), bf16), kind((HEADS * PAD, P_SIZE), f32), kind((PAD, PAD), f32)], 1,
     )(exchange(products))
     ts = exchange(
-        call(row_kernel, "row", kind((BLOCKS, T_ROWS + PAD, rows), bf16), 2)(t, spread_logits(logit_part))
+        call(row_kernel, "row", kind((BLOCKS, T_ROWS, rows), bf16), 2)(t, spread_logits(logit_part))
     )
     pair = kind((2, part, rows), bf16)
     logits, grads, grad_scores = call(

time: 139 us -> 140 us (level)
  Pallas kernels: 13.3 us -> 18.7 us
  local copies, waits for them, and re-layouts: 3.07 us -> 0.02 us
    pallas_call x1, Pallas kernels: 0.87 us -> 6.92 us  [local(): call(functools.partial(scores_kernel, score_scale), 'scores', kind((BLOCK...]
    unnamed x9 -> x5, local copies, waits for them, and re-layouts: 3.06 us -> 0.01 us
where the time goes in v7:
time: 140 us; the launch traced here: 139 us
  blocking collectives  72.6 us (52%)
  starting transfers between devices  24.1 us (17%)
  waiting for transfers between devices  21.9 us (16%)
  Pallas kernels  18.7 us (13%)
  between operations  2.07 us (1%)
    all_to_all x3, blocking collectives, exchange(): return lax.all_to_all(value, ('y', 'x'), 0, 0)  72.6 us
    ppermute x2, starting transfers between devices, to_place(): return lax.ppermute(value, ('z', 'core', 'y', 'x'), pairs)  11.6 us
    ppermute x2, waiting for transfers between devices, to_place(): return lax.ppermute(value, ('z', 'core', 'y', 'x'), pairs)  10.5 us
    ppermute x1, starting transfers between devices, spread_logits(): return lax.ppermute(value, ('z', 'core', 'y', 'x'), pairs)  8.65 us
    ppermute x3, waiting for transfers between devices, along_z(): return lax.ppermute(value, ('z', 'core'), pairs)  7.97 us
    pallas_call x1, Pallas kernels, local(): call(functools.partial(scores_kernel, score_scale), 'scores', kind((BLOCK...  6.92 us
    pallas_call x1, Pallas kernels, local(): call(functools.partial(backward_kernel, width, score_scale), 'backward',...  3.91 us
    ppermute x3, starting transfers between devices, along_z(): return lax.ppermute(value, ('z', 'core'), pairs)  3.66 us
  transfers between devices with their start and end apart: 8, of which 6 were waited for; matrix products, arithmetic and copies ran while one was open for 0% of the time, Pallas kernels for 2%

profile of v7, /device:TPU:12, one launch (start us, length us, event | category | flops | bytes accessed | tf_op | source)
XLA Modules:
  0.0 139.3 jit_solution(11195032182729064625)
XLA Ops:
  0.6 6.9 %scores.1 = bf16[16,416,128]{2,1,0:T(8,128)(2,1)} custom-call(bf16[128,5120]{1,0:T(8,128)(2,1)} %bitcast.13, bf16[256,5120]{1,0:T(8,128)(2,1)} %bitcast.9), custom_call_target="tpu_custom_call" | custom-call | tf_op jit(solution)/shard_map/scores/pallas_call | solution.py:398
  7.6 28.4 %all_to_all.15.in_ref.q_ref.mixed_ref = bf16[16,416,128]{2,1,0:T(8,128)(2,1)S(1)} all-to-all(bf16[16,416,128]{2,1,0:T(8,128)(2,1)} %scores.1), channel_id=1, replica_groups=mesh['z'=8,'core'=2,'y'=4,'x'=4] {'y','x'}, dimensions={0} | all-to-all | bytes 3407872 | tf_op jit(solution)/shard_map/all_to_all | solution.py:57
  36.0 0.1 collective-permute-start
  37.4 0.0 copy-done.1
  37.4 1.7 %sinkhorn.1 = (f32[96,128]{1,0:T(8,128)S(1)}, f32[96,128]{1,0:T(8,128)S(1)}, f32[3,256,128]{2,1,0:T(8,128)S(1)}, bf16[256,2048]{1,0:T(8,128)(2,1)S(1)}) custom-call(bf16[16,416,128]{2,1,0:T(8,128)(2,1)S(1)} %all_to_all.15.in_ref.q_ref.mixed_ref, s32[1]{0:T(128)S(6)} %copy.10.len_ref, s32[1]{0:T(128)S(6)} %copy.11.label_ref), custom_call_target="tpu_custom_call" | custom-call | tf_op jit(solution)/shard_map/sinkhorn/pallas_call | solution.py:412
  39.2 0.0 collective-permute-done.other_ref
  39.2 1.7 %forward.1 = (bf16[16,304,128]{2,1,0:T(8,128)(2,1)S(1)}, f32[256,320]{1,0:T(8,128)S(1)}) custom-call(bf16[16,416,128]{2,1,0:T(8,128)(2,1)S(1)} %all_to_all.15.in_ref.q_ref.mixed_ref, bf16[16,160,128]{2,1,0:T(8,128)(2,1)S(1)} %collective-permute-done.other_ref, bf16[32,320]{1,0:T(8,128)(2,1)S(1)} %bitcast.11, bf16[256,2048]{1,0:T(8,128)(2,1)S(1)} %get-tuple-element.26.plan_ref), custom_call_target="tpu_custom_call" | custom-call | tf_op jit(solution)/shard_map/forward/pallas_call | solution.py:416
  40.9 22.9 %all_to_all.16.in_ref = bf16[16,304,128]{2,1,0:T(8,128)(2,1)S(1)} all-to-all(bf16[16,304,128]{2,1,0:T(8,128)(2,1)S(1)} %get-tuple-element.27), channel_id=1, replica_groups=mesh['z'=8,'core'=2,'y'=4,'x'=4] {'y','x'}, dimensions={0} | all-to-all | bytes 2490368 | tf_op jit(solution)/shard_map/all_to_all | solution.py:57
  63.8 0.2 sum.1
  64.0 8.7 %collective-permute-start.1 = (f32[16,16]{1,0:T(8,128)S(1)}, f32[16,16]{1,0:T(8,128)S(1)}, u32[]{:S(2)}, u32[]{:S(2)}) collective-permute-start(f32[16,16]{1,0:T(8,128)S(1)} %get-tuple-element.29), channel_id=1, source_target_pairs={{0,0},{17,1},{34,2},{51,3},{68,4},{85,5},{102,6},{119,7},{136,8},{... | collective-permute-start | bytes 3080 | tf_op jit(solution)/shard_map/ppermute | solution.py:383
  72.7 1.3 collective-permute-done.1.logit_ref
  74.0 0.2 row.1
  74.2 21.3 %all_to_all.17.t_ref = bf16[16,288,128]{2,1,0:T(8,128)(2,1)S(1)} all-to-all(bf16[16,288,128]{2,1,0:T(8,128)(2,1)S(1)} %row.1), channel_id=1, replica_groups=mesh['z'=8,'core'=2,'y'=4,'x'=4] {'y','x'}, dimensions={0} | all-to-all | bytes 2359296 | tf_op jit(solution)/shard_map/all_to_all | solution.py:57
  95.5 3.9 %backward.1 = (f32[1,16]{1,0:T(1,128)}, f32[16,128]{1,0:T(8,128)S(1)}, bf16[256,2048]{1,0:T(8,128)(2,1)S(1)}) custom-call(bf16[16,416,128]{2,1,0:T(8,128)(2,1)S(1)} %all_to_all.15.in_ref.q_ref.mixed_ref, bf16[16,288,128]{2,1,0:T(8,128)(2,1)S(1)} %all_to_all.17.t_ref, f32[96,128]{1,0:T(8,128)S(1)} %get-tuple-element.30.rs_ref, ...), custom_call_target="tpu_custom_call" | custom-call | tf_op jit(solution)/shard_map/backward/pallas_call | solution.py:429
  99.4 0.0 copy-done
  99.4 1.5 %parts.1 = (bf16[2,320,128]{2,1,0:T(8,128)(2,1)S(1)}, bf16[2,320,128]{2,1,0:T(8,128)(2,1)S(1)}, bf16[2,320,128]{2,1,0:T(8,128)(2,1)S(1)}, bf16[2,320,128]{2,1,0:T(8,128)(2,1)S(1)}, bf16[8,320,128]{2,1,0:T(8,128)(2,1)S(1)}) custom-call(bf16[256,2048]{1,0:T(8,128)(2,1)S(1)} %get-tuple-element.35.gs_ref, f32[16,128]{1,0:T(8,128)S(1)} %get-tuple-element.36.grads_ref, ...), custom_call_target="tpu_custom_call" | custom-call | tf_op jit(solution)/shard_map/parts/pallas_call | solution.py:439
  100.9 0.1 collective-permute-start.2
  101.0 2.1 %collective-permute-done.2.other_ref = bf16[8,320,128]{2,1,0:T(8,128)(2,1)S(1)} collective-permute-done((bf16[8,320,128]{2,1,0:T(8,128)(2,1)S(1)}, bf16[8,320,128]{2,1,0:T(8,128)(2,1)S(1)}, u32[]{:S(2)}, u32[]{:S(2)}) %collective-permute-start.2) | collective-permute-done | bytes 655392 | tf_op jit(solution)/shard_map/ppermute | solution.py:448
  103.1 0.2 cores.1
  103.3 1.2 collective-permute-start.3
  104.4 2.5 %collective-permute-start.4 = (bf16[2,320,128]{2,1,0:T(8,128)(2,1)S(1)}, bf16[2,320,128]{2,1,0:T(8,128)(2,1)S(1)}, u32[]{:S(2)}, u32[]{:S(2)}) collective-permute-start(bf16[2,320,128]{2,1,0:T(8,128)(2,1)S(1)} %get-tuple-element.45), channel_id=1, source_target_pairs={{0,224},{16,240},{32,0},{48,16},{64,32},{80,48},{96,64},{112,80},{... | collective-permute-start | bytes 491528 | tf_op jit(solution)/shard_map/ppermute | solution.py:368
  106.9 0.0 collective-permute-start.5
  106.9 4.4 %collective-permute-done.3.o1 = bf16[2,320,128]{2,1,0:T(8,128)(2,1)S(1)} collective-permute-done((bf16[2,320,128]{2,1,0:T(8,128)(2,1)S(1)}, bf16[2,320,128]{2,1,0:T(8,128)(2,1)S(1)}, u32[]{:S(2)}, u32[]{:S(2)}) %collective-permute-start.3) | collective-permute-done | bytes 163872 | tf_op jit(solution)/shard_map/ppermute | solution.py:368
  111.3 0.8 collective-permute-done.4.o2
  112.1 2.8 %collective-permute-done.5.o3 = bf16[2,320,128]{2,1,0:T(8,128)(2,1)S(1)} collective-permute-done((bf16[2,320,128]{2,1,0:T(8,128)(2,1)S(1)}, bf16[2,320,128]{2,1,0:T(8,128)(2,1)S(1)}, u32[]{:S(2)}, u32[]{:S(2)}) %collective-permute-start.5) | collective-permute-done | bytes 163872 | tf_op jit(solution)/shard_map/ppermute | solution.py:368
  114.9 0.1 chips.1
  115.0 5.9 %collective-permute-start.6 = (bf16[320,128]{1,0:T(8,128)(2,1)S(1)}, bf16[320,128]{1,0:T(8,128)(2,1)S(1)}, u32[]{:S(2)}, u32[]{:S(2)}) collective-permute-start(bf16[320,128]{1,0:T(8,128)(2,1)S(1)} %get-tuple-element.47), channel_id=1, source_target_pairs={{0,0},{1,17},{2,34},{3,51},{4,68},{5,85},{6,102},{7,119},{8,136},{... | collective-permute-start | bytes 245768 | tf_op jit(solution)/shard_map/ppermute | solution.py:378
  120.9 5.7 %collective-permute-start.7 = (bf16[320,128]{1,0:T(8,128)(2,1)S(1)}, bf16[320,128]{1,0:T(8,128)(2,1)S(1)}, u32[]{:S(2)}, u32[]{:S(2)}) collective-permute-start(bf16[320,128]{1,0:T(8,128)(2,1)S(1)} %get-tuple-element.48), channel_id=1, source_target_pairs={{0,8},{1,25},{2,42},{3,59},{4,76},{5,93},{6,110},{7,127},{8,128},{... | collective-permute-start | bytes 245768 | tf_op jit(solution)/shard_map/ppermute | solution.py:378
  126.6 1.6 %references.1 = f32[2,320,128]{2,1,0:T(8,128)} custom-call(bf16[256,2048]{1,0:T(8,128)(2,1)S(1)} %get-tuple-element.35.gs_ref, bf16[16,416,128]{2,1,0:T(8,128)(2,1)S(1)} %all_to_all.15.in_ref.q_ref.mixed_ref, bf16[16,160,128]{2,1,0:T(8,128)(2,1)S(1)} %collective-permute-done.other_ref), custom_call_target="tpu_custom_call" | custom-call | flops 335544320 | bytes 1048576 | tf_op jit(solution)/shard_map/references/pallas_call | solution.py:454
  128.2 0.0 collective-permute-done.6.u0
  128.2 10.4 %collective-permute-done.7.u1 = bf16[320,128]{1,0:T(8,128)(2,1)S(1)} collective-permute-done((bf16[320,128]{1,0:T(8,128)(2,1)S(1)}, bf16[320,128]{1,0:T(8,128)(2,1)S(1)}, u32[]{:S(2)}, u32[]{:S(2)}) %collective-permute-start.7) | collective-permute-done | bytes 81952 | tf_op jit(solution)/shard_map/ppermute | solution.py:378
  138.7 0.7 last.1
  (5 shorter events, 0.1 us)
Async XLA Ops:
  35.9 1.4 %copy-start.1 = (bf16[2,320,10]{1,0,2:T(2,128)(2,1)S(1)}, bf16[2,320,10]{1,0,2:T(2,128)(2,1)}, u32[]{:S(2)}) copy-start(bf16[2,320,10]{1,0,2:T(2,128)(2,1)} %param.7) | copy-start | bytes 38404
  36.0 3.2 %collective-permute-start = (bf16[16,160,128]{2,1,0:T(8,128)(2,1)S(1)}, bf16[16,160,128]{2,1,0:T(8,128)(2,1)S(1)}, u32[]{:S(2)}, u32[]{:S(2)}) collective-permute-start(bf16[16,160,128]{2,1,0:T(8,128)(2,1)S(1)} %peel.1), channel_id=1, source_target_pairs={{0,16},{16,0},{1,17},{17,1},{2,18},{18,2},{3,19},{19,3},{4,20},{20... | collective-permute-start | bytes 1966088 | tf_op jit(solution)/shard_map/ppermute | solution.py:407
  64.0 10.0 %collective-permute-start.1 = (f32[16,16]{1,0:T(8,128)S(1)}, f32[16,16]{1,0:T(8,128)S(1)}, u32[]{:S(2)}, u32[]{:S(2)}) collective-permute-start(f32[16,16]{1,0:T(8,128)S(1)} %get-tuple-element.29), channel_id=1, source_target_pairs={{0,0},{17,1},{34,2},{51,3},{68,4},{85,5},{102,6},{119,7},{136,8},{... | collective-permute-start | bytes 3080 | tf_op jit(solution)/shard_map/ppermute | solution.py:383
  95.5 3.9 %copy-start = (bf16[2,128,5120]{2,1,0:T(8,128)(2,1)S(1)}, bf16[2,128,5120]{2,1,0:T(8,128)(2,1)}, u32[]{:S(2)}) copy-start(bf16[2,128,5120]{2,1,0:T(8,128)(2,1)} %param.6) | copy-start | bytes 7864324
  100.9 2.2 %collective-permute-start.2 = (bf16[8,320,128]{2,1,0:T(8,128)(2,1)S(1)}, bf16[8,320,128]{2,1,0:T(8,128)(2,1)S(1)}, u32[]{:S(2)}, u32[]{:S(2)}) collective-permute-start(bf16[8,320,128]{2,1,0:T(8,128)(2,1)S(1)} %get-tuple-element.42), channel_id=1, source_target_pairs={{0,16},{16,0},{1,17},{17,1},{2,18},{18,2},{3,19},{19,3},{4,20},{20... | collective-permute-start | bytes 1966088 | tf_op jit(solution)/shard_map/ppermute | solution.py:448
  103.3 8.1 %collective-permute-start.3 = (bf16[2,320,128]{2,1,0:T(8,128)(2,1)S(1)}, bf16[2,320,128]{2,1,0:T(8,128)(2,1)S(1)}, u32[]{:S(2)}, u32[]{:S(2)}) collective-permute-start(bf16[2,320,128]{2,1,0:T(8,128)(2,1)S(1)} %get-tuple-element.44), channel_id=1, source_target_pairs={{0,32},{16,48},{32,64},{48,80},{64,96},{80,112},{96,128},{112,144}... | collective-permute-start | bytes 491528 | tf_op jit(solution)/shard_map/ppermute | solution.py:368
  104.4 7.7 %collective-permute-start.4 = (bf16[2,320,128]{2,1,0:T(8,128)(2,1)S(1)}, bf16[2,320,128]{2,1,0:T(8,128)(2,1)S(1)}, u32[]{:S(2)}, u32[]{:S(2)}) collective-permute-start(bf16[2,320,128]{2,1,0:T(8,128)(2,1)S(1)} %get-tuple-element.45), channel_id=1, source_target_pairs={{0,224},{16,240},{32,0},{48,16},{64,32},{80,48},{96,64},{112,80},{... | collective-permute-start | bytes 491528 | tf_op jit(solution)/shard_map/ppermute | solution.py:368
  106.9 8.0 %collective-permute-start.5 = (bf16[2,320,128]{2,1,0:T(8,128)(2,1)S(1)}, bf16[2,320,128]{2,1,0:T(8,128)(2,1)S(1)}, u32[]{:S(2)}, u32[]{:S(2)}) collective-permute-start(bf16[2,320,128]{2,1,0:T(8,128)(2,1)S(1)} %get-tuple-element.46), channel_id=1, source_target_pairs={{0,64},{16,208},{32,96},{48,240},{64,128},{80,16},{96,160},{112,48... | collective-permute-start | bytes 491528 | tf_op jit(solution)/shard_map/ppermute | solution.py:368
  115.0 13.2 %collective-permute-start.6 = (bf16[320,128]{1,0:T(8,128)(2,1)S(1)}, bf16[320,128]{1,0:T(8,128)(2,1)S(1)}, u32[]{:S(2)}, u32[]{:S(2)}) collective-permute-start(bf16[320,128]{1,0:T(8,128)(2,1)S(1)} %get-tuple-element.47), channel_id=1, source_target_pairs={{0,0},{1,17},{2,34},{3,51},{4,68},{5,85},{6,102},{7,119},{8,136},{... | collective-permute-start | bytes 245768 | tf_op jit(solution)/shard_map/ppermute | solution.py:378
  120.9 17.8 %collective-permute-start.7 = (bf16[320,128]{1,0:T(8,128)(2,1)S(1)}, bf16[320,128]{1,0:T(8,128)(2,1)S(1)}, u32[]{:S(2)}, u32[]{:S(2)}) collective-permute-start(bf16[320,128]{1,0:T(8,128)(2,1)S(1)} %get-tuple-element.48), channel_id=1, source_target_pairs={{0,8},{1,25},{2,42},{3,59},{4,76},{5,93},{6,110},{7,127},{8,128},{... | collective-permute-start | bytes 245768 | tf_op jit(solution)/shard_map/ppermute | solution.py:378

commit v8 on v7

--- a/solution.py
+++ b/solution.py
@@ -29,7 +29,6 @@
 MOVE = 4
 M_ROWS = PAD
 VMEM = pl.BlockSpec(memory_space=pltpu.VMEM)
-HBM = pl.BlockSpec(memory_space=pltpu.HBM)
 SMEM = pl.BlockSpec(memory_space=pltpu.SMEM)
 NT = (((1,), (1,)), ((), ()))
 TN = (((0,), (0,)), ((), ()))
@@ -54,29 +53,31 @@
 
 
 def exchange(value):
-    return lax.all_to_all(value, ("y", "x"), 0, 0)
-
-
-def scores_kernel(scale, f_ref, r_hbm, out_ref, r_ref, turned_ref, sems):
-    half = out_ref.shape[1] - REFS
+    return lax.all_to_all(value, ("x", "y"), 0, 0)
+
+
+def at(j):
+    return j % SIDE * SIDE + j // SIDE
+
+
+def split_kernel(f_ref, out_ref, turned_ref):
+    half = out_ref.shape[1]
     part = 2 * half
-    steps, rows = r_ref.shape[:2]
-    loads = []
-    for k in range(steps):
-        loads.append(pltpu.make_async_copy(r_hbm.at[pl.ds(k * rows, rows)], r_ref.at[k], sems.at[k]))
-        loads[k].start()
     for j in range(BLOCKS // 2):
         where = slice(2 * part * j, 2 * part * (j + 1))
         turned_ref[where, :] = jnp.transpose(f_ref[:, where])
     core = lax.axis_index("core")
     for j in range(BLOCKS):
-        out_ref[j, :half, :] = turned_ref[pl.ds(pl.multiple_of(part * j + half * core, half), half), :]
-    for k in range(steps):
-        loads[k].wait()
-        scores = lax.dot_general(r_ref[k], f_ref[...], NT, preferred_element_type=f32)
-        kernel = jnp.exp(scores * scale).astype(bf16)
-        for j in range(BLOCKS):
-            out_ref[j, half + k * rows : half + (k + 1) * rows, :] = kernel
+        out_ref[at(j)] = turned_ref[pl.ds(pl.multiple_of(part * j + half * core, half), half), :]
+
+
+def scores_kernel(scale, f_ref, r_ref, half_ref, out_ref):
+    half = half_ref.shape[1]
+    scores = lax.dot_general(r_ref[...], f_ref[...], NT, preferred_element_type=f32)
+    kernel = jnp.exp(scores * scale).astype(bf16)
+    for j in range(BLOCKS):
+        out_ref[j, :half, :] = half_ref[j]
+        out_ref[j, half:, :] = kernel
 
 
 def peel_kernel(in_ref, out_ref):
@@ -90,8 +91,8 @@
     half, rows = other_ref.shape[1:]
     for j in range(BLOCKS):
         here = slice(j * rows, (j + 1) * rows)
-        out_ref[pl.ds(pl.multiple_of(core * half, half), half), here] = mixed_ref[j, :half, :]
-        out_ref[pl.ds(pl.multiple_of((1 - core) * half, half), half), here] = other_ref[j]
+        out_ref[pl.ds(pl.multiple_of(core * half, half), half), here] = mixed_ref[at(j), :half, :]
+        out_ref[pl.ds(pl.multiple_of((1 - core) * half, half), half), here] = other_ref[at(j)]
 
 
 def diagonal():
@@ -119,7 +120,7 @@
             here = slice(h * P_SIZE, (h + 1) * P_SIZE)
             acc = jnp.zeros((P_SIZE, rows), f32)
             for s in range(BLOCKS):
-                k = q_ref[s, low + h * P_SIZE : low + (h + 1) * P_SIZE, :].astype(f32)
+                k = q_ref[at(s), low + h * P_SIZE : low + (h + 1) * P_SIZE, :].astype(f32)
                 weighted = k if t == 0 else k * col_ref[t - 1, here, :]
                 total = jnp.sum(weighted, axis=0, keepdims=True)
                 scale = masses[s] / total
@@ -132,7 +133,7 @@
     for h in range(HEADS):
         here = slice(h * P_SIZE, (h + 1) * P_SIZE)
         for s in range(BLOCKS):
-            k = q_ref[s, low + h * P_SIZE : low + (h + 1) * P_SIZE, :].astype(f32)
+            k = q_ref[at(s), low + h * P_SIZE : low + (h + 1) * P_SIZE, :].astype(f32)
             place = ((ITERS - 1) * HEADS + h) * BLOCKS + s
             plan = rs_ref[place : place + 1, :] * k * col_ref[ITERS - 1, here, :]
             plan_ref[here, s * rows : (s + 1) * rows] = plan.astype(bf16)
@@ -163,12 +164,12 @@
         )
         for k in range(4):
             here = slice(k * rows, (k + 1) * rows)
-            out_ref[4 * i + k, :REFS, :] = wide[:REFS, here].astype(bf16)
+            out_ref[at(4 * i + k), :REFS, :] = wide[:REFS, here].astype(bf16)
             for h in range(HEADS):
                 low = REFS + h * PAD
                 value = jnp.where(kind < CLASSES, wide[low : low + PAD, here], tails[h])
-                out_ref[4 * i + k, low : low + PAD, :] = value.astype(bf16)
-            out_ref[4 * i + k, T_ROWS:, :] = first
+                out_ref[at(4 * i + k), low : low + PAD, :] = value.astype(bf16)
+            out_ref[at(4 * i + k), T_ROWS:, :] = first
 
 
 def add_blocks(ref, low, high):
@@ -222,7 +223,7 @@
     section = 2 * lax.axis_index("z") + lax.axis_index("core")
     total = jnp.zeros((PAD, PAD), f32)
     for other in range(BLOCKS):
-        total = total + ref[lax.rem(other + BLOCKS - section, BLOCKS), REFS : REFS + PAD, :PAD].astype(f32)
+        total = total + ref[at(lax.rem(other + BLOCKS - section, BLOCKS)), REFS : REFS + PAD, :PAD].astype(f32)
     return total[CLASSES : CLASSES + 1] + total[CLASSES + 1 : CLASSES + 2]
 
 
@@ -257,10 +258,10 @@
         second = first * pull
 
         def load(s):
-            return q_ref[s, base + h * P_SIZE : base + (h + 1) * P_SIZE, :].astype(f32)
+            return q_ref[at(s), base + h * P_SIZE : base + (h + 1) * P_SIZE, :].astype(f32)
 
         def grad_plan(s, u):
-            return first * u - second * t_ref[s, here, :].astype(f32)
+            return first * u - second * t_ref[at(s), here, :].astype(f32)
 
         def row(ref, t, s):
             place = (t * HEADS + h) * BLOCKS + s
@@ -272,7 +273,7 @@
 
         acc = jnp.zeros((P_SIZE, rows), f32)
         for s in range(BLOCKS):
-            v = t_ref[s, REFS + h * PAD : REFS + (h + 1) * PAD, :].astype(f32)
+            v = t_ref[at(s), REFS + h * PAD : REFS + (h + 1) * PAD, :].astype(f32)
             u = jnp.sum(grads * v, axis=0, keepdims=True) / size
             put(u_ref, 0, s, u)
             weighted = grad_plan(s, u) * load(s)
@@ -394,15 +395,10 @@
 
     half = part // 2
     halves = kind((BLOCKS, half, rows), bf16)
-    steps = 4
+    split = call(split_kernel, "split", halves, 1, scratch=[pltpu.VMEM((width, rows), bf16)])(feats)
     mixed = call(
-        functools.partial(scores_kernel, score_scale), "scores", kind((BLOCKS, half + REFS, rows), bf16), [VMEM, HBM],
-        scratch=[
-            pltpu.VMEM((steps, REFS // steps, width), bf16), pltpu.VMEM((width, rows), bf16),
-            pltpu.SemaphoreType.DMA((steps,)),
-        ],
-        mib=60,
-    )(feats, refs)
+        functools.partial(scores_kernel, score_scale), "scores", kind((BLOCKS, half + REFS, rows), bf16), 3
+    )(feats, refs, split)
     mixed = exchange(mixed)
     other = lax.ppermute(call(peel_kernel, "peel", halves, 1)(mixed), "core", [(0, 1), (1, 0)])
     weights = jnp.pad(jnp.transpose(classifier, (0, 2, 1)), ((0, 0), (0, PAD - CLASSES), (0, 0)))

time: 140 us -> 138 us (0.986)
  Pallas kernels: 18.7 us -> 13.4 us
  local copies, waits for them, and re-layouts: 0.02 us -> 3.07 us
    pallas_call x1, Pallas kernels: 6.92 us -> 0.87 us  [local(): call(functools.partial(scores_kernel, score_scale), 'scores', kind((BLOCK...]
    unnamed x5 -> x9, local copies, waits for them, and re-layouts: 0.01 us -> 3.06 us
where the time goes in v8:
time: 138 us
  blocking collectives  72.7 us (53%)
  starting transfers between devices  24.8 us (18%)
  waiting for transfers between devices  21.7 us (16%)
  Pallas kernels  13.4 us (10%)
  local copies, waits for them, and re-layouts  3.07 us (2%)
  between operations  2.09 us (2%)
    all_to_all x3, blocking collectives, exchange(): return lax.all_to_all(value, ('x', 'y'), 0, 0)  72.7 us
    ppermute x2, starting transfers between devices, to_place(): return lax.ppermute(value, ('z', 'core', 'y', 'x'), pairs)  12 us
    ppermute x2, waiting for transfers between devices, to_place(): return lax.ppermute(value, ('z', 'core', 'y', 'x'), pairs)  10.2 us
    ppermute x1, starting transfers between devices, spread_logits(): return lax.ppermute(value, ('z', 'core', 'y', 'x'), pairs)  8.65 us
    ppermute x3, waiting for transfers between devices, along_z(): return lax.ppermute(value, ('z', 'core'), pairs)  8.03 us
    pallas_call x1, Pallas kernels, local(): call(functools.partial(backward_kernel, width, score_scale), 'backward',...  4 us
    ppermute x3, starting transfers between devices, along_z(): return lax.ppermute(value, ('z', 'core'), pairs)  3.8 us
    unnamed x9, local copies, waits for them, and re-layouts  3.06 us
  transfers between devices with their start and end apart: 8, of which 6 were waited for; matrix products, arithmetic and copies ran while one was open for 0% of the time, Pallas kernels for 2%

profile of v8, /device:TPU:12, one launch (start us, length us, event | category | flops | bytes accessed | tf_op | source)
XLA Modules:
  0.0 137.7 jit_solution(4264830989333155237)
XLA Ops:
  0.6 1.3 copy-done.2
  1.9 0.6 split.1.half_ref
  2.6 0.0 copy-start
  2.6 1.7 %copy-done = bf16[2,128,5120]{2,1,0:T(8,128)(2,1)S(1)} copy-done((bf16[2,128,5120]{2,1,0:T(8,128)(2,1)S(1)}, bf16[2,128,5120]{2,1,0:T(8,128)(2,1)}, u32[]{:S(2)}) %copy-start) | copy-done | bytes 2621464
  4.3 0.9 scores.1
  5.2 28.2 %all_to_all.15.in_ref.q_ref.mixed_ref = bf16[16,416,128]{2,1,0:T(8,128)(2,1)S(1)} all-to-all(bf16[16,416,128]{2,1,0:T(8,128)(2,1)S(1)} %scores.1), channel_id=1, replica_groups=mesh['z'=8,'core'=2,'y'=4,'x'=4] {'x','y'}, dimensions={0} | all-to-all | bytes 3407872 | tf_op jit(solution)/shard_map/all_to_all | solution.py:56
  33.5 0.1 collective-permute-start
  34.9 1.7 %sinkhorn.1 = (f32[96,128]{1,0:T(8,128)S(1)}, f32[96,128]{1,0:T(8,128)S(1)}, f32[3,256,128]{2,1,0:T(8,128)S(1)}, bf16[256,2048]{1,0:T(8,128)(2,1)S(1)}) custom-call(bf16[16,416,128]{2,1,0:T(8,128)(2,1)S(1)} %all_to_all.15.in_ref.q_ref.mixed_ref, s32[1]{0:T(128)S(6)} %copy.10.len_ref, s32[1]{0:T(128)S(6)} %copy.11.label_ref), custom_call_target="tpu_custom_call" | custom-call | tf_op jit(solution)/shard_map/sinkhorn/pallas_call | solution.py:408
  36.7 1.7 %forward.1 = (bf16[16,304,128]{2,1,0:T(8,128)(2,1)S(1)}, f32[256,320]{1,0:T(8,128)S(1)}) custom-call(bf16[16,416,128]{2,1,0:T(8,128)(2,1)S(1)} %all_to_all.15.in_ref.q_ref.mixed_ref, bf16[16,160,128]{2,1,0:T(8,128)(2,1)S(1)} %collective-permute-done.other_ref, bf16[32,320]{1,0:T(8,128)(2,1)S(1)} %bitcast.13, bf16[256,2048]{1,0:T(8,128)(2,1)S(1)} %get-tuple-element.26.plan_ref), custom_call_target="tpu_custom_call" | custom-call | tf_op jit(solution)/shard_map/forward/pallas_call | solution.py:412
  38.4 23.2 %all_to_all.16.in_ref = bf16[16,304,128]{2,1,0:T(8,128)(2,1)S(1)} all-to-all(bf16[16,304,128]{2,1,0:T(8,128)(2,1)S(1)} %get-tuple-element.27), channel_id=1, replica_groups=mesh['z'=8,'core'=2,'y'=4,'x'=4] {'x','y'}, dimensions={0} | all-to-all | bytes 2490368 | tf_op jit(solution)/shard_map/all_to_all | solution.py:56
  61.6 0.2 sum.1
  61.8 8.7 %collective-permute-start.1 = (f32[16,16]{1,0:T(8,128)S(1)}, f32[16,16]{1,0:T(8,128)S(1)}, u32[]{:S(2)}, u32[]{:S(2)}) collective-permute-start(f32[16,16]{1,0:T(8,128)S(1)} %get-tuple-element.29), channel_id=1, source_target_pairs={{0,0},{17,1},{34,2},{51,3},{68,4},{85,5},{102,6},{119,7},{136,8},{... | collective-permute-start | bytes 3080 | tf_op jit(solution)/shard_map/ppermute | solution.py:384
  70.4 1.3 collective-permute-done.1.logit_ref
  71.8 0.2 row.1
  71.9 21.3 %all_to_all.17.t_ref = bf16[16,288,128]{2,1,0:T(8,128)(2,1)S(1)} all-to-all(bf16[16,288,128]{2,1,0:T(8,128)(2,1)S(1)} %row.1), channel_id=1, replica_groups=mesh['z'=8,'core'=2,'y'=4,'x'=4] {'x','y'}, dimensions={0} | all-to-all | bytes 2359296 | tf_op jit(solution)/shard_map/all_to_all | solution.py:56
  93.3 4.0 %backward.1 = (f32[1,16]{1,0:T(1,128)}, f32[16,128]{1,0:T(8,128)S(1)}, bf16[256,2048]{1,0:T(8,128)(2,1)S(1)}) custom-call(bf16[16,416,128]{2,1,0:T(8,128)(2,1)S(1)} %all_to_all.15.in_ref.q_ref.mixed_ref, bf16[16,288,128]{2,1,0:T(8,128)(2,1)S(1)} %all_to_all.17.t_ref, f32[96,128]{1,0:T(8,128)S(1)} %get-tuple-element.30.rs_ref, ...), custom_call_target="tpu_custom_call" | custom-call | tf_op jit(solution)/shard_map/backward/pallas_call | solution.py:425
  97.3 1.5 %parts.1 = (bf16[2,320,128]{2,1,0:T(8,128)(2,1)S(1)}, bf16[2,320,128]{2,1,0:T(8,128)(2,1)S(1)}, bf16[2,320,128]{2,1,0:T(8,128)(2,1)S(1)}, bf16[2,320,128]{2,1,0:T(8,128)(2,1)S(1)}, bf16[8,320,128]{2,1,0:T(8,128)(2,1)S(1)}) custom-call(bf16[256,2048]{1,0:T(8,128)(2,1)S(1)} %get-tuple-element.35.gs_ref, f32[16,128]{1,0:T(8,128)S(1)} %get-tuple-element.36.grads_ref, ...), custom_call_target="tpu_custom_call" | custom-call | tf_op jit(solution)/shard_map/parts/pallas_call | solution.py:435
  98.8 0.3 collective-permute-start.2
  99.1 2.1 %collective-permute-done.2.other_ref = bf16[8,320,128]{2,1,0:T(8,128)(2,1)S(1)} collective-permute-done((bf16[8,320,128]{2,1,0:T(8,128)(2,1)S(1)}, bf16[8,320,128]{2,1,0:T(8,128)(2,1)S(1)}, u32[]{:S(2)}, u32[]{:S(2)}) %collective-permute-start.2) | collective-permute-done | bytes 655392 | tf_op jit(solution)/shard_map/ppermute | solution.py:444
  101.2 0.2 cores.1
  101.3 1.1 collective-permute-start.3
  102.4 2.7 %collective-permute-start.4 = (bf16[2,320,128]{2,1,0:T(8,128)(2,1)S(1)}, bf16[2,320,128]{2,1,0:T(8,128)(2,1)S(1)}, u32[]{:S(2)}, u32[]{:S(2)}) collective-permute-start(bf16[2,320,128]{2,1,0:T(8,128)(2,1)S(1)} %get-tuple-element.45), channel_id=1, source_target_pairs={{0,224},{16,240},{32,0},{48,16},{64,32},{80,48},{96,64},{112,80},{... | collective-permute-start | bytes 491528 | tf_op jit(solution)/shard_map/ppermute | solution.py:369
  105.1 4.4 %collective-permute-done.3.o1 = bf16[2,320,128]{2,1,0:T(8,128)(2,1)S(1)} collective-permute-done((bf16[2,320,128]{2,1,0:T(8,128)(2,1)S(1)}, bf16[2,320,128]{2,1,0:T(8,128)(2,1)S(1)}, u32[]{:S(2)}, u32[]{:S(2)}) %collective-permute-start.3) | collective-permute-done | bytes 163872 | tf_op jit(solution)/shard_map/ppermute | solution.py:369
  109.5 0.8 collective-permute-done.4.o2
  110.3 2.9 %collective-permute-done.5.o3 = bf16[2,320,128]{2,1,0:T(8,128)(2,1)S(1)} collective-permute-done((bf16[2,320,128]{2,1,0:T(8,128)(2,1)S(1)}, bf16[2,320,128]{2,1,0:T(8,128)(2,1)S(1)}, u32[]{:S(2)}, u32[]{:S(2)}) %collective-permute-start.5) | collective-permute-done | bytes 163872 | tf_op jit(solution)/shard_map/ppermute | solution.py:369
  113.2 0.1 chips.1
  113.2 5.7 %collective-permute-start.6 = (bf16[320,128]{1,0:T(8,128)(2,1)S(1)}, bf16[320,128]{1,0:T(8,128)(2,1)S(1)}, u32[]{:S(2)}, u32[]{:S(2)}) collective-permute-start(bf16[320,128]{1,0:T(8,128)(2,1)S(1)} %get-tuple-element.47), channel_id=1, source_target_pairs={{0,0},{1,17},{2,34},{3,51},{4,68},{5,85},{6,102},{7,119},{8,136},{... | collective-permute-start | bytes 245768 | tf_op jit(solution)/shard_map/ppermute | solution.py:379
  119.0 6.2 %collective-permute-start.7 = (bf16[320,128]{1,0:T(8,128)(2,1)S(1)}, bf16[320,128]{1,0:T(8,128)(2,1)S(1)}, u32[]{:S(2)}, u32[]{:S(2)}) collective-permute-start(bf16[320,128]{1,0:T(8,128)(2,1)S(1)} %get-tuple-element.48), channel_id=1, source_target_pairs={{0,8},{1,25},{2,42},{3,59},{4,76},{5,93},{6,110},{7,127},{8,128},{... | collective-permute-start | bytes 245768 | tf_op jit(solution)/shard_map/ppermute | solution.py:379
  125.2 1.6 %references.1 = f32[2,320,128]{2,1,0:T(8,128)} custom-call(bf16[256,2048]{1,0:T(8,128)(2,1)S(1)} %get-tuple-element.35.gs_ref, bf16[16,416,128]{2,1,0:T(8,128)(2,1)S(1)} %all_to_all.15.in_ref.q_ref.mixed_ref, bf16[16,160,128]{2,1,0:T(8,128)(2,1)S(1)} %collective-permute-done.other_ref), custom_call_target="tpu_custom_call" | custom-call | flops 335544320 | bytes 1048576 | tf_op jit(solution)/shard_map/references/pallas_call | solution.py:450
  126.8 0.0 collective-permute-done.6.u0
  126.8 10.2 %collective-permute-done.7.u1 = bf16[320,128]{1,0:T(8,128)(2,1)S(1)} collective-permute-done((bf16[320,128]{1,0:T(8,128)(2,1)S(1)}, bf16[320,128]{1,0:T(8,128)(2,1)S(1)}, u32[]{:S(2)}, u32[]{:S(2)}) %collective-permute-start.7) | collective-permute-done | bytes 81952 | tf_op jit(solution)/shard_map/ppermute | solution.py:379
  137.1 0.7 last.1
  (10 shorter events, 0.1 us)
Async XLA Ops:
  0.6 1.3 copy-start.2
  2.6 1.7 %copy-start = (bf16[2,128,5120]{2,1,0:T(8,128)(2,1)S(1)}, bf16[2,128,5120]{2,1,0:T(8,128)(2,1)}, u32[]{:S(2)}) copy-start(bf16[2,128,5120]{2,1,0:T(8,128)(2,1)} %param.6) | copy-start | bytes 7864324
  33.4 1.4 %copy-start.3 = (bf16[2,320,10]{1,0,2:T(2,128)(2,1)S(1)}, bf16[2,320,10]{1,0,2:T(2,128)(2,1)}, u32[]{:S(2)}) copy-start(bf16[2,320,10]{1,0,2:T(2,128)(2,1)} %param.7) | copy-start | bytes 38404
  33.5 3.2 %collective-permute-start = (bf16[16,160,128]{2,1,0:T(8,128)(2,1)S(1)}, bf16[16,160,128]{2,1,0:T(8,128)(2,1)S(1)}, u32[]{:S(2)}, u32[]{:S(2)}) collective-permute-start(bf16[16,160,128]{2,1,0:T(8,128)(2,1)S(1)} %peel.1), channel_id=1, source_target_pairs={{0,16},{16,0},{1,17},{17,1},{2,18},{18,2},{3,19},{19,3},{4,20},{20... | collective-permute-start | bytes 1966088 | tf_op jit(solution)/shard_map/ppermute | solution.py:403
  61.8 10.0 %collective-permute-start.1 = (f32[16,16]{1,0:T(8,128)S(1)}, f32[16,16]{1,0:T(8,128)S(1)}, u32[]{:S(2)}, u32[]{:S(2)}) collective-permute-start(f32[16,16]{1,0:T(8,128)S(1)} %get-tuple-element.29), channel_id=1, source_target_pairs={{0,0},{17,1},{34,2},{51,3},{68,4},{85,5},{102,6},{119,7},{136,8},{... | collective-permute-start | bytes 3080 | tf_op jit(solution)/shard_map/ppermute | solution.py:384
  93.3 4.0 %copy-start.1 = (bf16[2,128,5120]{2,1,0:T(8,128)(2,1)S(1)}, bf16[2,128,5120]{2,1,0:T(8,128)(2,1)}, u32[]{:S(2)}) copy-start(bf16[2,128,5120]{2,1,0:T(8,128)(2,1)} %param.6) | copy-start | bytes 7864324
  98.8 2.4 %collective-permute-start.2 = (bf16[8,320,128]{2,1,0:T(8,128)(2,1)S(1)}, bf16[8,320,128]{2,1,0:T(8,128)(2,1)S(1)}, u32[]{:S(2)}, u32[]{:S(2)}) collective-permute-start(bf16[8,320,128]{2,1,0:T(8,128)(2,1)S(1)} %get-tuple-element.42), channel_id=1, source_target_pairs={{0,16},{16,0},{1,17},{17,1},{2,18},{18,2},{3,19},{19,3},{4,20},{20... | collective-permute-start | bytes 1966088 | tf_op jit(solution)/shard_map/ppermute | solution.py:444
  101.3 8.2 %collective-permute-start.3 = (bf16[2,320,128]{2,1,0:T(8,128)(2,1)S(1)}, bf16[2,320,128]{2,1,0:T(8,128)(2,1)S(1)}, u32[]{:S(2)}, u32[]{:S(2)}) collective-permute-start(bf16[2,320,128]{2,1,0:T(8,128)(2,1)S(1)} %get-tuple-element.44), channel_id=1, source_target_pairs={{0,32},{16,48},{32,64},{48,80},{64,96},{80,112},{96,128},{112,144}... | collective-permute-start | bytes 491528 | tf_op jit(solution)/shard_map/ppermute | solution.py:369
  102.4 7.9 %collective-permute-start.4 = (bf16[2,320,128]{2,1,0:T(8,128)(2,1)S(1)}, bf16[2,320,128]{2,1,0:T(8,128)(2,1)S(1)}, u32[]{:S(2)}, u32[]{:S(2)}) collective-permute-start(bf16[2,320,128]{2,1,0:T(8,128)(2,1)S(1)} %get-tuple-element.45), channel_id=1, source_target_pairs={{0,224},{16,240},{32,0},{48,16},{64,32},{80,48},{96,64},{112,80},{... | collective-permute-start | bytes 491528 | tf_op jit(solution)/shard_map/ppermute | solution.py:369
  105.1 8.0 %collective-permute-start.5 = (bf16[2,320,128]{2,1,0:T(8,128)(2,1)S(1)}, bf16[2,320,128]{2,1,0:T(8,128)(2,1)S(1)}, u32[]{:S(2)}, u32[]{:S(2)}) collective-permute-start(bf16[2,320,128]{2,1,0:T(8,128)(2,1)S(1)} %get-tuple-element.46), channel_id=1, source_target_pairs={{0,64},{16,208},{32,96},{48,240},{64,128},{80,16},{96,160},{112,48... | collective-permute-start | bytes 491528 | tf_op jit(solution)/shard_map/ppermute | solution.py:369
  113.2 13.6 %collective-permute-start.6 = (bf16[320,128]{1,0:T(8,128)(2,1)S(1)}, bf16[320,128]{1,0:T(8,128)(2,1)S(1)}, u32[]{:S(2)}, u32[]{:S(2)}) collective-permute-start(bf16[320,128]{1,0:T(8,128)(2,1)S(1)} %get-tuple-element.47), channel_id=1, source_target_pairs={{0,0},{1,17},{2,34},{3,51},{4,68},{5,85},{6,102},{7,119},{8,136},{... | collective-permute-start | bytes 245768 | tf_op jit(solution)/shard_map/ppermute | solution.py:379
  119.0 18.1 %collective-permute-start.7 = (bf16[320,128]{1,0:T(8,128)(2,1)S(1)}, bf16[320,128]{1,0:T(8,128)(2,1)S(1)}, u32[]{:S(2)}, u32[]{:S(2)}) collective-permute-start(bf16[320,128]{1,0:T(8,128)(2,1)S(1)} %get-tuple-element.48), channel_id=1, source_target_pairs={{0,8},{1,25},{2,42},{3,59},{4,76},{5,93},{6,110},{7,127},{8,128},{... | collective-permute-start | bytes 245768 | tf_op jit(solution)/shard_map/ppermute | solution.py:379

commit v9 on v8

--- a/solution.py
+++ b/solution.py
@@ -60,7 +60,7 @@
     return j % SIDE * SIDE + j // SIDE
 
 
-def split_kernel(f_ref, out_ref, turned_ref):
+def split_kernel(f_ref, len_ref, label_ref, out_ref, turned_ref):
     half = out_ref.shape[1]
     part = 2 * half
     for j in range(BLOCKS // 2):
@@ -292,15 +292,19 @@
                 put(grs_ref, t, s, grad_rowsum)
                 if t > 0:
                     acc = acc + k * grad_rowsum
+        gain = score_scale * col_ref[ITERS - 1, here, :] * first
+        loss = score_scale * col_ref[ITERS - 1, here, :] * second
+        for t in range(ITERS):
+            gt_ref[t] = score_scale * gt_ref[t]
         for s in range(BLOCKS):
-            total = row(rs_ref, ITERS - 1, s) * col_ref[ITERS - 1, here, :] * grad_plan(s, row(u_ref, 0, s))
-            for t in range(ITERS):
+            inner = gain * row(u_ref, 0, s) - loss * t_ref[at(s), here, :].astype(f32) + gt_ref[ITERS - 1]
+            total = row(rs_ref, ITERS - 1, s) * inner
+            for t in range(ITERS - 1):
                 total = total + row(rs_ref, t, s) * gt_ref[t]
-                if t > 0:
-                    total = total + row(grs_ref, t, s) * col_ref[t - 1, here, :]
-                else:
-                    total = total + row(grs_ref, t, s)
-            gs_ref[here, s * rows : (s + 1) * rows] = (score_scale * total * load(s)).astype(bf16)
+                total = total + (score_scale * row(grs_ref, t + 1, s)) * col_ref[t, here, :]
+            total = total + score_scale * row(grs_ref, 0, s)
+            value = (total * load(s)).astype(bf16)
+            gs_ref[here, s * rows : (s + 1) * rows] = value
 
 
 def parts_kernel(
@@ -395,15 +399,18 @@
 
     half = part // 2
     halves = kind((BLOCKS, half, rows), bf16)
-    split = call(split_kernel, "split", halves, 1, scratch=[pltpu.VMEM((width, rows), bf16)])(feats)
+    split = call(
+        split_kernel, "split", halves, [VMEM, SMEM, SMEM], scratch=[pltpu.VMEM((width, rows), bf16)], flops=3 * 10**9
+    )(feats, lengths, labels)
     mixed = call(
         functools.partial(scores_kernel, score_scale), "scores", kind((BLOCKS, half + REFS, rows), bf16), 3
     )(feats, refs, split)
+    weights = jnp.pad(jnp.transpose(classifier, (0, 2, 1)), ((0, 0), (0, PAD - CLASSES), (0, 0)))
+    weights = weights.reshape(HEADS * PAD, part)
+
+    mixed, weights = lax.optimization_barrier((mixed, weights))
     mixed = exchange(mixed)
     other = lax.ppermute(call(peel_kernel, "peel", halves, 1)(mixed), "core", [(0, 1), (1, 0)])
-    weights = jnp.pad(jnp.transpose(classifier, (0, 2, 1)), ((0, 0), (0, PAD - CLASSES), (0, 0)))
-    weights = weights.reshape(HEADS * PAD, part)
-
     scales = kind((ITERS * HEADS * BLOCKS, rows), f32)
     rs, rt, col, plan = call(
         sinkhorn_kernel, "sinkhorn",

time: 138 us -> 138 us (level)
    unnamed x9 -> x5, local copies, waits for them, and re-layouts: 3.06 us -> 3.12 us
  transfers between devices with their start and end apart: 8 -> 8, of which waited for: 6 -> 7; matrix products, arithmetic and copies ran while one was open for 0% -> 0% of each run, Pallas kernels for 2% -> 2%
where the time goes in v9:
time: 138 us; the launch traced here: 137 us
  blocking collectives  72.4 us (52%)
  starting transfers between devices  24.8 us (18%)
  waiting for transfers between devices  21.6 us (16%)
  Pallas kernels  13.3 us (10%)
  local copies, waits for them, and re-layouts  3.13 us (2%)
  between operations  2.05 us (1%)
    all_to_all x3, blocking collectives, exchange(): return lax.all_to_all(value, ('x', 'y'), 0, 0)  72.4 us
    ppermute x2, starting transfers between devices, to_place(): return lax.ppermute(value, ('z', 'core', 'y', 'x'), pairs)  12 us
    ppermute x2, waiting for transfers between devices, to_place(): return lax.ppermute(value, ('z', 'core', 'y', 'x'), pairs)  10.2 us
    ppermute x1, starting transfers between devices, spread_logits(): return lax.ppermute(value, ('z', 'core', 'y', 'x'), pairs)  8.65 us
    ppermute x3, waiting for transfers between devices, along_z(): return lax.ppermute(value, ('z', 'core'), pairs)  7.68 us
    pallas_call x1, Pallas kernels, local(): call(functools.partial(backward_kernel, width, score_scale), 'backward',...  3.98 us
    ppermute x3, starting transfers between devices, along_z(): return lax.ppermute(value, ('z', 'core'), pairs)  3.71 us
    unnamed x5, local copies, waits for them, and re-layouts  3.12 us
  transfers between devices with their start and end apart: 8, of which 7 were waited for; matrix products, arithmetic and copies ran while one was open for 0% of the time, Pallas kernels for 2%

profile of v9, /device:TPU:12, one launch (start us, length us, event | category | flops | bytes accessed | tf_op | source)
XLA Modules:
  0.0 137.3 jit_solution(8140353960529846107)
XLA Ops:
  1.9 0.7 copy.9
  2.7 1.3 copy-done.1
  4.0 0.6 split.1.half_ref
  4.6 1.1 copy-done
  5.7 0.9 scores.1
  6.6 28.2 %all_to_all.15.in_ref.q_ref.mixed_ref = bf16[16,416,128]{2,1,0:T(8,128)(2,1)S(1)} all-to-all(bf16[16,416,128]{2,1,0:T(8,128)(2,1)S(1)} %scores.1), channel_id=1, replica_groups=mesh['z'=8,'core'=2,'y'=4,'x'=4] {'x','y'}, dimensions={0} | all-to-all | bytes 3407872 | tf_op jit(solution)/shard_map/all_to_all | solution.py:56
  34.8 0.1 collective-permute-start
  34.9 1.7 %sinkhorn.1 = (f32[96,128]{1,0:T(8,128)S(1)}, f32[96,128]{1,0:T(8,128)S(1)}, f32[3,256,128]{2,1,0:T(8,128)S(1)}, bf16[256,2048]{1,0:T(8,128)(2,1)S(1)}) custom-call(bf16[16,416,128]{2,1,0:T(8,128)(2,1)S(1)} %all_to_all.15.in_ref.q_ref.mixed_ref, s32[1]{0:T(128)S(6)} %copy.10.len_ref, s32[1]{0:T(128)S(6)} %copy.11.label_ref), custom_call_target="tpu_custom_call" | custom-call | tf_op jit(solution)/shard_map/sinkhorn/pallas_call | solution.py:415
  36.7 0.3 collective-permute-done.other_ref
  37.0 1.7 %forward.1 = (bf16[16,304,128]{2,1,0:T(8,128)(2,1)S(1)}, f32[256,320]{1,0:T(8,128)S(1)}) custom-call(bf16[16,416,128]{2,1,0:T(8,128)(2,1)S(1)} %all_to_all.15.in_ref.q_ref.mixed_ref, bf16[16,160,128]{2,1,0:T(8,128)(2,1)S(1)} %collective-permute-done.other_ref, bf16[32,320]{1,0:T(8,128)(2,1)S(1)} %bitcast.13, bf16[256,2048]{1,0:T(8,128)(2,1)S(1)} %get-tuple-element.30.plan_ref), custom_call_target="tpu_custom_call" | custom-call | tf_op jit(solution)/shard_map/forward/pallas_call | solution.py:419
  38.7 22.8 %all_to_all.16.in_ref = bf16[16,304,128]{2,1,0:T(8,128)(2,1)S(1)} all-to-all(bf16[16,304,128]{2,1,0:T(8,128)(2,1)S(1)} %get-tuple-element.31), channel_id=1, replica_groups=mesh['z'=8,'core'=2,'y'=4,'x'=4] {'x','y'}, dimensions={0} | all-to-all | bytes 2490368 | tf_op jit(solution)/shard_map/all_to_all | solution.py:56
  61.5 0.2 sum.1
  61.7 8.7 %collective-permute-start.1 = (f32[16,16]{1,0:T(8,128)S(1)}, f32[16,16]{1,0:T(8,128)S(1)}, u32[]{:S(2)}, u32[]{:S(2)}) collective-permute-start(f32[16,16]{1,0:T(8,128)S(1)} %get-tuple-element.33), channel_id=1, source_target_pairs={{0,0},{17,1},{34,2},{51,3},{68,4},{85,5},{102,6},{119,7},{136,8},{... | collective-permute-start | bytes 3080 | tf_op jit(solution)/shard_map/ppermute | solution.py:388
  70.3 1.3 collective-permute-done.1.logit_ref
  71.7 0.2 row.1
  71.8 21.4 %all_to_all.17.t_ref = bf16[16,288,128]{2,1,0:T(8,128)(2,1)S(1)} all-to-all(bf16[16,288,128]{2,1,0:T(8,128)(2,1)S(1)} %row.1), channel_id=1, replica_groups=mesh['z'=8,'core'=2,'y'=4,'x'=4] {'x','y'}, dimensions={0} | all-to-all | bytes 2359296 | tf_op jit(solution)/shard_map/all_to_all | solution.py:56
  93.3 4.0 %backward.1 = (f32[1,16]{1,0:T(1,128)}, f32[16,128]{1,0:T(8,128)S(1)}, bf16[256,2048]{1,0:T(8,128)(2,1)S(1)}) custom-call(bf16[16,416,128]{2,1,0:T(8,128)(2,1)S(1)} %all_to_all.15.in_ref.q_ref.mixed_ref, bf16[16,288,128]{2,1,0:T(8,128)(2,1)S(1)} %all_to_all.17.t_ref, f32[96,128]{1,0:T(8,128)S(1)} %get-tuple-element.34.rs_ref, ...), custom_call_target="tpu_custom_call" | custom-call | tf_op jit(solution)/shard_map/backward/pallas_call | solution.py:432
  97.2 1.5 %parts.1 = (bf16[2,320,128]{2,1,0:T(8,128)(2,1)S(1)}, bf16[2,320,128]{2,1,0:T(8,128)(2,1)S(1)}, bf16[2,320,128]{2,1,0:T(8,128)(2,1)S(1)}, bf16[2,320,128]{2,1,0:T(8,128)(2,1)S(1)}, bf16[8,320,128]{2,1,0:T(8,128)(2,1)S(1)}) custom-call(bf16[256,2048]{1,0:T(8,128)(2,1)S(1)} %get-tuple-element.39.gs_ref, f32[16,128]{1,0:T(8,128)S(1)} %get-tuple-element.40.grads_ref, ...), custom_call_target="tpu_custom_call" | custom-call | tf_op jit(solution)/shard_map/parts/pallas_call | solution.py:442
  98.8 0.3 collective-permute-start.2
  99.0 2.1 %collective-permute-done.2.other_ref = bf16[8,320,128]{2,1,0:T(8,128)(2,1)S(1)} collective-permute-done((bf16[8,320,128]{2,1,0:T(8,128)(2,1)S(1)}, bf16[8,320,128]{2,1,0:T(8,128)(2,1)S(1)}, u32[]{:S(2)}, u32[]{:S(2)}) %collective-permute-start.2) | collective-permute-done | bytes 655392 | tf_op jit(solution)/shard_map/ppermute | solution.py:451
  101.1 0.2 cores.1
  101.3 1.1 collective-permute-start.3
  102.4 2.3 %collective-permute-start.4 = (bf16[2,320,128]{2,1,0:T(8,128)(2,1)S(1)}, bf16[2,320,128]{2,1,0:T(8,128)(2,1)S(1)}, u32[]{:S(2)}, u32[]{:S(2)}) collective-permute-start(bf16[2,320,128]{2,1,0:T(8,128)(2,1)S(1)} %get-tuple-element.49), channel_id=1, source_target_pairs={{0,224},{16,240},{32,0},{48,16},{64,32},{80,48},{96,64},{112,80},{... | collective-permute-start | bytes 491528 | tf_op jit(solution)/shard_map/ppermute | solution.py:373
  104.7 0.3 collective-permute-start.5
  105.0 4.1 %collective-permute-done.3.o1 = bf16[2,320,128]{2,1,0:T(8,128)(2,1)S(1)} collective-permute-done((bf16[2,320,128]{2,1,0:T(8,128)(2,1)S(1)}, bf16[2,320,128]{2,1,0:T(8,128)(2,1)S(1)}, u32[]{:S(2)}, u32[]{:S(2)}) %collective-permute-start.3) | collective-permute-done | bytes 163872 | tf_op jit(solution)/shard_map/ppermute | solution.py:373
  109.1 1.2 collective-permute-done.4.o2
  110.3 2.3 %collective-permute-done.5.o3 = bf16[2,320,128]{2,1,0:T(8,128)(2,1)S(1)} collective-permute-done((bf16[2,320,128]{2,1,0:T(8,128)(2,1)S(1)}, bf16[2,320,128]{2,1,0:T(8,128)(2,1)S(1)}, u32[]{:S(2)}, u32[]{:S(2)}) %collective-permute-start.5) | collective-permute-done | bytes 163872 | tf_op jit(solution)/shard_map/ppermute | solution.py:373
  112.8 5.7 %collective-permute-start.6 = (bf16[320,128]{1,0:T(8,128)(2,1)S(1)}, bf16[320,128]{1,0:T(8,128)(2,1)S(1)}, u32[]{:S(2)}, u32[]{:S(2)}) collective-permute-start(bf16[320,128]{1,0:T(8,128)(2,1)S(1)} %get-tuple-element.51), channel_id=1, source_target_pairs={{0,0},{1,17},{2,34},{3,51},{4,68},{5,85},{6,102},{7,119},{8,136},{... | collective-permute-start | bytes 245768 | tf_op jit(solution)/shard_map/ppermute | solution.py:383
  118.5 6.3 %collective-permute-start.7 = (bf16[320,128]{1,0:T(8,128)(2,1)S(1)}, bf16[320,128]{1,0:T(8,128)(2,1)S(1)}, u32[]{:S(2)}, u32[]{:S(2)}) collective-permute-start(bf16[320,128]{1,0:T(8,128)(2,1)S(1)} %get-tuple-element.52), channel_id=1, source_target_pairs={{0,8},{1,25},{2,42},{3,59},{4,76},{5,93},{6,110},{7,127},{8,128},{... | collective-permute-start | bytes 245768 | tf_op jit(solution)/shard_map/ppermute | solution.py:383
  124.8 1.6 %references.1 = f32[2,320,128]{2,1,0:T(8,128)} custom-call(bf16[256,2048]{1,0:T(8,128)(2,1)S(1)} %get-tuple-element.39.gs_ref, bf16[16,416,128]{2,1,0:T(8,128)(2,1)S(1)} %all_to_all.15.in_ref.q_ref.mixed_ref, bf16[16,160,128]{2,1,0:T(8,128)(2,1)S(1)} %collective-permute-done.other_ref), custom_call_target="tpu_custom_call" | custom-call | flops 335544320 | bytes 1048576 | tf_op jit(solution)/shard_map/references/pallas_call | solution.py:457
  126.4 10.2 %collective-permute-done.7.u1 = bf16[320,128]{1,0:T(8,128)(2,1)S(1)} collective-permute-done((bf16[320,128]{1,0:T(8,128)(2,1)S(1)}, bf16[320,128]{1,0:T(8,128)(2,1)S(1)}, u32[]{:S(2)}, u32[]{:S(2)}) %collective-permute-start.7) | collective-permute-done | bytes 81952 | tf_op jit(solution)/shard_map/ppermute | solution.py:383
  136.6 0.7 last.1
  (6 shorter events, 0.1 us)
Async XLA Ops:
  2.7 1.3 copy-start.1
  4.0 1.7 %copy-start = (bf16[2,128,5120]{2,1,0:T(8,128)(2,1)S(1)}, bf16[2,128,5120]{2,1,0:T(8,128)(2,1)}, u32[]{:S(2)}) copy-start(bf16[2,128,5120]{2,1,0:T(8,128)(2,1)} %param.6) | copy-start | bytes 7864324
  34.8 2.2 %collective-permute-start = (bf16[16,160,128]{2,1,0:T(8,128)(2,1)S(1)}, bf16[16,160,128]{2,1,0:T(8,128)(2,1)S(1)}, u32[]{:S(2)}, u32[]{:S(2)}) collective-permute-start(bf16[16,160,128]{2,1,0:T(8,128)(2,1)S(1)} %peel.1), channel_id=1, source_target_pairs={{0,16},{16,0},{1,17},{17,1},{2,18},{18,2},{3,19},{19,3},{4,20},{20... | collective-permute-start | bytes 1966088 | tf_op jit(solution)/shard_map/ppermute | solution.py:413
  61.7 10.0 %collective-permute-start.1 = (f32[16,16]{1,0:T(8,128)S(1)}, f32[16,16]{1,0:T(8,128)S(1)}, u32[]{:S(2)}, u32[]{:S(2)}) collective-permute-start(f32[16,16]{1,0:T(8,128)S(1)} %get-tuple-element.33), channel_id=1, source_target_pairs={{0,0},{17,1},{34,2},{51,3},{68,4},{85,5},{102,6},{119,7},{136,8},{... | collective-permute-start | bytes 3080 | tf_op jit(solution)/shard_map/ppermute | solution.py:388
  98.8 2.4 %collective-permute-start.2 = (bf16[8,320,128]{2,1,0:T(8,128)(2,1)S(1)}, bf16[8,320,128]{2,1,0:T(8,128)(2,1)S(1)}, u32[]{:S(2)}, u32[]{:S(2)}) collective-permute-start(bf16[8,320,128]{2,1,0:T(8,128)(2,1)S(1)} %get-tuple-element.46), channel_id=1, source_target_pairs={{0,16},{16,0},{1,17},{17,1},{2,18},{18,2},{3,19},{19,3},{4,20},{20... | collective-permute-start | bytes 1966088 | tf_op jit(solution)/shard_map/ppermute | solution.py:451
  101.3 7.8 %collective-permute-start.3 = (bf16[2,320,128]{2,1,0:T(8,128)(2,1)S(1)}, bf16[2,320,128]{2,1,0:T(8,128)(2,1)S(1)}, u32[]{:S(2)}, u32[]{:S(2)}) collective-permute-start(bf16[2,320,128]{2,1,0:T(8,128)(2,1)S(1)} %get-tuple-element.48), channel_id=1, source_target_pairs={{0,32},{16,48},{32,64},{48,80},{64,96},{80,112},{96,128},{112,144}... | collective-permute-start | bytes 491528 | tf_op jit(solution)/shard_map/ppermute | solution.py:373
  102.4 8.0 %collective-permute-start.4 = (bf16[2,320,128]{2,1,0:T(8,128)(2,1)S(1)}, bf16[2,320,128]{2,1,0:T(8,128)(2,1)S(1)}, u32[]{:S(2)}, u32[]{:S(2)}) collective-permute-start(bf16[2,320,128]{2,1,0:T(8,128)(2,1)S(1)} %get-tuple-element.49), channel_id=1, source_target_pairs={{0,224},{16,240},{32,0},{48,16},{64,32},{80,48},{96,64},{112,80},{... | collective-permute-start | bytes 491528 | tf_op jit(solution)/shard_map/ppermute | solution.py:373
  104.7 8.0 %collective-permute-start.5 = (bf16[2,320,128]{2,1,0:T(8,128)(2,1)S(1)}, bf16[2,320,128]{2,1,0:T(8,128)(2,1)S(1)}, u32[]{:S(2)}, u32[]{:S(2)}) collective-permute-start(bf16[2,320,128]{2,1,0:T(8,128)(2,1)S(1)} %get-tuple-element.50), channel_id=1, source_target_pairs={{0,64},{16,208},{32,96},{48,240},{64,128},{80,16},{96,160},{112,48... | collective-permute-start | bytes 491528 | tf_op jit(solution)/shard_map/ppermute | solution.py:373
  112.8 13.7 %collective-permute-start.6 = (bf16[320,128]{1,0:T(8,128)(2,1)S(1)}, bf16[320,128]{1,0:T(8,128)(2,1)S(1)}, u32[]{:S(2)}, u32[]{:S(2)}) collective-permute-start(bf16[320,128]{1,0:T(8,128)(2,1)S(1)} %get-tuple-element.51), channel_id=1, source_target_pairs={{0,0},{1,17},{2,34},{3,51},{4,68},{5,85},{6,102},{7,119},{8,136},{... | collective-permute-start | bytes 245768 | tf_op jit(solution)/shard_map/ppermute | solution.py:383
  118.5 18.1 %collective-permute-start.7 = (bf16[320,128]{1,0:T(8,128)(2,1)S(1)}, bf16[320,128]{1,0:T(8,128)(2,1)S(1)}, u32[]{:S(2)}, u32[]{:S(2)}) collective-permute-start(bf16[320,128]{1,0:T(8,128)(2,1)S(1)} %get-tuple-element.52), channel_id=1, source_target_pairs={{0,8},{1,25},{2,42},{3,59},{4,76},{5,93},{6,110},{7,127},{8,128},{... | collective-permute-start | bytes 245768 | tf_op jit(solution)/shard_map/ppermute | solution.py:383

commit v10 on v9

--- a/solution.py
+++ b/solution.py
@@ -60,7 +60,7 @@
     return j % SIDE * SIDE + j // SIDE
 
 
-def split_kernel(f_ref, len_ref, label_ref, out_ref, turned_ref):
+def split_kernel(f_ref, out_ref, turned_ref):
     half = out_ref.shape[1]
     part = 2 * half
     for j in range(BLOCKS // 2):
@@ -399,18 +399,16 @@
 
     half = part // 2
     halves = kind((BLOCKS, half, rows), bf16)
-    split = call(
-        split_kernel, "split", halves, [VMEM, SMEM, SMEM], scratch=[pltpu.VMEM((width, rows), bf16)], flops=3 * 10**9
-    )(feats, lengths, labels)
+    split = call(split_kernel, "split", halves, 1, scratch=[pltpu.VMEM((width, rows), bf16)], flops=3 * 10**9)(feats)
     mixed = call(
         functools.partial(scores_kernel, score_scale), "scores", kind((BLOCKS, half + REFS, rows), bf16), 3
     )(feats, refs, split)
+    mixed = exchange(mixed)
+    other = lax.ppermute(call(peel_kernel, "peel", halves, 1)(mixed), "core", [(0, 1), (1, 0)])
     weights = jnp.pad(jnp.transpose(classifier, (0, 2, 1)), ((0, 0), (0, PAD - CLASSES), (0, 0)))
     weights = weights.reshape(HEADS * PAD, part)
 
-    mixed, weights = lax.optimization_barrier((mixed, weights))
-    mixed = exchange(mixed)
-    other = lax.ppermute(call(peel_kernel, "peel", halves, 1)(mixed), "core", [(0, 1), (1, 0)])
+
     scales = kind((ITERS * HEADS * BLOCKS, rows), f32)
     rs, rt, col, plan = call(
         sinkhorn_kernel, "sinkhorn",

time: 138 us -> 137 us (level)
    unnamed x5 -> x7, local copies, waits for them, and re-layouts: 3.12 us -> 2.41 us
  transfers between devices with their start and end apart: 8 -> 8, of which waited for: 7 -> 6; matrix products, arithmetic and copies ran while one was open for 0% -> 0% of each run, Pallas kernels for 2% -> 2%
where the time goes in v10:
time: 137 us
  blocking collectives  72.7 us (53%)
  starting transfers between devices  24.8 us (18%)
  waiting for transfers between devices  21.7 us (16%)
  Pallas kernels  13.3 us (10%)
  local copies, waits for them, and re-layouts  2.42 us (2%)
  between operations  2.08 us (2%)
    all_to_all x3, blocking collectives, exchange(): return lax.all_to_all(value, ('x', 'y'), 0, 0)  72.7 us
    ppermute x2, starting transfers between devices, to_place(): return lax.ppermute(value, ('z', 'core', 'y', 'x'), pairs)  12 us
    ppermute x2, waiting for transfers between devices, to_place(): return lax.ppermute(value, ('z', 'core', 'y', 'x'), pairs)  10.2 us
    ppermute x1, starting transfers between devices, spread_logits(): return lax.ppermute(value, ('z', 'core', 'y', 'x'), pairs)  8.65 us
    ppermute x3, waiting for transfers between devices, along_z(): return lax.ppermute(value, ('z', 'core'), pairs)  8.03 us
    pallas_call x1, Pallas kernels, local(): call(functools.partial(backward_kernel, width, score_scale), 'backward',...  3.98 us
    ppermute x3, starting transfers between devices, along_z(): return lax.ppermute(value, ('z', 'core'), pairs)  3.79 us
  transfers between devices with their start and end apart: 8, of which 6 were waited for; matrix products, arithmetic and copies ran while one was open for 0% of the time, Pallas kernels for 2%

profile of v10, /device:TPU:12, one launch (start us, length us, event | category | flops | bytes accessed | tf_op | source)
XLA Modules:
  0.0 137.0 jit_solution(636156469265797035)
XLA Ops:
  0.6 1.3 copy-done.1
  1.9 0.6 split.1.half_ref
  2.6 1.1 copy-done
  3.7 0.9 scores.1
  4.6 28.2 %all_to_all.15.in_ref.q_ref.mixed_ref = bf16[16,416,128]{2,1,0:T(8,128)(2,1)S(1)} all-to-all(bf16[16,416,128]{2,1,0:T(8,128)(2,1)S(1)} %scores.1), channel_id=1, replica_groups=mesh['z'=8,'core'=2,'y'=4,'x'=4] {'x','y'}, dimensions={0} | all-to-all | bytes 3407872 | tf_op jit(solution)/shard_map/all_to_all | solution.py:56
  32.8 0.1 collective-permute-start
  34.2 1.7 %sinkhorn.1 = (f32[96,128]{1,0:T(8,128)S(1)}, f32[96,128]{1,0:T(8,128)S(1)}, f32[3,256,128]{2,1,0:T(8,128)S(1)}, bf16[256,2048]{1,0:T(8,128)(2,1)S(1)}) custom-call(bf16[16,416,128]{2,1,0:T(8,128)(2,1)S(1)} %all_to_all.15.in_ref.q_ref.mixed_ref, s32[1]{0:T(128)S(6)} %copy.10.len_ref, s32[1]{0:T(128)S(6)} %copy.11.label_ref), custom_call_target="tpu_custom_call" | custom-call | tf_op jit(solution)/shard_map/sinkhorn/pallas_call | solution.py:413
  36.0 0.0 collective-permute-done.other_ref
  36.0 1.7 %forward.1 = (bf16[16,304,128]{2,1,0:T(8,128)(2,1)S(1)}, f32[256,320]{1,0:T(8,128)S(1)}) custom-call(bf16[16,416,128]{2,1,0:T(8,128)(2,1)S(1)} %all_to_all.15.in_ref.q_ref.mixed_ref, bf16[16,160,128]{2,1,0:T(8,128)(2,1)S(1)} %collective-permute-done.other_ref, bf16[32,320]{1,0:T(8,128)(2,1)S(1)} %bitcast.13, bf16[256,2048]{1,0:T(8,128)(2,1)S(1)} %get-tuple-element.26.plan_ref), custom_call_target="tpu_custom_call" | custom-call | tf_op jit(solution)/shard_map/forward/pallas_call | solution.py:417
  37.7 23.2 %all_to_all.16.in_ref = bf16[16,304,128]{2,1,0:T(8,128)(2,1)S(1)} all-to-all(bf16[16,304,128]{2,1,0:T(8,128)(2,1)S(1)} %get-tuple-element.27), channel_id=1, replica_groups=mesh['z'=8,'core'=2,'y'=4,'x'=4] {'x','y'}, dimensions={0} | all-to-all | bytes 2490368 | tf_op jit(solution)/shard_map/all_to_all | solution.py:56
  60.9 0.2 sum.1
  61.1 8.7 %collective-permute-start.1 = (f32[16,16]{1,0:T(8,128)S(1)}, f32[16,16]{1,0:T(8,128)S(1)}, u32[]{:S(2)}, u32[]{:S(2)}) collective-permute-start(f32[16,16]{1,0:T(8,128)S(1)} %get-tuple-element.29), channel_id=1, source_target_pairs={{0,0},{17,1},{34,2},{51,3},{68,4},{85,5},{102,6},{119,7},{136,8},{... | collective-permute-start | bytes 3080 | tf_op jit(solution)/shard_map/ppermute | solution.py:388
  69.7 1.3 collective-permute-done.1.logit_ref
  71.1 0.2 row.1
  71.2 21.4 %all_to_all.17.t_ref = bf16[16,288,128]{2,1,0:T(8,128)(2,1)S(1)} all-to-all(bf16[16,288,128]{2,1,0:T(8,128)(2,1)S(1)} %row.1), channel_id=1, replica_groups=mesh['z'=8,'core'=2,'y'=4,'x'=4] {'x','y'}, dimensions={0} | all-to-all | bytes 2359296 | tf_op jit(solution)/shard_map/all_to_all | solution.py:56
  92.6 4.0 %backward.1 = (f32[1,16]{1,0:T(1,128)}, f32[16,128]{1,0:T(8,128)S(1)}, bf16[256,2048]{1,0:T(8,128)(2,1)S(1)}) custom-call(bf16[16,416,128]{2,1,0:T(8,128)(2,1)S(1)} %all_to_all.15.in_ref.q_ref.mixed_ref, bf16[16,288,128]{2,1,0:T(8,128)(2,1)S(1)} %all_to_all.17.t_ref, f32[96,128]{1,0:T(8,128)S(1)} %get-tuple-element.30.rs_ref, ...), custom_call_target="tpu_custom_call" | custom-call | tf_op jit(solution)/shard_map/backward/pallas_call | solution.py:430
  96.6 1.5 %parts.1 = (bf16[2,320,128]{2,1,0:T(8,128)(2,1)S(1)}, bf16[2,320,128]{2,1,0:T(8,128)(2,1)S(1)}, bf16[2,320,128]{2,1,0:T(8,128)(2,1)S(1)}, bf16[2,320,128]{2,1,0:T(8,128)(2,1)S(1)}, bf16[8,320,128]{2,1,0:T(8,128)(2,1)S(1)}) custom-call(bf16[256,2048]{1,0:T(8,128)(2,1)S(1)} %get-tuple-element.35.gs_ref, f32[16,128]{1,0:T(8,128)S(1)} %get-tuple-element.36.grads_ref, ...), custom_call_target="tpu_custom_call" | custom-call | tf_op jit(solution)/shard_map/parts/pallas_call | solution.py:440
  98.1 0.3 collective-permute-start.2
  98.4 2.1 %collective-permute-done.2.other_ref = bf16[8,320,128]{2,1,0:T(8,128)(2,1)S(1)} collective-permute-done((bf16[8,320,128]{2,1,0:T(8,128)(2,1)S(1)}, bf16[8,320,128]{2,1,0:T(8,128)(2,1)S(1)}, u32[]{:S(2)}, u32[]{:S(2)}) %collective-permute-start.2) | collective-permute-done | bytes 655392 | tf_op jit(solution)/shard_map/ppermute | solution.py:449
  100.4 0.2 cores.1
  100.6 1.1 collective-permute-start.3
  101.7 2.7 %collective-permute-start.4 = (bf16[2,320,128]{2,1,0:T(8,128)(2,1)S(1)}, bf16[2,320,128]{2,1,0:T(8,128)(2,1)S(1)}, u32[]{:S(2)}, u32[]{:S(2)}) collective-permute-start(bf16[2,320,128]{2,1,0:T(8,128)(2,1)S(1)} %get-tuple-element.45), channel_id=1, source_target_pairs={{0,224},{16,240},{32,0},{48,16},{64,32},{80,48},{96,64},{112,80},{... | collective-permute-start | bytes 491528 | tf_op jit(solution)/shard_map/ppermute | solution.py:373
  104.4 0.0 collective-permute-start.5
  104.4 4.4 %collective-permute-done.3.o1 = bf16[2,320,128]{2,1,0:T(8,128)(2,1)S(1)} collective-permute-done((bf16[2,320,128]{2,1,0:T(8,128)(2,1)S(1)}, bf16[2,320,128]{2,1,0:T(8,128)(2,1)S(1)}, u32[]{:S(2)}, u32[]{:S(2)}) %collective-permute-start.3) | collective-permute-done | bytes 163872 | tf_op jit(solution)/shard_map/ppermute | solution.py:373
  108.8 0.8 collective-permute-done.4.o2
  109.6 2.9 %collective-permute-done.5.o3 = bf16[2,320,128]{2,1,0:T(8,128)(2,1)S(1)} collective-permute-done((bf16[2,320,128]{2,1,0:T(8,128)(2,1)S(1)}, bf16[2,320,128]{2,1,0:T(8,128)(2,1)S(1)}, u32[]{:S(2)}, u32[]{:S(2)}) %collective-permute-start.5) | collective-permute-done | bytes 163872 | tf_op jit(solution)/shard_map/ppermute | solution.py:373
  112.4 0.1 chips.1
  112.5 5.7 %collective-permute-start.6 = (bf16[320,128]{1,0:T(8,128)(2,1)S(1)}, bf16[320,128]{1,0:T(8,128)(2,1)S(1)}, u32[]{:S(2)}, u32[]{:S(2)}) collective-permute-start(bf16[320,128]{1,0:T(8,128)(2,1)S(1)} %get-tuple-element.47), channel_id=1, source_target_pairs={{0,0},{1,17},{2,34},{3,51},{4,68},{5,85},{6,102},{7,119},{8,136},{... | collective-permute-start | bytes 245768 | tf_op jit(solution)/shard_map/ppermute | solution.py:383
  118.3 6.2 %collective-permute-start.7 = (bf16[320,128]{1,0:T(8,128)(2,1)S(1)}, bf16[320,128]{1,0:T(8,128)(2,1)S(1)}, u32[]{:S(2)}, u32[]{:S(2)}) collective-permute-start(bf16[320,128]{1,0:T(8,128)(2,1)S(1)} %get-tuple-element.48), channel_id=1, source_target_pairs={{0,8},{1,25},{2,42},{3,59},{4,76},{5,93},{6,110},{7,127},{8,128},{... | collective-permute-start | bytes 245768 | tf_op jit(solution)/shard_map/ppermute | solution.py:383
  124.5 1.6 %references.1 = f32[2,320,128]{2,1,0:T(8,128)} custom-call(bf16[256,2048]{1,0:T(8,128)(2,1)S(1)} %get-tuple-element.35.gs_ref, bf16[16,416,128]{2,1,0:T(8,128)(2,1)S(1)} %all_to_all.15.in_ref.q_ref.mixed_ref, bf16[16,160,128]{2,1,0:T(8,128)(2,1)S(1)} %collective-permute-done.other_ref), custom_call_target="tpu_custom_call" | custom-call | flops 335544320 | bytes 1048576 | tf_op jit(solution)/shard_map/references/pallas_call | solution.py:455
  126.1 10.2 %collective-permute-done.7.u1 = bf16[320,128]{1,0:T(8,128)(2,1)S(1)} collective-permute-done((bf16[320,128]{1,0:T(8,128)(2,1)S(1)}, bf16[320,128]{1,0:T(8,128)(2,1)S(1)}, u32[]{:S(2)}, u32[]{:S(2)}) %collective-permute-start.7) | collective-permute-done | bytes 81952 | tf_op jit(solution)/shard_map/ppermute | solution.py:383
  136.3 0.7 last.1
  (8 shorter events, 0.1 us)
Async XLA Ops:
  0.6 1.3 copy-start.1
  1.9 1.7 %copy-start = (bf16[2,128,5120]{2,1,0:T(8,128)(2,1)S(1)}, bf16[2,128,5120]{2,1,0:T(8,128)(2,1)}, u32[]{:S(2)}) copy-start(bf16[2,128,5120]{2,1,0:T(8,128)(2,1)} %param.6) | copy-start | bytes 7864324
  32.7 1.4 %copy-start.2 = (bf16[2,320,10]{1,0,2:T(2,128)(2,1)S(1)}, bf16[2,320,10]{1,0,2:T(2,128)(2,1)}, u32[]{:S(2)}) copy-start(bf16[2,320,10]{1,0,2:T(2,128)(2,1)} %param.7) | copy-start | bytes 38404
  32.8 3.2 %collective-permute-start = (bf16[16,160,128]{2,1,0:T(8,128)(2,1)S(1)}, bf16[16,160,128]{2,1,0:T(8,128)(2,1)S(1)}, u32[]{:S(2)}, u32[]{:S(2)}) collective-permute-start(bf16[16,160,128]{2,1,0:T(8,128)(2,1)S(1)} %peel.1), channel_id=1, source_target_pairs={{0,16},{16,0},{1,17},{17,1},{2,18},{18,2},{3,19},{19,3},{4,20},{20... | collective-permute-start | bytes 1966088 | tf_op jit(solution)/shard_map/ppermute | solution.py:407
  61.1 10.0 %collective-permute-start.1 = (f32[16,16]{1,0:T(8,128)S(1)}, f32[16,16]{1,0:T(8,128)S(1)}, u32[]{:S(2)}, u32[]{:S(2)}) collective-permute-start(f32[16,16]{1,0:T(8,128)S(1)} %get-tuple-element.29), channel_id=1, source_target_pairs={{0,0},{17,1},{34,2},{51,3},{68,4},{85,5},{102,6},{119,7},{136,8},{... | collective-permute-start | bytes 3080 | tf_op jit(solution)/shard_map/ppermute | solution.py:388
  98.1 2.4 %collective-permute-start.2 = (bf16[8,320,128]{2,1,0:T(8,128)(2,1)S(1)}, bf16[8,320,128]{2,1,0:T(8,128)(2,1)S(1)}, u32[]{:S(2)}, u32[]{:S(2)}) collective-permute-start(bf16[8,320,128]{2,1,0:T(8,128)(2,1)S(1)} %get-tuple-element.42), channel_id=1, source_target_pairs={{0,16},{16,0},{1,17},{17,1},{2,18},{18,2},{3,19},{19,3},{4,20},{20... | collective-permute-start | bytes 1966088 | tf_op jit(solution)/shard_map/ppermute | solution.py:449
  100.6 8.2 %collective-permute-start.3 = (bf16[2,320,128]{2,1,0:T(8,128)(2,1)S(1)}, bf16[2,320,128]{2,1,0:T(8,128)(2,1)S(1)}, u32[]{:S(2)}, u32[]{:S(2)}) collective-permute-start(bf16[2,320,128]{2,1,0:T(8,128)(2,1)S(1)} %get-tuple-element.44), channel_id=1, source_target_pairs={{0,32},{16,48},{32,64},{48,80},{64,96},{80,112},{96,128},{112,144}... | collective-permute-start | bytes 491528 | tf_op jit(solution)/shard_map/ppermute | solution.py:373
  101.7 7.9 %collective-permute-start.4 = (bf16[2,320,128]{2,1,0:T(8,128)(2,1)S(1)}, bf16[2,320,128]{2,1,0:T(8,128)(2,1)S(1)}, u32[]{:S(2)}, u32[]{:S(2)}) collective-permute-start(bf16[2,320,128]{2,1,0:T(8,128)(2,1)S(1)} %get-tuple-element.45), channel_id=1, source_target_pairs={{0,224},{16,240},{32,0},{48,16},{64,32},{80,48},{96,64},{112,80},{... | collective-permute-start | bytes 491528 | tf_op jit(solution)/shard_map/ppermute | solution.py:373
  104.4 8.0 %collective-permute-start.5 = (bf16[2,320,128]{2,1,0:T(8,128)(2,1)S(1)}, bf16[2,320,128]{2,1,0:T(8,128)(2,1)S(1)}, u32[]{:S(2)}, u32[]{:S(2)}) collective-permute-start(bf16[2,320,128]{2,1,0:T(8,128)(2,1)S(1)} %get-tuple-element.46), channel_id=1, source_target_pairs={{0,64},{16,208},{32,96},{48,240},{64,128},{80,16},{96,160},{112,48... | collective-permute-start | bytes 491528 | tf_op jit(solution)/shard_map/ppermute | solution.py:373
  112.5 13.6 %collective-permute-start.6 = (bf16[320,128]{1,0:T(8,128)(2,1)S(1)}, bf16[320,128]{1,0:T(8,128)(2,1)S(1)}, u32[]{:S(2)}, u32[]{:S(2)}) collective-permute-start(bf16[320,128]{1,0:T(8,128)(2,1)S(1)} %get-tuple-element.47), channel_id=1, source_target_pairs={{0,0},{1,17},{2,34},{3,51},{4,68},{5,85},{6,102},{7,119},{8,136},{... | collective-permute-start | bytes 245768 | tf_op jit(solution)/shard_map/ppermute | solution.py:383
  118.3 18.1 %collective-permute-start.7 = (bf16[320,128]{1,0:T(8,128)(2,1)S(1)}, bf16[320,128]{1,0:T(8,128)(2,1)S(1)}, u32[]{:S(2)}, u32[]{:S(2)}) collective-permute-start(bf16[320,128]{1,0:T(8,128)(2,1)S(1)} %get-tuple-element.48), channel_id=1, source_target_pairs={{0,8},{1,25},{2,42},{3,59},{4,76},{5,93},{6,110},{7,127},{8,128},{... | collective-permute-start | bytes 245768 | tf_op jit(solution)/shard_map/ppermute | solution.py:383

commit v11 on v10

--- a/solution.py
+++ b/solution.py
@@ -307,10 +307,21 @@
             gs_ref[here, s * rows : (s + 1) * rows] = value
 
 
-def parts_kernel(
-    width, gs_ref, grads_ref, m_ref, wt_ref, raw_ref, plan_ref, refs_ref,
-    p0, p1, p2, p3, other_ref, left_ref, right_ref, wide_ref,
-):
+def put_products(core, gs_ref, plan_ref, left_ref, right_ref, wide_ref):
+    z = lax.axis_index("z")
+    place = lax.axis_index("y") * SIDE + lax.axis_index("x")
+    rows = right_ref.shape[1] // DEPTH
+    for k in range(4):
+        for b in range(2):
+            step = jnp.where(core == 0, CHIPS[0][k], CHIPS[1][k]) + 4 * b
+            block = lax.bitwise_xor(2 * lax.rem(z + step, DEPTH) + core, place)
+            here = slice((2 * k + b) * rows, (2 * k + b + 1) * rows)
+            right_ref[:REFS, here] = gs_ref[:, lanes(block, rows)]
+            right_ref[REFS:, here] = plan_ref[:, lanes(block, rows)]
+    wide_ref[...] = lax.dot_general(left_ref[...], right_ref[...], TN, preferred_element_type=f32).astype(bf16)
+
+
+def away_kernel(width, gs_ref, grads_ref, m_ref, wt_ref, raw_ref, plan_ref, refs_ref, other_ref, left_ref, right_ref, wide_ref):
     rows = other_ref.shape[2]
     part = raw_ref.shape[1]
     size = float(P_SIZE)
@@ -324,22 +335,17 @@
         normed = jnp.sum(grads[:, :1] * wt_ref[h * PAD : (h + 1) * PAD, :].astype(f32), axis=0, keepdims=True) / size
         grad_raw = (inverse * (normed - raw_ref[here, :] * pull)).astype(bf16)
         left_ref[REFS + h * P_SIZE : REFS + (h + 1) * P_SIZE, :] = (size * grad_raw.astype(f32)).astype(bf16)
-    right_ref[:REFS, :] = gs_ref[...]
-    right_ref[REFS:, :] = plan_ref[...]
-    wide_ref[...] = lax.dot_general(left_ref[...], right_ref[...], TN, preferred_element_type=f32)
-    core, z = lax.axis_index("core"), lax.axis_index("z")
-    outs = (p0, p1, p2, p3)
-
-    def take(step, which):
-        block = lax.bitwise_xor(2 * lax.rem(z + step, DEPTH) + which, place)
-        return wide_ref[:, lanes(block, rows)].astype(bf16)
-
-    for k in range(4):
+    put_products(1 - lax.axis_index("core"), gs_ref, plan_ref, left_ref, right_ref, wide_ref)
+    for k in range(DEPTH):
+        other_ref[k] = wide_ref[:, k * rows : (k + 1) * rows]
+
+
+def mine_kernel(gs_ref, plan_ref, left_ref, p0, p1, p2, p3, right_ref, wide_ref):
+    rows = p0.shape[2]
+    put_products(lax.axis_index("core"), gs_ref, plan_ref, left_ref, right_ref, wide_ref)
+    for k, out in enumerate((p0, p1, p2, p3)):
         for b in range(2):
-            step = jnp.where(core == 0, CHIPS[0][k], CHIPS[1][k]) + 4 * b
-            outs[k][b] = take(step, core)
-            step = jnp.where(core == 0, CHIPS[1][k], CHIPS[0][k]) + 4 * b
-            other_ref[2 * k + b] = take(step, 1 - core)
+            out[b] = wide_ref[:, (2 * k + b) * rows : (2 * k + b + 1) * rows]
 
 
 def cores_kernel(p0, p1, p2, p3, other_ref, o0, o1, o2, o3):
@@ -437,16 +443,13 @@
             pltpu.VMEM((HEADS * BLOCKS, rows), f32),
         ],
     )(mixed, ts, rs, rt, col, moments, labels)
-    *mine, away = call(
-        functools.partial(parts_kernel, width), "parts", [pair] * 4 + [kind((DEPTH, part, rows), bf16)], 7,
-        scratch=[
-            pltpu.VMEM((2 * REFS, part), bf16),
-            pltpu.VMEM((2 * REFS, everything), bf16),
-            pltpu.VMEM((part, everything), f32),
-        ],
-        mib=12,
+    products_scratch = [pltpu.VMEM((2 * REFS, DEPTH * rows), bf16), pltpu.VMEM((part, DEPTH * rows), bf16)]
+    away, left = call(
+        functools.partial(away_kernel, width), "away", [kind((DEPTH, part, rows), bf16), kind((2 * REFS, part), bf16)], 7,
+        scratch=products_scratch,
     )(grad_scores, grads, moments, weights, raw, plan, refs)
     away = lax.ppermute(away, "core", [(0, 1), (1, 0)])
+    mine = call(mine_kernel, "mine", [pair] * 4, 3, scratch=products_scratch, flops=10**9)(grad_scores, plan, left)
     o = call(cores_kernel, "cores", [pair] * 4, 5)(*mine, away)
     o = [o[0]] + [along_z(o[k], k) for k in (1, 2, 3)]
     u = call(chips_kernel, "chips", [kind((part, rows), bf16)] * 2, 4)(*o)

time: 137 us -> 137 us (level)
  transfers between devices with their start and end apart: 8 -> 8, of which waited for: 6 -> 6; matrix products, arithmetic and copies ran while one was open for 0% -> 0% of each run, Pallas kernels for 2% -> 3%
where the time goes in v11:
time: 137 us; the launch traced here: 136 us
  blocking collectives  72.7 us (53%)
  starting transfers between devices  24.8 us (18%)
  waiting for transfers between devices  20.9 us (15%)
  Pallas kernels  13.6 us (10%)
  local copies, waits for them, and re-layouts  2.42 us (2%)
  between operations  2.09 us (2%)
    all_to_all x3, blocking collectives, exchange(): return lax.all_to_all(value, ('x', 'y'), 0, 0)  72.7 us
    ppermute x2, starting transfers between devices, to_place(): return lax.ppermute(value, ('z', 'core', 'y', 'x'), pairs)  12 us
    ppermute x2, waiting for transfers between devices, to_place(): return lax.ppermute(value, ('z', 'core', 'y', 'x'), pairs)  10.2 us
    ppermute x1, starting transfers between devices, spread_logits(): return lax.ppermute(value, ('z', 'core', 'y', 'x'), pairs)  8.65 us
    ppermute x3, waiting for transfers between devices, along_z(): return lax.ppermute(value, ('z', 'core'), pairs)  8.02 us
    pallas_call x1, Pallas kernels, local(): call(functools.partial(backward_kernel, width, score_scale), 'backward',...  3.99 us
    ppermute x3, starting transfers between devices, along_z(): return lax.ppermute(value, ('z', 'core'), pairs)  3.8 us
  transfers between devices with their start and end apart: 8, of which 6 were waited for; matrix products, arithmetic and copies ran while one was open for 0% of the time, Pallas kernels for 3%

profile of v11, /device:TPU:12, one launch (start us, length us, event | category | flops | bytes accessed | tf_op | source)
XLA Modules:
  0.0 136.5 jit_solution(9364456791896132593)
XLA Ops:
  0.6 1.3 copy-done.1
  1.9 0.6 split.1.half_ref
  2.6 1.1 copy-done
  3.7 0.9 scores.1
  4.6 28.2 %all_to_all.15.in_ref.q_ref.mixed_ref = bf16[16,416,128]{2,1,0:T(8,128)(2,1)S(1)} all-to-all(bf16[16,416,128]{2,1,0:T(8,128)(2,1)S(1)} %scores.1), channel_id=1, replica_groups=mesh['z'=8,'core'=2,'y'=4,'x'=4] {'x','y'}, dimensions={0} | all-to-all | bytes 3407872 | tf_op jit(solution)/shard_map/all_to_all | solution.py:56
  32.8 0.1 collective-permute-start
  34.2 1.7 %sinkhorn.1 = (f32[96,128]{1,0:T(8,128)S(1)}, f32[96,128]{1,0:T(8,128)S(1)}, f32[3,256,128]{2,1,0:T(8,128)S(1)}, bf16[256,2048]{1,0:T(8,128)(2,1)S(1)}) custom-call(bf16[16,416,128]{2,1,0:T(8,128)(2,1)S(1)} %all_to_all.15.in_ref.q_ref.mixed_ref, s32[1]{0:T(128)S(6)} %copy.10.len_ref, s32[1]{0:T(128)S(6)} %copy.11.label_ref), custom_call_target="tpu_custom_call" | custom-call | tf_op jit(solution)/shard_map/sinkhorn/pallas_call | solution.py:419
  36.0 0.0 collective-permute-done.other_ref
  36.0 1.7 %forward.1 = (bf16[16,304,128]{2,1,0:T(8,128)(2,1)S(1)}, f32[256,320]{1,0:T(8,128)S(1)}) custom-call(bf16[16,416,128]{2,1,0:T(8,128)(2,1)S(1)} %all_to_all.15.in_ref.q_ref.mixed_ref, bf16[16,160,128]{2,1,0:T(8,128)(2,1)S(1)} %collective-permute-done.other_ref, bf16[32,320]{1,0:T(8,128)(2,1)S(1)} %bitcast.13, bf16[256,2048]{1,0:T(8,128)(2,1)S(1)} %get-tuple-element.27.plan_ref), custom_call_target="tpu_custom_call" | custom-call | tf_op jit(solution)/shard_map/forward/pallas_call | solution.py:423
  37.7 23.2 %all_to_all.16.in_ref = bf16[16,304,128]{2,1,0:T(8,128)(2,1)S(1)} all-to-all(bf16[16,304,128]{2,1,0:T(8,128)(2,1)S(1)} %get-tuple-element.28), channel_id=1, replica_groups=mesh['z'=8,'core'=2,'y'=4,'x'=4] {'x','y'}, dimensions={0} | all-to-all | bytes 2490368 | tf_op jit(solution)/shard_map/all_to_all | solution.py:56
  60.9 0.2 sum.1
  61.0 8.7 %collective-permute-start.1 = (f32[16,16]{1,0:T(8,128)S(1)}, f32[16,16]{1,0:T(8,128)S(1)}, u32[]{:S(2)}, u32[]{:S(2)}) collective-permute-start(f32[16,16]{1,0:T(8,128)S(1)} %get-tuple-element.30), channel_id=1, source_target_pairs={{0,0},{17,1},{34,2},{51,3},{68,4},{85,5},{102,6},{119,7},{136,8},{... | collective-permute-start | bytes 3080 | tf_op jit(solution)/shard_map/ppermute | solution.py:394
  69.7 1.3 collective-permute-done.1.logit_ref
  71.0 0.2 row.1
  71.2 21.4 %all_to_all.17.t_ref = bf16[16,288,128]{2,1,0:T(8,128)(2,1)S(1)} all-to-all(bf16[16,288,128]{2,1,0:T(8,128)(2,1)S(1)} %row.1), channel_id=1, replica_groups=mesh['z'=8,'core'=2,'y'=4,'x'=4] {'x','y'}, dimensions={0} | all-to-all | bytes 2359296 | tf_op jit(solution)/shard_map/all_to_all | solution.py:56
  92.6 4.0 %backward.1 = (f32[1,16]{1,0:T(1,128)}, f32[16,128]{1,0:T(8,128)S(1)}, bf16[256,2048]{1,0:T(8,128)(2,1)S(1)}) custom-call(bf16[16,416,128]{2,1,0:T(8,128)(2,1)S(1)} %all_to_all.15.in_ref.q_ref.mixed_ref, bf16[16,288,128]{2,1,0:T(8,128)(2,1)S(1)} %all_to_all.17.t_ref, f32[96,128]{1,0:T(8,128)S(1)} %get-tuple-element.31.rs_ref, ...), custom_call_target="tpu_custom_call" | custom-call | tf_op jit(solution)/shard_map/backward/pallas_call | solution.py:436
  96.6 1.0 away.1
  97.5 0.3 collective-permute-start.2
  97.8 0.8 mine.1
  98.6 1.3 collective-permute-done.2.other_ref
  99.9 0.2 cores.1
  100.1 1.1 collective-permute-start.3
  101.2 2.7 %collective-permute-start.4 = (bf16[2,320,128]{2,1,0:T(8,128)(2,1)S(1)}, bf16[2,320,128]{2,1,0:T(8,128)(2,1)S(1)}, u32[]{:S(2)}, u32[]{:S(2)}) collective-permute-start(bf16[2,320,128]{2,1,0:T(8,128)(2,1)S(1)} %get-tuple-element.47), channel_id=1, source_target_pairs={{0,224},{16,240},{32,0},{48,16},{64,32},{80,48},{96,64},{112,80},{... | collective-permute-start | bytes 491528 | tf_op jit(solution)/shard_map/ppermute | solution.py:379
  103.9 4.4 %collective-permute-done.3.o1 = bf16[2,320,128]{2,1,0:T(8,128)(2,1)S(1)} collective-permute-done((bf16[2,320,128]{2,1,0:T(8,128)(2,1)S(1)}, bf16[2,320,128]{2,1,0:T(8,128)(2,1)S(1)}, u32[]{:S(2)}, u32[]{:S(2)}) %collective-permute-start.3) | collective-permute-done | bytes 163872 | tf_op jit(solution)/shard_map/ppermute | solution.py:379
  108.3 0.8 collective-permute-done.4.o2
  109.1 2.8 %collective-permute-done.5.o3 = bf16[2,320,128]{2,1,0:T(8,128)(2,1)S(1)} collective-permute-done((bf16[2,320,128]{2,1,0:T(8,128)(2,1)S(1)}, bf16[2,320,128]{2,1,0:T(8,128)(2,1)S(1)}, u32[]{:S(2)}, u32[]{:S(2)}) %collective-permute-start.5) | collective-permute-done | bytes 163872 | tf_op jit(solution)/shard_map/ppermute | solution.py:379
  111.9 0.1 chips.1
  112.0 5.7 %collective-permute-start.6 = (bf16[320,128]{1,0:T(8,128)(2,1)S(1)}, bf16[320,128]{1,0:T(8,128)(2,1)S(1)}, u32[]{:S(2)}, u32[]{:S(2)}) collective-permute-start(bf16[320,128]{1,0:T(8,128)(2,1)S(1)} %get-tuple-element.49), channel_id=1, source_target_pairs={{0,0},{1,17},{2,34},{3,51},{4,68},{5,85},{6,102},{7,119},{8,136},{... | collective-permute-start | bytes 245768 | tf_op jit(solution)/shard_map/ppermute | solution.py:389
  117.7 6.3 %collective-permute-start.7 = (bf16[320,128]{1,0:T(8,128)(2,1)S(1)}, bf16[320,128]{1,0:T(8,128)(2,1)S(1)}, u32[]{:S(2)}, u32[]{:S(2)}) collective-permute-start(bf16[320,128]{1,0:T(8,128)(2,1)S(1)} %get-tuple-element.50), channel_id=1, source_target_pairs={{0,8},{1,25},{2,42},{3,59},{4,76},{5,93},{6,110},{7,127},{8,128},{... | collective-permute-start | bytes 245768 | tf_op jit(solution)/shard_map/ppermute | solution.py:389
  124.0 1.6 %references.1 = f32[2,320,128]{2,1,0:T(8,128)} custom-call(bf16[256,2048]{1,0:T(8,128)(2,1)S(1)} %get-tuple-element.36.gs_ref, bf16[16,416,128]{2,1,0:T(8,128)(2,1)S(1)} %all_to_all.15.in_ref.q_ref.mixed_ref, bf16[16,160,128]{2,1,0:T(8,128)(2,1)S(1)} %collective-permute-done.other_ref), custom_call_target="tpu_custom_call" | custom-call | flops 335544320 | bytes 1048576 | tf_op jit(solution)/shard_map/references/pallas_call | solution.py:458
  125.6 10.2 %collective-permute-done.7.u1 = bf16[320,128]{1,0:T(8,128)(2,1)S(1)} collective-permute-done((bf16[320,128]{1,0:T(8,128)(2,1)S(1)}, bf16[320,128]{1,0:T(8,128)(2,1)S(1)}, u32[]{:S(2)}, u32[]{:S(2)}) %collective-permute-start.7) | collective-permute-done | bytes 81952 | tf_op jit(solution)/shard_map/ppermute | solution.py:389
  135.8 0.7 last.1
  (9 shorter events, 0.1 us)
Async XLA Ops:
  0.6 1.3 copy-start.1
  1.9 1.7 %copy-start = (bf16[2,128,5120]{2,1,0:T(8,128)(2,1)S(1)}, bf16[2,128,5120]{2,1,0:T(8,128)(2,1)}, u32[]{:S(2)}) copy-start(bf16[2,128,5120]{2,1,0:T(8,128)(2,1)} %param.6) | copy-start | bytes 7864324
  32.7 1.4 %copy-start.2 = (bf16[2,320,10]{1,0,2:T(2,128)(2,1)S(1)}, bf16[2,320,10]{1,0,2:T(2,128)(2,1)}, u32[]{:S(2)}) copy-start(bf16[2,320,10]{1,0,2:T(2,128)(2,1)} %param.7) | copy-start | bytes 38404
  32.8 3.2 %collective-permute-start = (bf16[16,160,128]{2,1,0:T(8,128)(2,1)S(1)}, bf16[16,160,128]{2,1,0:T(8,128)(2,1)S(1)}, u32[]{:S(2)}, u32[]{:S(2)}) collective-permute-start(bf16[16,160,128]{2,1,0:T(8,128)(2,1)S(1)} %peel.1), channel_id=1, source_target_pairs={{0,16},{16,0},{1,17},{17,1},{2,18},{18,2},{3,19},{19,3},{4,20},{20... | collective-permute-start | bytes 1966088 | tf_op jit(solution)/shard_map/ppermute | solution.py:413
  61.0 10.0 %collective-permute-start.1 = (f32[16,16]{1,0:T(8,128)S(1)}, f32[16,16]{1,0:T(8,128)S(1)}, u32[]{:S(2)}, u32[]{:S(2)}) collective-permute-start(f32[16,16]{1,0:T(8,128)S(1)} %get-tuple-element.30), channel_id=1, source_target_pairs={{0,0},{17,1},{34,2},{51,3},{68,4},{85,5},{102,6},{119,7},{136,8},{... | collective-permute-start | bytes 3080 | tf_op jit(solution)/shard_map/ppermute | solution.py:394
  97.5 2.4 %collective-permute-start.2 = (bf16[8,320,128]{2,1,0:T(8,128)(2,1)S(1)}, bf16[8,320,128]{2,1,0:T(8,128)(2,1)S(1)}, u32[]{:S(2)}, u32[]{:S(2)}) collective-permute-start(bf16[8,320,128]{2,1,0:T(8,128)(2,1)S(1)} %get-tuple-element.44), channel_id=1, source_target_pairs={{0,16},{16,0},{1,17},{17,1},{2,18},{18,2},{3,19},{19,3},{4,20},{20... | collective-permute-start | bytes 1966088 | tf_op jit(solution)/shard_map/ppermute | solution.py:451
  100.1 8.2 %collective-permute-start.3 = (bf16[2,320,128]{2,1,0:T(8,128)(2,1)S(1)}, bf16[2,320,128]{2,1,0:T(8,128)(2,1)S(1)}, u32[]{:S(2)}, u32[]{:S(2)}) collective-permute-start(bf16[2,320,128]{2,1,0:T(8,128)(2,1)S(1)} %get-tuple-element.46), channel_id=1, source_target_pairs={{0,32},{16,48},{32,64},{48,80},{64,96},{80,112},{96,128},{112,144}... | collective-permute-start | bytes 491528 | tf_op jit(solution)/shard_map/ppermute | solution.py:379
  101.2 7.9 %collective-permute-start.4 = (bf16[2,320,128]{2,1,0:T(8,128)(2,1)S(1)}, bf16[2,320,128]{2,1,0:T(8,128)(2,1)S(1)}, u32[]{:S(2)}, u32[]{:S(2)}) collective-permute-start(bf16[2,320,128]{2,1,0:T(8,128)(2,1)S(1)} %get-tuple-element.47), channel_id=1, source_target_pairs={{0,224},{16,240},{32,0},{48,16},{64,32},{80,48},{96,64},{112,80},{... | collective-permute-start | bytes 491528 | tf_op jit(solution)/shard_map/ppermute | solution.py:379
  103.9 8.0 %collective-permute-start.5 = (bf16[2,320,128]{2,1,0:T(8,128)(2,1)S(1)}, bf16[2,320,128]{2,1,0:T(8,128)(2,1)S(1)}, u32[]{:S(2)}, u32[]{:S(2)}) collective-permute-start(bf16[2,320,128]{2,1,0:T(8,128)(2,1)S(1)} %get-tuple-element.48), channel_id=1, source_target_pairs={{0,64},{16,208},{32,96},{48,240},{64,128},{80,16},{96,160},{112,48... | collective-permute-start | bytes 491528 | tf_op jit(solution)/shard_map/ppermute | solution.py:379
  112.0 13.6 %collective-permute-start.6 = (bf16[320,128]{1,0:T(8,128)(2,1)S(1)}, bf16[320,128]{1,0:T(8,128)(2,1)S(1)}, u32[]{:S(2)}, u32[]{:S(2)}) collective-permute-start(bf16[320,128]{1,0:T(8,128)(2,1)S(1)} %get-tuple-element.49), channel_id=1, source_target_pairs={{0,0},{1,17},{2,34},{3,51},{4,68},{5,85},{6,102},{7,119},{8,136},{... | collective-permute-start | bytes 245768 | tf_op jit(solution)/shard_map/ppermute | solution.py:389
  117.7 18.1 %collective-permute-start.7 = (bf16[320,128]{1,0:T(8,128)(2,1)S(1)}, bf16[320,128]{1,0:T(8,128)(2,1)S(1)}, u32[]{:S(2)}, u32[]{:S(2)}) collective-permute-start(bf16[320,128]{1,0:T(8,128)(2,1)S(1)} %get-tuple-element.50), channel_id=1, source_target_pairs={{0,8},{1,25},{2,42},{3,59},{4,76},{5,93},{6,110},{7,127},{8,128},{... | collective-permute-start | bytes 245768 | tf_op jit(solution)/shard_map/ppermute | solution.py:389
